TPU v7x, 32 devices: a whole 2x2x4 slice. The times are simulated.
32 devices in a mesh: grp: 2 (over y), seq: 4 (over z), rep: 4 (over x, core).
Axes of the slice: x: 2, y: 2, z: 4, core: 2. Of those that a mesh axis runs over, the one named last changes fastest.
Arguments:
- patches: bfloat16 [16, 384, 1024], P(('grp', 'rep'), 'seq'), parts along dimension 0, may hold values from -14 to 14, as said below
- kept_index: int32 [16, 384], P(('grp', 'rep'), 'seq'), parts along dimension 0, may hold values from 0 to 1023, as said below
- kept_count: int32 [16, 4], P(('grp', 'rep'), 'seq'), parts along dimension 0, may hold values from 48 to 96, as said below
- cotangent: bfloat16 [16, 384, 1024], P(('grp', 'rep'), 'seq'), parts along dimension 0, may hold values from -6 to 6
- w_qkv: bfloat16 [1024, 3072], replicated, may hold values from -1.3 to 1.3
- w_out: bfloat16 [1024, 1024], replicated, may hold values from -0.1875 to 0.1875
- gain: float32 [1024], replicated, may hold values from 0.1 to 1.9
Outputs:
- encoded: bfloat16 [16, 384, 1024], P(('grp', 'rep'), 'seq'), parts along dimension 0
- d_patches: bfloat16 [16, 384, 1024], P(('grp', 'rep'), 'seq'), parts along dimension 0
- d_w_qkv: float32 [2048, 3072], P('grp', 'seq'), parts along dimension 0
- d_w_out: float32 [2048, 1024], P('grp', 'seq'), parts along dimension 0
There are 2 independent parts, one for each index of `grp`. A program takes and returns all parts, laid end to end along the dimension named above; an argument that names none is the same for every part. Nothing has to cross between parts.
Inputs may be any that keep to these rules, and one draw needn't show every extreme that they name: `kept_count`: each shard keeps between half of its 96 slots and all of them; in every sample some shard fills all 96 slots. `kept_index`: slots of shard j hold distinct positions from j * 256 to (j + 1) * 256 - 1, ascending over the first kept_count slots; later slots hold unused positions of the shard. `patches`: slots past a shard's kept count hold arbitrary values.
All inputs are finite; a program needn't handle non-finite values.
Results may differ from a plain program's by a relative error of at most 0.007.
Values may be sent and summed in bfloat16 or wider, within the bound.
No kernel may reach another device: no remote copies, remote signals or barrier semaphores. Data moves between devices by JAX's collectives and lax.ppermute only.
A program may use at most 128 MiB of HBM per device.

v0:
```python
import jax
import jax.numpy as jnp
from jax import lax
from jax.sharding import PartitionSpec as P

HEADS = 16
GRID_COLS = 512


epsilon = 1e-06


def position_table(position, model_width):
    quarter = model_width // 4
    frequency = jnp.exp(-jnp.log(10000.0) * jnp.arange(quarter, dtype=jnp.float32) / quarter)
    grid_row = (position // GRID_COLS).astype(jnp.float32)
    grid_col = (position % GRID_COLS).astype(jnp.float32)
    row_phase = grid_row[..., None] * frequency
    col_phase = grid_col[..., None] * frequency
    return jnp.concatenate(
        [jnp.sin(row_phase), jnp.cos(row_phase), jnp.sin(col_phase), jnp.cos(col_phase)], axis=-1
    )


def normalize(hidden, gain):
    center = hidden - jnp.mean(hidden, axis=-1, keepdims=True)
    spread = jnp.mean(center * center, axis=-1, keepdims=True)
    inv_std = lax.rsqrt(spread + epsilon)
    unit_rows = center * inv_std
    return ((unit_rows * gain).astype(jnp.bfloat16), unit_rows, inv_std)


def norm_backward(d_normed, gain, unit_rows, inv_std):
    scaled = d_normed * gain
    return inv_std * (
        scaled
        - jnp.mean(scaled, axis=-1, keepdims=True)
        - unit_rows * jnp.mean(scaled * unit_rows, axis=-1, keepdims=True)
    )


def head_block(query_rows, grad_rows, key_rows, value_rows, live_keys, score_scale):
    scores = jnp.dot(query_rows, key_rows.T, preferred_element_type=jnp.float32) * score_scale
    scores = jnp.where(live_keys[None, :], scores, -1e30)
    top_score = jnp.max(scores, axis=1, keepdims=True)
    raised = jnp.exp(scores - top_score)
    probability = raised / jnp.sum(raised, axis=1, keepdims=True)
    rounded = probability.astype(jnp.bfloat16)
    attended = jnp.dot(rounded, value_rows, preferred_element_type=jnp.float32).astype(jnp.bfloat16)
    d_value = jnp.dot(rounded.T, grad_rows, preferred_element_type=jnp.float32)
    d_prob = jnp.dot(grad_rows, value_rows.T, preferred_element_type=jnp.float32)
    d_score = (
        probability * (d_prob - jnp.sum(probability * d_prob, axis=1, keepdims=True)) * score_scale
    ).astype(jnp.bfloat16)
    d_query = jnp.dot(d_score, key_rows, preferred_element_type=jnp.float32)
    d_key = jnp.dot(d_score.T, query_rows, preferred_element_type=jnp.float32)
    return (attended, d_query, d_key, d_value)


def attend(query_rows, grad_rows, key_rows, value_rows, live_keys, score_scale):
    row_count = query_rows.shape[0]
    blocks = max(1, row_count // 512)
    while row_count % blocks:
        blocks -= 1
    block_rows = row_count // blocks
    query_blocks = query_rows.reshape(blocks, block_rows, query_rows.shape[1])
    grad_blocks = grad_rows.reshape(blocks, block_rows, grad_rows.shape[1])

    def block_step(carry, pieces):
        key_total, value_total = carry
        attended, d_query, d_key, d_value = head_block(
            pieces[0], pieces[1], key_rows, value_rows, live_keys, score_scale
        )
        return ((key_total + d_key, value_total + d_value), (attended, d_query))

    empty = jnp.zeros(key_rows.shape, jnp.float32)
    (key_total, value_total), (attended, d_query) = lax.scan(
        block_step, (empty, empty), (query_blocks, grad_blocks)
    )
    return (attended.reshape(row_count, -1), d_query.reshape(row_count, -1), key_total, value_total)


def shards(patches, kept_index, kept_count, cotangent, w_qkv, w_out, gain):
    groups = lax.axis_size("seq")
    samples, slot_count, model_width = patches.shape
    head_size = model_width // HEADS
    per_device = max(1, HEADS // groups)
    splits = max(1, groups // HEADS)
    head_groups = groups // splits
    band_width = per_device * head_size
    part_rows = slot_count // splits
    slot_ids = jnp.arange(slot_count, dtype=jnp.int32)
    live_slots = slot_ids[None, :] < kept_count
    hidden = patches.astype(jnp.float32) + position_table(kept_index, model_width)
    normed, unit_rows, inv_std = normalize(hidden, gain)
    flat_normed = normed.reshape(samples * slot_count, model_width)
    packed = jnp.dot(flat_normed, w_qkv, preferred_element_type=jnp.float32).astype(jnp.bfloat16)
    packed = packed.reshape(samples, slot_count, 3 * model_width)
    live_grad = jnp.where(live_slots[:, :, None], cotangent, jnp.zeros_like(cotangent))
    flat_grad = live_grad.reshape(samples * slot_count, model_width)
    d_attended = jnp.dot(flat_grad, w_out.T, preferred_element_type=jnp.float32).astype(
        jnp.bfloat16
    )
    d_attended = d_attended.reshape(samples, slot_count, model_width)

    def to_owners(tensor_block):
        arranged = tensor_block.reshape(samples, splits, part_rows, head_groups, band_width)
        return arranged.transpose(3, 1, 0, 2, 4).reshape(groups, samples, part_rows, band_width)

    key_value_send = jnp.concatenate(
        [
            packed[:, :, model_width : 2 * model_width].reshape(
                samples, slot_count, head_groups, band_width
            ),
            packed[:, :, 2 * model_width :].reshape(samples, slot_count, head_groups, band_width),
        ],
        axis=3,
    )
    key_value_send = key_value_send.transpose(2, 0, 1, 3)
    key_value_send = jnp.broadcast_to(
        key_value_send[:, None], (head_groups, splits, samples, slot_count, 2 * band_width)
    )
    key_value_send = key_value_send.reshape(groups, samples, slot_count, 2 * band_width)
    got_query, got_grad, got_pair = (
        lax.all_to_all(
            to_owners(packed[:, :, :model_width]), "seq", split_axis=0, concat_axis=0, tiled=True
        ),
        lax.all_to_all(to_owners(d_attended), "seq", split_axis=0, concat_axis=0, tiled=True),
        lax.all_to_all(key_value_send, "seq", split_axis=0, concat_axis=0, tiled=True),
    )
    all_counts = lax.all_gather(kept_count, "seq", axis=1, tiled=True)
    live_keys = (slot_ids[None, None, :] < all_counts[:, :, None]).reshape(
        samples, groups * slot_count
    )

    def rows_by_head(tensor_block, row_count):
        arranged = tensor_block.transpose(1, 0, 2, 3).reshape(
            samples, groups * row_count, per_device, head_size
        )
        return arranged.transpose(0, 2, 1, 3)

    query_heads = rows_by_head(got_query, part_rows)
    grad_heads = rows_by_head(got_grad, part_rows)
    key_heads = rows_by_head(got_pair[..., :band_width], slot_count)
    value_heads = rows_by_head(got_pair[..., band_width:], slot_count)
    score_scale = head_size ** (-0.5)

    def one_head(query_rows, grad_rows, key_rows, value_rows, key_live):
        return attend(query_rows, grad_rows, key_rows, value_rows, key_live, score_scale)

    per_head = jax.vmap(one_head, in_axes=(0, 0, 0, 0, None))
    outputs, d_query, d_key, d_value = jax.vmap(per_head)(
        query_heads, grad_heads, key_heads, value_heads, live_keys
    )

    def back_to_sources(tensor_block, row_count):
        arranged = tensor_block.transpose(0, 2, 1, 3).reshape(
            samples, groups, row_count, band_width
        )
        return arranged.transpose(1, 0, 2, 3)

    query_send = back_to_sources(d_query, part_rows).astype(jnp.bfloat16)
    back_out, back_query = (
        lax.all_to_all(
            back_to_sources(outputs, part_rows), "seq", split_axis=0, concat_axis=0, tiled=True
        ),
        lax.all_to_all(query_send, "seq", split_axis=0, concat_axis=0, tiled=True),
    )
    key_value_grad = jnp.concatenate(
        [back_to_sources(d_key, slot_count), back_to_sources(d_value, slot_count)], axis=3
    )
    back_pair = lax.all_to_all(
        key_value_grad.astype(jnp.bfloat16), "seq", split_axis=0, concat_axis=0, tiled=True
    ).astype(key_value_grad.dtype)

    def from_owners(tensor_block):
        arranged = tensor_block.reshape(head_groups, splits, samples, part_rows, band_width)
        return arranged.transpose(2, 1, 3, 0, 4).reshape(samples, slot_count, model_width)

    attended = from_owners(back_out)
    summed_pair = jnp.sum(
        back_pair.reshape(head_groups, splits, samples, slot_count, 2 * band_width), axis=1
    )
    summed_pair = summed_pair.transpose(1, 2, 0, 3)
    key_grad_rows = (
        summed_pair[..., :band_width].reshape(samples, slot_count, model_width).astype(jnp.bfloat16)
    )
    value_grad_rows = (
        summed_pair[..., band_width:].reshape(samples, slot_count, model_width).astype(jnp.bfloat16)
    )
    d_packed = jnp.concatenate([from_owners(back_query), key_grad_rows, value_grad_rows], axis=2)
    flat_attended = attended.reshape(samples * slot_count, model_width)
    projected = jnp.dot(flat_attended, w_out, preferred_element_type=jnp.float32).reshape(
        samples, slot_count, model_width
    )
    encoded = jnp.where(live_slots[:, :, None], hidden + projected, 0.0).astype(jnp.bfloat16)
    flat_packed = d_packed.reshape(samples * slot_count, 3 * model_width)
    d_normed = jnp.dot(flat_packed, w_qkv.T, preferred_element_type=jnp.float32).reshape(
        samples, slot_count, model_width
    )
    d_hidden = norm_backward(d_normed, gain, unit_rows, inv_std)
    d_patches = jnp.where(
        live_slots[:, :, None], live_grad.astype(jnp.float32) + d_hidden, 0.0
    ).astype(jnp.bfloat16)
    columns = flat_grad
    out_part = lax.psum_scatter(
        jnp.dot(columns.T, flat_attended, preferred_element_type=jnp.float32),
        "seq",
        scatter_dimension=0,
        tiled=True,
    ).T
    my_columns = lax.all_to_all(flat_packed, "seq", split_axis=1, concat_axis=0, tiled=True)
    columns = my_columns
    qkv_part = jnp.dot(
        lax.all_gather(flat_normed, "seq", axis=0, tiled=True).T,
        columns,
        preferred_element_type=jnp.float32,
    )
    qkv_grad, out_grad = lax.psum((qkv_part, out_part), "rep")
    return (encoded, d_patches, qkv_grad, out_grad)


def solution(mesh):
    in_specs = (
        P(("grp", "rep"), "seq", None),
        P(("grp", "rep"), "seq"),
        P(("grp", "rep"), "seq"),
        P(("grp", "rep"), "seq", None),
        P(),
        P(),
        P(),
    )
    out_specs = (
        P(("grp", "rep"), "seq", None),
        P(("grp", "rep"), "seq", None),
        P("grp", "seq"),
        P("grp", "seq"),
    )
    return jax.shard_map(shards, mesh=mesh, in_specs=in_specs, out_specs=out_specs, check_vma=False)
```

profile of v0, /device:TPU:9, one launch (start us, length us, event | category | flops | bytes accessed | tf_op | source)
XLA Modules:
  0.0 351.3 jit_solution(6985804067993119079)
XLA Ops:
  11.8 4.3 %convolution_convert_fusion = bf16[192,3072]{1,0:T(8,128)(2,1)S(1)} fusion(bf16[192,1024]{1,0:T(8,128)(2,1)S(1)} %bitcast.187, bf16[1024,3072]{1,0:T(8,128)(2,1)} %param.11), kind=kOutput, calls=%fused_computation.9 | convolution fusion | flops 1208549376 | bytes 7864320 | tf_op jit(solution)/shard_map/dot_general | solution.py:97
  19.9 4.8 %all-to-all-start = ((bf16[4,2,96,256]{3,2,1,0:T(8,128)(2,1)}), bf16[4,2,96,256]{3,2,1,0:T(8,128)(2,1)S(1)}, u32[]{:S(2)}, u32[]{:S(2)}) async-start(bf16[4,2,96,256]{3,2,1,0:T(8,128)(2,1)} %copy.61), calls=%async_computation | async-start | bytes 786432 | tf_op jit(solution)/shard_map/all_to_all | solution.py:125
  32.8 6.9 %all-to-all-start.1 = ((bf16[4,2,96,512]{3,2,1,0:T(8,128)(2,1)}), bf16[4,2,96,512]{3,2,1,0:T(8,128)(2,1)}, u32[]{:S(2)}, u32[]{:S(2)}) async-start(bf16[4,2,96,512]{3,2,1,0:T(8,128)(2,1)} %copy.63), calls=%async_computation.1 | async-start | bytes 1572864 | tf_op jit(solution)/shard_map/all_to_all | solution.py:129
  40.4 24.6 %all-gather = s32[4,1,2]{2,1,0:T(1,128)S(1)} all-gather(s32[1,1,2]{2,1,0:T(1,128)S(1)} %bitcast.194), channel_id=1, replica_groups=mesh['grp'=2,'seq'=4,'rep'=4] {'seq'}, dimensions={0}, use_global_device_ids=true | all-gather | bytes 40 | tf_op jit(solution)/shard_map/all_gather | solution.py:131
  74.6 5.1 %fusion.87 = (f32[2,4,384]{2,1,0:T(4,128)S(1)}, f32[2,4,384,384]{2,3,1,0:T(8,128)}) fusion(pred[2,384]{1,0:T(4,128)(4,1)S(1)} %broadcast_compare_fusion, bf16[2,384,4,64]{1,3,2,0:T(8,128)(2,1)} %reshape.167, bf16[2,384,4,64]{1,3,2,0:T(8,128)(2,1)} %reshape.164), kind=kOutput, calls=%fused_computation.102 | convolution fusion | flops 155713920 | bytes 5518080 | tf_op jit(solution)/shard_map/vmap(vmap())/while/body/eval_jaxpr/sub | solution.py:46
  79.7 3.6 %fusion.46 = bf16[2,384,4,64]{1,3,2,0:T(8,128)(2,1)} fusion(bf16[2,384,4,64]{1,3,2,0:T(8,128)(2,1)S(1)} %copy-done.10, f32[2,4,384,384]{2,3,1,0:T(8,128)} %get-tuple-element.78, f32[2,4,384]{2,1,0:T(4,128)S(1)} %get-tuple-element.77), kind=kOutput, calls=%fused_computation.34 | convolution fusion | flops 153550848 | bytes 5517312 | tf_op jit(solution)/shard_map/vmap(vmap())/while/body/eval_jaxpr/dot_general | solution.py:49
  85.7 4.8 %all-to-all-start.2 = ((bf16[4,2,96,256]{3,2,1,0:T(8,128)(2,1)}), bf16[4,2,96,256]{3,2,1,0:T(8,128)(2,1)S(1)}, u32[]{:S(2)}, u32[]{:S(2)}) async-start(bf16[4,2,96,256]{3,2,1,0:T(8,128)(2,1)} %copy.67), calls=%async_computation.2 | async-start | bytes 786432 | tf_op jit(solution)/shard_map/all_to_all | solution.py:164
  92.5 4.6 %all-to-all-done.2 = bf16[4,2,96,256]{3,2,1,0:T(8,128)(2,1)S(1)} async-done(((bf16[4,2,96,256]{3,2,1,0:T(8,128)(2,1)}), bf16[4,2,96,256]{3,2,1,0:T(8,128)(2,1)S(1)}, u32[]{:S(2)}, u32[]{:S(2)}) %all-to-all-start.2) | async-done | bytes 393248 | tf_op jit(solution)/shard_map/all_to_all | solution.py:164
  99.2 3.8 %fusion.97 = f32[1024,1024]{1,0:T(8,128)} fusion(bf16[192,1024]{1,0:T(8,128)(2,1)} %bitcast.170, bf16[192,1024]{1,0:T(8,128)(2,1)S(1)} %bitcast.184), kind=kOutput, calls=%fused_computation.104 | convolution fusion | flops 402653184 | bytes 4980736 | tf_op jit(solution)/shard_map/dot_general | solution.py:207
  103.1 2.6 convolution_convert_fusion.1
  108.8 10.7 %all_to_all.49 = bf16[4,2,96,256]{3,2,1,0:T(8,128)(2,1)} all-to-all(bf16[4,2,96,256]{3,2,1,0:T(8,128)(2,1)S(1)} %bitcast.182), channel_id=1, replica_groups=mesh['grp'=2,'seq'=4,'rep'=4] {'seq'}, dimensions={0} | all-to-all | bytes 786432 | tf_op jit(solution)/shard_map/all_to_all | solution.py:128
  121.5 2.3 reshape.173
  123.8 4.1 %fusion.57 = f32[2,4,384,384]{2,3,1,0:T(8,128)} fusion(bf16[2,384,4,64]{1,3,2,0:T(8,128)(2,1)} %reshape.168, bf16[2,384,4,64]{1,3,2,0:T(8,128)(2,1)} %reshape.173), kind=kOutput, calls=%fused_computation.58 | convolution fusion | flops 150994944 | bytes 5505024 | tf_op jit(solution)/shard_map/vmap(vmap())/while/body/eval_jaxpr/dot_general | solution.py:51
  127.9 8.9 %fusion.42 = bf16[2,384,4,64]{1,3,2,0:T(8,128)(2,1)} fusion(f32[2,4,384,384]{2,3,1,0:T(8,128)} %fusion.57, bf16[2,384,4,64]{1,3,2,0:T(8,128)(2,1)} %reshape.167, f32[2,4,384,384]{2,3,1,0:T(8,128)} %get-tuple-element.78, f32[2,4,384]{2,1,0:T(4,128)S(1)} %get-tuple-element.77), kind=kOutput, calls=%fused_computation.32 | convolution fusion | flops 159452544 | bytes 10235904 | tf_op jit(solution)/shard_map/vmap(vmap())/while/body/eval_jaxpr/dot_general | solution.py:55
  136.7 2.1 convert_element_type.93
  141.0 5.4 %all-to-all-start.4 = ((bf16[4,2,96,256]{3,2,1,0:T(8,128)(2,1)}), bf16[4,2,96,256]{3,2,1,0:T(8,128)(2,1)}, u32[]{:S(2)}, u32[]{:S(2)}) async-start(bf16[4,2,96,256]{3,2,1,0:T(8,128)(2,1)} %copy.72), calls=%async_computation.4 | async-start | bytes 786432 | tf_op jit(solution)/shard_map/all_to_all | solution.py:167
  146.4 8.9 %fusion.39 = bf16[2,384,4,64]{1,3,2,0:T(8,128)(2,1)} fusion(f32[2,4,384,384]{2,3,1,0:T(8,128)} %fusion.57, bf16[2,384,4,64]{1,3,2,0:T(8,128)(2,1)} %reshape.164, f32[2,4,384,384]{2,3,1,0:T(8,128)} %get-tuple-element.78, f32[2,4,384]{2,1,0:T(4,128)S(1)} %get-tuple-element.77), kind=kOutput, calls=%fused_computation.31 | convolution fusion | flops 159452544 | bytes 10235904 | tf_op jit(solution)/shard_map/vmap(vmap())/while/body/eval_jaxpr/dot_general | solution.py:56
  155.3 2.2 reshape.175
  157.5 4.1 %fusion.45 = bf16[2,384,4,64]{1,3,2,0:T(8,128)(2,1)} fusion(bf16[2,384,4,64]{1,3,2,0:T(8,128)(2,1)} %reshape.173, f32[2,4,384,384]{2,3,1,0:T(8,128)} %get-tuple-element.78, f32[2,4,384]{2,1,0:T(4,128)S(1)} %get-tuple-element.77), kind=kOutput, calls=%fused_computation.33 | convolution fusion | flops 153550848 | bytes 5517312 | tf_op jit(solution)/shard_map/vmap(vmap())/while/body/eval_jaxpr/dot_general | solution.py:50
  161.6 2.1 reshape.176
  163.7 3.0 pad_maximum_fusion.1
  166.7 2.3 copy.76
  169.1 4.6 %all-to-all-start.5 = ((bf16[4,2,96,512]{3,2,1,0:T(8,128)(2,1)}), bf16[4,2,96,512]{3,2,1,0:T(8,128)(2,1)}, u32[]{:S(2)}, u32[]{:S(2)}) async-start(bf16[4,2,96,512]{3,2,1,0:T(8,128)(2,1)} %copy.76), calls=%async_computation.5 | async-start | bytes 1572864 | tf_op jit(solution)/shard_map/all_to_all | solution.py:172
  176.5 35.1 %all-to-all-done.5 = bf16[4,2,96,512]{3,2,1,0:T(8,128)(2,1)} async-done(((bf16[4,2,96,512]{3,2,1,0:T(8,128)(2,1)}), bf16[4,2,96,512]{3,2,1,0:T(8,128)(2,1)}, u32[]{:S(2)}, u32[]{:S(2)}) %all-to-all-start.5) | async-done | bytes 786464 | tf_op jit(solution)/shard_map/all_to_all | solution.py:172
  214.9 5.3 %all-to-all-start.6 = ((bf16[192,4,768]{2,0,1:T(8,128)(2,1)}), bf16[192,4,768]{2,0,1:T(8,128)(2,1)}, u32[]{:S(2)}, u32[]{:S(2)}) async-start(bf16[192,4,768]{2,0,1:T(8,128)(2,1)} %bitcast.164), calls=%async_computation.6 | async-start | bytes 2359296 | tf_op jit(solution)/shard_map/all_to_all | solution.py:212
  220.1 22.9 %all-to-all-done.6 = bf16[192,4,768]{2,0,1:T(8,128)(2,1)} async-done(((bf16[192,4,768]{2,0,1:T(8,128)(2,1)}), bf16[192,4,768]{2,0,1:T(8,128)(2,1)}, u32[]{:S(2)}, u32[]{:S(2)}) %all-to-all-start.6) | async-done | bytes 1179680 | tf_op jit(solution)/shard_map/all_to_all | solution.py:212
  243.0 4.8 %fusion.96 = f32[1024,768]{1,0:T(8,128)} fusion(bf16[768,1024]{1,0:T(8,128)(2,1)} %all-gather.3.cloned.1.call-done, bf16[768,768]{1,0:T(8,128)(2,1)} %bitcast.39), kind=kOutput, calls=%fused_computation.103 | convolution fusion | flops 1207959552 | bytes 5898240 | tf_op jit(solution)/shard_map/dot_general | solution.py:214
  250.9 2.4 fusion.36
  254.4 5.2 %fusion.83 = (f32[2,96]{1,0:T(2,128)S(1)}, f32[2,96]{1,0:T(2,128)S(1)}, f32[2,96,1024]{2,1,0:T(8,128)S(1)}) fusion(f32[2,96]{1,0:T(2,128)S(1)} %add_rsqrt_fusion, f32[2,96,1024]{2,1,0:T(8,128)S(1)} %get-tuple-element.61, f32[2,96]{1,0:T(2,128)S(1)} %broadcast_multiply_fusion.2, f32[1024]{0:T(1024)S(1)} %copy-done.12, bf16[1024,3072]{1,0:T(8,128)(2,1)} %param.11, ...), kind=kOutput, calls=%fused_computation.98 | convolution fusion | flops 1212677632 | bytes 9051136 | tf_op jit(solution)/shard_map/dot_general | solution.py:198
  260.8 77.7 %all-reduce.3.cloned.1.call-done = (f32[1024,768]{1,0:T(8,128)}, f32[1024,256]{0,1:T(8,128)}) async-done(((f32[1024,768]{1,0:T(8,128)}, f32[1024,256]{0,1:T(8,128)}), (f32[1024,768]{1,0:T(8,128)}, f32[1024,256]{0,1:T(8,128)})) %all-reduce.3.cloned.1.call-update) | async-done | bytes 4194320 | tf_op jit(solution)/shard_map/psum | solution.py:219
  338.5 2.5 copy.84
  341.0 3.8 %copy.102 = f32[1024,768]{1,0:T(8,128)} copy(f32[1024,768]{1,0:T(8,128)} %get-tuple-element.84) | data formatting | bytes 6291456
  (92 shorter events, 51.8 us)
Async XLA Ops:
  7.2 95.9 %copy-start = (bf16[1024,1024]{1,0:T(8,128)(2,1)S(1)}, bf16[1024,1024]{1,0:T(8,128)(2,1)}, u32[]{:S(2)}) copy-start(bf16[1024,1024]{1,0:T(8,128)(2,1)} %param.12) | copy-start | bytes 6291460
  11.8 4.3 %copy-start.8 = (bf16[2,96,1024]{2,1,0:T(8,128)(2,1)}, bf16[2,96,1024]{2,1,0:T(8,128)(2,1)S(1)}, u32[]{:S(2)}) copy-start(bf16[2,96,1024]{2,1,0:T(8,128)(2,1)S(1)} %multiply_convert_fusion.1) | copy-start | bytes 1179652
  17.1 23.3 %copy-start.13 = (s32[2,1]{0,1:T(1,128)S(1)}, s32[2,1]{0,1:T(1,128)}, u32[]{:S(2)}) copy-start(s32[2,1]{0,1:T(1,128)} %param.9) | copy-start | bytes 28
  19.9 12.9 %all-to-all-start = ((bf16[4,2,96,256]{3,2,1,0:T(8,128)(2,1)}), bf16[4,2,96,256]{3,2,1,0:T(8,128)(2,1)S(1)}, u32[]{:S(2)}, u32[]{:S(2)}) async-start(bf16[4,2,96,256]{3,2,1,0:T(8,128)(2,1)} %copy.61), calls=%async_computation | async-start | bytes 786432 | tf_op jit(solution)/shard_map/all_to_all | solution.py:125
  32.8 32.6 %copy-start.5 = (bf16[4,2,96,256]{3,2,1,0:T(8,128)(2,1)}, bf16[4,2,96,256]{3,2,1,0:T(8,128)(2,1)S(1)}, u32[]{:S(2)}) copy-start(bf16[4,2,96,256]{3,2,1,0:T(8,128)(2,1)S(1)} %all-to-all-done) | copy-start | bytes 1179652
  32.8 35.0 %all-to-all-start.1 = ((bf16[4,2,96,512]{3,2,1,0:T(8,128)(2,1)}), bf16[4,2,96,512]{3,2,1,0:T(8,128)(2,1)}, u32[]{:S(2)}, u32[]{:S(2)}) async-start(bf16[4,2,96,512]{3,2,1,0:T(8,128)(2,1)} %copy.63), calls=%async_computation.1 | async-start | bytes 1572864 | tf_op jit(solution)/shard_map/all_to_all | solution.py:129
  39.7 180.4 %all-gather.3.cloned.1.call-start = ((), (), s32[]{:S(2)}) async-start(), calls=%async_computation.8 | async-start | bytes 1966080 | tf_op jit(solution)/shard_map/all_gather | solution.py:215
  74.6 5.1 %copy-start.10 = (bf16[2,384,4,64]{1,3,2,0:T(8,128)(2,1)S(1)}, bf16[2,384,4,64]{1,3,2,0:T(8,128)(2,1)}, u32[]{:S(2)}) copy-start(bf16[2,384,4,64]{1,3,2,0:T(8,128)(2,1)} %reshape.168) | copy-start | bytes 1179652
  85.7 11.4 %all-to-all-start.2 = ((bf16[4,2,96,256]{3,2,1,0:T(8,128)(2,1)}), bf16[4,2,96,256]{3,2,1,0:T(8,128)(2,1)S(1)}, u32[]{:S(2)}, u32[]{:S(2)}) async-start(bf16[4,2,96,256]{3,2,1,0:T(8,128)(2,1)} %copy.67), calls=%async_computation.2 | async-start | bytes 786432 | tf_op jit(solution)/shard_map/all_to_all | solution.py:164
  90.6 157.3 %reduce-scatter.2.cloned.1.call-start = ((), (), s32[]{:S(2)}) async-start(), calls=%async_computation.9 | async-start | bytes 5242880 | tf_op jit(solution)/shard_map/reduce_scatter | solution.py:206
  97.1 0.7 copy-start.7
  141.0 28.1 %all-to-all-start.4 = ((bf16[4,2,96,256]{3,2,1,0:T(8,128)(2,1)}), bf16[4,2,96,256]{3,2,1,0:T(8,128)(2,1)}, u32[]{:S(2)}, u32[]{:S(2)}) async-start(bf16[4,2,96,256]{3,2,1,0:T(8,128)(2,1)} %copy.72), calls=%async_computation.4 | async-start | bytes 786432 | tf_op jit(solution)/shard_map/all_to_all | solution.py:167
  169.1 42.5 %all-to-all-start.5 = ((bf16[4,2,96,512]{3,2,1,0:T(8,128)(2,1)}), bf16[4,2,96,512]{3,2,1,0:T(8,128)(2,1)}, u32[]{:S(2)}, u32[]{:S(2)}) async-start(bf16[4,2,96,512]{3,2,1,0:T(8,128)(2,1)} %copy.76), calls=%async_computation.5 | async-start | bytes 1572864 | tf_op jit(solution)/shard_map/all_to_all | solution.py:172
  174.9 0.7 copy-start.1
  211.6 2.1 copy-start.6
  212.8 0.8 copy-start.2
  212.8 0.9 copy-start.4
  214.9 28.1 %all-to-all-start.6 = ((bf16[192,4,768]{2,0,1:T(8,128)(2,1)}), bf16[192,4,768]{2,0,1:T(8,128)(2,1)}, u32[]{:S(2)}, u32[]{:S(2)}) async-start(bf16[192,4,768]{2,0,1:T(8,128)(2,1)} %bitcast.164), calls=%async_computation.6 | async-start | bytes 2359296 | tf_op jit(solution)/shard_map/all_to_all | solution.py:212
  220.1 118.4 %all-reduce.3.cloned.1.call-start = ((), (), s32[]{:S(2)}) async-start(), calls=%async_computation.10 | async-start | bytes 8388608 | tf_op jit(solution)/shard_map/psum | solution.py:219
  247.8 6.6 %copy-start.12 = (f32[1024]{0:T(1024)S(1)}, f32[1024]{0:T(1024)}, u32[]{:S(2)}) copy-start(f32[1024]{0:T(1024)} %param.13) | copy-start | bytes 12292
  250.9 3.4 copy-start.3
  250.9 3.5 copy-start.11
  254.4 5.2 %copy-start.9 = (bf16[2,96,1024]{2,1,0:T(8,128)(2,1)S(1)}, bf16[2,96,1024]{2,1,0:T(8,128)(2,1)}, u32[]{:S(2)}) copy-start(bf16[2,96,1024]{2,1,0:T(8,128)(2,1)} %param.10) | copy-start | bytes 1179652
Sparse Core Ops, SparseCore 0:
  42.1 41.3 all-gather.2
  103.2 116.5 reduce-scatter.1
  248.0 90.4 all-reduce.2
where the time goes:
time: 355 us; the launch traced here: 351 us
  waiting for transfers between devices  143 us (40%)
  matrix products  57.9 us (16%)
  local copies, waits for them, and re-layouts  57.6 us (16%)
  blocking collectives  35.3 us (10%)
  starting transfers between devices  31.7 us (9%)
  between operations  14 us (4%)
  other arithmetic  12.2 us (3%)
    psum x1, waiting for transfers between devices, shards(): qkv_grad, out_grad = lax.psum((qkv_part, out_part), 'rep')  77.7 us
    all_to_all x1, waiting for transfers between devices, shards(): lax.all_to_all(key_value_grad.astype(jnp.bfloat16), 'seq', split_axis=0,...  35.1 us
    all_gather x1, blocking collectives, shards(): all_counts = lax.all_gather(kept_count, 'seq', axis=1, tiled=True)  24.6 us
    all_to_all x1, waiting for transfers between devices, shards(): lax.all_to_all(flat_packed, 'seq', split_axis=1, concat_axis=0, tiled=True)  22.9 us
    all_to_all x1, blocking collectives, shards(): lax.all_to_all(to_owners(d_attended), 'seq', split_axis=0, concat_axis=0,...  10.7 us
    dot_general x1, matrix products, head_block(): d_key = jnp.dot(d_score.T, query_rows, preferred_element_type=jnp.float32)  8.91 us
    unnamed x34, local copies, waits for them, and re-layouts  8.91 us
    dot_general x1, matrix products, head_block(): d_query = jnp.dot(d_score, key_rows, preferred_element_type=jnp.float32)  8.88 us
  transfers between devices with their start and end apart: 9, of which 5 were waited for; matrix products, arithmetic and copies ran while one was open for 30% of the time, Pallas kernels for 0%

commit v1 on v0

--- a/solution.py
+++ b/solution.py
@@ -1,6 +1,11 @@
+import functools
+
 import jax
 import jax.numpy as jnp
+import numpy as np
 from jax import lax
+from jax.experimental import pallas as pl
+from jax.experimental.pallas import tpu as pltpu
 from jax.sharding import PartitionSpec as P
 
 HEADS = 16
@@ -220,6 +225,473 @@
     return (encoded, d_patches, qkv_grad, out_grad)
 
 
+AXES = ("seq", "rep")
+MARK = 1024.0
+VMEM = 40 * 1024 * 1024
+
+
+def line_perm(move, reps):
+    pairs = []
+    for z in range(4):
+        for rep in range(reps):
+            x, c = rep // 2, rep % 2
+            to_x, to_c, to_z = move(x, c, z)
+            pairs.append((z * reps + rep, to_z * reps + 2 * to_x + to_c))
+    return pairs
+
+
+def sine_cosine(phase):
+    turns = jnp.floor(phase * np.float32(2.0 / np.pi) + 0.5)
+    rest = phase - turns * np.float32(1.5703125)
+    rest = rest - turns * np.float32(4.837512969970703125e-4)
+    rest = rest - turns * np.float32(7.54978995489188216e-8)
+    square = rest * rest
+    sine = rest + rest * square * (
+        np.float32(-1.6666654611e-1)
+        + square * (np.float32(8.3321608736e-3) + square * np.float32(-1.9515295891e-4))
+    )
+    cosine = (
+        1.0
+        - 0.5 * square
+        + square
+        * square
+        * (
+            np.float32(4.166664568298827e-2)
+            + square * (np.float32(-1.388731625493765e-3) + square * np.float32(2.443315711809948e-5))
+        )
+    )
+    quadrant = turns.astype(jnp.int32) & 3
+    swap = (quadrant & 1) == 1
+    first = jnp.where(swap, cosine, sine)
+    second = jnp.where(swap, sine, cosine)
+    first = jnp.where(quadrant >= 2, -first, first)
+    second = jnp.where((quadrant == 1) | (quadrant == 2), -second, second)
+    return first, second
+
+
+def live_column(count, rows):
+    return lax.broadcasted_iota(jnp.int32, (rows, 1), 0) < count
+
+
+def grad_kernel(place, count_ref, cot_ref, *grad_refs):
+    par = place[0]
+    for k in range(2):
+        s = k ^ par
+        live = live_column(count_ref[s, 0], cot_ref.shape[1])
+        grad = cot_ref[s]
+        grad_refs[k][...] = jnp.where(live, grad, jnp.zeros_like(grad))
+
+
+def norm_kernel(place, count_ref, patch_ref, index_ref, freq_ref, gain_ref, n0_ref, n1_ref, hidden_ref):
+    par = place[0]
+    rows = patch_ref.shape[1]
+    width = patch_ref.shape[2]
+    freq = freq_ref[...]
+    for k, out_ref in enumerate((n0_ref, n1_ref)):
+        s = k ^ par
+        position = index_ref[s]
+        grid_row = (position // GRID_COLS).astype(jnp.float32)
+        grid_col = (position % GRID_COLS).astype(jnp.float32)
+        pieces = sine_cosine(grid_row * freq) + sine_cosine(grid_col * freq)
+        table = jnp.concatenate(pieces, axis=1)
+        hidden = patch_ref[s].astype(jnp.float32) + table
+        hidden_ref[k] = hidden
+        center = hidden - jnp.mean(hidden, axis=-1, keepdims=True)
+        spread = jnp.mean(center * center, axis=-1, keepdims=True)
+        normed = center * lax.rsqrt(spread + epsilon) * gain_ref[...]
+        live = live_column(count_ref[s, 0], rows)
+        out_ref[...] = jnp.where(live, normed, MARK).astype(out_ref.dtype)
+
+
+def dot_nn(a, b):
+    return jnp.dot(a, b, preferred_element_type=jnp.float32)
+
+
+def dot_nt(a, b):
+    return lax.dot_general(a, b, (((1,), (1,)), ((), ())), preferred_element_type=jnp.float32)
+
+
+def dot_tn(a, b):
+    return lax.dot_general(a, b, (((0,), (0,)), ((), ())), preferred_element_type=jnp.float32)
+
+
+def attend_kernel(
+    place, n0, n1, n2, n3, g0, g1, g2, g3, wq, wk, wv, wo,
+    att_own, att_oth, dp_own, dp_oth, dwo_send, dwo_keep,
+    norm_s, grad_s, bias_s,
+):
+    step = pl.program_id(0)
+    block = n0.shape[0]
+    rows = 4 * block
+    half = 2 * block
+
+    @pl.when(step == 0)
+    def _():
+        for i, (n_ref, g_ref) in enumerate(((n0, g0), (n1, g1), (n2, g2), (n3, g3))):
+            at = pl.ds(i * block, block)
+            value = n_ref[...]
+            live = value[:, 0:1].astype(jnp.float32) < MARK
+            norm_s[at, :] = jnp.where(live, value, jnp.zeros_like(value))
+            bias_s[at, :] = jnp.where(live, 0.0, -1e30) + jnp.zeros((block, 128), jnp.float32)
+            grad_s[at, :] = g_ref[...]
+
+    normed = norm_s[...]
+    grads = grad_s[...]
+    bias = bias_s[:, 0:1]
+    queries = dot_nn(normed, wq[...]).astype(jnp.bfloat16)
+    keys = dot_nn(normed, wk[...]).astype(jnp.bfloat16)
+    values = dot_nn(normed, wv[...]).astype(jnp.bfloat16)
+    d_att = dot_nt(grads, wo[...]).astype(jnp.bfloat16)
+    low = lax.broadcasted_iota(jnp.int32, (rows, 128), 1) < 64
+    scale = jnp.bfloat16(0.125)
+    zero = jnp.zeros((rows, 128), jnp.bfloat16)
+    for pair in range(wq.shape[1] // 128):
+        cols = slice(128 * pair, 128 * pair + 128)
+        q = queries[:, cols] * scale
+        k = keys[:, cols]
+        v = values[:, cols]
+        g = d_att[:, cols]
+        v_t = v.T
+        k_t = (k * scale).T
+        att_t, dq_t, dk, dv = [], [], [], []
+        for h in range(2):
+            mine = low if h == 0 else jnp.logical_not(low)
+            scores = dot_nt(k, jnp.where(mine, q, zero)) + bias
+            raised = jnp.exp(scores - jnp.max(scores, axis=0, keepdims=True))
+            prob = raised * (1.0 / jnp.sum(raised, axis=0, keepdims=True))
+            weights = prob.astype(jnp.bfloat16)
+            part = slice(64 * h, 64 * h + 64)
+            att_t.append(dot_nn(v_t[part], weights))
+            dv.append(dot_nn(weights, g))
+            d_prob = dot_nt(v, jnp.where(mine, g, zero))
+            total = jnp.sum(prob * d_prob, axis=0, keepdims=True)
+            d_score = (prob * (d_prob - total)).astype(jnp.bfloat16)
+            dq_t.append(dot_nn(k_t[part], d_score))
+            dk.append(dot_nn(d_score, q))
+        att_pair_t = jnp.concatenate(att_t, axis=0).astype(jnp.bfloat16)
+        att_pair = att_pair_t.T
+        dq_pair = jnp.concatenate(dq_t, axis=0).astype(jnp.bfloat16).T
+        dk_pair = jnp.where(low, dk[0], dk[1]).astype(jnp.bfloat16)
+        dv_pair = jnp.where(low, dv[0], dv[1]).astype(jnp.bfloat16)
+        att_own[:, cols] = att_pair[:half]
+        att_oth[:, cols] = att_pair[half:]
+        for t, piece in enumerate((dq_pair, dk_pair, dv_pair)):
+            dp_own[t, :, cols] = piece[:half]
+            dp_oth[t, :, cols] = piece[half:]
+        d_out = dot_nn(att_pair_t, grads).astype(jnp.bfloat16)
+
+        @pl.when(step == 0)
+        def _():
+            dwo_send[cols, :] = d_out
+
+        @pl.when(step == 1)
+        def _():
+            dwo_keep[cols, :] = d_out
+
+
+def pack_kernel(place, own, got, s0, s1, s2, s3, rows_ref):
+    c, z = place[1], place[2]
+    width = own.shape[2]
+    mine_low = c == 0
+    for t in range(3):
+        a, b = own[t], got[t]
+        rows_ref[:, 2 * t * width : (2 * t + 1) * width] = jnp.where(mine_low, a, b)
+        rows_ref[:, (2 * t + 1) * width : (2 * t + 2) * width] = jnp.where(mine_low, b, a)
+    slab = s0.shape[1]
+    for k, out in enumerate((s0, s1, s2, s3)):
+        out[...] = rows_ref[:, pl.ds(pl.multiple_of((z ^ k) * slab, 128), slab)]
+
+
+def d_normed_kernel(rows_ref, w_ref, o0, o1, total):
+    step = pl.program_id(0)
+    term = dot_nt(rows_ref[...], w_ref[...])
+
+    @pl.when(step == 0)
+    def _():
+        total[...] = term
+
+    @pl.when(step > 0)
+    def _():
+        total[...] += term
+
+    @pl.when(step == pl.num_programs(0) - 1)
+    def _():
+        half = o0.shape[0]
+        o0[...] = total[:half].astype(o0.dtype)
+        o1[...] = total[half:].astype(o1.dtype)
+
+
+def encode_kernel(place, count_ref, a0, a1, b0, b1, w_ref, hidden_ref, out_ref):
+    par, half = place[0], place[2] // 2
+    width = a0.shape[1]
+    w_own = w_ref[pl.ds(pl.multiple_of(half * width, width), width), :]
+    w_oth = w_ref[pl.ds(pl.multiple_of((1 - half) * width, width), width), :]
+    for k, (a, b) in enumerate(((a0, b0), (a1, b1))):
+        s = k ^ par
+        projected = dot_nn(a[...], w_own) + dot_nn(b[...], w_oth)
+        live = live_column(count_ref[s, 0], a.shape[0])
+        out_ref[s] = jnp.where(live, hidden_ref[k] + projected, 0.0).astype(out_ref.dtype)
+
+
+def patch_grad_kernel(place, count_ref, d0, d1, g0, g1, hidden_ref, gain_ref, out_ref):
+    par = place[0]
+    for k, (d_ref, g_ref) in enumerate(((d0, g0), (d1, g1))):
+        s = k ^ par
+        hidden = hidden_ref[k]
+        center = hidden - jnp.mean(hidden, axis=-1, keepdims=True)
+        spread = jnp.mean(center * center, axis=-1, keepdims=True)
+        inv_std = lax.rsqrt(spread + epsilon)
+        unit = center * inv_std
+        d_hidden = norm_backward(d_ref[...].astype(jnp.float32), gain_ref[...], unit, inv_std)
+        live = live_column(count_ref[s, 0], hidden.shape[0])
+        value = g_ref[...].astype(jnp.float32) + d_hidden
+        out_ref[s] = jnp.where(live, value, 0.0).astype(out_ref.dtype)
+
+
+def weight_kernel(place, normed_ref, s0, s1, s2, s3, send_ref, pass_ref, keep_ref, total):
+    step = pl.program_id(0)
+    z = place[2]
+    rows = s0.shape[0]
+    total[...] = jnp.zeros_like(total)
+    for k, slab in enumerate((s0, s1, s2, s3)):
+        total[...] += dot_tn(normed_ref[z ^ k], slab[...])
+
+    @pl.when(step == 0)
+    def _():
+        send_ref[0] = total[...].astype(send_ref.dtype)
+
+    @pl.when(step == 1)
+    def _():
+        send_ref[1] = total[...].astype(send_ref.dtype)
+
+    @pl.when(step == 2)
+    def _():
+        pass_ref[...] = total[...]
+
+    @pl.when(step == 3)
+    def _():
+        keep_ref[...] = total[...]
+
+
+def finish_kernel(place, a, b, c, d, out_ref):
+    step = pl.program_id(0)
+    for i, ref in enumerate((a, b, c, d)):
+
+        @pl.when(step == i)
+        def _():
+            out_ref[...] = ref[...].astype(out_ref.dtype)
+
+
+def whole(shape):
+    return pl.BlockSpec(shape, lambda *_: (0,) * len(shape))
+
+
+def call(kernel, place, args, specs, outs, out_specs, grid=(1,), scratch=(), cost=None):
+    return pl.pallas_call(
+        kernel,
+        out_shape=outs,
+        grid_spec=pltpu.PrefetchScalarGridSpec(
+            num_scalar_prefetch=1,
+            grid=grid,
+            in_specs=specs,
+            out_specs=out_specs,
+            scratch_shapes=list(scratch),
+        ),
+        compiler_params=pltpu.CompilerParams(vmem_limit_bytes=VMEM),
+        cost_estimate=cost,
+    )(place, *args)
+
+
+SMEM_SPEC = pl.BlockSpec(memory_space=pltpu.SMEM)
+
+
+def struct(shape, dtype):
+    return jax.ShapeDtypeStruct(shape, dtype)
+
+
+def chip_shards(patches, kept_index, kept_count, cotangent, w_qkv, w_out, gain):
+    bf16, f32 = jnp.bfloat16, jnp.float32
+    samples, slots, width = patches.shape
+    reps = lax.axis_size("rep")
+    rep = lax.axis_index("rep")
+    z = lax.axis_index("seq")
+    c, x = rep % 2, rep // 2
+    place = jnp.stack([z % 2, c, z, x]).astype(jnp.int32)
+    own_width = width // 2
+    quarter = width // 4
+    slab = 3 * width // 4
+
+    def send(value, move):
+        return lax.ppermute(value, AXES, line_perm(move, reps))
+
+    def to_core(value):
+        return send(value, lambda x, c, z: (x, 1 - c, z))
+
+    def to_x(value):
+        return send(value, lambda x, c, z: (1 - x, c, z))
+
+    def to_chip(value, k):
+        return send(value, lambda x, c, z: (x, z >> 1, 2 * c + (k ^ (z & 1))))
+
+    def to_rows(value, k, other):
+        return send(value, lambda x, c, z: (x, z >> 1, 2 * (c ^ other) + (k ^ (z & 1))))
+
+    def along(value, k):
+        return send(value, lambda x, c, z: (x, c, z ^ k))
+
+    block = (slots, width)
+    block_spec = whole(block)
+    block_out = struct(block, bf16)
+    all_spec = whole((samples, slots, width))
+
+    grad = call(
+        grad_kernel, place, (kept_count, cotangent), [SMEM_SPEC, all_spec], [block_out] * 2, [block_spec] * 2
+    )
+    frequency = jnp.exp(-jnp.log(10000.0) * jnp.arange(width // 4, dtype=f32) / (width // 4))
+    gain_row = gain.reshape(1, width)
+    n0, n1, hidden = call(
+        norm_kernel,
+        place,
+        (kept_count, patches, kept_index.reshape(samples, slots, 1), frequency.reshape(1, -1), gain_row),
+        [SMEM_SPEC, all_spec, whole((samples, slots, 1)), whole((1, width // 4)), whole((1, width))],
+        [block_out, block_out, struct(patches.shape, f32)],
+        [block_spec, block_spec, all_spec],
+    )
+    got_g = [to_chip(grad[k], k) for k in range(2)]
+    got_n = [to_chip(n, k) for k, n in enumerate((n0, n1))]
+    oth_g = [to_core(v) for v in got_g]
+    oth_n = [to_core(v) for v in got_n]
+
+    heads = quarter
+
+    def head_block(step, place):
+        return 2 * place[1] + (place[3] ^ (1 - step))
+
+    def col_block(step, place):
+        return place[3] ^ (1 - step)
+
+    w_specs = [
+        pl.BlockSpec((width, heads), lambda i, p, t=t: (0, 4 * t + head_block(i, p))) for t in range(3)
+    ] + [pl.BlockSpec((heads, width), lambda i, p: (head_block(i, p), 0))]
+    rows2 = 2 * slots
+    att_spec = pl.BlockSpec((rows2, heads), lambda i, p: (0, col_block(i, p)))
+    dp_spec = pl.BlockSpec((3, rows2, heads), lambda i, p: (0, 0, col_block(i, p)))
+    att_out = struct((rows2, own_width), bf16)
+    dp_out = struct((3, rows2, own_width), bf16)
+    dwo_out = struct((heads, width), bf16)
+    att_own, att_oth, dp_own, dp_oth, dwo_send, dwo_keep = call(
+        attend_kernel,
+        place,
+        (*got_n, *oth_n, *got_g, *oth_g, w_qkv, w_qkv, w_qkv, w_out),
+        [block_spec] * 8 + w_specs,
+        [att_out, att_out, dp_out, dp_out, dwo_out, dwo_out],
+        [att_spec, att_spec, dp_spec, dp_spec, whole((heads, width)), whole((heads, width))],
+        grid=(2,),
+        scratch=[
+            pltpu.VMEM((4 * slots, width), bf16),
+            pltpu.VMEM((4 * slots, width), bf16),
+            pltpu.VMEM((4 * slots, 128), f32),
+        ],
+        cost=pl.CostEstimate(flops=5_000_000_000, bytes_accessed=8_000_000, transcendentals=1_200_000),
+    )
+    dp_got = to_core(dp_oth)
+    normed_all = lax.all_gather(jnp.concatenate(got_n, axis=0), "seq", axis=0, tiled=False)
+
+    slab_out = struct((rows2, slab), bf16)
+    *slabs, dp_rows = call(
+        pack_kernel,
+        place,
+        (dp_own, dp_got),
+        [whole((3, rows2, own_width))] * 2,
+        [slab_out] * 4 + [struct((rows2, 3 * width), bf16)],
+        [whole((rows2, slab))] * 4 + [whole((rows2, 3 * width))],
+    )
+    slabs = [slabs[0]] + [along(slabs[k], k) for k in range(1, 4)]
+
+    back_own = [to_rows(att_own[k * slots : (k + 1) * slots], k, 0) for k in range(2)]
+    back_oth = [to_rows(att_oth[k * slots : (k + 1) * slots], k, 1) for k in range(2)]
+
+    dn = pl.pallas_call(
+        d_normed_kernel,
+        grid=(3,),
+        in_specs=[pl.BlockSpec((rows2, width), lambda i: (0, i)), pl.BlockSpec((width, width), lambda i: (0, i))],
+        out_specs=[pl.BlockSpec(block, lambda i: (0, 0))] * 2,
+        out_shape=[block_out] * 2,
+        scratch_shapes=[pltpu.VMEM((rows2, width), f32)],
+        compiler_params=pltpu.CompilerParams(vmem_limit_bytes=VMEM),
+    )(dp_rows, w_qkv)
+    back_dn = [to_rows(dn[k], k, 0) for k in range(2)]
+
+    dwo_sum = dwo_keep.astype(f32) + to_x(dwo_send).astype(f32)
+    dwo_sum = dwo_sum.astype(bf16).reshape(heads, 4, quarter)
+
+    def columns_of(k):
+        return lax.dynamic_index_in_dim(dwo_sum, z ^ k, 1, keepdims=False)
+
+    dwo = columns_of(0).astype(f32)
+    for k in range(1, 4):
+        dwo = dwo + along(columns_of(k), k).astype(f32)
+    dwo = dwo.astype(bf16)
+
+    encoded = call(
+        encode_kernel,
+        place,
+        (kept_count, *back_own, *back_oth, w_out, hidden),
+        [SMEM_SPEC] + [whole((slots, own_width))] * 4 + [whole((width, width)), all_spec],
+        struct(patches.shape, bf16),
+        all_spec,
+    )
+
+    def quarter_of(step, place):
+        core = place[1] ^ (1 - step // 2)
+        return 2 * core + (place[3] ^ (1 - step % 2))
+
+    part = (quarter, slab)
+    w_send, w_pass, w_keep = call(
+        weight_kernel,
+        place,
+        (normed_all, *slabs),
+        [pl.BlockSpec((4, rows2, quarter), lambda i, p: (0, 0, quarter_of(i, p)))] + [whole((rows2, slab))] * 4,
+        [struct((2,) + part, bf16), struct(part, f32), struct(part, f32)],
+        [whole((2,) + part), whole(part), whole(part)],
+        grid=(4,),
+        scratch=[pltpu.VMEM(part, f32)],
+    )
+    w_got = to_core(w_send)
+    w_got_x = to_x((w_pass + w_got[0].astype(f32)).astype(bf16))
+    dwq = (w_keep + w_got[1].astype(f32) + w_got_x.astype(f32)).astype(bf16)
+
+    d_patches = call(
+        patch_grad_kernel,
+        place,
+        (kept_count, *back_dn, *grad, hidden, gain_row),
+        [SMEM_SPEC] + [block_spec] * 4 + [all_spec, whole((1, width))],
+        struct(patches.shape, bf16),
+        all_spec,
+    )
+
+    def spread(value, columns):
+        by_x = to_x(value)
+        by_core = to_core(value)
+        by_both = to_core(by_x)
+
+        def at(i, p):
+            core = p[1] ^ (i // 2)
+            return (2 * core + (p[3] ^ (i % 2)), 0)
+
+        return call(
+            finish_kernel,
+            place,
+            (value, by_x, by_core, by_both),
+            [whole((quarter, columns))] * 4,
+            struct((width, columns), f32),
+            pl.BlockSpec((quarter, columns), at),
+            grid=(4,),
+        )
+
+    return (encoded, d_patches, spread(dwq, slab), spread(dwo, quarter))
+
+
 def solution(mesh):
     in_specs = (
         P(("grp", "rep"), "seq", None),
@@ -236,4 +708,12 @@
         P("grp", "seq"),
         P("grp", "seq"),
     )
-    return jax.shard_map(shards, mesh=mesh, in_specs=in_specs, out_specs=out_specs, check_vma=False)
+    chips = mesh.shape["seq"] == 4 and mesh.shape["rep"] % 2 == 0 and HEADS % 8 == 0
+
+    def run(patches, *rest):
+        per_device = patches.shape[0] // (mesh.shape["grp"] * mesh.shape["rep"])
+        body = chip_shards if chips and per_device == 2 else shards
+        inner = jax.shard_map(body, mesh=mesh, in_specs=in_specs, out_specs=out_specs, check_vma=False)
+        return inner(patches, *rest)
+
+    return run

time: 355 us -> 195 us (0.55)
  waiting for transfers between devices: 143 us -> 73.8 us
  matrix products: 57.9 us -> 0 us
  blocking collectives: 35.3 us -> 0 us
  Pallas kernels: 0 us -> 34.1 us
  local copies, waits for them, and re-layouts: 57.6 us -> 30.6 us
  other arithmetic: 12.2 us -> 5.73 us
    psum x1 -> x0, waiting for transfers between devices: 77.7 us -> none  [shards(): qkv_grad, out_grad = lax.psum((qkv_part, out_part), 'rep')]
    ppermute x0 -> x30, waiting for transfers between devices: none -> 73.8 us  [send(): return lax.ppermute(value, AXES, line_perm(move, reps))]
    all_to_all x6 -> x0, waiting for transfers between devices: 64.2 us -> none  [the longest x1 35.1 us: shards(): lax.all_to_all(key_value_grad.astype(jnp.bfloat16), 'seq', split_axis=0,...]
    dot_general x11 -> x0, matrix products: 52.8 us -> none  [the longest x1 8.91 us: head_block(): d_key = jnp.dot(d_score.T, query_rows, preferred_element_type=jnp.float32)]
    ppermute x0 -> x30, starting transfers between devices: none -> 34.2 us  [send(): return lax.ppermute(value, AXES, line_perm(move, reps))]
    pallas_call x0 -> x10, Pallas kernels: none -> 34.1 us  [the longest x9 30.8 us: call(): pl.pallas_call(kernel, out_shape=outs, grid_spec=pltpu.PrefetchScalarGrid...]
    all_to_all x6 -> x0, starting transfers between devices: 31.7 us -> none  [the longest x1 6.87 us: shards(): lax.all_to_all(key_value_send, 'seq', split_axis=0, concat_axis=0, tiled=...]
    all_gather x1 -> x0, blocking collectives: 24.6 us -> none  [shards(): all_counts = lax.all_gather(kept_count, 'seq', axis=1, tiled=True)]
  transfers between devices with their start and end apart: 9 -> 31, of which waited for: 5 -> 14; matrix products, arithmetic and copies ran while one was open for 30% -> 9% of each run, Pallas kernels for 0% -> 13%
where the time goes in v1:
time: 195 us; the launch traced here: 193 us
  waiting for transfers between devices  73.8 us (38%)
  starting transfers between devices  34.2 us (18%)
  Pallas kernels  34.1 us (17%)
  local copies, waits for them, and re-layouts  30.6 us (16%)
  between operations  14.4 us (7%)
  other arithmetic  5.73 us (3%)
    ppermute x30, waiting for transfers between devices, send(): return lax.ppermute(value, AXES, line_perm(move, reps))  73.8 us
    ppermute x30, starting transfers between devices, send(): return lax.ppermute(value, AXES, line_perm(move, reps))  34.2 us
    pallas_call x9, Pallas kernels, call(): pl.pallas_call(kernel, out_shape=outs, grid_spec=pltpu.PrefetchScalarGrid...  30.8 us
    unnamed x54, local copies, waits for them, and re-layouts  18.6 us
    dynamic_slice x4, local copies, waits for them, and re-layouts, columns_of(): return lax.dynamic_index_in_dim(dwo_sum, z ^ k, 1, keepdims=False)  6.87 us
  transfers between devices with their start and end apart: 31, of which 14 were waited for; matrix products, arithmetic and copies ran while one was open for 9% of the time, Pallas kernels for 13%

profile of v1, /device:TPU:9, one launch (start us, length us, event | category | flops | bytes accessed | tf_op | source)
XLA Modules:
  0.0 192.9 jit_solution(6031492837279369685)
XLA Ops:
  10.7 2.0 %shard_map.102 = (bf16[96,1024]{1,0:T(8,128)(2,1)S(1)}, bf16[96,1024]{1,0:T(8,128)(2,1)S(1)}, f32[2,96,1024]{2,1,0:T(8,128)S(1)}) custom-call(s32[4]{0:T(128)S(1)} %pad_add_fusion.place, s32[2,1]{1,0:T(2,128)S(1)} %copy.18.count_ref, bf16[2,96,1024]{2,1,0:T(8,128)(2,1)S(1)} %copy-done.8, s32[2,96,1]{2,1,0:T(8,128)S(1)} %copy.16.index_ref, ...), custom_call_target="tpu_custom_call" | custom-call | tf_op jit(solution)/shard_map/pallas_call | solution.py:490
  12.7 4.8 %collective-permute-start = (bf16[96,1024]{1,0:T(8,128)(2,1)S(1)}, bf16[96,1024]{1,0:T(8,128)(2,1)S(1)}, u32[]{:S(2)}, u32[]{:S(2)}) collective-permute-start(bf16[96,1024]{1,0:T(8,128)(2,1)S(1)} %get-tuple-element.25), channel_id=1, source_target_pairs={{0,0},{1,8},{2,2},{3,10},{4,4},{5,12},{6,6},{7,14},{8,1},{9,9},{10... | collective-permute-start | bytes 589832 | tf_op jit(solution)/shard_map/ppermute | solution.py:525
  17.6 6.7 %collective-permute-done.n0 = bf16[96,1024]{1,0:T(8,128)(2,1)S(1)} collective-permute-done((bf16[96,1024]{1,0:T(8,128)(2,1)S(1)}, bf16[96,1024]{1,0:T(8,128)(2,1)S(1)}, u32[]{:S(2)}, u32[]{:S(2)}) %collective-permute-start) | collective-permute-done | bytes 196640 | tf_op jit(solution)/shard_map/ppermute | solution.py:525
  24.3 2.1 %collective-permute-done.1.n1 = bf16[96,1024]{1,0:T(8,128)(2,1)S(1)} collective-permute-done((bf16[96,1024]{1,0:T(8,128)(2,1)S(1)}, bf16[96,1024]{1,0:T(8,128)(2,1)S(1)}, u32[]{:S(2)}, u32[]{:S(2)}) %collective-permute-start.1) | collective-permute-done | bytes 196640 | tf_op jit(solution)/shard_map/ppermute | solution.py:525
  29.3 3.2 %collective-permute-start.4 = (bf16[96,1024]{1,0:T(8,128)(2,1)S(1)}, bf16[96,1024]{1,0:T(8,128)(2,1)S(1)}, u32[]{:S(2)}, u32[]{:S(2)}) collective-permute-start(bf16[96,1024]{1,0:T(8,128)(2,1)S(1)} %get-tuple-element.27.g0), channel_id=1, source_target_pairs={{0,0},{1,8},{2,2},{3,10},{4,4},{5,12},{6,6},{7,14},{8,1},{9,9},{10... | collective-permute-start | bytes 589832 | tf_op jit(solution)/shard_map/ppermute | solution.py:525
  35.6 1.7 collective-permute-done.4.g0
  37.3 18.7 %collective-permute-done.5.g1 = bf16[96,1024]{1,0:T(8,128)(2,1)S(1)} collective-permute-done((bf16[96,1024]{1,0:T(8,128)(2,1)S(1)}, bf16[96,1024]{1,0:T(8,128)(2,1)S(1)}, u32[]{:S(2)}, u32[]{:S(2)}) %collective-permute-start.5) | collective-permute-done | bytes 196640 | tf_op jit(solution)/shard_map/ppermute | solution.py:525
  57.4 2.8 %copy-done = bf16[1024,3072]{1,0:T(8,128)(2,1)S(1)} copy-done((bf16[1024,3072]{1,0:T(8,128)(2,1)S(1)}, bf16[1024,3072]{1,0:T(8,128)(2,1)}, u32[]{:S(2)}) %copy-start) | copy-done | bytes 6291480
  60.2 12.0 %shard_map.104 = (bf16[192,512]{1,0:T(8,128)(2,1)S(1)}, bf16[192,512]{1,0:T(8,128)(2,1)S(1)}, bf16[3,192,512]{2,1,0:T(8,128)(2,1)S(1)}, bf16[3,192,512]{2,1,0:T(...) custom-call(s32[4]{0:T(128)S(1)} %pad_add_fusion.place, ...), custom_call_target="tpu_custom_call" | custom-call | flops 5000000000 | bytes 8000000 | tf_op jit(solution)/shard_map/pallas_call | solution.py:490
  72.4 1.9 collective-permute-done.12.got
  76.4 2.2 %collective-permute-start.17 = (bf16[192,768]{1,0:T(8,128)(2,1)S(1)}, bf16[192,768]{1,0:T(8,128)(2,1)S(1)}, u32[]{:S(2)}, u32[]{:S(2)}) collective-permute-start(bf16[192,768]{1,0:T(8,128)(2,1)S(1)} %get-tuple-element.40), channel_id=1, source_target_pairs={{0,12},{1,13},{2,14},{3,15},{4,8},{5,9},{6,10},{7,11},{8,4},{9,5},... | collective-permute-start | bytes 884744 | tf_op jit(solution)/shard_map/ppermute | solution.py:525
  78.6 8.0 %collective-permute-done.15.s1 = bf16[192,768]{1,0:T(8,128)(2,1)S(1)} collective-permute-done((bf16[192,768]{1,0:T(8,128)(2,1)S(1)}, bf16[192,768]{1,0:T(8,128)(2,1)S(1)}, u32[]{:S(2)}, u32[]{:S(2)}) %collective-permute-start.15) | collective-permute-done | bytes 294944 | tf_op jit(solution)/shard_map/ppermute | solution.py:525
  86.7 2.9 %collective-permute-done.16.s2 = bf16[192,768]{1,0:T(8,128)(2,1)S(1)} collective-permute-done((bf16[192,768]{1,0:T(8,128)(2,1)S(1)}, bf16[192,768]{1,0:T(8,128)(2,1)S(1)}, u32[]{:S(2)}, u32[]{:S(2)}) %collective-permute-start.16) | collective-permute-done | bytes 294944 | tf_op jit(solution)/shard_map/ppermute | solution.py:525
  90.3 14.0 %collective-permute-done.17.s3 = bf16[192,768]{1,0:T(8,128)(2,1)S(1)} collective-permute-done((bf16[192,768]{1,0:T(8,128)(2,1)S(1)}, bf16[192,768]{1,0:T(8,128)(2,1)S(1)}, u32[]{:S(2)}, u32[]{:S(2)}) %collective-permute-start.17) | collective-permute-done | bytes 294944 | tf_op jit(solution)/shard_map/ppermute | solution.py:525
  108.4 3.7 %shard_map.109 = (bf16[2,256,768]{2,1,0:T(8,128)(2,1)S(1)}, f32[256,768]{1,0:T(8,128)S(1)}, f32[256,768]{1,0:T(8,128)S(1)}) custom-call(s32[4]{0:T(128)S(1)} %pad_add_fusion.place, bf16[4,192,1024]{2,1,0:T(8,128)(2,1)S(1)} %bitcast.24, bf16[192,768]{1,0:T(8,128)(2,1)S(1)} %get-tuple-element.37.s0, bf16[192,768]{1,0:T(8,128)(2,1)S(1)} %collective-permute-done.15.s1, ...), custom_call_target="tpu_custom_call" | custom-call | tf_op jit(solution)/shard_map/pallas_call | solution.py:490
  113.4 1.9 collective-permute-done.18
  119.1 1.9 collective-permute-start.8
  121.1 4.8 %collective-permute-done.19 = bf16[256,768]{1,0:T(8,128)(2,1)} collective-permute-done((bf16[256,768]{1,0:T(8,128)(2,1)S(1)}, bf16[256,768]{1,0:T(8,128)(2,1)}, u32[]{:S(2)}, u32[]{:S(2)}) %collective-permute-start.19) | collective-permute-done | bytes 393248 | tf_op jit(solution)/shard_map/ppermute | solution.py:525
  128.7 8.4 %collective-permute-done.23 = bf16[256,1024]{1,0:T(8,128)(2,1)} collective-permute-done((bf16[256,1024]{1,0:T(8,128)(2,1)}, bf16[256,1024]{1,0:T(8,128)(2,1)}, u32[]{:S(2)}, u32[]{:S(2)}) %collective-permute-start.23) | collective-permute-done | bytes 524320 | tf_op jit(solution)/shard_map/ppermute | solution.py:525
  137.1 2.2 %add_convert_fusion = bf16[256,1024]{1,0:T(8,128)(2,1)} fusion(bf16[256,1024]{1,0:T(8,128)(2,1)} %collective-permute-done.23, bf16[256,1024]{1,0:T(8,128)(2,1)} %copy-done.7), kind=kLoop, calls=%fused_computation | loop fusion | flops 1048576 | bytes 1572864 | tf_op jit(solution)/shard_map/convert_element_type | solution.py:626
  139.4 2.1 %copy.20 = bf16[256,1024]{0,1:T(8,128)(2,1)} copy(bf16[256,1024]{1,0:T(8,128)(2,1)} %add_convert_fusion) | data formatting | bytes 1048576 | tf_op jit(solution)/shard_map/convert_element_type | solution.py:626
  141.4 1.9 constant_dynamic-slice_fusion.3
  148.3 2.6 %collective-permute-start.24 = (bf16[256,256]{1,0:T(8,128)(2,1)}, bf16[256,256]{1,0:T(8,128)(2,1)}, u32[]{:S(2)}, u32[]{:S(2)}) collective-permute-start(bf16[256,256]{1,0:T(8,128)(2,1)} %bitcast.28), channel_id=1, source_target_pairs={{0,4},{1,5},{2,6},{3,7},{4,0},{5,1},{6,2},{7,3},{8,12},{9,13},{10,... | collective-permute-start | bytes 393224 | tf_op jit(solution)/shard_map/ppermute | solution.py:525
  152.7 2.8 %copy-done.1 = bf16[1024,3072]{1,0:T(8,128)(2,1)S(1)} copy-done((bf16[1024,3072]{1,0:T(8,128)(2,1)S(1)}, bf16[1024,3072]{1,0:T(8,128)(2,1)}, u32[]{:S(2)}) %copy-start.1) | copy-done | bytes 6291480
  156.7 3.3 %shard_map.107 = (bf16[96,1024]{1,0:T(8,128)(2,1)S(1)}, bf16[96,1024]{1,0:T(8,128)(2,1)S(1)}) custom-call(bf16[192,3072]{1,0:T(8,128)(2,1)S(1)} %copy-done.5, bf16[1024,3072]{1,0:T(8,128)(2,1)S(1)} %copy-done.1), custom_call_target="tpu_custom_call" | custom-call | tf_op jit(solution)/shard_map/pallas_call | solution.py:614
  160.0 2.9 %collective-permute-start.10 = (bf16[96,512]{1,0:T(8,128)(2,1)S(1)}, bf16[96,512]{1,0:T(8,128)(2,1)S(1)}, u32[]{:S(2)}, u32[]{:S(2)}) collective-permute-start(bf16[96,512]{1,0:T(8,128)(2,1)S(1)} %copy-done.25), channel_id=1, source_target_pairs={{0,8},{1,0},{2,10},{3,2},{4,12},{5,4},{6,14},{7,6},{8,9},{9,1},{10... | collective-permute-start | bytes 294920 | tf_op jit(solution)/shard_map/ppermute | solution.py:525
  164.0 2.1 %collective-permute-start.13 = (bf16[96,1024]{1,0:T(8,128)(2,1)S(1)}, bf16[96,1024]{1,0:T(8,128)(2,1)S(1)}, u32[]{:S(2)}, u32[]{:S(2)}) collective-permute-start(bf16[96,1024]{1,0:T(8,128)(2,1)S(1)} %get-tuple-element.35), channel_id=1, source_target_pairs={{0,0},{1,8},{2,2},{3,10},{4,4},{5,12},{6,6},{7,14},{8,1},{9,9},{10... | collective-permute-start | bytes 589832 | tf_op jit(solution)/shard_map/ppermute | solution.py:525
  169.1 3.4 %collective-permute-start.14 = (bf16[96,1024]{1,0:T(8,128)(2,1)S(1)}, bf16[96,1024]{1,0:T(8,128)(2,1)S(1)}, u32[]{:S(2)}, u32[]{:S(2)}) collective-permute-start(bf16[96,1024]{1,0:T(8,128)(2,1)S(1)} %get-tuple-element.36), channel_id=1, source_target_pairs={{0,4},{1,12},{2,6},{3,14},{4,0},{5,8},{6,2},{7,10},{8,5},{9,13},{1... | collective-permute-start | bytes 589832 | tf_op jit(solution)/shard_map/ppermute | solution.py:525
  173.8 3.1 %shard_map.105 = bf16[2,96,1024]{2,1,0:T(8,128)(2,1)} custom-call(s32[4]{0:T(128)S(1)} %pad_add_fusion.place, s32[2,1]{1,0:T(2,128)S(1)} %copy.18.count_ref, bf16[96,512]{1,0:T(8,128)(2,1)} %collective-permute-done.8.a0, bf16[96,512]{1,0:T(8,128)(2,1)} %collective-permute-done.9.a1, bf16[96,512]{1,0:T(8,128)(2,1)S(1)} %collective-permute-done.10.b0, ...), custom_call_target="tpu_custom_call" | custom-call | tf_op jit(solution)/shard_map/pallas_call | solution.py:490
  177.7 2.4 %shard_map.108 = bf16[2,96,1024]{2,1,0:T(8,128)(2,1)} custom-call(s32[4]{0:T(128)S(1)} %pad_add_fusion.place, s32[2,1]{1,0:T(2,128)S(1)} %copy.18.count_ref, bf16[96,1024]{1,0:T(8,128)(2,1)S(1)} %collective-permute-done.13.d0, bf16[96,1024]{1,0:T(8,128)(2,1)S(1)} %collective-permute-done.14.d1, bf16[96,1024]{1,0:T(8,128)(2,1)S(1)} %copy-done.18, ...), custom_call_target="tpu_custom_call" | custom-call | tf_op jit(solution)/shard_map/pallas_call | solution.py:490
  180.1 2.2 %shard_map.111 = f32[1024,256]{1,0:T(8,128)} custom-call(s32[4]{0:T(128)S(1)} %pad_add_fusion.place, bf16[256,256]{1,0:T(8,128)(2,1)S(1)} %fusion.5.a, bf16[256,256]{1,0:T(8,128)(2,1)S(1)} %collective-permute-done.27.b, bf16[256,256]{1,0:T(8,128)(2,1)S(1)} %collective-permute-done.28.c, bf16[256,256]{1,0:T(8,128)(2,1)S(1)} %collective-permute-done.29.d), custom_call_target="tpu_custom_call" | custom-call | tf_op jit(solution)/shard_map/pallas_call | solution.py:490
  182.3 3.7 %shard_map.110 = f32[1024,768]{1,0:T(8,128)} custom-call(s32[4]{0:T(128)S(1)} %pad_add_fusion.place, bf16[256,768]{1,0:T(8,128)(2,1)S(1)} %fusion.2.a, bf16[256,768]{1,0:T(8,128)(2,1)} %collective-permute-done.20.b, bf16[256,768]{1,0:T(8,128)(2,1)S(1)} %collective-permute-done.21.c, bf16[256,768]{1,0:T(8,128)(2,1)S(1)} %collective-permute-done.22.d), custom_call_target="tpu_custom_call" | custom-call | tf_op jit(solution)/shard_map/pallas_call | solution.py:490
  (110 shorter events, 40.2 us)
Async XLA Ops:
  7.2 50.3 %copy-start.2 = (bf16[1024,1024]{1,0:T(8,128)(2,1)S(1)}, bf16[1024,1024]{1,0:T(8,128)(2,1)}, u32[]{:S(2)}) copy-start(bf16[1024,1024]{1,0:T(8,128)(2,1)} %w_ref.2) | copy-start | bytes 6291460
  7.2 97.9 %all-gather.3.cloned.1.call-start = ((), (), s32[]{:S(2)}) async-start(), calls=%async_computation | async-start | bytes 1966080 | tf_op jit(solution)/shard_map/all_gather | solution.py:598
  12.7 11.6 %collective-permute-start = (bf16[96,1024]{1,0:T(8,128)(2,1)S(1)}, bf16[96,1024]{1,0:T(8,128)(2,1)S(1)}, u32[]{:S(2)}, u32[]{:S(2)}) collective-permute-start(bf16[96,1024]{1,0:T(8,128)(2,1)S(1)} %get-tuple-element.25), channel_id=1, source_target_pairs={{0,0},{1,8},{2,2},{3,10},{4,4},{5,12},{6,6},{7,14},{8,1},{9,9},{10... | collective-permute-start | bytes 589832 | tf_op jit(solution)/shard_map/ppermute | solution.py:525
  17.5 8.9 %collective-permute-start.1 = (bf16[96,1024]{1,0:T(8,128)(2,1)S(1)}, bf16[96,1024]{1,0:T(8,128)(2,1)S(1)}, u32[]{:S(2)}, u32[]{:S(2)}) collective-permute-start(bf16[96,1024]{1,0:T(8,128)(2,1)S(1)} %get-tuple-element.26), channel_id=1, source_target_pairs={{0,4},{1,12},{2,6},{3,14},{4,0},{5,8},{6,2},{7,10},{8,5},{9,13},{1... | collective-permute-start | bytes 589832 | tf_op jit(solution)/shard_map/ppermute | solution.py:525
  29.3 8.0 %collective-permute-start.4 = (bf16[96,1024]{1,0:T(8,128)(2,1)S(1)}, bf16[96,1024]{1,0:T(8,128)(2,1)S(1)}, u32[]{:S(2)}, u32[]{:S(2)}) collective-permute-start(bf16[96,1024]{1,0:T(8,128)(2,1)S(1)} %get-tuple-element.27.g0), channel_id=1, source_target_pairs={{0,0},{1,8},{2,2},{3,10},{4,4},{5,12},{6,6},{7,14},{8,1},{9,9},{10... | collective-permute-start | bytes 589832 | tf_op jit(solution)/shard_map/ppermute | solution.py:525
  33.2 22.8 %collective-permute-start.5 = (bf16[96,1024]{1,0:T(8,128)(2,1)S(1)}, bf16[96,1024]{1,0:T(8,128)(2,1)S(1)}, u32[]{:S(2)}, u32[]{:S(2)}) collective-permute-start(bf16[96,1024]{1,0:T(8,128)(2,1)S(1)} %get-tuple-element.28.g1), channel_id=1, source_target_pairs={{0,4},{1,12},{2,6},{3,14},{4,0},{5,8},{6,2},{7,10},{8,5},{9,13},{1... | collective-permute-start | bytes 589832 | tf_op jit(solution)/shard_map/ppermute | solution.py:525
  35.1 20.9 %collective-permute-start.2 = (bf16[96,1024]{1,0:T(8,128)(2,1)S(1)}, bf16[96,1024]{1,0:T(8,128)(2,1)S(1)}, u32[]{:S(2)}, u32[]{:S(2)}) collective-permute-start(bf16[96,1024]{1,0:T(8,128)(2,1)S(1)} %collective-permute-done.n0), channel_id=1, source_target_pairs={{0,1},{1,0},{2,3},{3,2},{4,5},{5,4},{6,7},{7,6},{8,9},{9,8},{10,11... | collective-permute-start | bytes 589832 | tf_op jit(solution)/shard_map/ppermute | solution.py:525
  35.1 20.9 %collective-permute-start.3 = (bf16[96,1024]{1,0:T(8,128)(2,1)S(1)}, bf16[96,1024]{1,0:T(8,128)(2,1)S(1)}, u32[]{:S(2)}, u32[]{:S(2)}) collective-permute-start(bf16[96,1024]{1,0:T(8,128)(2,1)S(1)} %collective-permute-done.1.n1), channel_id=1, source_target_pairs={{0,1},{1,0},{2,3},{3,2},{4,5},{5,4},{6,7},{7,6},{8,9},{9,8},{10,11... | collective-permute-start | bytes 589832 | tf_op jit(solution)/shard_map/ppermute | solution.py:525
  37.3 18.7 %collective-permute-start.6 = (bf16[96,1024]{1,0:T(8,128)(2,1)S(1)}, bf16[96,1024]{1,0:T(8,128)(2,1)S(1)}, u32[]{:S(2)}, u32[]{:S(2)}) collective-permute-start(bf16[96,1024]{1,0:T(8,128)(2,1)S(1)} %collective-permute-done.4.g0), channel_id=1, source_target_pairs={{0,1},{1,0},{2,3},{3,2},{4,5},{5,4},{6,7},{7,6},{8,9},{9,8},{10,11... | collective-permute-start | bytes 589832 | tf_op jit(solution)/shard_map/ppermute | solution.py:525
  56.0 1.4 collective-permute-start.7
  72.2 2.0 %collective-permute-start.12 = (bf16[3,192,512]{2,1,0:T(8,128)(2,1)S(1)}, bf16[3,192,512]{2,1,0:T(8,128)(2,1)S(1)}, u32[]{:S(2)}, u32[]{:S(2)}) collective-permute-start(bf16[3,192,512]{2,1,0:T(8,128)(2,1)S(1)} %get-tuple-element.33), channel_id=1, source_target_pairs={{0,1},{1,0},{2,3},{3,2},{4,5},{5,4},{6,7},{7,6},{8,9},{9,8},{10,11... | collective-permute-start | bytes 1769480 | tf_op jit(solution)/shard_map/ppermute | solution.py:525
  76.0 10.7 %collective-permute-start.15 = (bf16[192,768]{1,0:T(8,128)(2,1)S(1)}, bf16[192,768]{1,0:T(8,128)(2,1)S(1)}, u32[]{:S(2)}, u32[]{:S(2)}) collective-permute-start(bf16[192,768]{1,0:T(8,128)(2,1)S(1)} %get-tuple-element.38), channel_id=1, source_target_pairs={{0,4},{1,5},{2,6},{3,7},{4,0},{5,1},{6,2},{7,3},{8,12},{9,13},{10,... | collective-permute-start | bytes 884744 | tf_op jit(solution)/shard_map/ppermute | solution.py:525
  76.0 13.6 %collective-permute-start.16 = (bf16[192,768]{1,0:T(8,128)(2,1)S(1)}, bf16[192,768]{1,0:T(8,128)(2,1)S(1)}, u32[]{:S(2)}, u32[]{:S(2)}) collective-permute-start(bf16[192,768]{1,0:T(8,128)(2,1)S(1)} %get-tuple-element.39), channel_id=1, source_target_pairs={{0,8},{1,9},{2,10},{3,11},{4,12},{5,13},{6,14},{7,15},{8,0},{9,1},... | collective-permute-start | bytes 884744 | tf_op jit(solution)/shard_map/ppermute | solution.py:525
  76.4 27.9 %collective-permute-start.17 = (bf16[192,768]{1,0:T(8,128)(2,1)S(1)}, bf16[192,768]{1,0:T(8,128)(2,1)S(1)}, u32[]{:S(2)}, u32[]{:S(2)}) collective-permute-start(bf16[192,768]{1,0:T(8,128)(2,1)S(1)} %get-tuple-element.40), channel_id=1, source_target_pairs={{0,12},{1,13},{2,14},{3,15},{4,8},{5,9},{6,10},{7,11},{8,4},{9,5},... | collective-permute-start | bytes 884744 | tf_op jit(solution)/shard_map/ppermute | solution.py:525
  112.1 3.2 %collective-permute-start.18 = (bf16[2,256,768]{2,1,0:T(8,128)(2,1)S(1)}, bf16[2,256,768]{2,1,0:T(8,128)(2,1)S(1)}, u32[]{:S(2)}, u32[]{:S(2)}) collective-permute-start(bf16[2,256,768]{2,1,0:T(8,128)(2,1)S(1)} %get-tuple-element.42), channel_id=1, source_target_pairs={{0,1},{1,0},{2,3},{3,2},{4,5},{5,4},{6,7},{7,6},{8,9},{9,8},{10,11... | collective-permute-start | bytes 2359304 | tf_op jit(solution)/shard_map/ppermute | solution.py:525
  115.4 10.5 %collective-permute-start.19 = (bf16[256,768]{1,0:T(8,128)(2,1)S(1)}, bf16[256,768]{1,0:T(8,128)(2,1)}, u32[]{:S(2)}, u32[]{:S(2)}) collective-permute-start(bf16[256,768]{1,0:T(8,128)(2,1)S(1)} %fusion), channel_id=1, source_target_pairs={{0,2},{1,3},{2,0},{3,1},{4,6},{5,7},{6,4},{7,5},{8,10},{9,11},{10,... | collective-permute-start | bytes 1179656 | tf_op jit(solution)/shard_map/ppermute | solution.py:525
  116.7 20.4 %collective-permute-start.23 = (bf16[256,1024]{1,0:T(8,128)(2,1)}, bf16[256,1024]{1,0:T(8,128)(2,1)}, u32[]{:S(2)}, u32[]{:S(2)}) collective-permute-start(bf16[256,1024]{1,0:T(8,128)(2,1)} %get-tuple-element.45), channel_id=1, source_target_pairs={{0,2},{1,3},{2,0},{3,1},{4,6},{5,7},{6,4},{7,5},{8,10},{9,11},{10,... | collective-permute-start | bytes 1572872 | tf_op jit(solution)/shard_map/ppermute | solution.py:525
  119.1 29.2 %collective-permute-start.8 = (bf16[96,512]{1,0:T(8,128)(2,1)}, bf16[96,512]{1,0:T(8,128)(2,1)}, u32[]{:S(2)}, u32[]{:S(2)}) collective-permute-start(bf16[96,512]{1,0:T(8,128)(2,1)} %get-tuple-element.53), channel_id=1, source_target_pairs={{0,0},{1,8},{2,2},{3,10},{4,4},{5,12},{6,6},{7,14},{8,1},{9,9},{10... | collective-permute-start | bytes 294920 | tf_op jit(solution)/shard_map/ppermute | solution.py:525
  121.0 39.0 %collective-permute-start.9 = (bf16[96,512]{1,0:T(8,128)(2,1)}, bf16[96,512]{1,0:T(8,128)(2,1)}, u32[]{:S(2)}, u32[]{:S(2)}) collective-permute-start(bf16[96,512]{1,0:T(8,128)(2,1)} %get-tuple-element.52), channel_id=1, source_target_pairs={{0,4},{1,12},{2,6},{3,14},{4,0},{5,8},{6,2},{7,10},{8,5},{9,13},{1... | collective-permute-start | bytes 294920 | tf_op jit(solution)/shard_map/ppermute | solution.py:525
  127.4 38.8 %collective-permute-start.20 = (bf16[256,768]{1,0:T(8,128)(2,1)S(1)}, bf16[256,768]{1,0:T(8,128)(2,1)}, u32[]{:S(2)}, u32[]{:S(2)}) collective-permute-start(bf16[256,768]{1,0:T(8,128)(2,1)S(1)} %fusion.2.a), channel_id=1, source_target_pairs={{0,2},{1,3},{2,0},{3,1},{4,6},{5,7},{6,4},{7,5},{8,10},{9,11},{10,... | collective-permute-start | bytes 1179656 | tf_op jit(solution)/shard_map/ppermute | solution.py:525
  145.0 18.0 %collective-permute-start.26 = (bf16[256,256]{1,0:T(8,128)(2,1)}, bf16[256,256]{1,0:T(8,128)(2,1)}, u32[]{:S(2)}, u32[]{:S(2)}) collective-permute-start(bf16[256,256]{1,0:T(8,128)(2,1)} %bitcast.30), channel_id=1, source_target_pairs={{0,12},{1,13},{2,14},{3,15},{4,8},{5,9},{6,10},{7,11},{8,4},{9,5},... | collective-permute-start | bytes 393224 | tf_op jit(solution)/shard_map/ppermute | solution.py:525
  146.6 17.4 %collective-permute-start.25 = (bf16[256,256]{1,0:T(8,128)(2,1)}, bf16[256,256]{1,0:T(8,128)(2,1)}, u32[]{:S(2)}, u32[]{:S(2)}) collective-permute-start(bf16[256,256]{1,0:T(8,128)(2,1)} %bitcast.29), channel_id=1, source_target_pairs={{0,8},{1,9},{2,10},{3,11},{4,12},{5,13},{6,14},{7,15},{8,0},{9,1},... | collective-permute-start | bytes 393224 | tf_op jit(solution)/shard_map/ppermute | solution.py:525
  148.3 17.8 %collective-permute-start.24 = (bf16[256,256]{1,0:T(8,128)(2,1)}, bf16[256,256]{1,0:T(8,128)(2,1)}, u32[]{:S(2)}, u32[]{:S(2)}) collective-permute-start(bf16[256,256]{1,0:T(8,128)(2,1)} %bitcast.28), channel_id=1, source_target_pairs={{0,4},{1,5},{2,6},{3,7},{4,0},{5,1},{6,2},{7,3},{8,12},{9,13},{10,... | collective-permute-start | bytes 393224 | tf_op jit(solution)/shard_map/ppermute | solution.py:525
  160.0 7.8 %collective-permute-start.10 = (bf16[96,512]{1,0:T(8,128)(2,1)S(1)}, bf16[96,512]{1,0:T(8,128)(2,1)S(1)}, u32[]{:S(2)}, u32[]{:S(2)}) collective-permute-start(bf16[96,512]{1,0:T(8,128)(2,1)S(1)} %copy-done.25), channel_id=1, source_target_pairs={{0,8},{1,0},{2,10},{3,2},{4,12},{5,4},{6,14},{7,6},{8,9},{9,1},{10... | collective-permute-start | bytes 294920 | tf_op jit(solution)/shard_map/ppermute | solution.py:525
  162.9 6.2 %collective-permute-start.11 = (bf16[96,512]{1,0:T(8,128)(2,1)S(1)}, bf16[96,512]{1,0:T(8,128)(2,1)S(1)}, u32[]{:S(2)}, u32[]{:S(2)}) collective-permute-start(bf16[96,512]{1,0:T(8,128)(2,1)S(1)} %copy-done.24), channel_id=1, source_target_pairs={{0,12},{1,4},{2,14},{3,6},{4,8},{5,0},{6,10},{7,2},{8,13},{9,5},{1... | collective-permute-start | bytes 294920 | tf_op jit(solution)/shard_map/ppermute | solution.py:525
  164.0 9.8 %collective-permute-start.13 = (bf16[96,1024]{1,0:T(8,128)(2,1)S(1)}, bf16[96,1024]{1,0:T(8,128)(2,1)S(1)}, u32[]{:S(2)}, u32[]{:S(2)}) collective-permute-start(bf16[96,1024]{1,0:T(8,128)(2,1)S(1)} %get-tuple-element.35), channel_id=1, source_target_pairs={{0,0},{1,8},{2,2},{3,10},{4,4},{5,12},{6,6},{7,14},{8,1},{9,9},{10... | collective-permute-start | bytes 589832 | tf_op jit(solution)/shard_map/ppermute | solution.py:525
  166.1 16.2 %collective-permute-start.21 = (bf16[256,768]{1,0:T(8,128)(2,1)S(1)}, bf16[256,768]{1,0:T(8,128)(2,1)S(1)}, u32[]{:S(2)}, u32[]{:S(2)}) collective-permute-start(bf16[256,768]{1,0:T(8,128)(2,1)S(1)} %fusion.2.a), channel_id=1, source_target_pairs={{0,1},{1,0},{2,3},{3,2},{4,5},{5,4},{6,7},{7,6},{8,9},{9,8},{10,11... | collective-permute-start | bytes 1179656 | tf_op jit(solution)/shard_map/ppermute | solution.py:525
  166.2 16.1 %collective-permute-start.22 = (bf16[256,768]{1,0:T(8,128)(2,1)}, bf16[256,768]{1,0:T(8,128)(2,1)S(1)}, u32[]{:S(2)}, u32[]{:S(2)}) collective-permute-start(bf16[256,768]{1,0:T(8,128)(2,1)} %collective-permute-done.20.b), channel_id=1, source_target_pairs={{0,1},{1,0},{2,3},{3,2},{4,5},{5,4},{6,7},{7,6},{8,9},{9,8},{10,11... | collective-permute-start | bytes 1179656 | tf_op jit(solution)/shard_map/ppermute | solution.py:525
  167.8 5.1 %collective-permute-start.27 = (bf16[256,256]{1,0:T(8,128)(2,1)S(1)}, bf16[256,256]{1,0:T(8,128)(2,1)S(1)}, u32[]{:S(2)}, u32[]{:S(2)}) collective-permute-start(bf16[256,256]{1,0:T(8,128)(2,1)S(1)} %fusion.5.a), channel_id=1, source_target_pairs={{0,2},{1,3},{2,0},{3,1},{4,6},{5,7},{6,4},{7,5},{8,10},{9,11},{10,... | collective-permute-start | bytes 393224 | tf_op jit(solution)/shard_map/ppermute | solution.py:525
  169.1 8.6 %collective-permute-start.14 = (bf16[96,1024]{1,0:T(8,128)(2,1)S(1)}, bf16[96,1024]{1,0:T(8,128)(2,1)S(1)}, u32[]{:S(2)}, u32[]{:S(2)}) collective-permute-start(bf16[96,1024]{1,0:T(8,128)(2,1)S(1)} %get-tuple-element.36), channel_id=1, source_target_pairs={{0,4},{1,12},{2,6},{3,14},{4,0},{5,8},{6,2},{7,10},{8,5},{9,13},{1... | collective-permute-start | bytes 589832 | tf_op jit(solution)/shard_map/ppermute | solution.py:525
  172.9 7.2 %collective-permute-start.28 = (bf16[256,256]{1,0:T(8,128)(2,1)S(1)}, bf16[256,256]{1,0:T(8,128)(2,1)S(1)}, u32[]{:S(2)}, u32[]{:S(2)}) collective-permute-start(bf16[256,256]{1,0:T(8,128)(2,1)S(1)} %fusion.5.a), channel_id=1, source_target_pairs={{0,1},{1,0},{2,3},{3,2},{4,5},{5,4},{6,7},{7,6},{8,9},{9,8},{10,11... | collective-permute-start | bytes 393224 | tf_op jit(solution)/shard_map/ppermute | solution.py:525
  173.8 6.4 %collective-permute-start.29 = (bf16[256,256]{1,0:T(8,128)(2,1)S(1)}, bf16[256,256]{1,0:T(8,128)(2,1)S(1)}, u32[]{:S(2)}, u32[]{:S(2)}) collective-permute-start(bf16[256,256]{1,0:T(8,128)(2,1)S(1)} %collective-permute-done.27.b), channel_id=1, source_target_pairs={{0,1},{1,0},{2,3},{3,2},{4,5},{5,4},{6,7},{7,6},{8,9},{9,8},{10,11... | collective-permute-start | bytes 393224 | tf_op jit(solution)/shard_map/ppermute | solution.py:525
  (25 other events, 123.3 us)
Sparse Core Ops, SparseCore 0:
  27.3 39.4 all-gather.2

commit v2 on v0

--- a/solution.py
+++ b/solution.py
@@ -1,6 +1,11 @@
+import functools
+
 import jax
 import jax.numpy as jnp
+import numpy as np
 from jax import lax
+from jax.experimental import pallas as pl
+from jax.experimental.pallas import tpu as pltpu
 from jax.sharding import PartitionSpec as P
 
 HEADS = 16
@@ -220,6 +225,465 @@
     return (encoded, d_patches, qkv_grad, out_grad)
 
 
+AXES = ("seq", "rep")
+MARK = 1024.0
+MIB = 1024 * 1024
+
+
+def line_perm(move, reps):
+    pairs = []
+    for z in range(4):
+        for rep in range(reps):
+            x, c = rep // 2, rep % 2
+            to_x, to_c, to_z = move(x, c, z)
+            pairs.append((z * reps + rep, to_z * reps + 2 * to_x + to_c))
+    return pairs
+
+
+def sine_cosine(phase):
+    turns = jnp.floor(phase * np.float32(2.0 / np.pi) + 0.5)
+    rest = phase - turns * np.float32(1.5703125)
+    rest = rest - turns * np.float32(4.837512969970703125e-4)
+    rest = rest - turns * np.float32(7.54978995489188216e-8)
+    square = rest * rest
+    sine = rest + rest * square * (
+        np.float32(-1.6666654611e-1)
+        + square * (np.float32(8.3321608736e-3) + square * np.float32(-1.9515295891e-4))
+    )
+    cosine = (
+        1.0
+        - 0.5 * square
+        + square
+        * square
+        * (
+            np.float32(4.166664568298827e-2)
+            + square * (np.float32(-1.388731625493765e-3) + square * np.float32(2.443315711809948e-5))
+        )
+    )
+    quadrant = turns.astype(jnp.int32) & 3
+    swap = (quadrant & 1) == 1
+    first = jnp.where(swap, cosine, sine)
+    second = jnp.where(swap, sine, cosine)
+    first = jnp.where(quadrant >= 2, -first, first)
+    second = jnp.where((quadrant == 1) | (quadrant == 2), -second, second)
+    return first, second
+
+
+def live_column(count, rows):
+    return lax.broadcasted_iota(jnp.int32, (rows, 1), 0) < count
+
+
+def dot_nn(a, b):
+    return jnp.dot(a, b, preferred_element_type=jnp.float32)
+
+
+def dot_nt(a, b):
+    return lax.dot_general(a, b, (((1,), (1,)), ((), ())), preferred_element_type=jnp.float32)
+
+
+PAR, CORE, LINE, SIDE, KEPT = range(5)
+
+
+def norm_kernel(place, patch_ref, cot_ref, index_ref, gain_ref, p0_ref, p1_ref, hidden_ref):
+    par = place[PAR]
+    rows, width = patch_ref.shape[1:]
+    quarter = width // 4
+    order = lax.broadcasted_iota(jnp.int32, (1, quarter), 1).astype(jnp.float32)
+    freq = jnp.exp(-np.log(np.float32(10000.0)) * order / quarter)
+    diagonal = lax.broadcasted_iota(jnp.int32, (rows, rows), 0) == lax.broadcasted_iota(
+        jnp.int32, (rows, rows), 1
+    )
+    for k, out_ref in enumerate((p0_ref, p1_ref)):
+        s = k ^ par
+        live = live_column(place[KEPT + s], rows)
+        position = index_ref[pl.ds(s, 1), :]
+        grid_row = (position // GRID_COLS).astype(jnp.float32)
+        grid_col = (position % GRID_COLS).astype(jnp.float32)
+        grid_row = jnp.sum(jnp.where(diagonal, grid_row, 0.0), axis=1, keepdims=True)
+        grid_col = jnp.sum(jnp.where(diagonal, grid_col, 0.0), axis=1, keepdims=True)
+        pieces = sine_cosine(grid_row * freq) + sine_cosine(grid_col * freq)
+        hidden = patch_ref[s].astype(jnp.float32) + jnp.concatenate(pieces, axis=1)
+        hidden_ref[k] = hidden
+        center = hidden - jnp.mean(hidden, axis=-1, keepdims=True)
+        spread = jnp.mean(center * center, axis=-1, keepdims=True)
+        normed = center * lax.rsqrt(spread + epsilon) * gain_ref[...]
+        out_ref[:rows, :] = jnp.where(live, normed, MARK).astype(out_ref.dtype)
+        grad = cot_ref[s]
+        out_ref[rows:, :] = jnp.where(live, grad, jnp.zeros_like(grad))
+
+
+def stage_kernel(place, q_in, k_in, v_in, o_in, q_out, k_out, v_out, o_out):
+    q_out[...] = q_in[...]
+    k_out[...] = k_in[...]
+    v_out[...] = v_in[...]
+    o_out[...] = o_in[...]
+
+
+def attend_kernel(
+    place, p0, p1, p2, p3, wq, wk, wv, wo,
+    att0, att1, att2, att3, dp_own, dp_oth, att_send, att_keep, dp_send, dp_keep,
+    norm_s, grad_s,
+):
+    block = p0.shape[0] // 2
+    rows = 4 * block
+    half = 2 * block
+    biases = []
+    for i, ref in enumerate((p0, p1, p2, p3)):
+        at = slice(i * block, (i + 1) * block)
+        value = ref[:block, :]
+        live = value[:, 0:1].astype(jnp.float32) < MARK
+        norm_s[at, :] = jnp.where(live, value, jnp.zeros_like(value))
+        grad_s[at, :] = ref[block:, :]
+        biases.append(jnp.where(live, 0.0, -1e30))
+    bias = jnp.concatenate(biases, axis=0)
+    low = lax.broadcasted_iota(jnp.int32, (rows, 128), 1) < 64
+    scale = jnp.bfloat16(0.125)
+    zero = jnp.zeros((rows, 128), jnp.bfloat16)
+    first = place[SIDE] == 0
+    for j in range(wq.shape[1] // 128):
+        cols = slice(128 * j, 128 * j + 128)
+        if j % 2 == 0:
+            two = slice(128 * j, 128 * j + 256)
+            normed = norm_s[...]
+            queries = dot_nn(normed, wq[:, two]).astype(jnp.bfloat16)
+            keys = dot_nn(normed, wk[:, two]).astype(jnp.bfloat16)
+            values = dot_nn(normed, wv[:, two]).astype(jnp.bfloat16)
+            d_att = dot_nt(grad_s[...], wo[two, :]).astype(jnp.bfloat16)
+        here = slice(128 * (j % 2), 128 * (j % 2) + 128)
+        q = queries[:, here] * scale
+        k = keys[:, here]
+        v = values[:, here]
+        g = d_att[:, here]
+        v_t = v.T
+        k_t = (k * scale).T
+        att_t, dq_t, dk, dv = [], [], [], []
+        for h in range(2):
+            mine = low if h == 0 else jnp.logical_not(low)
+            scores = dot_nt(k, jnp.where(mine, q, zero)) + bias
+            raised = jnp.exp(scores - jnp.max(scores, axis=0, keepdims=True))
+            prob = raised * (1.0 / jnp.sum(raised, axis=0, keepdims=True))
+            weights = prob.astype(jnp.bfloat16)
+            part = slice(64 * h, 64 * h + 64)
+            att_t.append(dot_nn(v_t[part], weights))
+            dv.append(dot_nn(weights, g))
+            d_prob = dot_nt(v, jnp.where(mine, g, zero))
+            total = jnp.sum(prob * d_prob, axis=0, keepdims=True)
+            d_score = (prob * (d_prob - total)).astype(jnp.bfloat16)
+            dq_t.append(dot_nn(k_t[part], d_score))
+            dk.append(dot_nn(d_score, q))
+        att_pair_t = jnp.concatenate(att_t, axis=0).astype(jnp.bfloat16)
+        att_pair = att_pair_t.T
+        dq_pair_t = jnp.concatenate(dq_t, axis=0).astype(jnp.bfloat16)
+        dk_pair = jnp.where(low, dk[0], dk[1]).astype(jnp.bfloat16)
+        dv_pair = jnp.where(low, dv[0], dv[1]).astype(jnp.bfloat16)
+        for i, out in enumerate((att0, att1, att2, att3)):
+            out[:, cols] = att_pair[i * block : (i + 1) * block]
+        for t, piece in enumerate((dq_pair_t.T, dk_pair, dv_pair)):
+            dp_own[t, :, cols] = piece[:half]
+            dp_oth[t, :, cols] = piece[half:]
+        at = slice(64 * j, 64 * j + 64)
+        att_keep[at, :] = jnp.where(first, att_pair_t[:64], att_pair_t[64:])
+        att_send[at, :] = jnp.where(first, att_pair_t[64:], att_pair_t[:64])
+        for t, piece in enumerate((dq_pair_t, dk_pair.T, dv_pair.T)):
+            at = slice(64 * (4 * t + j), 64 * (4 * t + j) + 64)
+            dp_keep[at, :] = jnp.where(first, piece[:64], piece[64:])
+            dp_send[at, :] = jnp.where(first, piece[64:], piece[:64])
+
+
+def in_order(place, own, got):
+    pieces = []
+    low = place == 0
+    for j in range(own.shape[1] // 128):
+        a, b = own[:, 128 * j : 128 * j + 128], got[:, 128 * j : 128 * j + 128]
+        pieces += [jnp.where(low, a, b), jnp.where(low, b, a)]
+    return jnp.concatenate(pieces, axis=1)
+
+
+def d_normed_kernel(place, own, got, w_ref, o0, o1, total):
+    step = pl.program_id(0)
+    term = dot_nt(in_order(place[CORE], own[step], got[step]), w_ref[...])
+
+    @pl.when(step == 0)
+    def _():
+        total[...] = term
+
+    @pl.when(step > 0)
+    def _():
+        total[...] += term
+
+    @pl.when(step == pl.num_programs(0) - 1)
+    def _():
+        half = o0.shape[0]
+        o0[...] = total[:half].astype(o0.dtype)
+        o1[...] = total[half:].astype(o1.dtype)
+
+
+def out_weight_kernel(place, keep, got, p0, p1, p2, p3, r0, r1, r2, r3, o0, o1, o2, o3, tokens, total):
+    block = p0.shape[0] // 2
+    rows = 4 * block
+    for i, ref in enumerate((p0, p1, p2, p3, r0, r1, r2, r3)):
+        tokens[i * block : (i + 1) * block, :] = ref[block:, :]
+    total[...] = dot_nn(keep[...], tokens[:rows, :]) + dot_nn(got[...], tokens[rows:, :])
+    columns = o0.shape[1]
+    for k, out in enumerate((o0, o1, o2, o3)):
+        at = pl.multiple_of((place[LINE] ^ k) * columns, 128)
+        out[...] = total[:, pl.ds(at, columns)].astype(out.dtype)
+
+
+def weight_kernel(place, keep, got, p0, p1, p2, p3, r0, r1, r2, r3, o0, o1, o2, o3, tokens):
+    block = p0.shape[0] // 2
+    rows = 4 * block
+    for i, ref in enumerate((p0, p1, p2, p3, r0, r1, r2, r3)):
+        tokens[i * block : (i + 1) * block, :] = ref[:block, :]
+    count = o0.shape[0]
+    for k, out in enumerate((o0, o1, o2, o3)):
+        at = pl.ds(pl.multiple_of((place[LINE] ^ k) * count, 16), count)
+        value = dot_nn(keep[at, :], tokens[:rows, :]) + dot_nn(got[at, :], tokens[rows:, :])
+        out[...] = value.astype(out.dtype)
+
+
+def sum_kernel(a0, a1, a2, a3, b0, b1, b2, b3, out):
+    f32 = jnp.float32
+    count = a0.shape[0]
+    value = (a0[...].astype(f32) + a1[...].astype(f32)) + (a2[...].astype(f32) + a3[...].astype(f32))
+    out[:count, :] = value.astype(out.dtype)
+    value = (b0[...].astype(f32) + b1[...].astype(f32)) + (b2[...].astype(f32) + b3[...].astype(f32))
+    value = value.astype(out.dtype)
+    columns = b0.shape[1]
+    for j in range(4):
+        out[count:, columns * j : columns * j + columns] = value[64 * j : 64 * j + 64, :]
+
+
+def finish_kernel(place, own, by_x, by_core, by_both, wide, narrow):
+    core_low, side_low = place[CORE] == 0, place[SIDE] == 0
+    count = own.shape[0] - 64
+    columns = narrow.shape[1]
+
+    def pick(at, c, x, part):
+        a = jnp.where(side_low == (x == 0), own[at, part], by_x[at, part])
+        b = jnp.where(side_low == (x == 0), by_core[at, part], by_both[at, part])
+        return jnp.where(core_low == (c == 0), a, b)
+
+    for c in range(2):
+        for i in range(count // 64):
+            at = slice(64 * i, 64 * i + 64)
+            both = jnp.concatenate([pick(at, c, x, slice(None)) for x in range(2)], axis=0)
+            col = 128 * (2 * i + c)
+            wide[:, col : col + 128] = both.T.astype(wide.dtype)
+        for j in range(4):
+            for x in range(2):
+                row = 128 * (2 * j + c) + 64 * x
+                part = slice(columns * j, columns * j + columns)
+                narrow[row : row + 64, :] = pick(slice(count, None), c, x, part).astype(narrow.dtype)
+
+
+def encode_kernel(place, a0, a1, b0, b1, w_ref, hidden_ref, out_ref):
+    par, core = place[PAR], place[LINE] // 2
+    for k, (a, b) in enumerate(((a0, b0), (a1, b1))):
+        s = k ^ par
+        projected = dot_nn(in_order(core, a[...], b[...]), w_ref[...])
+        live = live_column(place[KEPT + s], a.shape[0])
+        out_ref[s] = jnp.where(live, hidden_ref[k] + projected, 0.0).astype(out_ref.dtype)
+
+
+def patch_grad_kernel(place, d0, d1, p0, p1, hidden_ref, gain_ref, out_ref):
+    par = place[PAR]
+    rows = d0.shape[0]
+    for k, (d_ref, p_ref) in enumerate(((d0, p0), (d1, p1))):
+        s = k ^ par
+        hidden = hidden_ref[k]
+        center = hidden - jnp.mean(hidden, axis=-1, keepdims=True)
+        spread = jnp.mean(center * center, axis=-1, keepdims=True)
+        inv_std = lax.rsqrt(spread + epsilon)
+        unit = center * inv_std
+        d_hidden = norm_backward(d_ref[...].astype(jnp.float32), gain_ref[...], unit, inv_std)
+        live = live_column(place[KEPT + s], rows)
+        value = p_ref[rows:, :].astype(jnp.float32) + d_hidden
+        out_ref[s] = jnp.where(live, value, 0.0).astype(out_ref.dtype)
+
+
+SMEM_SPEC = pl.BlockSpec(memory_space=pltpu.SMEM)
+VMEM_SPEC = pl.BlockSpec(memory_space=pltpu.VMEM)
+
+
+def struct(shape, dtype=jnp.bfloat16):
+    return jax.ShapeDtypeStruct(shape, dtype)
+
+
+def call(kernel, args, outs, limit, place=None, scratch=(), flops=0, moved=1_000_000):
+    specs = [VMEM_SPEC] * len(args)
+    if place is not None:
+        args, specs = (place, *args), [SMEM_SPEC] + specs
+    single = not isinstance(outs, list)
+    return pl.pallas_call(
+        kernel,
+        in_specs=specs,
+        out_specs=VMEM_SPEC if single else [VMEM_SPEC] * len(outs),
+        out_shape=outs,
+        scratch_shapes=list(scratch),
+        compiler_params=pltpu.CompilerParams(vmem_limit_bytes=limit * MIB),
+        cost_estimate=pl.CostEstimate(flops=flops, bytes_accessed=moved, transcendentals=0),
+    )(*args)
+
+
+def chip_shards(patches, kept_index, kept_count, cotangent, w_qkv, w_out, gain):
+    bf16, f32 = jnp.bfloat16, jnp.float32
+    samples, slots, width = patches.shape
+    reps = lax.axis_size("rep")
+    rep = lax.axis_index("rep")
+    z = lax.axis_index("seq")
+    core, x = rep & 1, rep >> 1
+    place = jnp.concatenate(
+        [jnp.stack([z & 1, core, z, x]).astype(jnp.int32), kept_count.reshape(samples)]
+    )
+    own_width = width // 2
+    quarter = width // 4
+    rows = 4 * slots
+
+    def send(value, move):
+        return lax.ppermute(value, AXES, line_perm(move, reps))
+
+    def to_core(value):
+        return send(value, lambda x, c, z: (x, 1 - c, z))
+
+    def to_x(value):
+        return send(value, lambda x, c, z: (1 - x, c, z))
+
+    def to_chip(value, k):
+        return send(value, lambda x, c, z: (x, z >> 1, 2 * c + (k ^ (z & 1))))
+
+    def to_rows(value, k, other):
+        return send(value, lambda x, c, z: (x, z >> 1, 2 * (c ^ other) + (k ^ (z & 1))))
+
+    def along(value, k):
+        return send(value, lambda x, c, z: (x, c, z ^ k))
+
+    gain_row = gain.reshape(1, width)
+    pay = struct((2 * slots, width))
+    *mine, hidden = call(
+        norm_kernel,
+        (patches, cotangent, kept_index, gain_row),
+        [pay, pay, struct(patches.shape, f32)],
+        16,
+        place,
+        moved=4_000_000,
+    )
+    got = [to_chip(mine[k], k) for k in range(2)]
+
+    wide, tall = (width, 128), (128, width)
+    blocks = own_width // 128
+    staged = pl.pallas_call(
+        stage_kernel,
+        grid_spec=pltpu.PrefetchScalarGridSpec(
+            num_scalar_prefetch=1,
+            grid=(blocks,),
+            in_specs=[
+                pl.BlockSpec(wide, lambda j, p, t=t: (0, (width // 128) * t + 2 * j + p[CORE])) for t in range(3)
+            ]
+            + [pl.BlockSpec(tall, lambda j, p: (2 * j + p[CORE], 0))],
+            out_specs=[pl.BlockSpec(wide, lambda j, p: (0, j))] * 3 + [pl.BlockSpec(tall, lambda j, p: (j, 0))],
+        ),
+        out_shape=[struct((width, own_width))] * 3 + [struct((own_width, width))],
+        compiler_params=pltpu.CompilerParams(vmem_limit_bytes=8 * MIB),
+        cost_estimate=pl.CostEstimate(flops=0, bytes_accessed=8_000_000, transcendentals=0),
+    )(place, w_qkv, w_qkv, w_qkv, w_out)
+
+    here = got + [to_core(v) for v in got]
+    from_x = [to_x(v) for v in got]
+    there = from_x + [to_core(v) for v in from_x]
+
+    att = struct((slots, own_width))
+    d_rows = struct((3, 2 * slots, own_width))
+    att_t = struct((quarter, rows))
+    dp_t = struct((3 * quarter, rows))
+    *atts, dp_own, dp_oth, att_send, att_keep, dp_send, dp_keep = call(
+        attend_kernel,
+        (*here, *staged),
+        [att] * 4 + [d_rows] * 2 + [att_t] * 2 + [dp_t] * 2,
+        32,
+        place,
+        scratch=[pltpu.VMEM((rows, width), bf16)] * 2,
+        flops=6_000_000_000,
+        moved=20_000_000,
+    )
+    att_got = to_x(att_send)
+    dp_got = to_x(dp_send)
+    dp_core = to_core(dp_oth)
+    back_att = [to_rows(atts[k], k, 0) for k in range(2)] + [to_rows(atts[2 + k], k, 1) for k in range(2)]
+
+    d_normed = pl.pallas_call(
+        d_normed_kernel,
+        grid_spec=pltpu.PrefetchScalarGridSpec(
+            num_scalar_prefetch=1,
+            grid=(3,),
+            in_specs=[pl.BlockSpec(d_rows.shape, lambda i, p: (0, 0, 0))] * 2
+            + [pl.BlockSpec((width, width), lambda i, p: (0, i))],
+            out_specs=[pl.BlockSpec((slots, width), lambda i, p: (0, 0))] * 2,
+            scratch_shapes=[pltpu.VMEM((2 * slots, width), f32)],
+        ),
+        out_shape=[struct((slots, width))] * 2,
+        compiler_params=pltpu.CompilerParams(vmem_limit_bytes=16 * MIB),
+        cost_estimate=pl.CostEstimate(flops=1_200_000_000, bytes_accessed=8_000_000, transcendentals=0),
+    )(place, dp_own, dp_core, w_qkv)
+    back_dn = [to_rows(d_normed[k], k, 0) for k in range(2)]
+
+    out_part = struct((quarter, quarter))
+    dwo = call(
+        out_weight_kernel,
+        (att_keep, att_got, *here, *there),
+        [out_part] * 4,
+        12,
+        place,
+        scratch=[pltpu.VMEM((2 * rows, width), bf16), pltpu.VMEM((quarter, width), f32)],
+        flops=400_000_000,
+        moved=4_000_000,
+    )
+    dwo = [dwo[0]] + [along(dwo[k], k) for k in range(1, 4)]
+    in_part = struct((3 * quarter // 4, width))
+    dwq = call(
+        weight_kernel,
+        (dp_keep, dp_got, *here, *there),
+        [in_part] * 4,
+        12,
+        place,
+        scratch=[pltpu.VMEM((2 * rows, width), bf16)],
+        flops=1_200_000_000,
+        moved=6_000_000,
+    )
+    dwq = [dwq[0]] + [along(dwq[k], k) for k in range(1, 4)]
+
+    encoded = call(
+        encode_kernel,
+        (*back_att, w_out, hidden),
+        struct(patches.shape),
+        12,
+        place,
+        flops=400_000_000,
+        moved=5_000_000,
+    )
+    d_patches = call(
+        patch_grad_kernel,
+        (*back_dn, *mine, hidden, gain_row),
+        struct(patches.shape),
+        8,
+        place,
+        moved=4_000_000,
+    )
+    sums = call(sum_kernel, (*dwq, *dwo), struct((quarter, width)), 8, moved=2_500_000)
+    by_x = to_x(sums)
+    by_core = to_core(sums)
+    by_both = to_core(by_x)
+    qkv_grad, out_grad = call(
+        finish_kernel,
+        (sums, by_x, by_core, by_both),
+        [struct((width, 3 * quarter), f32), struct((width, quarter), f32)],
+        12,
+        place,
+        moved=6_000_000,
+    )
+    return (encoded, d_patches, qkv_grad, out_grad)
+
+
 def solution(mesh):
     in_specs = (
         P(("grp", "rep"), "seq", None),
@@ -236,4 +700,12 @@
         P("grp", "seq"),
         P("grp", "seq"),
     )
-    return jax.shard_map(shards, mesh=mesh, in_specs=in_specs, out_specs=out_specs, check_vma=False)
+    chips = mesh.shape["seq"] == 4 and mesh.shape["rep"] % 2 == 0 and HEADS % 8 == 0
+
+    def run(patches, *rest):
+        per_device = patches.shape[0] // (mesh.shape["grp"] * mesh.shape["rep"])
+        body = chip_shards if chips and per_device == 2 else shards
+        inner = jax.shard_map(body, mesh=mesh, in_specs=in_specs, out_specs=out_specs, check_vma=False)
+        return inner(patches, *rest)
+
+    return run

time: 355 us -> 162 us (0.46)
  waiting for transfers between devices: 143 us -> 84.5 us
  matrix products: 57.9 us -> 0 us
  local copies, waits for them, and re-layouts: 57.6 us -> 8.49 us
  blocking collectives: 35.3 us -> 0 us
  Pallas kernels: 0 us -> 27.7 us
  between operations: 14 us -> 0.83 us
  other arithmetic: 12.2 us -> 0.01 us
  starting transfers between devices: 31.7 us -> 39 us
    ppermute x0 -> x26, waiting for transfers between devices: none -> 84.5 us  [send(): return lax.ppermute(value, AXES, line_perm(move, reps))]
    psum x1 -> x0, waiting for transfers between devices: 77.7 us -> none  [shards(): qkv_grad, out_grad = lax.psum((qkv_part, out_part), 'rep')]
    all_to_all x6 -> x0, waiting for transfers between devices: 64.2 us -> none  [the longest x1 35.1 us: shards(): lax.all_to_all(key_value_grad.astype(jnp.bfloat16), 'seq', split_axis=0,...]
    dot_general x11 -> x0, matrix products: 52.8 us -> none  [the longest x1 8.91 us: head_block(): d_key = jnp.dot(d_score.T, query_rows, preferred_element_type=jnp.float32)]
    ppermute x0 -> x26, starting transfers between devices: none -> 39 us  [send(): return lax.ppermute(value, AXES, line_perm(move, reps))]
    all_to_all x6 -> x0, starting transfers between devices: 31.7 us -> none  [the longest x1 6.87 us: shards(): lax.all_to_all(key_value_send, 'seq', split_axis=0, concat_axis=0, tiled=...]
    pallas_call x0 -> x10, Pallas kernels: none -> 27.7 us  [the longest x8 21.6 us: call(): pl.pallas_call(kernel, in_specs=specs, out_specs=VMEM_SPEC if single else...]
    all_gather x1 -> x0, blocking collectives: 24.6 us -> none  [shards(): all_counts = lax.all_gather(kept_count, 'seq', axis=1, tiled=True)]
  transfers between devices with their start and end apart: 9 -> 26, of which waited for: 5 -> 11; matrix products, arithmetic and copies ran while one was open for 30% -> 0% of each run, Pallas kernels for 0% -> 14%
where the time goes in v2:
time: 162 us; the launch traced here: 161 us
  waiting for transfers between devices  84.5 us (52%)
  starting transfers between devices  39 us (24%)
  Pallas kernels  27.7 us (17%)
  local copies, waits for them, and re-layouts  8.49 us (5%)
    ppermute x26, waiting for transfers between devices, send(): return lax.ppermute(value, AXES, line_perm(move, reps))  84.5 us
    ppermute x26, starting transfers between devices, send(): return lax.ppermute(value, AXES, line_perm(move, reps))  39 us
    pallas_call x8, Pallas kernels, call(): pl.pallas_call(kernel, in_specs=specs, out_specs=VMEM_SPEC if single else...  21.6 us
    unnamed x20, local copies, waits for them, and re-layouts  7.75 us
    pallas_call x1, Pallas kernels, chip_shards(): pl.pallas_call(d_normed_kernel, grid_spec=pltpu.PrefetchScalarGridSpec(nu...  3.77 us
  transfers between devices with their start and end apart: 26, of which 11 were waited for; matrix products, arithmetic and copies ran while one was open for 0% of the time, Pallas kernels for 14%

profile of v2, /device:TPU:9, one launch (start us, length us, event | category | flops | bytes accessed | tf_op | source)
XLA Modules:
  0.0 160.5 jit_solution(6818758451173979302)
XLA Ops:
  4.7 1.4 shard_map.102
  6.2 4.8 %collective-permute-start = (bf16[192,1024]{1,0:T(8,128)(2,1)S(1)}, bf16[192,1024]{1,0:T(8,128)(2,1)S(1)}, u32[]{:S(2)}, u32[]{:S(2)}) collective-permute-start(bf16[192,1024]{1,0:T(8,128)(2,1)S(1)} %get-tuple-element.33.p0), channel_id=1, source_target_pairs={{0,0},{1,8},{2,2},{3,10},{4,4},{5,12},{6,6},{7,14},{8,1},{9,9},{10... | collective-permute-start | bytes 1179656 | tf_op jit(solution)/shard_map/ppermute | solution.py:544
  11.0 13.0 %collective-permute-done.p0 = bf16[192,1024]{1,0:T(8,128)(2,1)S(1)} collective-permute-done((bf16[192,1024]{1,0:T(8,128)(2,1)S(1)}, bf16[192,1024]{1,0:T(8,128)(2,1)S(1)}, u32[]{:S(2)}, u32[]{:S(2)}) %collective-permute-start) | collective-permute-done | bytes 393248 | tf_op jit(solution)/shard_map/ppermute | solution.py:544
  24.1 4.2 %collective-permute-done.1.p1 = bf16[192,1024]{1,0:T(8,128)(2,1)S(1)} collective-permute-done((bf16[192,1024]{1,0:T(8,128)(2,1)S(1)}, bf16[192,1024]{1,0:T(8,128)(2,1)S(1)}, u32[]{:S(2)}, u32[]{:S(2)}) %collective-permute-start.1) | collective-permute-done | bytes 393248 | tf_op jit(solution)/shard_map/ppermute | solution.py:544
  28.3 2.8 %copy-done = bf16[1024,3072]{1,0:T(8,128)(2,1)S(1)} copy-done((bf16[1024,3072]{1,0:T(8,128)(2,1)S(1)}, bf16[1024,3072]{1,0:T(8,128)(2,1)}, u32[]{:S(2)}) %copy-start) | copy-done | bytes 6291480
  31.1 1.6 copy-done.1
  32.7 2.4 %shard_map.103 = (bf16[1024,512]{1,0:T(8,128)(2,1)S(1)}, bf16[1024,512]{1,0:T(8,128)(2,1)S(1)}, bf16[1024,512]{1,0:T(8,128)(2,1)S(1)}, bf16[512,1024]{1,0:T(8,128)(2,1)S(1)}) custom-call(s32[6]{0:T(128)S(1)} %concatenate.3.place, bf16[1024,3072]{1,0:T(8,128)(2,1)S(1)} %copy-done, bf16[1024,3072]{1,0:T(8,128)(2,1)S(1)} %copy-done, ...), custom_call_target="tpu_custom_call" | custom-call | bytes 8000000 | tf_op jit(solution)/shard_map/pallas_call | solution.py:575
  36.6 9.2 %shard_map.104 = (bf16[96,512]{1,0:T(8,128)(2,1)S(1)}, bf16[96,512]{1,0:T(8,128)(2,1)S(1)}, bf16[96,512]{1,0:T(8,128)(2,1)S(1)}, bf16[96,512]{1,0:T(8,128)(2,1)S...) custom-call(s32[6]{0:T(128)S(1)} %concatenate.3.place, ...), custom_call_target="tpu_custom_call" | custom-call | flops 6000000000 | bytes 20000000 | tf_op jit(solution)/shard_map/pallas_call | solution.py:518
  47.1 1.4 collective-permute-start.14
  48.5 5.2 %collective-permute-done.13.r1 = bf16[192,1024]{1,0:T(8,128)(2,1)S(1)} collective-permute-done((bf16[192,1024]{1,0:T(8,128)(2,1)S(1)}, bf16[192,1024]{1,0:T(8,128)(2,1)S(1)}, u32[]{:S(2)}, u32[]{:S(2)}) %collective-permute-start.13) | collective-permute-done | bytes 393248 | tf_op jit(solution)/shard_map/ppermute | solution.py:544
  53.7 2.3 %collective-permute-start.15 = (bf16[192,1024]{1,0:T(8,128)(2,1)S(1)}, bf16[192,1024]{1,0:T(8,128)(2,1)S(1)}, u32[]{:S(2)}, u32[]{:S(2)}) collective-permute-start(bf16[192,1024]{1,0:T(8,128)(2,1)S(1)} %collective-permute-done.13.r1), channel_id=1, source_target_pairs={{0,1},{1,0},{2,3},{3,2},{4,5},{5,4},{6,7},{7,6},{8,9},{9,8},{10,11... | collective-permute-start | bytes 1179656 | tf_op jit(solution)/shard_map/ppermute | solution.py:544
  57.4 9.0 %collective-permute-done.11.got = bf16[768,384]{1,0:T(8,128)(2,1)S(1)} collective-permute-done((bf16[768,384]{1,0:T(8,128)(2,1)S(1)}, bf16[768,384]{1,0:T(8,128)(2,1)S(1)}, u32[]{:S(2)}, u32[]{:S(2)}) %collective-permute-start.11) | collective-permute-done | bytes 589856 | tf_op jit(solution)/shard_map/ppermute | solution.py:544
  66.3 2.3 %shard_map.108 = (bf16[192,1024]{1,0:T(8,128)(2,1)S(1)}, bf16[192,1024]{1,0:T(8,128)(2,1)S(1)}, bf16[192,1024]{1,0:T(8,128)(2,1)S(1)}, bf16[192,1024]{1,0:T(8,128)(2,1)S(1)}) custom-call(s32[6]{0:T(128)S(1)} %concatenate.3.place, bf16[768,384]{1,0:T(8,128)(2,1)S(1)} %get-tuple-element.48.keep, bf16[768,384]{1,0:T(8,128)(2,1)S(1)} %collective-permute-done.11.got, ...), custom_call_target="tpu_custom_call" | custom-call | flops 1200000000 | bytes 6000000 | tf_op jit(solution)/shard_map/pallas_call | solution.py:518
  68.8 4.3 %collective-permute-start.17 = (bf16[192,1024]{1,0:T(8,128)(2,1)S(1)}, bf16[192,1024]{1,0:T(8,128)(2,1)S(1)}, u32[]{:S(2)}, u32[]{:S(2)}) collective-permute-start(bf16[192,1024]{1,0:T(8,128)(2,1)S(1)} %get-tuple-element.52), channel_id=1, source_target_pairs={{0,8},{1,9},{2,10},{3,11},{4,12},{5,13},{6,14},{7,15},{8,0},{9,1},... | collective-permute-start | bytes 1179656 | tf_op jit(solution)/shard_map/ppermute | solution.py:544
  73.1 1.3 shard_map.109
  75.7 1.5 collective-permute-start.21
  77.1 19.4 %collective-permute-done.20.b1 = bf16[256,256]{1,0:T(8,128)(2,1)S(1)} collective-permute-done((bf16[256,256]{1,0:T(8,128)(2,1)S(1)}, bf16[256,256]{1,0:T(8,128)(2,1)S(1)}, u32[]{:S(2)}, u32[]{:S(2)}) %collective-permute-start.20) | collective-permute-done | bytes 131104 | tf_op jit(solution)/shard_map/ppermute | solution.py:544
  96.5 4.3 %collective-permute-start.22 = (bf16[256,256]{1,0:T(8,128)(2,1)S(1)}, bf16[256,256]{1,0:T(8,128)(2,1)S(1)}, u32[]{:S(2)}, u32[]{:S(2)}) collective-permute-start(bf16[256,256]{1,0:T(8,128)(2,1)S(1)} %get-tuple-element.59), channel_id=1, source_target_pairs={{0,12},{1,13},{2,14},{3,15},{4,8},{5,9},{6,10},{7,11},{8,4},{9,5},... | collective-permute-start | bytes 393224 | tf_op jit(solution)/shard_map/ppermute | solution.py:544
  100.8 13.1 %collective-permute-done.21.b2 = bf16[256,256]{1,0:T(8,128)(2,1)S(1)} collective-permute-done((bf16[256,256]{1,0:T(8,128)(2,1)S(1)}, bf16[256,256]{1,0:T(8,128)(2,1)S(1)}, u32[]{:S(2)}, u32[]{:S(2)}) %collective-permute-start.21) | collective-permute-done | bytes 131104 | tf_op jit(solution)/shard_map/ppermute | solution.py:544
  113.9 2.8 %collective-permute-done.22.b3 = bf16[256,256]{1,0:T(8,128)(2,1)S(1)} collective-permute-done((bf16[256,256]{1,0:T(8,128)(2,1)S(1)}, bf16[256,256]{1,0:T(8,128)(2,1)S(1)}, u32[]{:S(2)}, u32[]{:S(2)}) %collective-permute-start.22) | collective-permute-done | bytes 131104 | tf_op jit(solution)/shard_map/ppermute | solution.py:544
  118.3 2.6 %collective-permute-start.8 = (bf16[3,192,512]{2,1,0:T(8,128)(2,1)S(1)}, bf16[3,192,512]{2,1,0:T(8,128)(2,1)S(1)}, u32[]{:S(2)}, u32[]{:S(2)}) collective-permute-start(bf16[3,192,512]{2,1,0:T(8,128)(2,1)S(1)} %get-tuple-element.45), channel_id=1, source_target_pairs={{0,1},{1,0},{2,3},{3,2},{4,5},{5,4},{6,7},{7,6},{8,9},{9,8},{10,11... | collective-permute-start | bytes 1769480 | tf_op jit(solution)/shard_map/ppermute | solution.py:544
  120.9 7.3 %collective-permute-done.23.by_x = bf16[256,1024]{1,0:T(8,128)(2,1)S(1)} collective-permute-done((bf16[256,1024]{1,0:T(8,128)(2,1)S(1)}, bf16[256,1024]{1,0:T(8,128)(2,1)S(1)}, u32[]{:S(2)}, u32[]{:S(2)}) %collective-permute-start.23) | collective-permute-done | bytes 524320 | tf_op jit(solution)/shard_map/ppermute | solution.py:544
  128.1 3.3 %collective-permute-start.25 = (bf16[256,1024]{1,0:T(8,128)(2,1)S(1)}, bf16[256,1024]{1,0:T(8,128)(2,1)S(1)}, u32[]{:S(2)}, u32[]{:S(2)}) collective-permute-start(bf16[256,1024]{1,0:T(8,128)(2,1)S(1)} %collective-permute-done.23.by_x), channel_id=1, source_target_pairs={{0,1},{1,0},{2,3},{3,2},{4,5},{5,4},{6,7},{7,6},{8,9},{9,8},{10,11... | collective-permute-start | bytes 1572872 | tf_op jit(solution)/shard_map/ppermute | solution.py:544
  131.4 1.9 %collective-permute-start.4 = (bf16[96,512]{1,0:T(8,128)(2,1)S(1)}, bf16[96,512]{1,0:T(8,128)(2,1)S(1)}, u32[]{:S(2)}, u32[]{:S(2)}) collective-permute-start(bf16[96,512]{1,0:T(8,128)(2,1)S(1)} %get-tuple-element.39), channel_id=1, source_target_pairs={{0,0},{1,8},{2,2},{3,10},{4,4},{5,12},{6,6},{7,14},{8,1},{9,9},{10... | collective-permute-start | bytes 294920 | tf_op jit(solution)/shard_map/ppermute | solution.py:544
  133.3 1.9 %collective-permute-start.5 = (bf16[96,512]{1,0:T(8,128)(2,1)S(1)}, bf16[96,512]{1,0:T(8,128)(2,1)S(1)}, u32[]{:S(2)}, u32[]{:S(2)}) collective-permute-start(bf16[96,512]{1,0:T(8,128)(2,1)S(1)} %get-tuple-element.40), channel_id=1, source_target_pairs={{0,4},{1,12},{2,6},{3,14},{4,0},{5,8},{6,2},{7,10},{8,5},{9,13},{1... | collective-permute-start | bytes 294920 | tf_op jit(solution)/shard_map/ppermute | solution.py:544
  135.2 3.8 %shard_map.106 = (bf16[96,1024]{1,0:T(8,128)(2,1)S(1)}, bf16[96,1024]{1,0:T(8,128)(2,1)S(1)}) custom-call(s32[6]{0:T(128)S(1)} %concatenate.3.place, bf16[3,192,512]{2,1,0:T(8,128)(2,1)S(1)} %get-tuple-element.44.own, bf16[3,192,512]{2,1,0:T(8,128)(2,1)S(1)} %collective-permute-done.8.got, bf16[1024,3072]{1,0:T(8,128)(2,1)S(1)} %bitcast.7), custom_call_target="tpu_custom_call" | custom-call | flops 1200000000 | bytes 8000000 | tf_op jit(solution)/shard_map/pallas_call | solution.py:614
  140.2 2.2 %collective-permute-done.5.a1 = bf16[96,512]{1,0:T(8,128)(2,1)S(1)} collective-permute-done((bf16[96,512]{1,0:T(8,128)(2,1)S(1)}, bf16[96,512]{1,0:T(8,128)(2,1)S(1)}, u32[]{:S(2)}, u32[]{:S(2)}) %collective-permute-start.5) | collective-permute-done | bytes 98336 | tf_op jit(solution)/shard_map/ppermute | solution.py:544
  142.5 2.9 %collective-permute-start.9 = (bf16[96,1024]{1,0:T(8,128)(2,1)S(1)}, bf16[96,1024]{1,0:T(8,128)(2,1)S(1)}, u32[]{:S(2)}, u32[]{:S(2)}) collective-permute-start(bf16[96,1024]{1,0:T(8,128)(2,1)S(1)} %get-tuple-element.46), channel_id=1, source_target_pairs={{0,0},{1,8},{2,2},{3,10},{4,4},{5,12},{6,6},{7,14},{8,1},{9,9},{10... | collective-permute-start | bytes 589832 | tf_op jit(solution)/shard_map/ppermute | solution.py:544
  145.5 8.0 %collective-permute-done.7.b1 = bf16[96,512]{1,0:T(8,128)(2,1)S(1)} collective-permute-done((bf16[96,512]{1,0:T(8,128)(2,1)S(1)}, bf16[96,512]{1,0:T(8,128)(2,1)S(1)}, u32[]{:S(2)}, u32[]{:S(2)}) %collective-permute-start.7) | collective-permute-done | bytes 98336 | tf_op jit(solution)/shard_map/ppermute | solution.py:544
  153.5 2.1 %shard_map.105 = bf16[2,96,1024]{2,1,0:T(8,128)(2,1)} custom-call(s32[6]{0:T(128)S(1)} %concatenate.3.place, bf16[96,512]{1,0:T(8,128)(2,1)S(1)} %collective-permute-done.4.a0, bf16[96,512]{1,0:T(8,128)(2,1)S(1)} %collective-permute-done.5.a1, bf16[96,512]{1,0:T(8,128)(2,1)S(1)} %collective-permute-done.6.b0, bf16[96,512]{1,0:T(8,128)(2,1)S(1)} %collective-permute-done.7.b1, ...), custom_call_target="tpu_custom_call" | custom-call | flops 400000000 | bytes 5000000 | tf_op jit(solution)/shard_map/pallas_call | solution.py:518
  155.6 1.9 %shard_map.107 = bf16[2,96,1024]{2,1,0:T(8,128)(2,1)} custom-call(s32[6]{0:T(128)S(1)} %concatenate.3.place, bf16[96,1024]{1,0:T(8,128)(2,1)S(1)} %collective-permute-done.9.d0, bf16[96,1024]{1,0:T(8,128)(2,1)S(1)} %collective-permute-done.10.d1, bf16[192,1024]{1,0:T(8,128)(2,1)S(1)} %get-tuple-element.33.p0, bf16[192,1024]{1,0:T(8,128)(2,1)S(1)} %get-tuple-element.34.p1, ...), custom_call_target="tpu_custom_call" | custom-call | bytes 4000000 | tf_op jit(solution)/shard_map/pallas_call | solution.py:518
  157.5 3.0 %shard_map.111 = (f32[1024,768]{1,0:T(8,128)}, f32[1024,256]{1,0:T(8,128)}) custom-call(s32[6]{0:T(128)S(1)} %concatenate.3.place, bf16[256,1024]{1,0:T(8,128)(2,1)S(1)} %shard_map.110.own, bf16[256,1024]{1,0:T(8,128)(2,1)S(1)} %collective-permute-done.23.by_x, bf16[256,1024]{1,0:T(8,128)(2,1)S(1)} %collective-permute-done.24.by_core, ...), custom_call_target="tpu_custom_call" | custom-call | bytes 6000000 | tf_op jit(solution)/shard_map/pallas_call | solution.py:518
  (52 shorter events, 12.5 us)
Async XLA Ops:
  6.2 17.9 %collective-permute-start = (bf16[192,1024]{1,0:T(8,128)(2,1)S(1)}, bf16[192,1024]{1,0:T(8,128)(2,1)S(1)}, u32[]{:S(2)}, u32[]{:S(2)}) collective-permute-start(bf16[192,1024]{1,0:T(8,128)(2,1)S(1)} %get-tuple-element.33.p0), channel_id=1, source_target_pairs={{0,0},{1,8},{2,2},{3,10},{4,4},{5,12},{6,6},{7,14},{8,1},{9,9},{10... | collective-permute-start | bytes 1179656 | tf_op jit(solution)/shard_map/ppermute | solution.py:544
  11.0 17.3 %collective-permute-start.1 = (bf16[192,1024]{1,0:T(8,128)(2,1)S(1)}, bf16[192,1024]{1,0:T(8,128)(2,1)S(1)}, u32[]{:S(2)}, u32[]{:S(2)}) collective-permute-start(bf16[192,1024]{1,0:T(8,128)(2,1)S(1)} %get-tuple-element.34.p1), channel_id=1, source_target_pairs={{0,4},{1,12},{2,6},{3,14},{4,0},{5,8},{6,2},{7,10},{8,5},{9,13},{1... | collective-permute-start | bytes 1179656 | tf_op jit(solution)/shard_map/ppermute | solution.py:544
  24.1 12.5 %collective-permute-start.2 = (bf16[192,1024]{1,0:T(8,128)(2,1)S(1)}, bf16[192,1024]{1,0:T(8,128)(2,1)S(1)}, u32[]{:S(2)}, u32[]{:S(2)}) collective-permute-start(bf16[192,1024]{1,0:T(8,128)(2,1)S(1)} %collective-permute-done.p0), channel_id=1, source_target_pairs={{0,1},{1,0},{2,3},{3,2},{4,5},{5,4},{6,7},{7,6},{8,9},{9,8},{10,11... | collective-permute-start | bytes 1179656 | tf_op jit(solution)/shard_map/ppermute | solution.py:544
  28.3 8.3 %collective-permute-start.3 = (bf16[192,1024]{1,0:T(8,128)(2,1)S(1)}, bf16[192,1024]{1,0:T(8,128)(2,1)S(1)}, u32[]{:S(2)}, u32[]{:S(2)}) collective-permute-start(bf16[192,1024]{1,0:T(8,128)(2,1)S(1)} %collective-permute-done.1.p1), channel_id=1, source_target_pairs={{0,1},{1,0},{2,3},{3,2},{4,5},{5,4},{6,7},{7,6},{8,9},{9,8},{10,11... | collective-permute-start | bytes 1179656 | tf_op jit(solution)/shard_map/ppermute | solution.py:544
  28.3 2.8 %copy-start = (bf16[1024,3072]{1,0:T(8,128)(2,1)S(1)}, bf16[1024,3072]{1,0:T(8,128)(2,1)}, u32[]{:S(2)}) copy-start(bf16[1024,3072]{1,0:T(8,128)(2,1)} %w_ref.3) | copy-start | bytes 18874372
  31.1 1.6 copy-start.1
  35.0 12.1 %collective-permute-start.12 = (bf16[192,1024]{1,0:T(8,128)(2,1)S(1)}, bf16[192,1024]{1,0:T(8,128)(2,1)S(1)}, u32[]{:S(2)}, u32[]{:S(2)}) collective-permute-start(bf16[192,1024]{1,0:T(8,128)(2,1)S(1)} %collective-permute-done.p0), channel_id=1, source_target_pairs={{0,2},{1,3},{2,0},{3,1},{4,6},{5,7},{6,4},{7,5},{8,10},{9,11},{10,... | collective-permute-start | bytes 1179656 | tf_op jit(solution)/shard_map/ppermute | solution.py:544
  36.3 17.4 %collective-permute-start.13 = (bf16[192,1024]{1,0:T(8,128)(2,1)S(1)}, bf16[192,1024]{1,0:T(8,128)(2,1)S(1)}, u32[]{:S(2)}, u32[]{:S(2)}) collective-permute-start(bf16[192,1024]{1,0:T(8,128)(2,1)S(1)} %collective-permute-done.1.p1), channel_id=1, source_target_pairs={{0,2},{1,3},{2,0},{3,1},{4,6},{5,7},{6,4},{7,5},{8,10},{9,11},{10,... | collective-permute-start | bytes 1179656 | tf_op jit(solution)/shard_map/ppermute | solution.py:544
  36.6 98.6 %slice-start = ((s8[6291456]{0:T(1024)(128)(4,1)}), s8[4194304]{0:T(1024)(128)(4,1)S(1)}, s32[]{:S(2)}) async-start(s8[6291456]{0:T(1024)(128)(4,1)} %bitcast.6), calls=%async_computation | async-start | bytes 8388608
  36.6 98.6 %slice-start.1 = ((s8[6291456]{0:T(1024)(128)(4,1)}), s8[2097152]{0:T(1024)(128)(4,1)S(1)}, s32[]{:S(2)}) async-start(s8[6291456]{0:T(1024)(128)(4,1)} %bitcast.6), calls=%async_computation.1 | async-start | bytes 4194304
  45.8 20.5 %collective-permute-start.11 = (bf16[768,384]{1,0:T(8,128)(2,1)S(1)}, bf16[768,384]{1,0:T(8,128)(2,1)S(1)}, u32[]{:S(2)}, u32[]{:S(2)}) collective-permute-start(bf16[768,384]{1,0:T(8,128)(2,1)S(1)} %get-tuple-element.49), channel_id=1, source_target_pairs={{0,2},{1,3},{2,0},{3,1},{4,6},{5,7},{6,4},{7,5},{8,10},{9,11},{10,... | collective-permute-start | bytes 1769480 | tf_op jit(solution)/shard_map/ppermute | solution.py:544
  47.1 10.1 %collective-permute-start.14 = (bf16[192,1024]{1,0:T(8,128)(2,1)S(1)}, bf16[192,1024]{1,0:T(8,128)(2,1)S(1)}, u32[]{:S(2)}, u32[]{:S(2)}) collective-permute-start(bf16[192,1024]{1,0:T(8,128)(2,1)S(1)} %collective-permute-done.12.r0), channel_id=1, source_target_pairs={{0,1},{1,0},{2,3},{3,2},{4,5},{5,4},{6,7},{7,6},{8,9},{9,8},{10,11... | collective-permute-start | bytes 1179656 | tf_op jit(solution)/shard_map/ppermute | solution.py:544
  53.7 3.7 %collective-permute-start.15 = (bf16[192,1024]{1,0:T(8,128)(2,1)S(1)}, bf16[192,1024]{1,0:T(8,128)(2,1)S(1)}, u32[]{:S(2)}, u32[]{:S(2)}) collective-permute-start(bf16[192,1024]{1,0:T(8,128)(2,1)S(1)} %collective-permute-done.13.r1), channel_id=1, source_target_pairs={{0,1},{1,0},{2,3},{3,2},{4,5},{5,4},{6,7},{7,6},{8,9},{9,8},{10,11... | collective-permute-start | bytes 1179656 | tf_op jit(solution)/shard_map/ppermute | solution.py:544
  56.0 17.1 %collective-permute-start.19 = (bf16[256,384]{1,0:T(8,128)(2,1)S(1)}, bf16[256,384]{1,0:T(8,128)(2,1)S(1)}, u32[]{:S(2)}, u32[]{:S(2)}) collective-permute-start(bf16[256,384]{1,0:T(8,128)(2,1)S(1)} %get-tuple-element.55), channel_id=1, source_target_pairs={{0,2},{1,3},{2,0},{3,1},{4,6},{5,7},{6,4},{7,5},{8,10},{9,11},{10,... | collective-permute-start | bytes 589832 | tf_op jit(solution)/shard_map/ppermute | solution.py:544
  68.7 48.0 %collective-permute-start.16 = (bf16[192,1024]{1,0:T(8,128)(2,1)S(1)}, bf16[192,1024]{1,0:T(8,128)(2,1)S(1)}, u32[]{:S(2)}, u32[]{:S(2)}) collective-permute-start(bf16[192,1024]{1,0:T(8,128)(2,1)S(1)} %get-tuple-element.51), channel_id=1, source_target_pairs={{0,4},{1,5},{2,6},{3,7},{4,0},{5,1},{6,2},{7,3},{8,12},{9,13},{10,... | collective-permute-start | bytes 1179656 | tf_op jit(solution)/shard_map/ppermute | solution.py:544
  68.8 47.9 %collective-permute-start.17 = (bf16[192,1024]{1,0:T(8,128)(2,1)S(1)}, bf16[192,1024]{1,0:T(8,128)(2,1)S(1)}, u32[]{:S(2)}, u32[]{:S(2)}) collective-permute-start(bf16[192,1024]{1,0:T(8,128)(2,1)S(1)} %get-tuple-element.52), channel_id=1, source_target_pairs={{0,8},{1,9},{2,10},{3,11},{4,12},{5,13},{6,14},{7,15},{8,0},{9,1},... | collective-permute-start | bytes 1179656 | tf_op jit(solution)/shard_map/ppermute | solution.py:544
  73.1 43.6 %collective-permute-start.18 = (bf16[192,1024]{1,0:T(8,128)(2,1)S(1)}, bf16[192,1024]{1,0:T(8,128)(2,1)S(1)}, u32[]{:S(2)}, u32[]{:S(2)}) collective-permute-start(bf16[192,1024]{1,0:T(8,128)(2,1)S(1)} %get-tuple-element.53), channel_id=1, source_target_pairs={{0,12},{1,13},{2,14},{3,15},{4,8},{5,9},{6,10},{7,11},{8,4},{9,5},... | collective-permute-start | bytes 1179656 | tf_op jit(solution)/shard_map/ppermute | solution.py:544
  74.4 22.1 %collective-permute-start.20 = (bf16[256,256]{1,0:T(8,128)(2,1)S(1)}, bf16[256,256]{1,0:T(8,128)(2,1)S(1)}, u32[]{:S(2)}, u32[]{:S(2)}) collective-permute-start(bf16[256,256]{1,0:T(8,128)(2,1)S(1)} %get-tuple-element.57), channel_id=1, source_target_pairs={{0,4},{1,5},{2,6},{3,7},{4,0},{5,1},{6,2},{7,3},{8,12},{9,13},{10,... | collective-permute-start | bytes 393224 | tf_op jit(solution)/shard_map/ppermute | solution.py:544
  75.7 38.2 %collective-permute-start.21 = (bf16[256,256]{1,0:T(8,128)(2,1)S(1)}, bf16[256,256]{1,0:T(8,128)(2,1)S(1)}, u32[]{:S(2)}, u32[]{:S(2)}) collective-permute-start(bf16[256,256]{1,0:T(8,128)(2,1)S(1)} %get-tuple-element.58), channel_id=1, source_target_pairs={{0,8},{1,9},{2,10},{3,11},{4,12},{5,13},{6,14},{7,15},{8,0},{9,1},... | collective-permute-start | bytes 393224 | tf_op jit(solution)/shard_map/ppermute | solution.py:544
  96.5 20.2 %collective-permute-start.22 = (bf16[256,256]{1,0:T(8,128)(2,1)S(1)}, bf16[256,256]{1,0:T(8,128)(2,1)S(1)}, u32[]{:S(2)}, u32[]{:S(2)}) collective-permute-start(bf16[256,256]{1,0:T(8,128)(2,1)S(1)} %get-tuple-element.59), channel_id=1, source_target_pairs={{0,12},{1,13},{2,14},{3,15},{4,8},{5,9},{6,10},{7,11},{8,4},{9,5},... | collective-permute-start | bytes 393224 | tf_op jit(solution)/shard_map/ppermute | solution.py:544
  117.0 11.2 %collective-permute-start.23 = (bf16[256,1024]{1,0:T(8,128)(2,1)S(1)}, bf16[256,1024]{1,0:T(8,128)(2,1)S(1)}, u32[]{:S(2)}, u32[]{:S(2)}) collective-permute-start(bf16[256,1024]{1,0:T(8,128)(2,1)S(1)} %shard_map.110.own), channel_id=1, source_target_pairs={{0,2},{1,3},{2,0},{3,1},{4,6},{5,7},{6,4},{7,5},{8,10},{9,11},{10,... | collective-permute-start | bytes 1572872 | tf_op jit(solution)/shard_map/ppermute | solution.py:544
  118.3 16.9 %collective-permute-start.8 = (bf16[3,192,512]{2,1,0:T(8,128)(2,1)S(1)}, bf16[3,192,512]{2,1,0:T(8,128)(2,1)S(1)}, u32[]{:S(2)}, u32[]{:S(2)}) collective-permute-start(bf16[3,192,512]{2,1,0:T(8,128)(2,1)S(1)} %get-tuple-element.45), channel_id=1, source_target_pairs={{0,1},{1,0},{2,3},{3,2},{4,5},{5,4},{6,7},{7,6},{8,9},{9,8},{10,11... | collective-permute-start | bytes 1769480 | tf_op jit(solution)/shard_map/ppermute | solution.py:544
  120.9 36.6 %collective-permute-start.24 = (bf16[256,1024]{1,0:T(8,128)(2,1)S(1)}, bf16[256,1024]{1,0:T(8,128)(2,1)S(1)}, u32[]{:S(2)}, u32[]{:S(2)}) collective-permute-start(bf16[256,1024]{1,0:T(8,128)(2,1)S(1)} %shard_map.110.own), channel_id=1, source_target_pairs={{0,1},{1,0},{2,3},{3,2},{4,5},{5,4},{6,7},{7,6},{8,9},{9,8},{10,11... | collective-permute-start | bytes 1572872 | tf_op jit(solution)/shard_map/ppermute | solution.py:544
  128.1 29.4 %collective-permute-start.25 = (bf16[256,1024]{1,0:T(8,128)(2,1)S(1)}, bf16[256,1024]{1,0:T(8,128)(2,1)S(1)}, u32[]{:S(2)}, u32[]{:S(2)}) collective-permute-start(bf16[256,1024]{1,0:T(8,128)(2,1)S(1)} %collective-permute-done.23.by_x), channel_id=1, source_target_pairs={{0,1},{1,0},{2,3},{3,2},{4,5},{5,4},{6,7},{7,6},{8,9},{9,8},{10,11... | collective-permute-start | bytes 1572872 | tf_op jit(solution)/shard_map/ppermute | solution.py:544
  131.4 7.6 %collective-permute-start.4 = (bf16[96,512]{1,0:T(8,128)(2,1)S(1)}, bf16[96,512]{1,0:T(8,128)(2,1)S(1)}, u32[]{:S(2)}, u32[]{:S(2)}) collective-permute-start(bf16[96,512]{1,0:T(8,128)(2,1)S(1)} %get-tuple-element.39), channel_id=1, source_target_pairs={{0,0},{1,8},{2,2},{3,10},{4,4},{5,12},{6,6},{7,14},{8,1},{9,9},{10... | collective-permute-start | bytes 294920 | tf_op jit(solution)/shard_map/ppermute | solution.py:544
  133.3 9.2 %collective-permute-start.5 = (bf16[96,512]{1,0:T(8,128)(2,1)S(1)}, bf16[96,512]{1,0:T(8,128)(2,1)S(1)}, u32[]{:S(2)}, u32[]{:S(2)}) collective-permute-start(bf16[96,512]{1,0:T(8,128)(2,1)S(1)} %get-tuple-element.40), channel_id=1, source_target_pairs={{0,4},{1,12},{2,6},{3,14},{4,0},{5,8},{6,2},{7,10},{8,5},{9,13},{1... | collective-permute-start | bytes 294920 | tf_op jit(solution)/shard_map/ppermute | solution.py:544
  135.2 10.2 %collective-permute-start.6 = (bf16[96,512]{1,0:T(8,128)(2,1)S(1)}, bf16[96,512]{1,0:T(8,128)(2,1)S(1)}, u32[]{:S(2)}, u32[]{:S(2)}) collective-permute-start(bf16[96,512]{1,0:T(8,128)(2,1)S(1)} %get-tuple-element.41), channel_id=1, source_target_pairs={{0,8},{1,0},{2,10},{3,2},{4,12},{5,4},{6,14},{7,6},{8,9},{9,1},{10... | collective-permute-start | bytes 294920 | tf_op jit(solution)/shard_map/ppermute | solution.py:544
  135.2 18.3 %copy-start.2 = (bf16[1024,1024]{1,0:T(8,128)(2,1)S(1)}, bf16[1024,1024]{1,0:T(8,128)(2,1)}, u32[]{:S(2)}) copy-start(bf16[1024,1024]{1,0:T(8,128)(2,1)} %w_ref.2) | copy-start | bytes 6291460
  139.0 16.6 %copy-start.6 = (f32[1024]{0:T(1024)S(1)}, f32[1024]{0:T(1024)}, u32[]{:S(2)}) copy-start(f32[1024]{0:T(1024)} %param.13) | copy-start | bytes 12292
  139.0 16.6 %collective-permute-start.10 = (bf16[96,1024]{1,0:T(8,128)(2,1)S(1)}, bf16[96,1024]{1,0:T(8,128)(2,1)S(1)}, u32[]{:S(2)}, u32[]{:S(2)}) collective-permute-start(bf16[96,1024]{1,0:T(8,128)(2,1)S(1)} %get-tuple-element.47), channel_id=1, source_target_pairs={{0,4},{1,12},{2,6},{3,14},{4,0},{5,8},{6,2},{7,10},{8,5},{9,13},{1... | collective-permute-start | bytes 589832 | tf_op jit(solution)/shard_map/ppermute | solution.py:544
  142.5 13.2 %collective-permute-start.9 = (bf16[96,1024]{1,0:T(8,128)(2,1)S(1)}, bf16[96,1024]{1,0:T(8,128)(2,1)S(1)}, u32[]{:S(2)}, u32[]{:S(2)}) collective-permute-start(bf16[96,1024]{1,0:T(8,128)(2,1)S(1)} %get-tuple-element.46), channel_id=1, source_target_pairs={{0,0},{1,8},{2,2},{3,10},{4,4},{5,12},{6,6},{7,14},{8,1},{9,9},{10... | collective-permute-start | bytes 589832 | tf_op jit(solution)/shard_map/ppermute | solution.py:544
  145.4 8.1 %collective-permute-start.7 = (bf16[96,512]{1,0:T(8,128)(2,1)S(1)}, bf16[96,512]{1,0:T(8,128)(2,1)S(1)}, u32[]{:S(2)}, u32[]{:S(2)}) collective-permute-start(bf16[96,512]{1,0:T(8,128)(2,1)S(1)} %get-tuple-element.42), channel_id=1, source_target_pairs={{0,12},{1,4},{2,14},{3,6},{4,8},{5,0},{6,10},{7,2},{8,13},{9,5},{1... | collective-permute-start | bytes 294920 | tf_op jit(solution)/shard_map/ppermute | solution.py:544
  (4 other events, 3.4 us)

commit v3 on v2

--- a/solution.py
+++ b/solution.py
@@ -284,46 +284,73 @@
 PAR, CORE, LINE, SIDE, KEPT = range(5)
 
 
-def norm_kernel(place, patch_ref, cot_ref, index_ref, gain_ref, p0_ref, p1_ref, hidden_ref):
+def norm_kernel(
+    place, patch_hbm, cot_hbm, index_hbm, gain_hbm, p0_ref, p1_ref, hidden_ref,
+    patch_ref, cot_ref, index_ref, gain_ref, sems,
+):
     par = place[PAR]
     rows, width = patch_ref.shape[1:]
     quarter = width // 4
+    copies = [
+        pltpu.make_async_copy(src, dst, sems.at[i])
+        for i, (src, dst) in enumerate(
+            ((index_hbm, index_ref), (patch_hbm, patch_ref), (gain_hbm, gain_ref), (cot_hbm, cot_ref))
+        )
+    ]
+    for copy in copies:
+        copy.start()
     order = lax.broadcasted_iota(jnp.int32, (1, quarter), 1).astype(jnp.float32)
     freq = jnp.exp(-np.log(np.float32(10000.0)) * order / quarter)
     diagonal = lax.broadcasted_iota(jnp.int32, (rows, rows), 0) == lax.broadcasted_iota(
         jnp.int32, (rows, rows), 1
     )
-    for k, out_ref in enumerate((p0_ref, p1_ref)):
-        s = k ^ par
-        live = live_column(place[KEPT + s], rows)
-        position = index_ref[pl.ds(s, 1), :]
+    copies[0].wait()
+    tables = []
+    for k in range(2):
+        position = index_ref[pl.ds(k ^ par, 1), :]
         grid_row = (position // GRID_COLS).astype(jnp.float32)
         grid_col = (position % GRID_COLS).astype(jnp.float32)
         grid_row = jnp.sum(jnp.where(diagonal, grid_row, 0.0), axis=1, keepdims=True)
         grid_col = jnp.sum(jnp.where(diagonal, grid_col, 0.0), axis=1, keepdims=True)
         pieces = sine_cosine(grid_row * freq) + sine_cosine(grid_col * freq)
-        hidden = patch_ref[s].astype(jnp.float32) + jnp.concatenate(pieces, axis=1)
+        tables.append(jnp.concatenate(pieces, axis=1))
+    copies[1].wait()
+    copies[2].wait()
+    for k, out_ref in enumerate((p0_ref, p1_ref)):
+        s = k ^ par
+        hidden = patch_ref[s].astype(jnp.float32) + tables[k]
         hidden_ref[k] = hidden
         center = hidden - jnp.mean(hidden, axis=-1, keepdims=True)
         spread = jnp.mean(center * center, axis=-1, keepdims=True)
         normed = center * lax.rsqrt(spread + epsilon) * gain_ref[...]
+        live = live_column(place[KEPT + s], rows)
         out_ref[:rows, :] = jnp.where(live, normed, MARK).astype(out_ref.dtype)
+    copies[3].wait()
+    for k, out_ref in enumerate((p0_ref, p1_ref)):
+        s = k ^ par
+        live = live_column(place[KEPT + s], rows)
         grad = cot_ref[s]
         out_ref[rows:, :] = jnp.where(live, grad, jnp.zeros_like(grad))
 
 
-def stage_kernel(place, q_in, k_in, v_in, o_in, q_out, k_out, v_out, o_out):
-    q_out[...] = q_in[...]
-    k_out[...] = k_in[...]
-    v_out[...] = v_in[...]
-    o_out[...] = o_in[...]
-
-
 def attend_kernel(
-    place, p0, p1, p2, p3, wq, wk, wv, wo,
-    att0, att1, att2, att3, dp_own, dp_oth, att_send, att_keep, dp_send, dp_keep,
-    norm_s, grad_s,
+    place, p0, p1, p2, p3, w_in_hbm, w_out_hbm,
+    att0, att1, att2, att3, dp_own, dp_oth, send_t, keep_t,
+    norm_s, grad_s, wq, wk, wv, wo, sems,
 ):
+    core = place[CORE]
+    width = p0.shape[1]
+    copies = []
+    for j in range(width // 256):
+        to = pl.ds(128 * j, 128)
+        row = pl.multiple_of(256 * j + 128 * core, 128)
+        pairs = [(w_out_hbm.at[pl.ds(row, 128), :], wo.at[to, :])]
+        for t, out in enumerate((wq, wk, wv)):
+            at = pl.multiple_of(t * width + 256 * j + 128 * core, 128)
+            pairs.append((w_in_hbm.at[:, pl.ds(at, 128)], out.at[:, to]))
+        copies += [pltpu.make_async_copy(a, b, sems.at[4 * j + i]) for i, (a, b) in enumerate(pairs)]
+    for copy in copies:
+        copy.start()
     block = p0.shape[0] // 2
     rows = 4 * block
     half = 2 * block
@@ -340,10 +367,12 @@
     scale = jnp.bfloat16(0.125)
     zero = jnp.zeros((rows, 128), jnp.bfloat16)
     first = place[SIDE] == 0
-    for j in range(wq.shape[1] // 128):
+    for j in range(width // 256):
         cols = slice(128 * j, 128 * j + 128)
         if j % 2 == 0:
             two = slice(128 * j, 128 * j + 256)
+            for copy in copies[4 * j : 4 * j + 8]:
+                copy.wait()
             normed = norm_s[...]
             queries = dot_nn(normed, wq[:, two]).astype(jnp.bfloat16)
             keys = dot_nn(normed, wk[:, two]).astype(jnp.bfloat16)
@@ -381,13 +410,10 @@
         for t, piece in enumerate((dq_pair_t.T, dk_pair, dv_pair)):
             dp_own[t, :, cols] = piece[:half]
             dp_oth[t, :, cols] = piece[half:]
-        at = slice(64 * j, 64 * j + 64)
-        att_keep[at, :] = jnp.where(first, att_pair_t[:64], att_pair_t[64:])
-        att_send[at, :] = jnp.where(first, att_pair_t[64:], att_pair_t[:64])
-        for t, piece in enumerate((dq_pair_t, dk_pair.T, dv_pair.T)):
+        for t, piece in enumerate((dq_pair_t, dk_pair.T, dv_pair.T, att_pair_t)):
             at = slice(64 * (4 * t + j), 64 * (4 * t + j) + 64)
-            dp_keep[at, :] = jnp.where(first, piece[:64], piece[64:])
-            dp_send[at, :] = jnp.where(first, piece[64:], piece[:64])
+            keep_t[at, :] = jnp.where(first, piece[:64], piece[64:])
+            send_t[at, :] = jnp.where(first, piece[64:], piece[:64])
 
 
 def in_order(place, own, got):
@@ -418,66 +444,7 @@
         o1[...] = total[half:].astype(o1.dtype)
 
 
-def out_weight_kernel(place, keep, got, p0, p1, p2, p3, r0, r1, r2, r3, o0, o1, o2, o3, tokens, total):
-    block = p0.shape[0] // 2
-    rows = 4 * block
-    for i, ref in enumerate((p0, p1, p2, p3, r0, r1, r2, r3)):
-        tokens[i * block : (i + 1) * block, :] = ref[block:, :]
-    total[...] = dot_nn(keep[...], tokens[:rows, :]) + dot_nn(got[...], tokens[rows:, :])
-    columns = o0.shape[1]
-    for k, out in enumerate((o0, o1, o2, o3)):
-        at = pl.multiple_of((place[LINE] ^ k) * columns, 128)
-        out[...] = total[:, pl.ds(at, columns)].astype(out.dtype)
-
-
-def weight_kernel(place, keep, got, p0, p1, p2, p3, r0, r1, r2, r3, o0, o1, o2, o3, tokens):
-    block = p0.shape[0] // 2
-    rows = 4 * block
-    for i, ref in enumerate((p0, p1, p2, p3, r0, r1, r2, r3)):
-        tokens[i * block : (i + 1) * block, :] = ref[:block, :]
-    count = o0.shape[0]
-    for k, out in enumerate((o0, o1, o2, o3)):
-        at = pl.ds(pl.multiple_of((place[LINE] ^ k) * count, 16), count)
-        value = dot_nn(keep[at, :], tokens[:rows, :]) + dot_nn(got[at, :], tokens[rows:, :])
-        out[...] = value.astype(out.dtype)
-
-
-def sum_kernel(a0, a1, a2, a3, b0, b1, b2, b3, out):
-    f32 = jnp.float32
-    count = a0.shape[0]
-    value = (a0[...].astype(f32) + a1[...].astype(f32)) + (a2[...].astype(f32) + a3[...].astype(f32))
-    out[:count, :] = value.astype(out.dtype)
-    value = (b0[...].astype(f32) + b1[...].astype(f32)) + (b2[...].astype(f32) + b3[...].astype(f32))
-    value = value.astype(out.dtype)
-    columns = b0.shape[1]
-    for j in range(4):
-        out[count:, columns * j : columns * j + columns] = value[64 * j : 64 * j + 64, :]
-
-
-def finish_kernel(place, own, by_x, by_core, by_both, wide, narrow):
-    core_low, side_low = place[CORE] == 0, place[SIDE] == 0
-    count = own.shape[0] - 64
-    columns = narrow.shape[1]
-
-    def pick(at, c, x, part):
-        a = jnp.where(side_low == (x == 0), own[at, part], by_x[at, part])
-        b = jnp.where(side_low == (x == 0), by_core[at, part], by_both[at, part])
-        return jnp.where(core_low == (c == 0), a, b)
-
-    for c in range(2):
-        for i in range(count // 64):
-            at = slice(64 * i, 64 * i + 64)
-            both = jnp.concatenate([pick(at, c, x, slice(None)) for x in range(2)], axis=0)
-            col = 128 * (2 * i + c)
-            wide[:, col : col + 128] = both.T.astype(wide.dtype)
-        for j in range(4):
-            for x in range(2):
-                row = 128 * (2 * j + c) + 64 * x
-                part = slice(columns * j, columns * j + columns)
-                narrow[row : row + 64, :] = pick(slice(count, None), c, x, part).astype(narrow.dtype)
-
-
-def encode_kernel(place, a0, a1, b0, b1, w_ref, hidden_ref, out_ref):
+def encode(place, a0, a1, b0, b1, w_ref, hidden_ref, out_ref):
     par, core = place[PAR], place[LINE] // 2
     for k, (a, b) in enumerate(((a0, b0), (a1, b1))):
         s = k ^ par
@@ -486,7 +453,7 @@
         out_ref[s] = jnp.where(live, hidden_ref[k] + projected, 0.0).astype(out_ref.dtype)
 
 
-def patch_grad_kernel(place, d0, d1, p0, p1, hidden_ref, gain_ref, out_ref):
+def patch_grad(place, d0, d1, p0, p1, hidden_ref, gain_ref, out_ref):
     par = place[PAR]
     rows = d0.shape[0]
     for k, (d_ref, p_ref) in enumerate(((d0, p0), (d1, p1))):
@@ -502,6 +469,66 @@
         out_ref[s] = jnp.where(live, value, 0.0).astype(out_ref.dtype)
 
 
+def return_kernel(place, a0, a1, b0, b1, w_ref, hidden_ref, d0, d1, m0, m1, gain_ref, encoded, d_patches):
+    encode(place, a0, a1, b0, b1, w_ref, hidden_ref, encoded)
+    patch_grad(place, d0, d1, m0, m1, hidden_ref, gain_ref, d_patches)
+
+
+def weight_kernel(
+    place, keep, got, p0, p1, p2, p3, r0, r1, r2, r3, d0, d1, a0, a1, b0, b1,
+    o0, o1, o2, o3, tokens, total,
+):
+    del d0, d1, a0, a1, b0, b1
+    block = p0.shape[0] // 2
+    rows = 4 * block
+    columns = o0.shape[0]
+    count = 3 * columns // 4
+    for i, ref in enumerate((p0, p1, p2, p3, r0, r1, r2, r3)):
+        tokens[i * block : (i + 1) * block, :] = ref[block:, :]
+    at = slice(4 * count, None)
+    total[...] = dot_nn(keep[at, :], tokens[:rows, :]) + dot_nn(got[at, :], tokens[rows:, :])
+    for k, out in enumerate((o0, o1, o2, o3)):
+        at = pl.multiple_of((place[LINE] ^ k) * columns, 128)
+        value = total[:, pl.ds(at, columns)].astype(out.dtype)
+        for j in range(4):
+            out[count:, columns * j : columns * j + columns] = value[64 * j : 64 * j + 64, :]
+    for i, ref in enumerate((p0, p1, p2, p3, r0, r1, r2, r3)):
+        tokens[i * block : (i + 1) * block, :] = ref[:block, :]
+    for k, out in enumerate((o0, o1, o2, o3)):
+        at = pl.ds(pl.multiple_of((place[LINE] ^ k) * count, 16), count)
+        value = dot_nn(keep[at, :], tokens[:rows, :]) + dot_nn(got[at, :], tokens[rows:, :])
+        out[:count, :] = value.astype(out.dtype)
+
+
+def sum_kernel(a0, a1, a2, a3, out):
+    f32 = jnp.float32
+    value = (a0[...].astype(f32) + a1[...].astype(f32)) + (a2[...].astype(f32) + a3[...].astype(f32))
+    out[...] = value.astype(out.dtype)
+
+
+def finish_kernel(place, own, by_x, by_core, by_both, wide, narrow):
+    core_low, side_low = place[CORE] == 0, place[SIDE] == 0
+    count = own.shape[0] - 64
+    columns = narrow.shape[1]
+
+    def pick(at, c, x, part):
+        a = jnp.where(side_low == (x == 0), own[at, part], by_x[at, part])
+        b = jnp.where(side_low == (x == 0), by_core[at, part], by_both[at, part])
+        return jnp.where(core_low == (c == 0), a, b)
+
+    for c in range(2):
+        for i in range(count // 64):
+            at = slice(64 * i, 64 * i + 64)
+            both = jnp.concatenate([pick(at, c, x, slice(None)) for x in range(2)], axis=0)
+            col = 128 * (2 * i + c)
+            wide[:, col : col + 128] = both.T.astype(wide.dtype)
+        for j in range(4):
+            for x in range(2):
+                row = 128 * (2 * j + c) + 64 * x
+                part = slice(columns * j, columns * j + columns)
+                narrow[row : row + 64, :] = pick(slice(count, None), c, x, part).astype(narrow.dtype)
+
+
 SMEM_SPEC = pl.BlockSpec(memory_space=pltpu.SMEM)
 VMEM_SPEC = pl.BlockSpec(memory_space=pltpu.VMEM)
 
@@ -510,8 +537,15 @@
     return jax.ShapeDtypeStruct(shape, dtype)
 
 
-def call(kernel, args, outs, limit, place=None, scratch=(), flops=0, moved=1_000_000):
-    specs = [VMEM_SPEC] * len(args)
+COST = pl.CostEstimate(flops=1000, bytes_accessed=1000, transcendentals=0)
+
+
+def in_hbm(value):
+    return pltpu.with_memory_space_constraint(value, pltpu.HBM)
+
+
+def call(kernel, args, outs, limit, place=None, scratch=(), specs=None):
+    specs = specs or [VMEM_SPEC] * len(args)
     if place is not None:
         args, specs = (place, *args), [SMEM_SPEC] + specs
     single = not isinstance(outs, list)
@@ -522,7 +556,7 @@
         out_shape=outs,
         scratch_shapes=list(scratch),
         compiler_params=pltpu.CompilerParams(vmem_limit_bytes=limit * MIB),
-        cost_estimate=pl.CostEstimate(flops=flops, bytes_accessed=moved, transcendentals=0),
+        cost_estimate=COST,
     )(*args)
 
 
@@ -560,54 +594,42 @@
 
     gain_row = gain.reshape(1, width)
     pay = struct((2 * slots, width))
+    hbm = pl.BlockSpec(memory_space=pl.ANY)
     *mine, hidden = call(
         norm_kernel,
-        (patches, cotangent, kept_index, gain_row),
+        tuple(in_hbm(v) for v in (patches, cotangent, kept_index, gain_row)),
         [pay, pay, struct(patches.shape, f32)],
-        16,
+        24,
         place,
-        moved=4_000_000,
+        scratch=[
+            pltpu.VMEM(patches.shape, bf16),
+            pltpu.VMEM(patches.shape, bf16),
+            pltpu.VMEM(kept_index.shape, jnp.int32),
+            pltpu.VMEM(gain_row.shape, f32),
+            pltpu.SemaphoreType.DMA((4,)),
+        ],
+        specs=[hbm] * 4,
     )
     got = [to_chip(mine[k], k) for k in range(2)]
-
-    wide, tall = (width, 128), (128, width)
-    blocks = own_width // 128
-    staged = pl.pallas_call(
-        stage_kernel,
-        grid_spec=pltpu.PrefetchScalarGridSpec(
-            num_scalar_prefetch=1,
-            grid=(blocks,),
-            in_specs=[
-                pl.BlockSpec(wide, lambda j, p, t=t: (0, (width // 128) * t + 2 * j + p[CORE])) for t in range(3)
-            ]
-            + [pl.BlockSpec(tall, lambda j, p: (2 * j + p[CORE], 0))],
-            out_specs=[pl.BlockSpec(wide, lambda j, p: (0, j))] * 3 + [pl.BlockSpec(tall, lambda j, p: (j, 0))],
-        ),
-        out_shape=[struct((width, own_width))] * 3 + [struct((own_width, width))],
-        compiler_params=pltpu.CompilerParams(vmem_limit_bytes=8 * MIB),
-        cost_estimate=pl.CostEstimate(flops=0, bytes_accessed=8_000_000, transcendentals=0),
-    )(place, w_qkv, w_qkv, w_qkv, w_out)
-
     here = got + [to_core(v) for v in got]
     from_x = [to_x(v) for v in got]
     there = from_x + [to_core(v) for v in from_x]
 
     att = struct((slots, own_width))
     d_rows = struct((3, 2 * slots, own_width))
-    att_t = struct((quarter, rows))
-    dp_t = struct((3 * quarter, rows))
-    *atts, dp_own, dp_oth, att_send, att_keep, dp_send, dp_keep = call(
+    half_t = struct((width, rows))
+    *atts, dp_own, dp_oth, send_t, keep_t = call(
         attend_kernel,
-        (*here, *staged),
-        [att] * 4 + [d_rows] * 2 + [att_t] * 2 + [dp_t] * 2,
-        32,
+        (*here, in_hbm(w_qkv), in_hbm(w_out)),
+        [att] * 4 + [d_rows] * 2 + [half_t] * 2,
+        36,
         place,
-        scratch=[pltpu.VMEM((rows, width), bf16)] * 2,
-        flops=6_000_000_000,
-        moved=20_000_000,
-    )
-    att_got = to_x(att_send)
-    dp_got = to_x(dp_send)
+        scratch=[pltpu.VMEM((rows, width), bf16)] * 2
+        + [pltpu.VMEM((width, own_width), bf16)] * 3
+        + [pltpu.VMEM((own_width, width), bf16), pltpu.SemaphoreType.DMA((4 * (width // 256),))],
+        specs=[VMEM_SPEC] * 4 + [hbm] * 2,
+    )
+    got_t = to_x(send_t)
     dp_core = to_core(dp_oth)
     back_att = [to_rows(atts[k], k, 0) for k in range(2)] + [to_rows(atts[2 + k], k, 1) for k in range(2)]
 
@@ -623,53 +645,29 @@
         ),
         out_shape=[struct((slots, width))] * 2,
         compiler_params=pltpu.CompilerParams(vmem_limit_bytes=16 * MIB),
-        cost_estimate=pl.CostEstimate(flops=1_200_000_000, bytes_accessed=8_000_000, transcendentals=0),
-    )(place, dp_own, dp_core, w_qkv)
+        cost_estimate=COST,
+    )(place, dp_own, dp_core, in_hbm(w_qkv))
     back_dn = [to_rows(d_normed[k], k, 0) for k in range(2)]
 
-    out_part = struct((quarter, quarter))
-    dwo = call(
-        out_weight_kernel,
-        (att_keep, att_got, *here, *there),
-        [out_part] * 4,
+    part = struct((quarter, width))
+    dw = call(
+        weight_kernel,
+        (keep_t, got_t, *here, *there, *back_dn, *back_att),
+        [part] * 4,
+        16,
+        place,
+        scratch=[pltpu.VMEM((2 * rows, width), bf16), pltpu.VMEM((quarter, width), f32)],
+        specs=[VMEM_SPEC] * 10 + [pl.BlockSpec(memory_space=pl.ANY)] * 6,
+    )
+    dw = [dw[0]] + [along(dw[k], k) for k in range(1, 4)]
+    encoded, d_patches = call(
+        return_kernel,
+        (*back_att, w_out, hidden, *back_dn, *mine, gain_row),
+        [struct(patches.shape)] * 2,
         12,
         place,
-        scratch=[pltpu.VMEM((2 * rows, width), bf16), pltpu.VMEM((quarter, width), f32)],
-        flops=400_000_000,
-        moved=4_000_000,
-    )
-    dwo = [dwo[0]] + [along(dwo[k], k) for k in range(1, 4)]
-    in_part = struct((3 * quarter // 4, width))
-    dwq = call(
-        weight_kernel,
-        (dp_keep, dp_got, *here, *there),
-        [in_part] * 4,
-        12,
-        place,
-        scratch=[pltpu.VMEM((2 * rows, width), bf16)],
-        flops=1_200_000_000,
-        moved=6_000_000,
-    )
-    dwq = [dwq[0]] + [along(dwq[k], k) for k in range(1, 4)]
-
-    encoded = call(
-        encode_kernel,
-        (*back_att, w_out, hidden),
-        struct(patches.shape),
-        12,
-        place,
-        flops=400_000_000,
-        moved=5_000_000,
-    )
-    d_patches = call(
-        patch_grad_kernel,
-        (*back_dn, *mine, hidden, gain_row),
-        struct(patches.shape),
-        8,
-        place,
-        moved=4_000_000,
-    )
-    sums = call(sum_kernel, (*dwq, *dwo), struct((quarter, width)), 8, moved=2_500_000)
+    )
+    sums = call(sum_kernel, dw, part, 8)
     by_x = to_x(sums)
     by_core = to_core(sums)
     by_both = to_core(by_x)
@@ -679,7 +677,6 @@
         [struct((width, 3 * quarter), f32), struct((width, quarter), f32)],
         12,
         place,
-        moved=6_000_000,
     )
     return (encoded, d_patches, qkv_grad, out_grad)
 

time: 162 us -> 152 us (0.938)
  starting transfers between devices: 39 us -> 28.1 us
  waiting for transfers between devices: 84.5 us -> 94.7 us
  local copies, waits for them, and re-layouts: 8.49 us -> 0.74 us
    ppermute x26 -> x22, starting transfers between devices: 39 us -> 28.1 us  [send(): return lax.ppermute(value, AXES, line_perm(move, reps))]
    ppermute x26 -> x22, waiting for transfers between devices: 84.5 us -> 94.7 us  [send(): return lax.ppermute(value, AXES, line_perm(move, reps))]
    unnamed x20 -> x4, local copies, waits for them, and re-layouts: 7.75 us -> 0.01 us
    pallas_call x1 -> x0, Pallas kernels: 2.38 us -> none  [chip_shards(): pl.pallas_call(stage_kernel, grid_spec=pltpu.PrefetchScalarGridSpec(num_s...]
    pallas_call x1, Pallas kernels: 3.77 us -> 5.58 us  [chip_shards(): pl.pallas_call(d_normed_kernel, grid_spec=pltpu.PrefetchScalarGridSpec(nu...]
    pallas_call x8 -> x6, Pallas kernels: 21.6 us -> 22.1 us  [call(): pl.pallas_call(kernel, in_specs=specs, out_specs=VMEM_SPEC if single else...]
  transfers between devices with their start and end apart: 26 -> 22, of which waited for: 11 -> 10; matrix products, arithmetic and copies ran while one was open for 0% -> 0% of each run, Pallas kernels for 14% -> 5%
where the time goes in v3:
time: 152 us
  waiting for transfers between devices  94.7 us (62%)
  starting transfers between devices  28.1 us (18%)
  Pallas kernels  27.7 us (18%)
    ppermute x22, waiting for transfers between devices, send(): return lax.ppermute(value, AXES, line_perm(move, reps))  94.7 us
    ppermute x22, starting transfers between devices, send(): return lax.ppermute(value, AXES, line_perm(move, reps))  28.1 us
    pallas_call x6, Pallas kernels, call(): pl.pallas_call(kernel, in_specs=specs, out_specs=VMEM_SPEC if single else...  22.1 us
    pallas_call x1, Pallas kernels, chip_shards(): pl.pallas_call(d_normed_kernel, grid_spec=pltpu.PrefetchScalarGridSpec(nu...  5.58 us
  transfers between devices with their start and end apart: 22, of which 10 were waited for; matrix products, arithmetic and copies ran while one was open for 0% of the time, Pallas kernels for 5%

profile of v3, /device:TPU:9, one launch (start us, length us, event | category | flops | bytes accessed | tf_op | source)
XLA Modules:
  0.0 152.1 jit_solution(4896541963878202778)
XLA Ops:
  0.6 0.7 concatenate.3.place
  1.4 2.2 %shard_map.102 = (bf16[192,1024]{1,0:T(8,128)(2,1)S(1)}, bf16[192,1024]{1,0:T(8,128)(2,1)S(1)}, f32[2,96,1024]{2,1,0:T(8,128)S(1)}) custom-call(s32[6]{0:T(128)S(1)} %concatenate.3.place, bf16[2,96,1024]{2,1,0:T(8,128)(2,1)} %patch_hbm.1, bf16[2,96,1024]{2,1,0:T(8,128)(2,1)} %cot_hbm.1, s32[2,96]{1,0:T(2,128)} %index_hbm.1, f32[1,1024]{1,0:T(1,128)} %bitcast.6), custom_call_target="tpu_custom_call" | custom-call | flops 1000 | bytes 1000 | tf_op jit(solution)/shard_map/pallas_call | solution.py:552
  3.6 4.8 %collective-permute-start = (bf16[192,1024]{1,0:T(8,128)(2,1)S(1)}, bf16[192,1024]{1,0:T(8,128)(2,1)S(1)}, u32[]{:S(2)}, u32[]{:S(2)}) collective-permute-start(bf16[192,1024]{1,0:T(8,128)(2,1)S(1)} %get-tuple-element.25.m0), channel_id=1, source_target_pairs={{0,0},{1,8},{2,2},{3,10},{4,4},{5,12},{6,6},{7,14},{8,1},{9,9},{10... | collective-permute-start | bytes 1179656 | tf_op jit(solution)/shard_map/ppermute | solution.py:578
  8.4 13.0 %collective-permute-done.p0 = bf16[192,1024]{1,0:T(8,128)(2,1)S(1)} collective-permute-done((bf16[192,1024]{1,0:T(8,128)(2,1)S(1)}, bf16[192,1024]{1,0:T(8,128)(2,1)S(1)}, u32[]{:S(2)}, u32[]{:S(2)}) %collective-permute-start) | collective-permute-done | bytes 393248 | tf_op jit(solution)/shard_map/ppermute | solution.py:578
  21.5 4.2 %collective-permute-done.1.p1 = bf16[192,1024]{1,0:T(8,128)(2,1)S(1)} collective-permute-done((bf16[192,1024]{1,0:T(8,128)(2,1)S(1)}, bf16[192,1024]{1,0:T(8,128)(2,1)S(1)}, u32[]{:S(2)}, u32[]{:S(2)}) %collective-permute-start.1) | collective-permute-done | bytes 393248 | tf_op jit(solution)/shard_map/ppermute | solution.py:578
  25.7 1.7 %collective-permute-done.3.p3 = bf16[192,1024]{1,0:T(8,128)(2,1)S(1)} collective-permute-done((bf16[192,1024]{1,0:T(8,128)(2,1)S(1)}, bf16[192,1024]{1,0:T(8,128)(2,1)S(1)}, u32[]{:S(2)}, u32[]{:S(2)}) %collective-permute-start.3) | collective-permute-done | bytes 393248 | tf_op jit(solution)/shard_map/ppermute | solution.py:578
  27.4 11.1 %shard_map.103 = (bf16[96,512]{1,0:T(8,128)(2,1)S(1)}, bf16[96,512]{1,0:T(8,128)(2,1)S(1)}, bf16[96,512]{1,0:T(8,128)(2,1)S(1)}, bf16[96,512]{1,0:T(8,128)(2,1)S...) custom-call(s32[6]{0:T(128)S(1)} %concatenate.3.place, ...), custom_call_target="tpu_custom_call" | custom-call | flops 1000 | bytes 1000 | tf_op jit(solution)/shard_map/pallas_call | solution.py:552
  38.7 1.2 collective-permute-start.12
  39.9 0.3 collective-permute-start.13
  40.2 1.2 collective-permute-start.11
  41.4 2.5 %collective-permute-start.4 = (bf16[96,512]{1,0:T(8,128)(2,1)S(1)}, bf16[96,512]{1,0:T(8,128)(2,1)S(1)}, u32[]{:S(2)}, u32[]{:S(2)}) collective-permute-start(bf16[96,512]{1,0:T(8,128)(2,1)S(1)} %get-tuple-element.27), channel_id=1, source_target_pairs={{0,0},{1,8},{2,2},{3,10},{4,4},{5,12},{6,6},{7,14},{8,1},{9,9},{10... | collective-permute-start | bytes 294920 | tf_op jit(solution)/shard_map/ppermute | solution.py:578
  43.9 5.2 %collective-permute-done.12.r0 = bf16[192,1024]{1,0:T(8,128)(2,1)S(1)} collective-permute-done((bf16[192,1024]{1,0:T(8,128)(2,1)S(1)}, bf16[192,1024]{1,0:T(8,128)(2,1)S(1)}, u32[]{:S(2)}, u32[]{:S(2)}) %collective-permute-start.12) | collective-permute-done | bytes 393248 | tf_op jit(solution)/shard_map/ppermute | solution.py:578
  49.1 4.1 %collective-permute-start.5 = (bf16[96,512]{1,0:T(8,128)(2,1)S(1)}, bf16[96,512]{1,0:T(8,128)(2,1)S(1)}, u32[]{:S(2)}, u32[]{:S(2)}) collective-permute-start(bf16[96,512]{1,0:T(8,128)(2,1)S(1)} %get-tuple-element.28), channel_id=1, source_target_pairs={{0,4},{1,12},{2,6},{3,14},{4,0},{5,8},{6,2},{7,10},{8,5},{9,13},{1... | collective-permute-start | bytes 294920 | tf_op jit(solution)/shard_map/ppermute | solution.py:578
  53.2 4.3 %collective-permute-done.13.r1 = bf16[192,1024]{1,0:T(8,128)(2,1)S(1)} collective-permute-done((bf16[192,1024]{1,0:T(8,128)(2,1)S(1)}, bf16[192,1024]{1,0:T(8,128)(2,1)S(1)}, u32[]{:S(2)}, u32[]{:S(2)}) %collective-permute-start.13) | collective-permute-done | bytes 393248 | tf_op jit(solution)/shard_map/ppermute | solution.py:578
  57.5 2.0 %collective-permute-start.14 = (bf16[192,1024]{1,0:T(8,128)(2,1)S(1)}, bf16[192,1024]{1,0:T(8,128)(2,1)S(1)}, u32[]{:S(2)}, u32[]{:S(2)}) collective-permute-start(bf16[192,1024]{1,0:T(8,128)(2,1)S(1)} %collective-permute-done.12.r0), channel_id=1, source_target_pairs={{0,1},{1,0},{2,3},{3,2},{4,5},{5,4},{6,7},{7,6},{8,9},{9,8},{10,11... | collective-permute-start | bytes 1179656 | tf_op jit(solution)/shard_map/ppermute | solution.py:578
  59.5 0.5 collective-permute-start.6
  60.0 3.6 %collective-permute-start.7 = (bf16[96,512]{1,0:T(8,128)(2,1)S(1)}, bf16[96,512]{1,0:T(8,128)(2,1)S(1)}, u32[]{:S(2)}, u32[]{:S(2)}) collective-permute-start(bf16[96,512]{1,0:T(8,128)(2,1)S(1)} %get-tuple-element.30), channel_id=1, source_target_pairs={{0,12},{1,4},{2,14},{3,6},{4,8},{5,0},{6,10},{7,2},{8,13},{9,5},{1... | collective-permute-start | bytes 294920 | tf_op jit(solution)/shard_map/ppermute | solution.py:578
  63.6 5.6 %shard_map.104 = (bf16[96,1024]{1,0:T(8,128)(2,1)S(1)}, bf16[96,1024]{1,0:T(8,128)(2,1)S(1)}) custom-call(s32[6]{0:T(128)S(1)} %concatenate.3.place, bf16[3,192,512]{2,1,0:T(8,128)(2,1)S(1)} %get-tuple-element.32.own, bf16[3,192,512]{2,1,0:T(8,128)(2,1)S(1)} %collective-permute-done.8.got, bf16[1024,3072]{1,0:T(8,128)(2,1)} %w_ref.2), custom_call_target="tpu_custom_call" | custom-call | flops 1000 | bytes 1000 | tf_op jit(solution)/shard_map/pallas_call | solution.py:636
  69.2 2.1 %collective-permute-start.9 = (bf16[96,1024]{1,0:T(8,128)(2,1)S(1)}, bf16[96,1024]{1,0:T(8,128)(2,1)S(1)}, u32[]{:S(2)}, u32[]{:S(2)}) collective-permute-start(bf16[96,1024]{1,0:T(8,128)(2,1)S(1)} %get-tuple-element.34), channel_id=1, source_target_pairs={{0,0},{1,8},{2,2},{3,10},{4,4},{5,12},{6,6},{7,14},{8,1},{9,9},{10... | collective-permute-start | bytes 589832 | tf_op jit(solution)/shard_map/ppermute | solution.py:578
  71.4 5.8 %collective-permute-done.9.d0 = bf16[96,1024]{1,0:T(8,128)(2,1)S(1)} collective-permute-done((bf16[96,1024]{1,0:T(8,128)(2,1)S(1)}, bf16[96,1024]{1,0:T(8,128)(2,1)S(1)}, u32[]{:S(2)}, u32[]{:S(2)}) %collective-permute-start.9) | collective-permute-done | bytes 196640 | tf_op jit(solution)/shard_map/ppermute | solution.py:578
  77.2 3.5 %collective-permute-done.10.d1 = bf16[96,1024]{1,0:T(8,128)(2,1)S(1)} collective-permute-done((bf16[96,1024]{1,0:T(8,128)(2,1)S(1)}, bf16[96,1024]{1,0:T(8,128)(2,1)S(1)}, u32[]{:S(2)}, u32[]{:S(2)}) %collective-permute-start.10) | collective-permute-done | bytes 196640 | tf_op jit(solution)/shard_map/ppermute | solution.py:578
  80.7 2.9 %shard_map.106 = (bf16[256,1024]{1,0:T(8,128)(2,1)S(1)}, bf16[256,1024]{1,0:T(8,128)(2,1)S(1)}, bf16[256,1024]{1,0:T(8,128)(2,1)S(1)}, bf16[256,1024]{1,0:T(8,128)(2,1)S(1)}) custom-call(s32[6]{0:T(128)S(1)} %concatenate.3.place, bf16[1024,384]{1,0:T(8,128)(2,1)S(1)} %get-tuple-element.38.keep, bf16[1024,384]{1,0:T(8,128)(2,1)S(1)} %collective-permute-done.11.got, ...), custom_call_target="tpu_custom_call" | custom-call | flops 1000 | bytes 1000 | tf_op jit(solution)/shard_map/pallas_call | solution.py:552
  83.8 2.6 %collective-permute-start.18 = (bf16[256,1024]{1,0:T(8,128)(2,1)S(1)}, bf16[256,1024]{1,0:T(8,128)(2,1)S(1)}, u32[]{:S(2)}, u32[]{:S(2)}) collective-permute-start(bf16[256,1024]{1,0:T(8,128)(2,1)S(1)} %get-tuple-element.43), channel_id=1, source_target_pairs={{0,12},{1,13},{2,14},{3,15},{4,8},{5,9},{6,10},{7,11},{8,4},{9,5},... | collective-permute-start | bytes 1572872 | tf_op jit(solution)/shard_map/ppermute | solution.py:578
  86.3 15.0 %collective-permute-done.16.a1 = bf16[256,1024]{1,0:T(8,128)(2,1)S(1)} collective-permute-done((bf16[256,1024]{1,0:T(8,128)(2,1)S(1)}, bf16[256,1024]{1,0:T(8,128)(2,1)S(1)}, u32[]{:S(2)}, u32[]{:S(2)}) %collective-permute-start.16) | collective-permute-done | bytes 524320 | tf_op jit(solution)/shard_map/ppermute | solution.py:578
  101.3 30.4 %collective-permute-done.18.a3 = bf16[256,1024]{1,0:T(8,128)(2,1)S(1)} collective-permute-done((bf16[256,1024]{1,0:T(8,128)(2,1)S(1)}, bf16[256,1024]{1,0:T(8,128)(2,1)S(1)}, u32[]{:S(2)}, u32[]{:S(2)}) %collective-permute-start.18) | collective-permute-done | bytes 524320 | tf_op jit(solution)/shard_map/ppermute | solution.py:578
  131.7 0.3 shard_map.107.own
  132.0 1.3 collective-permute-start.19
  133.3 0.5 collective-permute-start.20
  133.8 11.5 %collective-permute-done.19.by_x = bf16[256,1024]{1,0:T(8,128)(2,1)S(1)} collective-permute-done((bf16[256,1024]{1,0:T(8,128)(2,1)S(1)}, bf16[256,1024]{1,0:T(8,128)(2,1)S(1)}, u32[]{:S(2)}, u32[]{:S(2)}) %collective-permute-start.19) | collective-permute-done | bytes 524320 | tf_op jit(solution)/shard_map/ppermute | solution.py:578
  145.4 1.1 collective-permute-start.21
  146.4 2.6 %shard_map.105 = (bf16[2,96,1024]{2,1,0:T(8,128)(2,1)}, bf16[2,96,1024]{2,1,0:T(8,128)(2,1)}) custom-call(s32[6]{0:T(128)S(1)} %concatenate.3.place, bf16[96,512]{1,0:T(8,128)(2,1)S(1)} %collective-permute-done.4.a0, bf16[96,512]{1,0:T(8,128)(2,1)S(1)} %collective-permute-done.5.a1, bf16[96,512]{1,0:T(8,128)(2,1)S(1)} %collective-permute-done.6.b0, ...), custom_call_target="tpu_custom_call" | custom-call | flops 1000 | bytes 1000 | tf_op jit(solution)/shard_map/pallas_call | solution.py:552
  149.0 3.0 %shard_map.108 = (f32[1024,768]{1,0:T(8,128)}, f32[1024,256]{1,0:T(8,128)}) custom-call(s32[6]{0:T(128)S(1)} %concatenate.3.place, bf16[256,1024]{1,0:T(8,128)(2,1)S(1)} %shard_map.107.own, bf16[256,1024]{1,0:T(8,128)(2,1)S(1)} %collective-permute-done.19.by_x, bf16[256,1024]{1,0:T(8,128)(2,1)S(1)} %collective-permute-done.20.by_core, ...), custom_call_target="tpu_custom_call" | custom-call | flops 1000 | bytes 1000 | tf_op jit(solution)/shard_map/pallas_call | solution.py:552
  (24 shorter events, 0.5 us)
Async XLA Ops:
  3.6 17.9 %collective-permute-start = (bf16[192,1024]{1,0:T(8,128)(2,1)S(1)}, bf16[192,1024]{1,0:T(8,128)(2,1)S(1)}, u32[]{:S(2)}, u32[]{:S(2)}) collective-permute-start(bf16[192,1024]{1,0:T(8,128)(2,1)S(1)} %get-tuple-element.25.m0), channel_id=1, source_target_pairs={{0,0},{1,8},{2,2},{3,10},{4,4},{5,12},{6,6},{7,14},{8,1},{9,9},{10... | collective-permute-start | bytes 1179656 | tf_op jit(solution)/shard_map/ppermute | solution.py:578
  8.4 17.3 %collective-permute-start.1 = (bf16[192,1024]{1,0:T(8,128)(2,1)S(1)}, bf16[192,1024]{1,0:T(8,128)(2,1)S(1)}, u32[]{:S(2)}, u32[]{:S(2)}) collective-permute-start(bf16[192,1024]{1,0:T(8,128)(2,1)S(1)} %get-tuple-element.26.m1), channel_id=1, source_target_pairs={{0,4},{1,12},{2,6},{3,14},{4,0},{5,8},{6,2},{7,10},{8,5},{9,13},{1... | collective-permute-start | bytes 1179656 | tf_op jit(solution)/shard_map/ppermute | solution.py:578
  21.5 4.2 %collective-permute-start.2 = (bf16[192,1024]{1,0:T(8,128)(2,1)S(1)}, bf16[192,1024]{1,0:T(8,128)(2,1)S(1)}, u32[]{:S(2)}, u32[]{:S(2)}) collective-permute-start(bf16[192,1024]{1,0:T(8,128)(2,1)S(1)} %collective-permute-done.p0), channel_id=1, source_target_pairs={{0,1},{1,0},{2,3},{3,2},{4,5},{5,4},{6,7},{7,6},{8,9},{9,8},{10,11... | collective-permute-start | bytes 1179656 | tf_op jit(solution)/shard_map/ppermute | solution.py:578
  25.7 1.7 %collective-permute-start.3 = (bf16[192,1024]{1,0:T(8,128)(2,1)S(1)}, bf16[192,1024]{1,0:T(8,128)(2,1)S(1)}, u32[]{:S(2)}, u32[]{:S(2)}) collective-permute-start(bf16[192,1024]{1,0:T(8,128)(2,1)S(1)} %collective-permute-done.1.p1), channel_id=1, source_target_pairs={{0,1},{1,0},{2,3},{3,2},{4,5},{5,4},{6,7},{7,6},{8,9},{9,8},{10,11... | collective-permute-start | bytes 1179656 | tf_op jit(solution)/shard_map/ppermute | solution.py:578
  38.5 21.5 %collective-permute-start.8 = (bf16[3,192,512]{2,1,0:T(8,128)(2,1)S(1)}, bf16[3,192,512]{2,1,0:T(8,128)(2,1)S(1)}, u32[]{:S(2)}, u32[]{:S(2)}) collective-permute-start(bf16[3,192,512]{2,1,0:T(8,128)(2,1)S(1)} %get-tuple-element.33), channel_id=1, source_target_pairs={{0,1},{1,0},{2,3},{3,2},{4,5},{5,4},{6,7},{7,6},{8,9},{9,8},{10,11... | collective-permute-start | bytes 1769480 | tf_op jit(solution)/shard_map/ppermute | solution.py:578
  38.7 10.3 %collective-permute-start.12 = (bf16[192,1024]{1,0:T(8,128)(2,1)S(1)}, bf16[192,1024]{1,0:T(8,128)(2,1)S(1)}, u32[]{:S(2)}, u32[]{:S(2)}) collective-permute-start(bf16[192,1024]{1,0:T(8,128)(2,1)S(1)} %collective-permute-done.p0), channel_id=1, source_target_pairs={{0,2},{1,3},{2,0},{3,1},{4,6},{5,7},{6,4},{7,5},{8,10},{9,11},{10,... | collective-permute-start | bytes 1179656 | tf_op jit(solution)/shard_map/ppermute | solution.py:578
  39.9 17.5 %collective-permute-start.13 = (bf16[192,1024]{1,0:T(8,128)(2,1)S(1)}, bf16[192,1024]{1,0:T(8,128)(2,1)S(1)}, u32[]{:S(2)}, u32[]{:S(2)}) collective-permute-start(bf16[192,1024]{1,0:T(8,128)(2,1)S(1)} %collective-permute-done.1.p1), channel_id=1, source_target_pairs={{0,2},{1,3},{2,0},{3,1},{4,6},{5,7},{6,4},{7,5},{8,10},{9,11},{10,... | collective-permute-start | bytes 1179656 | tf_op jit(solution)/shard_map/ppermute | solution.py:578
  40.2 40.5 %collective-permute-start.11 = (bf16[1024,384]{1,0:T(8,128)(2,1)S(1)}, bf16[1024,384]{1,0:T(8,128)(2,1)S(1)}, u32[]{:S(2)}, u32[]{:S(2)}) collective-permute-start(bf16[1024,384]{1,0:T(8,128)(2,1)S(1)} %get-tuple-element.39), channel_id=1, source_target_pairs={{0,2},{1,3},{2,0},{3,1},{4,6},{5,7},{6,4},{7,5},{8,10},{9,11},{10,... | collective-permute-start | bytes 2359304 | tf_op jit(solution)/shard_map/ppermute | solution.py:578
  41.4 18.1 %collective-permute-start.4 = (bf16[96,512]{1,0:T(8,128)(2,1)S(1)}, bf16[96,512]{1,0:T(8,128)(2,1)S(1)}, u32[]{:S(2)}, u32[]{:S(2)}) collective-permute-start(bf16[96,512]{1,0:T(8,128)(2,1)S(1)} %get-tuple-element.27), channel_id=1, source_target_pairs={{0,0},{1,8},{2,2},{3,10},{4,4},{5,12},{6,6},{7,14},{8,1},{9,9},{10... | collective-permute-start | bytes 294920 | tf_op jit(solution)/shard_map/ppermute | solution.py:578
  49.1 10.5 %collective-permute-start.5 = (bf16[96,512]{1,0:T(8,128)(2,1)S(1)}, bf16[96,512]{1,0:T(8,128)(2,1)S(1)}, u32[]{:S(2)}, u32[]{:S(2)}) collective-permute-start(bf16[96,512]{1,0:T(8,128)(2,1)S(1)} %get-tuple-element.28), channel_id=1, source_target_pairs={{0,4},{1,12},{2,6},{3,14},{4,0},{5,8},{6,2},{7,10},{8,5},{9,13},{1... | collective-permute-start | bytes 294920 | tf_op jit(solution)/shard_map/ppermute | solution.py:578
  57.5 13.9 %collective-permute-start.14 = (bf16[192,1024]{1,0:T(8,128)(2,1)S(1)}, bf16[192,1024]{1,0:T(8,128)(2,1)S(1)}, u32[]{:S(2)}, u32[]{:S(2)}) collective-permute-start(bf16[192,1024]{1,0:T(8,128)(2,1)S(1)} %collective-permute-done.12.r0), channel_id=1, source_target_pairs={{0,1},{1,0},{2,3},{3,2},{4,5},{5,4},{6,7},{7,6},{8,9},{9,8},{10,11... | collective-permute-start | bytes 1179656 | tf_op jit(solution)/shard_map/ppermute | solution.py:578
  59.5 11.9 %collective-permute-start.15 = (bf16[192,1024]{1,0:T(8,128)(2,1)S(1)}, bf16[192,1024]{1,0:T(8,128)(2,1)S(1)}, u32[]{:S(2)}, u32[]{:S(2)}) collective-permute-start(bf16[192,1024]{1,0:T(8,128)(2,1)S(1)} %collective-permute-done.13.r1), channel_id=1, source_target_pairs={{0,1},{1,0},{2,3},{3,2},{4,5},{5,4},{6,7},{7,6},{8,9},{9,8},{10,11... | collective-permute-start | bytes 1179656 | tf_op jit(solution)/shard_map/ppermute | solution.py:578
  59.5 9.7 %collective-permute-start.6 = (bf16[96,512]{1,0:T(8,128)(2,1)S(1)}, bf16[96,512]{1,0:T(8,128)(2,1)S(1)}, u32[]{:S(2)}, u32[]{:S(2)}) collective-permute-start(bf16[96,512]{1,0:T(8,128)(2,1)S(1)} %get-tuple-element.29), channel_id=1, source_target_pairs={{0,8},{1,0},{2,10},{3,2},{4,12},{5,4},{6,14},{7,6},{8,9},{9,1},{10... | collective-permute-start | bytes 294920 | tf_op jit(solution)/shard_map/ppermute | solution.py:578
  60.0 11.3 %collective-permute-start.7 = (bf16[96,512]{1,0:T(8,128)(2,1)S(1)}, bf16[96,512]{1,0:T(8,128)(2,1)S(1)}, u32[]{:S(2)}, u32[]{:S(2)}) collective-permute-start(bf16[96,512]{1,0:T(8,128)(2,1)S(1)} %get-tuple-element.30), channel_id=1, source_target_pairs={{0,12},{1,4},{2,14},{3,6},{4,8},{5,0},{6,10},{7,2},{8,13},{9,5},{1... | collective-permute-start | bytes 294920 | tf_op jit(solution)/shard_map/ppermute | solution.py:578
  69.2 8.0 %collective-permute-start.9 = (bf16[96,1024]{1,0:T(8,128)(2,1)S(1)}, bf16[96,1024]{1,0:T(8,128)(2,1)S(1)}, u32[]{:S(2)}, u32[]{:S(2)}) collective-permute-start(bf16[96,1024]{1,0:T(8,128)(2,1)S(1)} %get-tuple-element.34), channel_id=1, source_target_pairs={{0,0},{1,8},{2,2},{3,10},{4,4},{5,12},{6,6},{7,14},{8,1},{9,9},{10... | collective-permute-start | bytes 589832 | tf_op jit(solution)/shard_map/ppermute | solution.py:578
  71.3 9.4 %collective-permute-start.10 = (bf16[96,1024]{1,0:T(8,128)(2,1)S(1)}, bf16[96,1024]{1,0:T(8,128)(2,1)S(1)}, u32[]{:S(2)}, u32[]{:S(2)}) collective-permute-start(bf16[96,1024]{1,0:T(8,128)(2,1)S(1)} %get-tuple-element.35), channel_id=1, source_target_pairs={{0,4},{1,12},{2,6},{3,14},{4,0},{5,8},{6,2},{7,10},{8,5},{9,13},{1... | collective-permute-start | bytes 589832 | tf_op jit(solution)/shard_map/ppermute | solution.py:578
  80.7 65.7 %copy-start = (bf16[1024,1024]{1,0:T(8,128)(2,1)S(1)}, bf16[1024,1024]{1,0:T(8,128)(2,1)}, u32[]{:S(2)}) copy-start(bf16[1024,1024]{1,0:T(8,128)(2,1)} %w_ref.3) | copy-start | bytes 6291460
  80.7 65.7 %copy-start.1 = (f32[1024]{0:T(1024)S(1)}, f32[1024]{0:T(1024)}, u32[]{:S(2)}) copy-start(f32[1024]{0:T(1024)} %param.13) | copy-start | bytes 12292
  83.6 17.7 %collective-permute-start.16 = (bf16[256,1024]{1,0:T(8,128)(2,1)S(1)}, bf16[256,1024]{1,0:T(8,128)(2,1)S(1)}, u32[]{:S(2)}, u32[]{:S(2)}) collective-permute-start(bf16[256,1024]{1,0:T(8,128)(2,1)S(1)} %get-tuple-element.41), channel_id=1, source_target_pairs={{0,4},{1,5},{2,6},{3,7},{4,0},{5,1},{6,2},{7,3},{8,12},{9,13},{10,... | collective-permute-start | bytes 1572872 | tf_op jit(solution)/shard_map/ppermute | solution.py:578
  83.7 17.6 %collective-permute-start.17 = (bf16[256,1024]{1,0:T(8,128)(2,1)S(1)}, bf16[256,1024]{1,0:T(8,128)(2,1)S(1)}, u32[]{:S(2)}, u32[]{:S(2)}) collective-permute-start(bf16[256,1024]{1,0:T(8,128)(2,1)S(1)} %get-tuple-element.42), channel_id=1, source_target_pairs={{0,8},{1,9},{2,10},{3,11},{4,12},{5,13},{6,14},{7,15},{8,0},{9,1},... | collective-permute-start | bytes 1572872 | tf_op jit(solution)/shard_map/ppermute | solution.py:578
  83.8 48.0 %collective-permute-start.18 = (bf16[256,1024]{1,0:T(8,128)(2,1)S(1)}, bf16[256,1024]{1,0:T(8,128)(2,1)S(1)}, u32[]{:S(2)}, u32[]{:S(2)}) collective-permute-start(bf16[256,1024]{1,0:T(8,128)(2,1)S(1)} %get-tuple-element.43), channel_id=1, source_target_pairs={{0,12},{1,13},{2,14},{3,15},{4,8},{5,9},{6,10},{7,11},{8,4},{9,5},... | collective-permute-start | bytes 1572872 | tf_op jit(solution)/shard_map/ppermute | solution.py:578
  132.0 13.4 %collective-permute-start.19 = (bf16[256,1024]{1,0:T(8,128)(2,1)S(1)}, bf16[256,1024]{1,0:T(8,128)(2,1)S(1)}, u32[]{:S(2)}, u32[]{:S(2)}) collective-permute-start(bf16[256,1024]{1,0:T(8,128)(2,1)S(1)} %shard_map.107.own), channel_id=1, source_target_pairs={{0,2},{1,3},{2,0},{3,1},{4,6},{5,7},{6,4},{7,5},{8,10},{9,11},{10,... | collective-permute-start | bytes 1572872 | tf_op jit(solution)/shard_map/ppermute | solution.py:578
  133.3 15.7 %collective-permute-start.20 = (bf16[256,1024]{1,0:T(8,128)(2,1)S(1)}, bf16[256,1024]{1,0:T(8,128)(2,1)S(1)}, u32[]{:S(2)}, u32[]{:S(2)}) collective-permute-start(bf16[256,1024]{1,0:T(8,128)(2,1)S(1)} %shard_map.107.own), channel_id=1, source_target_pairs={{0,1},{1,0},{2,3},{3,2},{4,5},{5,4},{6,7},{7,6},{8,9},{9,8},{10,11... | collective-permute-start | bytes 1572872 | tf_op jit(solution)/shard_map/ppermute | solution.py:578
  145.4 3.7 %collective-permute-start.21 = (bf16[256,1024]{1,0:T(8,128)(2,1)S(1)}, bf16[256,1024]{1,0:T(8,128)(2,1)S(1)}, u32[]{:S(2)}, u32[]{:S(2)}) collective-permute-start(bf16[256,1024]{1,0:T(8,128)(2,1)S(1)} %collective-permute-done.19.by_x), channel_id=1, source_target_pairs={{0,1},{1,0},{2,3},{3,2},{4,5},{5,4},{6,7},{7,6},{8,9},{9,8},{10,11... | collective-permute-start | bytes 1572872 | tf_op jit(solution)/shard_map/ppermute | solution.py:578

commit v4 on v3

--- a/solution.py
+++ b/solution.py
@@ -333,29 +333,32 @@
         out_ref[rows:, :] = jnp.where(live, grad, jnp.zeros_like(grad))
 
 
-def attend_kernel(
-    place, p0, p1, p2, p3, w_in_hbm, w_out_hbm,
-    att0, att1, att2, att3, dp_own, dp_oth, send_t, keep_t,
-    norm_s, grad_s, wq, wk, wv, wo, sems,
-):
-    core = place[CORE]
-    width = p0.shape[1]
+def load_weights(core, first_pair, w_in_hbm, w_out_hbm, wq, wk, wv, wo, sems):
+    width = w_out_hbm.shape[0]
     copies = []
-    for j in range(width // 256):
+    for j in range(wq.shape[1] // 128):
         to = pl.ds(128 * j, 128)
-        row = pl.multiple_of(256 * j + 128 * core, 128)
+        row = pl.multiple_of(256 * (first_pair + j) + 128 * core, 128)
         pairs = [(w_out_hbm.at[pl.ds(row, 128), :], wo.at[to, :])]
         for t, out in enumerate((wq, wk, wv)):
-            at = pl.multiple_of(t * width + 256 * j + 128 * core, 128)
+            at = pl.multiple_of(t * width + row, 128)
             pairs.append((w_in_hbm.at[:, pl.ds(at, 128)], out.at[:, to]))
         copies += [pltpu.make_async_copy(a, b, sems.at[4 * j + i]) for i, (a, b) in enumerate(pairs)]
     for copy in copies:
         copy.start()
-    block = p0.shape[0] // 2
+    return copies
+
+
+def attend_pairs(
+    place, first_pair, payloads, w_in_hbm, w_out_hbm, own, oth, keep_t, out_keep, send,
+    norm_s, grad_s, att_s, wq, wk, wv, wo, sems,
+):
+    copies = load_weights(place[CORE], first_pair, w_in_hbm, w_out_hbm, wq, wk, wv, wo, sems)
+    block = payloads[0].shape[0] // 2
     rows = 4 * block
     half = 2 * block
     biases = []
-    for i, ref in enumerate((p0, p1, p2, p3)):
+    for i, ref in enumerate(payloads):
         at = slice(i * block, (i + 1) * block)
         value = ref[:block, :]
         live = value[:, 0:1].astype(jnp.float32) < MARK
@@ -367,22 +370,20 @@
     scale = jnp.bfloat16(0.125)
     zero = jnp.zeros((rows, 128), jnp.bfloat16)
     first = place[SIDE] == 0
-    for j in range(width // 256):
+    count = wq.shape[1] // 128
+    for copy in copies:
+        copy.wait()
+    normed = norm_s[...]
+    queries = dot_nn(normed, wq[...]).astype(jnp.bfloat16)
+    keys = dot_nn(normed, wk[...]).astype(jnp.bfloat16)
+    values = dot_nn(normed, wv[...]).astype(jnp.bfloat16)
+    d_att = dot_nt(grad_s[...], wo[...]).astype(jnp.bfloat16)
+    for j in range(count):
         cols = slice(128 * j, 128 * j + 128)
-        if j % 2 == 0:
-            two = slice(128 * j, 128 * j + 256)
-            for copy in copies[4 * j : 4 * j + 8]:
-                copy.wait()
-            normed = norm_s[...]
-            queries = dot_nn(normed, wq[:, two]).astype(jnp.bfloat16)
-            keys = dot_nn(normed, wk[:, two]).astype(jnp.bfloat16)
-            values = dot_nn(normed, wv[:, two]).astype(jnp.bfloat16)
-            d_att = dot_nt(grad_s[...], wo[two, :]).astype(jnp.bfloat16)
-        here = slice(128 * (j % 2), 128 * (j % 2) + 128)
-        q = queries[:, here] * scale
-        k = keys[:, here]
-        v = values[:, here]
-        g = d_att[:, here]
+        q = queries[:, cols] * scale
+        k = keys[:, cols]
+        v = values[:, cols]
+        g = d_att[:, cols]
         v_t = v.T
         k_t = (k * scale).T
         att_t, dq_t, dk, dv = [], [], [], []
@@ -401,19 +402,31 @@
             dq_t.append(dot_nn(k_t[part], d_score))
             dk.append(dot_nn(d_score, q))
         att_pair_t = jnp.concatenate(att_t, axis=0).astype(jnp.bfloat16)
-        att_pair = att_pair_t.T
         dq_pair_t = jnp.concatenate(dq_t, axis=0).astype(jnp.bfloat16)
         dk_pair = jnp.where(low, dk[0], dk[1]).astype(jnp.bfloat16)
         dv_pair = jnp.where(low, dv[0], dv[1]).astype(jnp.bfloat16)
-        for i, out in enumerate((att0, att1, att2, att3)):
-            out[:, cols] = att_pair[i * block : (i + 1) * block]
-        for t, piece in enumerate((dq_pair_t.T, dk_pair, dv_pair)):
-            dp_own[t, :, cols] = piece[:half]
-            dp_oth[t, :, cols] = piece[half:]
-        for t, piece in enumerate((dq_pair_t, dk_pair.T, dv_pair.T, att_pair_t)):
-            at = slice(64 * (4 * t + j), 64 * (4 * t + j) + 64)
-            keep_t[at, :] = jnp.where(first, piece[:64], piece[64:])
-            send_t[at, :] = jnp.where(first, piece[64:], piece[:64])
+        for t, piece in enumerate((dq_pair_t.T, dk_pair, dv_pair, att_pair_t.T)):
+            own[t, :, cols] = piece[:half]
+            oth[t, :, cols] = piece[half:]
+        for t, piece in enumerate((dq_pair_t, dk_pair.T, dv_pair.T)):
+            at = slice(64 * j, 64 * j + 64)
+            part = slice(rows * t, rows * t + rows)
+            keep_t[at, part] = jnp.where(first, piece[:64], piece[64:])
+            send[at, part] = jnp.where(first, piece[64:], piece[:64])
+        at = slice(64 * j, 64 * j + 64)
+        att_s[0, at, :] = jnp.where(first, att_pair_t[:64], att_pair_t[64:])
+        att_s[1, at, :] = jnp.where(first, att_pair_t[64:], att_pair_t[:64])
+    out_keep[...] = dot_nn(att_s[0], grad_s[...])
+    send[:, 3 * rows :] = dot_nn(att_s[1], grad_s[...]).astype(send.dtype)
+
+
+def attend_first(place, p0, p1, p2, p3, *refs):
+    attend_pairs(place, 0, (p0, p1, p2, p3), *refs)
+
+
+def attend_second(place, p0, p1, p2, p3, w_in_hbm, w_out_hbm, after, *refs):
+    del after
+    attend_pairs(place, 2, (p0, p1, p2, p3), w_in_hbm, w_out_hbm, *refs)
 
 
 def in_order(place, own, got):
@@ -425,13 +438,23 @@
     return jnp.concatenate(pieces, axis=1)
 
 
-def d_normed_kernel(place, own, got, w_ref, o0, o1, total):
+def rows_kernel(place, own_a, got_a, own_b, got_b, w_ref, after, before, o0, o1, total):
+    del after, before
     step = pl.program_id(0)
-    term = dot_nt(in_order(place[CORE], own[step], got[step]), w_ref[...])
+    core = place[CORE]
+    block = o0.shape[0] // 2
+
+    def rows_of(t):
+        return jnp.concatenate([in_order(core, own_a[t], got_a[t]), in_order(core, own_b[t], got_b[t])], axis=1)
+
+    term = dot_nt(rows_of(step), w_ref[...])
 
     @pl.when(step == 0)
     def _():
         total[...] = term
+        att = rows_of(3)
+        o0[:block, :] = att[:block]
+        o1[:block, :] = att[block:]
 
     @pl.when(step > 0)
     def _():
@@ -439,94 +462,124 @@
 
     @pl.when(step == pl.num_programs(0) - 1)
     def _():
-        half = o0.shape[0]
-        o0[...] = total[:half].astype(o0.dtype)
-        o1[...] = total[half:].astype(o1.dtype)
-
-
-def encode(place, a0, a1, b0, b1, w_ref, hidden_ref, out_ref):
-    par, core = place[PAR], place[LINE] // 2
-    for k, (a, b) in enumerate(((a0, b0), (a1, b1))):
+        o0[block:, :] = total[:block].astype(o0.dtype)
+        o1[block:, :] = total[block:].astype(o1.dtype)
+
+
+def return_kernel(place, r0, r1, w_ref, hidden_ref, m0, m1, gain_ref, encoded, d_patches):
+    par = place[PAR]
+    rows = r0.shape[0] // 2
+    for k, (r_ref, m_ref) in enumerate(((r0, m0), (r1, m1))):
         s = k ^ par
-        projected = dot_nn(in_order(core, a[...], b[...]), w_ref[...])
-        live = live_column(place[KEPT + s], a.shape[0])
-        out_ref[s] = jnp.where(live, hidden_ref[k] + projected, 0.0).astype(out_ref.dtype)
-
-
-def patch_grad(place, d0, d1, p0, p1, hidden_ref, gain_ref, out_ref):
-    par = place[PAR]
-    rows = d0.shape[0]
-    for k, (d_ref, p_ref) in enumerate(((d0, p0), (d1, p1))):
-        s = k ^ par
+        live = live_column(place[KEPT + s], rows)
         hidden = hidden_ref[k]
+        projected = dot_nn(r_ref[:rows, :], w_ref[...])
+        encoded[s] = jnp.where(live, hidden + projected, 0.0).astype(encoded.dtype)
         center = hidden - jnp.mean(hidden, axis=-1, keepdims=True)
         spread = jnp.mean(center * center, axis=-1, keepdims=True)
         inv_std = lax.rsqrt(spread + epsilon)
         unit = center * inv_std
-        d_hidden = norm_backward(d_ref[...].astype(jnp.float32), gain_ref[...], unit, inv_std)
-        live = live_column(place[KEPT + s], rows)
-        value = p_ref[rows:, :].astype(jnp.float32) + d_hidden
-        out_ref[s] = jnp.where(live, value, 0.0).astype(out_ref.dtype)
-
-
-def return_kernel(place, a0, a1, b0, b1, w_ref, hidden_ref, d0, d1, m0, m1, gain_ref, encoded, d_patches):
-    encode(place, a0, a1, b0, b1, w_ref, hidden_ref, encoded)
-    patch_grad(place, d0, d1, m0, m1, hidden_ref, gain_ref, d_patches)
-
-
-def weight_kernel(
-    place, keep, got, p0, p1, p2, p3, r0, r1, r2, r3, d0, d1, a0, a1, b0, b1,
-    o0, o1, o2, o3, tokens, total,
+        d_hidden = norm_backward(r_ref[rows:, :].astype(jnp.float32), gain_ref[...], unit, inv_std)
+        value = m_ref[rows:, :].astype(jnp.float32) + d_hidden
+        d_patches[s] = jnp.where(live, value, 0.0).astype(d_patches.dtype)
+
+
+def put_out_part(place, out_keep, got, outs, total):
+    total[...] = out_keep[...] + got[:, got.shape[1] - total.shape[1] :].astype(jnp.float32)
+    columns = total.shape[1] // 4
+    tall = total.shape[0] // 4
+    for k, out in enumerate(outs):
+        at = pl.multiple_of((place[LINE] ^ k) * columns, 128)
+        value = total[:, pl.ds(at, columns)].astype(out.dtype)
+        base = out.shape[0] - tall
+        for j in range(4):
+            out[base:, columns * j : columns * j + columns] = value[tall * j : tall * j + tall, :]
+
+
+def piece_of(ref, at, rows):
+    t, j = at // 2, at % 2
+    return ref[64 * j : 64 * j + 64, rows * t : rows * t + rows]
+
+
+def weight_first(
+    place, keep, out_keep, got, p0, p1, p2, p3, n0, n1,
+    o0, o1, o2, o3, tokens, left, total, out_total,
 ):
-    del d0, d1, a0, a1, b0, b1
     block = p0.shape[0] // 2
     rows = 4 * block
-    columns = o0.shape[0]
-    count = 3 * columns // 4
-    for i, ref in enumerate((p0, p1, p2, p3, r0, r1, r2, r3)):
-        tokens[i * block : (i + 1) * block, :] = ref[block:, :]
-    at = slice(4 * count, None)
-    total[...] = dot_nn(keep[at, :], tokens[:rows, :]) + dot_nn(got[at, :], tokens[rows:, :])
+    for i, ref in enumerate((p0, p1, p2, p3)):
+        tokens[i * block : (i + 1) * block, :] = ref[:block, :]
+    tokens[rows : rows + 2 * block, :] = n0[...]
+    tokens[rows + 2 * block :, :] = n1[...]
+    for side, ref in enumerate((keep, got)):
+        for i, at in enumerate((0, 2, 4, 5)):
+            left[side, 64 * i : 64 * i + 64, :] = piece_of(ref, at, rows)
+    total[...] = dot_nn(left[0], tokens[:rows, :]) + dot_nn(left[1], tokens[rows:, :])
     for k, out in enumerate((o0, o1, o2, o3)):
-        at = pl.multiple_of((place[LINE] ^ k) * columns, 128)
-        value = total[:, pl.ds(at, columns)].astype(out.dtype)
-        for j in range(4):
-            out[count:, columns * j : columns * j + columns] = value[64 * j : 64 * j + 64, :]
-    for i, ref in enumerate((p0, p1, p2, p3, r0, r1, r2, r3)):
+        at = pl.multiple_of((place[LINE] ^ k) * 64, 64)
+        out[:64, :] = total[pl.ds(at, 64), :].astype(out.dtype)
+    put_out_part(place, out_keep, got, (o0, o1, o2, o3), out_total)
+
+
+def weight_second(
+    place, keep_a, got_a, keep_b, out_keep, got_b, p0, p1, p2, p3, n0, n1, after,
+    o0, o1, o2, o3, tokens, left, total, out_total,
+):
+    del after
+    block = p0.shape[0] // 2
+    rows = 4 * block
+    for i, ref in enumerate((p0, p1, p2, p3)):
         tokens[i * block : (i + 1) * block, :] = ref[:block, :]
+    tokens[rows : rows + 2 * block, :] = n0[...]
+    tokens[rows + 2 * block :, :] = n1[...]
+    for side, (a, b) in enumerate(((keep_a, keep_b), (got_a, got_b))):
+        for i, (ref, at) in enumerate(
+            ((a, 1), (b, 0), (b, 1), (a, 3), (b, 2), (b, 3), (b, 4), (b, 5))
+        ):
+            left[side, 64 * i : 64 * i + 64, :] = piece_of(ref, at, rows)
+    total[...] = dot_nn(left[0], tokens[:rows, :]) + dot_nn(left[1], tokens[rows:, :])
     for k, out in enumerate((o0, o1, o2, o3)):
-        at = pl.ds(pl.multiple_of((place[LINE] ^ k) * count, 16), count)
-        value = dot_nn(keep[at, :], tokens[:rows, :]) + dot_nn(got[at, :], tokens[rows:, :])
-        out[:count, :] = value.astype(out.dtype)
-
-
-def sum_kernel(a0, a1, a2, a3, out):
+        at = pl.multiple_of((place[LINE] ^ k) * 128, 128)
+        out[:128, :] = total[pl.ds(at, 128), :].astype(out.dtype)
+    put_out_part(place, out_keep, got_b, (o0, o1, o2, o3), out_total)
+
+
+def sum_kernel(a0, a1, a2, a3, *refs):
+    out = refs[-1]
     f32 = jnp.float32
     value = (a0[...].astype(f32) + a1[...].astype(f32)) + (a2[...].astype(f32) + a3[...].astype(f32))
     out[...] = value.astype(out.dtype)
 
 
-def finish_kernel(place, own, by_x, by_core, by_both, wide, narrow):
+def finish_kernel(place, a0, a1, a2, a3, b0, b1, b2, b3, wide, narrow):
     core_low, side_low = place[CORE] == 0, place[SIDE] == 0
-    count = own.shape[0] - 64
+    slab = place[LINE]
     columns = narrow.shape[1]
-
-    def pick(at, c, x, part):
-        a = jnp.where(side_low == (x == 0), own[at, part], by_x[at, part])
-        b = jnp.where(side_low == (x == 0), by_core[at, part], by_both[at, part])
-        return jnp.where(core_low == (c == 0), a, b)
-
+    spot = jnp.where(slab == 3, 0, slab)
+    spots = (spot, jnp.where(spot == 0, 1, 0), jnp.where(spot == 2, 1, 2))
+
+    def pick(refs, c, x, at, part):
+        own, by_x, by_core, by_both = refs
+        near = jnp.where(side_low == (x == 0), own[at, part], by_x[at, part])
+        far = jnp.where(side_low == (x == 0), by_core[at, part], by_both[at, part])
+        return jnp.where(core_low == (c == 0), near, far)
+
+    every = slice(None)
+    first, second = (a0, a1, a2, a3), (b0, b1, b2, b3)
     for c in range(2):
-        for i in range(count // 64):
-            at = slice(64 * i, 64 * i + 64)
-            both = jnp.concatenate([pick(at, c, x, slice(None)) for x in range(2)], axis=0)
-            col = 128 * (2 * i + c)
-            wide[:, col : col + 128] = both.T.astype(wide.dtype)
-        for j in range(4):
-            for x in range(2):
-                row = 128 * (2 * j + c) + 64 * x
+        for i, (refs, row) in enumerate(((first, 0), (second, 0), (second, 64))):
+            at = slice(row, row + 64)
+            both = jnp.concatenate([pick(refs, c, x, at, every) for x in range(2)], axis=0)
+            col = pl.multiple_of(128 * (2 * spots[i] + c), 128)
+            wide[:, pl.ds(col, 128)] = both.T.astype(wide.dtype)
+        for half, (refs, base) in enumerate(((first, 64), (second, 128))):
+            for j in range(4):
+                at = slice(base, base + 32)
                 part = slice(columns * j, columns * j + columns)
-                narrow[row : row + 64, :] = pick(slice(count, None), c, x, part).astype(narrow.dtype)
+                for x in range(2):
+                    pair, row = 2 * half + j // 2, 32 * (j % 2)
+                    row += 128 * (2 * pair + c) + 64 * x
+                    narrow[row : row + 32, :] = pick(refs, c, x, at, part).astype(narrow.dtype)
 
 
 SMEM_SPEC = pl.BlockSpec(memory_space=pltpu.SMEM)
@@ -612,68 +665,100 @@
     )
     got = [to_chip(mine[k], k) for k in range(2)]
     here = got + [to_core(v) for v in got]
-    from_x = [to_x(v) for v in got]
-    there = from_x + [to_core(v) for v in from_x]
-
-    att = struct((slots, own_width))
-    d_rows = struct((3, 2 * slots, own_width))
-    half_t = struct((width, rows))
-    *atts, dp_own, dp_oth, send_t, keep_t = call(
-        attend_kernel,
-        (*here, in_hbm(w_qkv), in_hbm(w_out)),
-        [att] * 4 + [d_rows] * 2 + [half_t] * 2,
-        36,
-        place,
-        scratch=[pltpu.VMEM((rows, width), bf16)] * 2
-        + [pltpu.VMEM((width, own_width), bf16)] * 3
-        + [pltpu.VMEM((own_width, width), bf16), pltpu.SemaphoreType.DMA((4 * (width // 256),))],
-        specs=[VMEM_SPEC] * 4 + [hbm] * 2,
-    )
-    got_t = to_x(send_t)
-    dp_core = to_core(dp_oth)
-    back_att = [to_rows(atts[k], k, 0) for k in range(2)] + [to_rows(atts[2 + k], k, 1) for k in range(2)]
-
-    d_normed = pl.pallas_call(
-        d_normed_kernel,
+    from_x = to_x(jnp.concatenate([v[:slots] for v in got], axis=0))
+    there = (from_x, to_core(from_x))
+
+    any_spec = pl.BlockSpec(memory_space=pl.ANY)
+    pairs = width // 512
+    half_rows = struct((4, 2 * slots, 128 * pairs))
+    out_half = (64 * pairs, width)
+    half_t = struct((64 * pairs, 3 * rows))
+    half_send = struct((64 * pairs, 3 * rows + width))
+
+    def attend(kernel, extra):
+        return call(
+            kernel,
+            (*here, in_hbm(w_qkv), in_hbm(w_out), *extra),
+            [half_rows] * 2 + [half_t, struct(out_half, f32), half_send],
+            32,
+            place,
+            scratch=[pltpu.VMEM((rows, width), bf16)] * 2
+            + [pltpu.VMEM((2, 64 * pairs, rows), bf16)]
+            + [pltpu.VMEM((width, 128 * pairs), bf16)] * 3
+            + [pltpu.VMEM((128 * pairs, width), bf16), pltpu.SemaphoreType.DMA((4 * pairs,))],
+            specs=[VMEM_SPEC] * 4 + [any_spec] * (2 + len(extra)),
+        )
+
+    own_a, oth_a, keep_a, out_keep_a, send_a = attend(attend_first, ())
+    got_a = to_x(send_a)
+    core_a = to_core(oth_a)
+    own_b, oth_b, keep_b, out_keep_b, send_b = attend(attend_second, (from_x,))
+    got_b = to_x(send_b)
+    core_b = to_core(oth_b)
+
+    def exchange(kernel, args, tall, scratch, after=()):
+        outs = call(
+            kernel,
+            (*args, *here, *there, *after),
+            [struct((tall, width))] * 4,
+            16,
+            place,
+            scratch=[pltpu.VMEM((2 * rows, width), bf16)] + scratch + [pltpu.VMEM(out_half, f32)],
+            specs=[VMEM_SPEC] * (len(args) + 6) + [any_spec] * len(after),
+        )
+        return [outs[0]] + [along(outs[k], k) for k in range(1, 4)]
+
+    def spread(parts, after=()):
+        sums = call(
+            sum_kernel,
+            (*parts, *after),
+            struct(parts[0].shape),
+            8,
+            specs=[VMEM_SPEC] * 4 + [any_spec] * len(after),
+        )
+        by_x = to_x(sums)
+        return (sums, by_x, to_core(sums), to_core(by_x))
+
+    parts = exchange(
+        weight_first,
+        (keep_a, out_keep_a, got_a),
+        96,
+        [pltpu.VMEM((2, 256, rows), bf16), pltpu.VMEM((256, width), f32)],
+    )
+    first = spread(parts)
+    parts = exchange(
+        weight_second,
+        (keep_a, got_a, keep_b, out_keep_b, got_b),
+        160,
+        [pltpu.VMEM((2, 512, rows), bf16), pltpu.VMEM((512, width), f32)],
+        (first[0],),
+    )
+    back = pl.pallas_call(
+        rows_kernel,
         grid_spec=pltpu.PrefetchScalarGridSpec(
             num_scalar_prefetch=1,
             grid=(3,),
-            in_specs=[pl.BlockSpec(d_rows.shape, lambda i, p: (0, 0, 0))] * 2
-            + [pl.BlockSpec((width, width), lambda i, p: (0, i))],
-            out_specs=[pl.BlockSpec((slots, width), lambda i, p: (0, 0))] * 2,
+            in_specs=[pl.BlockSpec(half_rows.shape, lambda i, p: (0, 0, 0))] * 4
+            + [pl.BlockSpec((width, width), lambda i, p: (0, i)), any_spec, any_spec],
+            out_specs=[pl.BlockSpec(pay.shape, lambda i, p: (0, 0))] * 2,
             scratch_shapes=[pltpu.VMEM((2 * slots, width), f32)],
         ),
-        out_shape=[struct((slots, width))] * 2,
-        compiler_params=pltpu.CompilerParams(vmem_limit_bytes=16 * MIB),
+        out_shape=[pay] * 2,
+        compiler_params=pltpu.CompilerParams(vmem_limit_bytes=20 * MIB),
         cost_estimate=COST,
-    )(place, dp_own, dp_core, in_hbm(w_qkv))
-    back_dn = [to_rows(d_normed[k], k, 0) for k in range(2)]
-
-    part = struct((quarter, width))
-    dw = call(
-        weight_kernel,
-        (keep_t, got_t, *here, *there, *back_dn, *back_att),
-        [part] * 4,
-        16,
-        place,
-        scratch=[pltpu.VMEM((2 * rows, width), bf16), pltpu.VMEM((quarter, width), f32)],
-        specs=[VMEM_SPEC] * 10 + [pl.BlockSpec(memory_space=pl.ANY)] * 6,
-    )
-    dw = [dw[0]] + [along(dw[k], k) for k in range(1, 4)]
+    )(place, own_a, core_a, own_b, core_b, in_hbm(w_qkv), parts[0], first[1])
+    second = spread(parts, (back[0],))
+    back = [to_rows(back[k], k, 0) for k in range(2)]
     encoded, d_patches = call(
         return_kernel,
-        (*back_att, w_out, hidden, *back_dn, *mine, gain_row),
+        (*back, w_out, hidden, *mine, gain_row),
         [struct(patches.shape)] * 2,
         12,
         place,
     )
-    sums = call(sum_kernel, dw, part, 8)
-    by_x = to_x(sums)
-    by_core = to_core(sums)
-    by_both = to_core(by_x)
     qkv_grad, out_grad = call(
         finish_kernel,
-        (sums, by_x, by_core, by_both),
+        (*first, *second),
         [struct((width, 3 * quarter), f32), struct((width, quarter), f32)],
         12,
         place,

time: 152 us -> 132 us (0.87); the launches traced: 152 us -> 130 us
  waiting for transfers between devices: 94.7 us -> 63.2 us
  starting transfers between devices: 28.1 us -> 34.3 us
  Pallas kernels: 27.7 us -> 30.9 us
    ppermute x22 -> x24, waiting for transfers between devices: 94.7 us -> 63.2 us  [send(): return lax.ppermute(value, AXES, line_perm(move, reps))]
    ppermute x22 -> x24, starting transfers between devices: 28.1 us -> 34.3 us  [send(): return lax.ppermute(value, AXES, line_perm(move, reps))]
    pallas_call x6 -> x9, Pallas kernels: 22.1 us -> 25 us  [call(): pl.pallas_call(kernel, in_specs=specs, out_specs=VMEM_SPEC if single else...]
  transfers between devices with their start and end apart: 22 -> 24, of which waited for: 10 -> 12; matrix products, arithmetic and copies ran while one was open for 0% -> 0% of each run, Pallas kernels for 5% -> 20%
where the time goes in v4:
time: 132 us; the launch traced here: 130 us
  waiting for transfers between devices  63.2 us (48%)
  starting transfers between devices  34.3 us (26%)
  Pallas kernels  30.9 us (23%)
    ppermute x24, waiting for transfers between devices, send(): return lax.ppermute(value, AXES, line_perm(move, reps))  63.2 us
    ppermute x24, starting transfers between devices, send(): return lax.ppermute(value, AXES, line_perm(move, reps))  34.3 us
    pallas_call x9, Pallas kernels, call(): pl.pallas_call(kernel, in_specs=specs, out_specs=VMEM_SPEC if single else...  25 us
    pallas_call x1, Pallas kernels, chip_shards(): pl.pallas_call(rows_kernel, grid_spec=pltpu.PrefetchScalarGridSpec(num_sc...  5.83 us
  transfers between devices with their start and end apart: 24, of which 12 were waited for; matrix products, arithmetic and copies ran while one was open for 0% of the time, Pallas kernels for 20%

profile of v4, /device:TPU:9, one launch (start us, length us, event | category | flops | bytes accessed | tf_op | source)
XLA Modules:
  0.0 129.9 jit_solution(12803787316251767854)
XLA Ops:
  1.4 2.2 %shard_map.102 = (bf16[192,1024]{1,0:T(8,128)(2,1)S(1)}, bf16[192,1024]{1,0:T(8,128)(2,1)S(1)}, f32[2,96,1024]{2,1,0:T(8,128)S(1)}) custom-call(s32[6]{0:T(128)S(1)} %concatenate.6.place, bf16[2,96,1024]{2,1,0:T(8,128)(2,1)} %patch_hbm.1, bf16[2,96,1024]{2,1,0:T(8,128)(2,1)} %cot_hbm.1, s32[2,96]{1,0:T(2,128)} %index_hbm.1, f32[1,1024]{1,0:T(1,128)} %bitcast.6), custom_call_target="tpu_custom_call" | custom-call | flops 1000 | bytes 1000 | tf_op jit(solution)/shard_map/pallas_call | solution.py:605
  3.6 4.8 %collective-permute-start = (bf16[192,1024]{1,0:T(8,128)(2,1)S(1)}, bf16[192,1024]{1,0:T(8,128)(2,1)S(1)}, u32[]{:S(2)}, u32[]{:S(2)}) collective-permute-start(bf16[192,1024]{1,0:T(8,128)(2,1)S(1)} %get-tuple-element.31.m0), channel_id=1, source_target_pairs={{0,0},{1,8},{2,2},{3,10},{4,4},{5,12},{6,6},{7,14},{8,1},{9,9},{10... | collective-permute-start | bytes 1179656 | tf_op jit(solution)/shard_map/ppermute | solution.py:631
  8.4 13.0 %collective-permute-done.p0 = bf16[192,1024]{1,0:T(8,128)(2,1)S(1)} collective-permute-done((bf16[192,1024]{1,0:T(8,128)(2,1)S(1)}, bf16[192,1024]{1,0:T(8,128)(2,1)S(1)}, u32[]{:S(2)}, u32[]{:S(2)}) %collective-permute-start) | collective-permute-done | bytes 393248 | tf_op jit(solution)/shard_map/ppermute | solution.py:631
  21.5 4.2 %collective-permute-done.1.p1 = bf16[192,1024]{1,0:T(8,128)(2,1)S(1)} collective-permute-done((bf16[192,1024]{1,0:T(8,128)(2,1)S(1)}, bf16[192,1024]{1,0:T(8,128)(2,1)S(1)}, u32[]{:S(2)}, u32[]{:S(2)}) %collective-permute-start.1) | collective-permute-done | bytes 393248 | tf_op jit(solution)/shard_map/ppermute | solution.py:631
  25.8 1.3 collective-permute-start.5
  27.4 6.8 %shard_map.103 = (bf16[4,192,256]{2,1,0:T(8,128)(2,1)S(1)}, bf16[4,192,256]{2,1,0:T(8,128)(2,1)S(1)}, bf16[128,1152]{1,0:T(8,128)(2,1)S(1)}, f32[128,1024]{1,0:T(8,128)S(1)}, bf16[128,2176]{1,0:T(8,128)(2,1)S(1)}) custom-call(s32[6]{0:T(128)S(1)} %concatenate.6.place, bf16[192,1024]{1,0:T(8,128)(2,1)S(1)} %collective-permute-done.p0, ...), custom_call_target="tpu_custom_call" | custom-call | flops 1000 | bytes 1000 | tf_op jit(solution)/shard_map/pallas_call | solution.py:605
  34.2 1.3 collective-permute-start.7
  36.0 1.4 %collective-permute-start.9 = (bf16[192,1024]{1,0:T(8,128)(2,1)S(1)}, bf16[192,1024]{1,0:T(8,128)(2,1)S(1)}, u32[]{:S(2)}, u32[]{:S(2)}) collective-permute-start(bf16[192,1024]{1,0:T(8,128)(2,1)S(1)} %collective-permute-done.5.after.n0), channel_id=1, source_target_pairs={{0,1},{1,0},{2,3},{3,2},{4,5},{5,4},{6,7},{7,6},{8,9},{9,8},{10,11... | collective-permute-start | bytes 1179656 | tf_op jit(solution)/shard_map/ppermute | solution.py:631
  37.4 6.8 %shard_map.104 = (bf16[4,192,256]{2,1,0:T(8,128)(2,1)S(1)}, bf16[4,192,256]{2,1,0:T(8,128)(2,1)S(1)}, bf16[128,1152]{1,0:T(8,128)(2,1)S(1)}, f32[128,1024]{1,0:T(8,128)S(1)}, bf16[128,2176]{1,0:T(8,128)(2,1)S(1)}) custom-call(s32[6]{0:T(128)S(1)} %concatenate.6.place, bf16[192,1024]{1,0:T(8,128)(2,1)S(1)} %collective-permute-done.p0, ...), custom_call_target="tpu_custom_call" | custom-call | flops 1000 | bytes 1000 | tf_op jit(solution)/shard_map/pallas_call | solution.py:605
  44.2 1.3 collective-permute-start.8
  45.4 2.6 %collective-permute-done.7.got.got_a = bf16[128,2176]{1,0:T(8,128)(2,1)S(1)} collective-permute-done((bf16[128,2176]{1,0:T(8,128)(2,1)S(1)}, bf16[128,2176]{1,0:T(8,128)(2,1)S(1)}, u32[]{:S(2)}, u32[]{:S(2)}) %collective-permute-start.7) | collective-permute-done | bytes 557088 | tf_op jit(solution)/shard_map/ppermute | solution.py:631
  48.0 1.4 %shard_map.105 = (bf16[96,1024]{1,0:T(8,128)(2,1)S(1)}, bf16[96,1024]{1,0:T(8,128)(2,1)S(1)}, bf16[96,1024]{1,0:T(8,128)(2,1)S(1)}, bf16[96,1024]{1,0:T(8,128)(2,1)S(1)}) custom-call(s32[6]{0:T(128)S(1)} %concatenate.6.place, bf16[128,1152]{1,0:T(8,128)(2,1)S(1)} %get-tuple-element.37.keep.keep_a, f32[128,1024]{1,0:T(8,128)S(1)} %get-tuple-element.42.out_keep, ...), custom_call_target="tpu_custom_call" | custom-call | flops 1000 | bytes 1000 | tf_op jit(solution)/shard_map/pallas_call | solution.py:605
  49.5 2.2 %collective-permute-start.6 = (bf16[4,192,256]{2,1,0:T(8,128)(2,1)S(1)}, bf16[4,192,256]{2,1,0:T(8,128)(2,1)S(1)}, u32[]{:S(2)}, u32[]{:S(2)}) collective-permute-start(bf16[4,192,256]{2,1,0:T(8,128)(2,1)S(1)} %get-tuple-element.36), channel_id=1, source_target_pairs={{0,1},{1,0},{2,3},{3,2},{4,5},{5,4},{6,7},{7,6},{8,9},{9,8},{10,11... | collective-permute-start | bytes 1179656 | tf_op jit(solution)/shard_map/ppermute | solution.py:631
  51.7 3.5 %collective-permute-start.11 = (bf16[96,1024]{1,0:T(8,128)(2,1)S(1)}, bf16[96,1024]{1,0:T(8,128)(2,1)S(1)}, u32[]{:S(2)}, u32[]{:S(2)}) collective-permute-start(bf16[96,1024]{1,0:T(8,128)(2,1)S(1)} %get-tuple-element.45), channel_id=1, source_target_pairs={{0,8},{1,9},{2,10},{3,11},{4,12},{5,13},{6,14},{7,15},{8,0},{9,1},... | collective-permute-start | bytes 589832 | tf_op jit(solution)/shard_map/ppermute | solution.py:631
  55.2 2.6 %collective-permute-start.4 = (bf16[4,192,256]{2,1,0:T(8,128)(2,1)S(1)}, bf16[4,192,256]{2,1,0:T(8,128)(2,1)S(1)}, u32[]{:S(2)}, u32[]{:S(2)}) collective-permute-start(bf16[4,192,256]{2,1,0:T(8,128)(2,1)S(1)} %get-tuple-element.34), channel_id=1, source_target_pairs={{0,1},{1,0},{2,3},{3,2},{4,5},{5,4},{6,7},{7,6},{8,9},{9,8},{10,11... | collective-permute-start | bytes 1179656 | tf_op jit(solution)/shard_map/ppermute | solution.py:631
  57.8 10.1 %collective-permute-done.11.a2 = bf16[96,1024]{1,0:T(8,128)(2,1)S(1)} collective-permute-done((bf16[96,1024]{1,0:T(8,128)(2,1)S(1)}, bf16[96,1024]{1,0:T(8,128)(2,1)S(1)}, u32[]{:S(2)}, u32[]{:S(2)}) %collective-permute-start.11) | collective-permute-done | bytes 196640 | tf_op jit(solution)/shard_map/ppermute | solution.py:631
  68.0 4.3 %collective-permute-done.12.a3 = bf16[96,1024]{1,0:T(8,128)(2,1)S(1)} collective-permute-done((bf16[96,1024]{1,0:T(8,128)(2,1)S(1)}, bf16[96,1024]{1,0:T(8,128)(2,1)S(1)}, u32[]{:S(2)}, u32[]{:S(2)}) %collective-permute-start.12) | collective-permute-done | bytes 196640 | tf_op jit(solution)/shard_map/ppermute | solution.py:631
  72.4 2.0 %shard_map.107 = (bf16[160,1024]{1,0:T(8,128)(2,1)S(1)}, bf16[160,1024]{1,0:T(8,128)(2,1)S(1)}, bf16[160,1024]{1,0:T(8,128)(2,1)S(1)}, bf16[160,1024]{1,0:T(8,128)(2,1)S(1)}) custom-call(s32[6]{0:T(128)S(1)} %concatenate.6.place, bf16[128,1152]{1,0:T(8,128)(2,1)S(1)} %get-tuple-element.37.keep.keep_a, ...), custom_call_target="tpu_custom_call" | custom-call | flops 1000 | bytes 1000 | tf_op jit(solution)/shard_map/pallas_call | solution.py:605
  74.5 3.3 %collective-permute-start.19 = (bf16[160,1024]{1,0:T(8,128)(2,1)S(1)}, bf16[160,1024]{1,0:T(8,128)(2,1)S(1)}, u32[]{:S(2)}, u32[]{:S(2)}) collective-permute-start(bf16[160,1024]{1,0:T(8,128)(2,1)S(1)} %get-tuple-element.54), channel_id=1, source_target_pairs={{0,8},{1,9},{2,10},{3,11},{4,12},{5,13},{6,14},{7,15},{8,0},{9,1},... | collective-permute-start | bytes 983048 | tf_op jit(solution)/shard_map/ppermute | solution.py:631
  77.7 1.2 collective-permute-start.13
  78.9 4.0 %collective-permute-done.13.before.a1 = bf16[96,1024]{1,0:T(8,128)(2,1)S(1)} collective-permute-done((bf16[96,1024]{1,0:T(8,128)(2,1)S(1)}, bf16[96,1024]{1,0:T(8,128)(2,1)S(1)}, u32[]{:S(2)}, u32[]{:S(2)}) %collective-permute-start.13) | collective-permute-done | bytes 196640 | tf_op jit(solution)/shard_map/ppermute | solution.py:631
  82.9 5.8 %shard_map.108 = (bf16[192,1024]{1,0:T(8,128)(2,1)S(1)}, bf16[192,1024]{1,0:T(8,128)(2,1)S(1)}) custom-call(s32[6]{0:T(128)S(1)} %concatenate.6.place, bf16[4,192,256]{2,1,0:T(8,128)(2,1)S(1)} %get-tuple-element.33.own_a, bf16[4,192,256]{2,1,0:T(8,128)(2,1)S(1)} %collective-permute-done.4.got_a, bf16[4,192,256]{2,1,0:T(8,128)(2,1)S(1)} %get-tuple-element.35.own_b, ...), custom_call_target="tpu_custom_call" | custom-call | flops 1000 | bytes 1000 | tf_op jit(solution)/shard_map/pallas_call | solution.py:736
  88.8 9.0 %collective-permute-done.19.a2 = bf16[160,1024]{1,0:T(8,128)(2,1)S(1)} collective-permute-done((bf16[160,1024]{1,0:T(8,128)(2,1)S(1)}, bf16[160,1024]{1,0:T(8,128)(2,1)S(1)}, u32[]{:S(2)}, u32[]{:S(2)}) %collective-permute-start.19) | collective-permute-done | bytes 327712 | tf_op jit(solution)/shard_map/ppermute | solution.py:631
  97.8 7.2 %collective-permute-done.20.a3 = bf16[160,1024]{1,0:T(8,128)(2,1)S(1)} collective-permute-done((bf16[160,1024]{1,0:T(8,128)(2,1)S(1)}, bf16[160,1024]{1,0:T(8,128)(2,1)S(1)}, u32[]{:S(2)}, u32[]{:S(2)}) %collective-permute-start.20) | collective-permute-done | bytes 327712 | tf_op jit(solution)/shard_map/ppermute | solution.py:631
  105.2 1.2 collective-permute-start.21
  106.4 4.2 %collective-permute-start.15 = (bf16[192,1024]{1,0:T(8,128)(2,1)S(1)}, bf16[192,1024]{1,0:T(8,128)(2,1)S(1)}, u32[]{:S(2)}, u32[]{:S(2)}) collective-permute-start(bf16[192,1024]{1,0:T(8,128)(2,1)S(1)} %get-tuple-element.49), channel_id=1, source_target_pairs={{0,4},{1,12},{2,6},{3,14},{4,0},{5,8},{6,2},{7,10},{8,5},{9,13},{1... | collective-permute-start | bytes 1179656 | tf_op jit(solution)/shard_map/ppermute | solution.py:631
  110.6 1.9 %collective-permute-start.14 = (bf16[192,1024]{1,0:T(8,128)(2,1)S(1)}, bf16[192,1024]{1,0:T(8,128)(2,1)S(1)}, u32[]{:S(2)}, u32[]{:S(2)}) collective-permute-start(bf16[192,1024]{1,0:T(8,128)(2,1)S(1)} %get-tuple-element.48.refs_0_), channel_id=1, source_target_pairs={{0,0},{1,8},{2,2},{3,10},{4,4},{5,12},{6,6},{7,14},{8,1},{9,9},{10... | collective-permute-start | bytes 1179656 | tf_op jit(solution)/shard_map/ppermute | solution.py:631
  112.6 2.8 %collective-permute-start.23 = (bf16[160,1024]{1,0:T(8,128)(2,1)S(1)}, bf16[160,1024]{1,0:T(8,128)(2,1)S(1)}, u32[]{:S(2)}, u32[]{:S(2)}) collective-permute-start(bf16[160,1024]{1,0:T(8,128)(2,1)S(1)} %collective-permute-done.21.b1), channel_id=1, source_target_pairs={{0,1},{1,0},{2,3},{3,2},{4,5},{5,4},{6,7},{7,6},{8,9},{9,8},{10,11... | collective-permute-start | bytes 983048 | tf_op jit(solution)/shard_map/ppermute | solution.py:631
  115.4 2.3 %collective-permute-done.15.r1 = bf16[192,1024]{1,0:T(8,128)(2,1)S(1)} collective-permute-done((bf16[192,1024]{1,0:T(8,128)(2,1)S(1)}, bf16[192,1024]{1,0:T(8,128)(2,1)S(1)}, u32[]{:S(2)}, u32[]{:S(2)}) %collective-permute-start.15) | collective-permute-done | bytes 393248 | tf_op jit(solution)/shard_map/ppermute | solution.py:631
  118.8 5.5 %collective-permute-done.14.r0 = bf16[192,1024]{1,0:T(8,128)(2,1)S(1)} collective-permute-done((bf16[192,1024]{1,0:T(8,128)(2,1)S(1)}, bf16[192,1024]{1,0:T(8,128)(2,1)S(1)}, u32[]{:S(2)}, u32[]{:S(2)}) %collective-permute-start.14) | collective-permute-done | bytes 393248 | tf_op jit(solution)/shard_map/ppermute | solution.py:631
  124.3 2.6 %shard_map.109 = (bf16[2,96,1024]{2,1,0:T(8,128)(2,1)}, bf16[2,96,1024]{2,1,0:T(8,128)(2,1)}) custom-call(s32[6]{0:T(128)S(1)} %concatenate.6.place, bf16[192,1024]{1,0:T(8,128)(2,1)S(1)} %collective-permute-done.14.r0, bf16[192,1024]{1,0:T(8,128)(2,1)S(1)} %collective-permute-done.15.r1, bf16[1024,1024]{1,0:T(8,128)(2,1)S(1)} %copy-done, ...), custom_call_target="tpu_custom_call" | custom-call | flops 1000 | bytes 1000 | tf_op jit(solution)/shard_map/pallas_call | solution.py:605
  126.9 3.0 %shard_map.111 = (f32[1024,768]{1,0:T(8,128)}, f32[1024,256]{1,0:T(8,128)}) custom-call(s32[6]{0:T(128)S(1)} %concatenate.6.place, bf16[96,1024]{1,0:T(8,128)(2,1)S(1)} %shard_map.106.after.a0, bf16[96,1024]{1,0:T(8,128)(2,1)S(1)} %collective-permute-done.13.before.a1, bf16[96,1024]{1,0:T(8,128)(2,1)S(1)} %collective-permute-done.16.a2, ...), custom_call_target="tpu_custom_call" | custom-call | flops 1000 | bytes 1000 | tf_op jit(solution)/shard_map/pallas_call | solution.py:605
  (34 shorter events, 3.4 us)
Async XLA Ops:
  3.6 17.9 %collective-permute-start = (bf16[192,1024]{1,0:T(8,128)(2,1)S(1)}, bf16[192,1024]{1,0:T(8,128)(2,1)S(1)}, u32[]{:S(2)}, u32[]{:S(2)}) collective-permute-start(bf16[192,1024]{1,0:T(8,128)(2,1)S(1)} %get-tuple-element.31.m0), channel_id=1, source_target_pairs={{0,0},{1,8},{2,2},{3,10},{4,4},{5,12},{6,6},{7,14},{8,1},{9,9},{10... | collective-permute-start | bytes 1179656 | tf_op jit(solution)/shard_map/ppermute | solution.py:631
  8.4 17.3 %collective-permute-start.1 = (bf16[192,1024]{1,0:T(8,128)(2,1)S(1)}, bf16[192,1024]{1,0:T(8,128)(2,1)S(1)}, u32[]{:S(2)}, u32[]{:S(2)}) collective-permute-start(bf16[192,1024]{1,0:T(8,128)(2,1)S(1)} %get-tuple-element.32.m1), channel_id=1, source_target_pairs={{0,4},{1,12},{2,6},{3,14},{4,0},{5,8},{6,2},{7,10},{8,5},{9,13},{1... | collective-permute-start | bytes 1179656 | tf_op jit(solution)/shard_map/ppermute | solution.py:631
  21.5 5.6 %collective-permute-start.2 = (bf16[192,1024]{1,0:T(8,128)(2,1)S(1)}, bf16[192,1024]{1,0:T(8,128)(2,1)S(1)}, u32[]{:S(2)}, u32[]{:S(2)}) collective-permute-start(bf16[192,1024]{1,0:T(8,128)(2,1)S(1)} %collective-permute-done.p0), channel_id=1, source_target_pairs={{0,1},{1,0},{2,3},{3,2},{4,5},{5,4},{6,7},{7,6},{8,9},{9,8},{10,11... | collective-permute-start | bytes 1179656 | tf_op jit(solution)/shard_map/ppermute | solution.py:631
  25.7 1.7 %collective-permute-start.3 = (bf16[192,1024]{1,0:T(8,128)(2,1)S(1)}, bf16[192,1024]{1,0:T(8,128)(2,1)S(1)}, u32[]{:S(2)}, u32[]{:S(2)}) collective-permute-start(bf16[192,1024]{1,0:T(8,128)(2,1)S(1)} %collective-permute-done.1.p1), channel_id=1, source_target_pairs={{0,1},{1,0},{2,3},{3,2},{4,5},{5,4},{6,7},{7,6},{8,9},{9,8},{10,11... | collective-permute-start | bytes 1179656 | tf_op jit(solution)/shard_map/ppermute | solution.py:631
  25.8 10.2 %collective-permute-start.5 = (bf16[192,1024]{1,0:T(8,128)(2,1)S(1)}, bf16[192,1024]{1,0:T(8,128)(2,1)S(1)}, u32[]{:S(2)}, u32[]{:S(2)}) collective-permute-start(bf16[192,1024]{1,0:T(8,128)(2,1)S(1)} %pad_maximum_fusion), channel_id=1, source_target_pairs={{0,2},{1,3},{2,0},{3,1},{4,6},{5,7},{6,4},{7,5},{8,10},{9,11},{10,... | collective-permute-start | bytes 1179656 | tf_op jit(solution)/shard_map/ppermute | solution.py:631
  34.2 13.8 %collective-permute-start.7 = (bf16[128,2176]{1,0:T(8,128)(2,1)S(1)}, bf16[128,2176]{1,0:T(8,128)(2,1)S(1)}, u32[]{:S(2)}, u32[]{:S(2)}) collective-permute-start(bf16[128,2176]{1,0:T(8,128)(2,1)S(1)} %get-tuple-element.38), channel_id=1, source_target_pairs={{0,2},{1,3},{2,0},{3,1},{4,6},{5,7},{6,4},{7,5},{8,10},{9,11},{10,... | collective-permute-start | bytes 1671176 | tf_op jit(solution)/shard_map/ppermute | solution.py:631
  36.0 9.4 %collective-permute-start.9 = (bf16[192,1024]{1,0:T(8,128)(2,1)S(1)}, bf16[192,1024]{1,0:T(8,128)(2,1)S(1)}, u32[]{:S(2)}, u32[]{:S(2)}) collective-permute-start(bf16[192,1024]{1,0:T(8,128)(2,1)S(1)} %collective-permute-done.5.after.n0), channel_id=1, source_target_pairs={{0,1},{1,0},{2,3},{3,2},{4,5},{5,4},{6,7},{7,6},{8,9},{9,8},{10,11... | collective-permute-start | bytes 1179656 | tf_op jit(solution)/shard_map/ppermute | solution.py:631
  44.2 28.2 %collective-permute-start.8 = (bf16[128,2176]{1,0:T(8,128)(2,1)S(1)}, bf16[128,2176]{1,0:T(8,128)(2,1)S(1)}, u32[]{:S(2)}, u32[]{:S(2)}) collective-permute-start(bf16[128,2176]{1,0:T(8,128)(2,1)S(1)} %get-tuple-element.41), channel_id=1, source_target_pairs={{0,2},{1,3},{2,0},{3,1},{4,6},{5,7},{6,4},{7,5},{8,10},{9,11},{10,... | collective-permute-start | bytes 1671176 | tf_op jit(solution)/shard_map/ppermute | solution.py:631
  49.4 5.8 %collective-permute-start.10 = (bf16[96,1024]{1,0:T(8,128)(2,1)S(1)}, bf16[96,1024]{1,0:T(8,128)(2,1)S(1)}, u32[]{:S(2)}, u32[]{:S(2)}) collective-permute-start(bf16[96,1024]{1,0:T(8,128)(2,1)S(1)} %get-tuple-element.44), channel_id=1, source_target_pairs={{0,4},{1,5},{2,6},{3,7},{4,0},{5,1},{6,2},{7,3},{8,12},{9,13},{10,... | collective-permute-start | bytes 589832 | tf_op jit(solution)/shard_map/ppermute | solution.py:631
  49.5 28.2 %collective-permute-start.6 = (bf16[4,192,256]{2,1,0:T(8,128)(2,1)S(1)}, bf16[4,192,256]{2,1,0:T(8,128)(2,1)S(1)}, u32[]{:S(2)}, u32[]{:S(2)}) collective-permute-start(bf16[4,192,256]{2,1,0:T(8,128)(2,1)S(1)} %get-tuple-element.36), channel_id=1, source_target_pairs={{0,1},{1,0},{2,3},{3,2},{4,5},{5,4},{6,7},{7,6},{8,9},{9,8},{10,11... | collective-permute-start | bytes 1179656 | tf_op jit(solution)/shard_map/ppermute | solution.py:631
  51.7 16.2 %collective-permute-start.11 = (bf16[96,1024]{1,0:T(8,128)(2,1)S(1)}, bf16[96,1024]{1,0:T(8,128)(2,1)S(1)}, u32[]{:S(2)}, u32[]{:S(2)}) collective-permute-start(bf16[96,1024]{1,0:T(8,128)(2,1)S(1)} %get-tuple-element.45), channel_id=1, source_target_pairs={{0,8},{1,9},{2,10},{3,11},{4,12},{5,13},{6,14},{7,15},{8,0},{9,1},... | collective-permute-start | bytes 589832 | tf_op jit(solution)/shard_map/ppermute | solution.py:631
  55.2 17.0 %collective-permute-start.12 = (bf16[96,1024]{1,0:T(8,128)(2,1)S(1)}, bf16[96,1024]{1,0:T(8,128)(2,1)S(1)}, u32[]{:S(2)}, u32[]{:S(2)}) collective-permute-start(bf16[96,1024]{1,0:T(8,128)(2,1)S(1)} %get-tuple-element.46), channel_id=1, source_target_pairs={{0,12},{1,13},{2,14},{3,15},{4,8},{5,9},{6,10},{7,11},{8,4},{9,5},... | collective-permute-start | bytes 589832 | tf_op jit(solution)/shard_map/ppermute | solution.py:631
  55.2 23.7 %collective-permute-start.4 = (bf16[4,192,256]{2,1,0:T(8,128)(2,1)S(1)}, bf16[4,192,256]{2,1,0:T(8,128)(2,1)S(1)}, u32[]{:S(2)}, u32[]{:S(2)}) collective-permute-start(bf16[4,192,256]{2,1,0:T(8,128)(2,1)S(1)} %get-tuple-element.34), channel_id=1, source_target_pairs={{0,1},{1,0},{2,3},{3,2},{4,5},{5,4},{6,7},{7,6},{8,9},{9,8},{10,11... | collective-permute-start | bytes 1179656 | tf_op jit(solution)/shard_map/ppermute | solution.py:631
  74.4 14.4 %collective-permute-start.18 = (bf16[160,1024]{1,0:T(8,128)(2,1)S(1)}, bf16[160,1024]{1,0:T(8,128)(2,1)S(1)}, u32[]{:S(2)}, u32[]{:S(2)}) collective-permute-start(bf16[160,1024]{1,0:T(8,128)(2,1)S(1)} %get-tuple-element.53), channel_id=1, source_target_pairs={{0,4},{1,5},{2,6},{3,7},{4,0},{5,1},{6,2},{7,3},{8,12},{9,13},{10,... | collective-permute-start | bytes 983048 | tf_op jit(solution)/shard_map/ppermute | solution.py:631
  74.5 23.4 %collective-permute-start.19 = (bf16[160,1024]{1,0:T(8,128)(2,1)S(1)}, bf16[160,1024]{1,0:T(8,128)(2,1)S(1)}, u32[]{:S(2)}, u32[]{:S(2)}) collective-permute-start(bf16[160,1024]{1,0:T(8,128)(2,1)S(1)} %get-tuple-element.54), channel_id=1, source_target_pairs={{0,8},{1,9},{2,10},{3,11},{4,12},{5,13},{6,14},{7,15},{8,0},{9,1},... | collective-permute-start | bytes 983048 | tf_op jit(solution)/shard_map/ppermute | solution.py:631
  77.7 27.3 %collective-permute-start.20 = (bf16[160,1024]{1,0:T(8,128)(2,1)S(1)}, bf16[160,1024]{1,0:T(8,128)(2,1)S(1)}, u32[]{:S(2)}, u32[]{:S(2)}) collective-permute-start(bf16[160,1024]{1,0:T(8,128)(2,1)S(1)} %get-tuple-element.55), channel_id=1, source_target_pairs={{0,12},{1,13},{2,14},{3,15},{4,8},{5,9},{6,10},{7,11},{8,4},{9,5},... | collective-permute-start | bytes 983048 | tf_op jit(solution)/shard_map/ppermute | solution.py:631
  77.7 5.2 %collective-permute-start.13 = (bf16[96,1024]{1,0:T(8,128)(2,1)S(1)}, bf16[96,1024]{1,0:T(8,128)(2,1)S(1)}, u32[]{:S(2)}, u32[]{:S(2)}) collective-permute-start(bf16[96,1024]{1,0:T(8,128)(2,1)S(1)} %shard_map.106.after.a0), channel_id=1, source_target_pairs={{0,2},{1,3},{2,0},{3,1},{4,6},{5,7},{6,4},{7,5},{8,10},{9,11},{10,... | collective-permute-start | bytes 589832 | tf_op jit(solution)/shard_map/ppermute | solution.py:631
  82.9 41.3 %copy-start = (bf16[1024,1024]{1,0:T(8,128)(2,1)S(1)}, bf16[1024,1024]{1,0:T(8,128)(2,1)}, u32[]{:S(2)}) copy-start(bf16[1024,1024]{1,0:T(8,128)(2,1)} %w_ref.3) | copy-start | bytes 6291460
  82.9 41.3 %copy-start.1 = (f32[1024]{0:T(1024)S(1)}, f32[1024]{0:T(1024)}, u32[]{:S(2)}) copy-start(f32[1024]{0:T(1024)} %param.13) | copy-start | bytes 12292
  105.2 7.4 %collective-permute-start.21 = (bf16[160,1024]{1,0:T(8,128)(2,1)S(1)}, bf16[160,1024]{1,0:T(8,128)(2,1)S(1)}, u32[]{:S(2)}, u32[]{:S(2)}) collective-permute-start(bf16[160,1024]{1,0:T(8,128)(2,1)S(1)} %shard_map.110.b0), channel_id=1, source_target_pairs={{0,2},{1,3},{2,0},{3,1},{4,6},{5,7},{6,4},{7,5},{8,10},{9,11},{10,... | collective-permute-start | bytes 983048 | tf_op jit(solution)/shard_map/ppermute | solution.py:631
  106.4 11.3 %collective-permute-start.15 = (bf16[192,1024]{1,0:T(8,128)(2,1)S(1)}, bf16[192,1024]{1,0:T(8,128)(2,1)S(1)}, u32[]{:S(2)}, u32[]{:S(2)}) collective-permute-start(bf16[192,1024]{1,0:T(8,128)(2,1)S(1)} %get-tuple-element.49), channel_id=1, source_target_pairs={{0,4},{1,12},{2,6},{3,14},{4,0},{5,8},{6,2},{7,10},{8,5},{9,13},{1... | collective-permute-start | bytes 1179656 | tf_op jit(solution)/shard_map/ppermute | solution.py:631
  110.6 13.7 %collective-permute-start.14 = (bf16[192,1024]{1,0:T(8,128)(2,1)S(1)}, bf16[192,1024]{1,0:T(8,128)(2,1)S(1)}, u32[]{:S(2)}, u32[]{:S(2)}) collective-permute-start(bf16[192,1024]{1,0:T(8,128)(2,1)S(1)} %get-tuple-element.48.refs_0_), channel_id=1, source_target_pairs={{0,0},{1,8},{2,2},{3,10},{4,4},{5,12},{6,6},{7,14},{8,1},{9,9},{10... | collective-permute-start | bytes 1179656 | tf_op jit(solution)/shard_map/ppermute | solution.py:631
  112.5 14.4 %collective-permute-start.22 = (bf16[160,1024]{1,0:T(8,128)(2,1)S(1)}, bf16[160,1024]{1,0:T(8,128)(2,1)S(1)}, u32[]{:S(2)}, u32[]{:S(2)}) collective-permute-start(bf16[160,1024]{1,0:T(8,128)(2,1)S(1)} %shard_map.110.b0), channel_id=1, source_target_pairs={{0,1},{1,0},{2,3},{3,2},{4,5},{5,4},{6,7},{7,6},{8,9},{9,8},{10,11... | collective-permute-start | bytes 983048 | tf_op jit(solution)/shard_map/ppermute | solution.py:631
  112.6 14.3 %collective-permute-start.23 = (bf16[160,1024]{1,0:T(8,128)(2,1)S(1)}, bf16[160,1024]{1,0:T(8,128)(2,1)S(1)}, u32[]{:S(2)}, u32[]{:S(2)}) collective-permute-start(bf16[160,1024]{1,0:T(8,128)(2,1)S(1)} %collective-permute-done.21.b1), channel_id=1, source_target_pairs={{0,1},{1,0},{2,3},{3,2},{4,5},{5,4},{6,7},{7,6},{8,9},{9,8},{10,11... | collective-permute-start | bytes 983048 | tf_op jit(solution)/shard_map/ppermute | solution.py:631
  115.4 11.5 %collective-permute-start.16 = (bf16[96,1024]{1,0:T(8,128)(2,1)S(1)}, bf16[96,1024]{1,0:T(8,128)(2,1)S(1)}, u32[]{:S(2)}, u32[]{:S(2)}) collective-permute-start(bf16[96,1024]{1,0:T(8,128)(2,1)S(1)} %shard_map.106.after.a0), channel_id=1, source_target_pairs={{0,1},{1,0},{2,3},{3,2},{4,5},{5,4},{6,7},{7,6},{8,9},{9,8},{10,11... | collective-permute-start | bytes 589832 | tf_op jit(solution)/shard_map/ppermute | solution.py:631
  117.6 9.2 %collective-permute-start.17 = (bf16[96,1024]{1,0:T(8,128)(2,1)S(1)}, bf16[96,1024]{1,0:T(8,128)(2,1)S(1)}, u32[]{:S(2)}, u32[]{:S(2)}) collective-permute-start(bf16[96,1024]{1,0:T(8,128)(2,1)S(1)} %collective-permute-done.13.before.a1), channel_id=1, source_target_pairs={{0,1},{1,0},{2,3},{3,2},{4,5},{5,4},{6,7},{7,6},{8,9},{9,8},{10,11... | collective-permute-start | bytes 589832 | tf_op jit(solution)/shard_map/ppermute | solution.py:631

commit v5 on v4

--- a/solution.py
+++ b/solution.py
@@ -484,16 +484,19 @@
         d_patches[s] = jnp.where(live, value, 0.0).astype(d_patches.dtype)
 
 
-def put_out_part(place, out_keep, got, outs, total):
-    total[...] = out_keep[...] + got[:, got.shape[1] - total.shape[1] :].astype(jnp.float32)
-    columns = total.shape[1] // 4
-    tall = total.shape[0] // 4
-    for k, out in enumerate(outs):
+def put_parts(place, total, out_keep, got, keep, send, out_total):
+    out_total[...] = out_keep[...] + got[:, got.shape[1] - out_total.shape[1] :].astype(jnp.float32)
+    columns = out_total.shape[1] // 4
+    tall = out_total.shape[0] // 4
+    count = total.shape[0] // 4
+    for k in range(4):
+        ref, spot = (keep, send)[k % 2], k // 2
+        at = pl.multiple_of((place[LINE] ^ k) * count, 64)
+        ref[spot, :count, :] = total[pl.ds(at, count), :].astype(ref.dtype)
         at = pl.multiple_of((place[LINE] ^ k) * columns, 128)
-        value = total[:, pl.ds(at, columns)].astype(out.dtype)
-        base = out.shape[0] - tall
+        value = out_total[:, pl.ds(at, columns)].astype(ref.dtype)
         for j in range(4):
-            out[base:, columns * j : columns * j + columns] = value[tall * j : tall * j + tall, :]
+            ref[spot, count:, columns * j : columns * j + columns] = value[tall * j : tall * j + tall, :]
 
 
 def piece_of(ref, at, rows):
@@ -503,7 +506,7 @@
 
 def weight_first(
     place, keep, out_keep, got, p0, p1, p2, p3, n0, n1,
-    o0, o1, o2, o3, tokens, left, total, out_total,
+    part_keep, part_send, tokens, left, total, out_total,
 ):
     block = p0.shape[0] // 2
     rows = 4 * block
@@ -515,15 +518,12 @@
         for i, at in enumerate((0, 2, 4, 5)):
             left[side, 64 * i : 64 * i + 64, :] = piece_of(ref, at, rows)
     total[...] = dot_nn(left[0], tokens[:rows, :]) + dot_nn(left[1], tokens[rows:, :])
-    for k, out in enumerate((o0, o1, o2, o3)):
-        at = pl.multiple_of((place[LINE] ^ k) * 64, 64)
-        out[:64, :] = total[pl.ds(at, 64), :].astype(out.dtype)
-    put_out_part(place, out_keep, got, (o0, o1, o2, o3), out_total)
+    put_parts(place, total, out_keep, got, part_keep, part_send, out_total)
 
 
 def weight_second(
     place, keep_a, got_a, keep_b, out_keep, got_b, p0, p1, p2, p3, n0, n1, after,
-    o0, o1, o2, o3, tokens, left, total, out_total,
+    part_keep, part_send, tokens, left, total, out_total,
 ):
     del after
     block = p0.shape[0] // 2
@@ -538,17 +538,17 @@
         ):
             left[side, 64 * i : 64 * i + 64, :] = piece_of(ref, at, rows)
     total[...] = dot_nn(left[0], tokens[:rows, :]) + dot_nn(left[1], tokens[rows:, :])
-    for k, out in enumerate((o0, o1, o2, o3)):
-        at = pl.multiple_of((place[LINE] ^ k) * 128, 128)
-        out[:128, :] = total[pl.ds(at, 128), :].astype(out.dtype)
-    put_out_part(place, out_keep, got_b, (o0, o1, o2, o3), out_total)
-
-
-def sum_kernel(a0, a1, a2, a3, *refs):
+    put_parts(place, total, out_keep, got_b, part_keep, part_send, out_total)
+
+
+def pair_kernel(keep, got, mine, send):
+    mine[...] = keep[0] + got[0].astype(jnp.float32)
+    send[...] = (keep[1] + got[1].astype(jnp.float32)).astype(send.dtype)
+
+
+def sum_kernel(mine, got, *refs):
     out = refs[-1]
-    f32 = jnp.float32
-    value = (a0[...].astype(f32) + a1[...].astype(f32)) + (a2[...].astype(f32) + a3[...].astype(f32))
-    out[...] = value.astype(out.dtype)
+    out[...] = (mine[...] + got[...].astype(jnp.float32)).astype(out.dtype)
 
 
 def finish_kernel(place, a0, a1, a2, a3, b0, b1, b2, b3, wide, narrow):
@@ -696,43 +696,50 @@
     got_b = to_x(send_b)
     core_b = to_core(oth_b)
 
-    def exchange(kernel, args, tall, scratch, after=()):
-        outs = call(
+    def parts_of(kernel, args, tall, scratch, after=()):
+        return call(
             kernel,
             (*args, *here, *there, *after),
-            [struct((tall, width))] * 4,
+            [struct((2, tall, width), f32), struct((2, tall, width))],
             16,
             place,
             scratch=[pltpu.VMEM((2 * rows, width), bf16)] + scratch + [pltpu.VMEM(out_half, f32)],
             specs=[VMEM_SPEC] * (len(args) + 6) + [any_spec] * len(after),
         )
-        return [outs[0]] + [along(outs[k], k) for k in range(1, 4)]
-
-    def spread(parts, after=()):
+
+    def pair_sums(keep, part):
+        shape = keep.shape[1:]
+        mine, part = call(pair_kernel, (keep, along(part, 1)), [struct(shape, f32), struct(shape)], 8)
+        return mine, part, along(part, 2)
+
+    def spread(mine, part, after=()):
         sums = call(
             sum_kernel,
-            (*parts, *after),
-            struct(parts[0].shape),
+            (mine, part, *after),
+            struct(part.shape),
             8,
-            specs=[VMEM_SPEC] * 4 + [any_spec] * len(after),
+            specs=[VMEM_SPEC] * 2 + [any_spec] * len(after),
         )
         by_x = to_x(sums)
         return (sums, by_x, to_core(sums), to_core(by_x))
 
-    parts = exchange(
+    keep, part = parts_of(
         weight_first,
         (keep_a, out_keep_a, got_a),
         96,
         [pltpu.VMEM((2, 256, rows), bf16), pltpu.VMEM((256, width), f32)],
     )
-    first = spread(parts)
-    parts = exchange(
+    first_sum, paired, first_got = pair_sums(keep, part)
+    keep, part = parts_of(
         weight_second,
         (keep_a, got_a, keep_b, out_keep_b, got_b),
         160,
         [pltpu.VMEM((2, 512, rows), bf16), pltpu.VMEM((512, width), f32)],
-        (first[0],),
-    )
+        (paired,),
+    )
+    started = part
+    second_sum, _, second_got = pair_sums(keep, part)
+    first = spread(first_sum, first_got)
     back = pl.pallas_call(
         rows_kernel,
         grid_spec=pltpu.PrefetchScalarGridSpec(
@@ -746,8 +753,8 @@
         out_shape=[pay] * 2,
         compiler_params=pltpu.CompilerParams(vmem_limit_bytes=20 * MIB),
         cost_estimate=COST,
-    )(place, own_a, core_a, own_b, core_b, in_hbm(w_qkv), parts[0], first[1])
-    second = spread(parts, (back[0],))
+    )(place, own_a, core_a, own_b, core_b, in_hbm(w_qkv), started, first[1])
+    second = spread(second_sum, second_got, (back[0],))
     back = [to_rows(back[k], k, 0) for k in range(2)]
     encoded, d_patches = call(
         return_kernel,

time: 132 us -> 128 us (0.970)
  the two profiles are of different devices: /device:TPU:9 before, /device:TPU:1 now
where the time goes in v5:
time: 128 us; the launch traced here: 127 us
  waiting for transfers between devices  59.5 us (46%)
  starting transfers between devices  35.3 us (28%)
  Pallas kernels  30.9 us (24%)
    ppermute x22, waiting for transfers between devices, send(): return lax.ppermute(value, AXES, line_perm(move, reps))  59.5 us
    ppermute x22, starting transfers between devices, send(): return lax.ppermute(value, AXES, line_perm(move, reps))  35.3 us
    pallas_call x11, Pallas kernels, call(): pl.pallas_call(kernel, in_specs=specs, out_specs=VMEM_SPEC if single else...  25.1 us
    pallas_call x1, Pallas kernels, chip_shards(): pl.pallas_call(rows_kernel, grid_spec=pltpu.PrefetchScalarGridSpec(num_sc...  5.82 us
  transfers between devices with their start and end apart: 22, of which 11 were waited for; matrix products, arithmetic and copies ran while one was open for 0% of the time, Pallas kernels for 19%

profile of v5, /device:TPU:1, one launch (start us, length us, event | category | flops | bytes accessed | tf_op | source)
XLA Modules:
  0.0 127.4 jit_solution(14730073331106856459)
XLA Ops:
  1.4 2.2 %shard_map.102 = (bf16[192,1024]{1,0:T(8,128)(2,1)S(1)}, bf16[192,1024]{1,0:T(8,128)(2,1)S(1)}, f32[2,96,1024]{2,1,0:T(8,128)S(1)}) custom-call(s32[6]{0:T(128)S(1)} %concatenate.6.place, bf16[2,96,1024]{2,1,0:T(8,128)(2,1)} %patch_hbm.1, bf16[2,96,1024]{2,1,0:T(8,128)(2,1)} %cot_hbm.1, s32[2,96]{1,0:T(2,128)} %index_hbm.1, f32[1,1024]{1,0:T(1,128)} %bitcast.6), custom_call_target="tpu_custom_call" | custom-call | flops 1000 | bytes 1000 | tf_op jit(solution)/shard_map/pallas_call | solution.py:605
  3.6 5.6 %collective-permute-start = (bf16[192,1024]{1,0:T(8,128)(2,1)S(1)}, bf16[192,1024]{1,0:T(8,128)(2,1)S(1)}, u32[]{:S(2)}, u32[]{:S(2)}) collective-permute-start(bf16[192,1024]{1,0:T(8,128)(2,1)S(1)} %get-tuple-element.31.m0), channel_id=1, source_target_pairs={{0,0},{1,8},{2,2},{3,10},{4,4},{5,12},{6,6},{7,14},{8,1},{9,9},{10... | collective-permute-start | bytes 1179656 | tf_op jit(solution)/shard_map/ppermute | solution.py:631
  10.3 12.8 %collective-permute-done.p0 = bf16[192,1024]{1,0:T(8,128)(2,1)S(1)} collective-permute-done((bf16[192,1024]{1,0:T(8,128)(2,1)S(1)}, bf16[192,1024]{1,0:T(8,128)(2,1)S(1)}, u32[]{:S(2)}, u32[]{:S(2)}) %collective-permute-start) | collective-permute-done | bytes 393248 | tf_op jit(solution)/shard_map/ppermute | solution.py:631
  23.7 1.3 %collective-permute-start.5 = (bf16[192,1024]{1,0:T(8,128)(2,1)S(1)}, bf16[192,1024]{1,0:T(8,128)(2,1)S(1)}, u32[]{:S(2)}, u32[]{:S(2)}) collective-permute-start(bf16[192,1024]{1,0:T(8,128)(2,1)S(1)} %pad_maximum_fusion), channel_id=1, source_target_pairs={{0,2},{1,3},{2,0},{3,1},{4,6},{5,7},{6,4},{7,5},{8,10},{9,11},{10,... | collective-permute-start | bytes 1179656 | tf_op jit(solution)/shard_map/ppermute | solution.py:631
  25.4 6.8 %shard_map.103 = (bf16[4,192,256]{2,1,0:T(8,128)(2,1)S(1)}, bf16[4,192,256]{2,1,0:T(8,128)(2,1)S(1)}, bf16[128,1152]{1,0:T(8,128)(2,1)S(1)}, f32[128,1024]{1,0:T(8,128)S(1)}, bf16[128,2176]{1,0:T(8,128)(2,1)S(1)}) custom-call(s32[6]{0:T(128)S(1)} %concatenate.6.place, bf16[192,1024]{1,0:T(8,128)(2,1)S(1)} %collective-permute-done.p0, ...), custom_call_target="tpu_custom_call" | custom-call | flops 1000 | bytes 1000 | tf_op jit(solution)/shard_map/pallas_call | solution.py:605
  32.2 1.3 %collective-permute-start.7 = (bf16[128,2176]{1,0:T(8,128)(2,1)S(1)}, bf16[128,2176]{1,0:T(8,128)(2,1)S(1)}, u32[]{:S(2)}, u32[]{:S(2)}) collective-permute-start(bf16[128,2176]{1,0:T(8,128)(2,1)S(1)} %get-tuple-element.38), channel_id=1, source_target_pairs={{0,2},{1,3},{2,0},{3,1},{4,6},{5,7},{6,4},{7,5},{8,10},{9,11},{10,... | collective-permute-start | bytes 1671176 | tf_op jit(solution)/shard_map/ppermute | solution.py:631
  35.3 6.8 %shard_map.104 = (bf16[4,192,256]{2,1,0:T(8,128)(2,1)S(1)}, bf16[4,192,256]{2,1,0:T(8,128)(2,1)S(1)}, bf16[128,1152]{1,0:T(8,128)(2,1)S(1)}, f32[128,1024]{1,0:T(8,128)S(1)}, bf16[128,2176]{1,0:T(8,128)(2,1)S(1)}) custom-call(s32[6]{0:T(128)S(1)} %concatenate.6.place, bf16[192,1024]{1,0:T(8,128)(2,1)S(1)} %collective-permute-done.p0, ...), custom_call_target="tpu_custom_call" | custom-call | flops 1000 | bytes 1000 | tf_op jit(solution)/shard_map/pallas_call | solution.py:605
  42.1 1.3 %collective-permute-start.8 = (bf16[128,2176]{1,0:T(8,128)(2,1)S(1)}, bf16[128,2176]{1,0:T(8,128)(2,1)S(1)}, u32[]{:S(2)}, u32[]{:S(2)}) collective-permute-start(bf16[128,2176]{1,0:T(8,128)(2,1)S(1)} %get-tuple-element.41), channel_id=1, source_target_pairs={{0,2},{1,3},{2,0},{3,1},{4,6},{5,7},{6,4},{7,5},{8,10},{9,11},{10,... | collective-permute-start | bytes 1671176 | tf_op jit(solution)/shard_map/ppermute | solution.py:631
  43.4 3.0 %collective-permute-done.7.got.got_a = bf16[128,2176]{1,0:T(8,128)(2,1)S(1)} collective-permute-done((bf16[128,2176]{1,0:T(8,128)(2,1)S(1)}, bf16[128,2176]{1,0:T(8,128)(2,1)S(1)}, u32[]{:S(2)}, u32[]{:S(2)}) %collective-permute-start.7) | collective-permute-done | bytes 557088 | tf_op jit(solution)/shard_map/ppermute | solution.py:631
  46.3 1.4 %shard_map.105 = (f32[2,96,1024]{2,1,0:T(8,128)S(1)}, bf16[2,96,1024]{2,1,0:T(8,128)(2,1)S(1)}) custom-call(s32[6]{0:T(128)S(1)} %concatenate.6.place, bf16[128,1152]{1,0:T(8,128)(2,1)S(1)} %get-tuple-element.37.keep.keep_a, f32[128,1024]{1,0:T(8,128)S(1)} %get-tuple-element.42.out_keep, bf16[128,2176]{1,0:T(8,128)(2,1)S(1)} %collective-permute-done.7.got.got_a, ...), custom_call_target="tpu_custom_call" | custom-call | flops 1000 | bytes 1000 | tf_op jit(solution)/shard_map/pallas_call | solution.py:605
  47.7 3.9 %collective-permute-start.10 = (bf16[2,96,1024]{2,1,0:T(8,128)(2,1)S(1)}, bf16[2,96,1024]{2,1,0:T(8,128)(2,1)S(1)}, u32[]{:S(2)}, u32[]{:S(2)}) collective-permute-start(bf16[2,96,1024]{2,1,0:T(8,128)(2,1)S(1)} %get-tuple-element.44), channel_id=1, source_target_pairs={{0,4},{1,5},{2,6},{3,7},{4,0},{5,1},{6,2},{7,3},{8,12},{9,13},{10,... | collective-permute-start | bytes 1179656 | tf_op jit(solution)/shard_map/ppermute | solution.py:631
  51.6 7.3 %collective-permute-done.10.got = bf16[2,96,1024]{2,1,0:T(8,128)(2,1)S(1)} collective-permute-done((bf16[2,96,1024]{2,1,0:T(8,128)(2,1)S(1)}, bf16[2,96,1024]{2,1,0:T(8,128)(2,1)S(1)}, u32[]{:S(2)}, u32[]{:S(2)}) %collective-permute-start.10) | collective-permute-done | bytes 393248 | tf_op jit(solution)/shard_map/ppermute | solution.py:631
  59.0 2.0 %shard_map.107 = (f32[2,160,1024]{2,1,0:T(8,128)S(1)}, bf16[2,160,1024]{2,1,0:T(8,128)(2,1)S(1)}) custom-call(s32[6]{0:T(128)S(1)} %concatenate.6.place, bf16[128,1152]{1,0:T(8,128)(2,1)S(1)} %get-tuple-element.37.keep.keep_a, bf16[128,2176]{1,0:T(8,128)(2,1)S(1)} %collective-permute-done.7.got.got_a, bf16[128,1152]{1,0:T(8,128)(2,1)S(1)} %get-tuple-element.39.keep_b, ...), custom_call_target="tpu_custom_call" | custom-call | flops 1000 | bytes 1000 | tf_op jit(solution)/shard_map/pallas_call | solution.py:605
  61.0 3.2 %collective-permute-start.17 = (bf16[2,160,1024]{2,1,0:T(8,128)(2,1)S(1)}, bf16[2,160,1024]{2,1,0:T(8,128)(2,1)S(1)}, u32[]{:S(2)}, u32[]{:S(2)}) collective-permute-start(bf16[2,160,1024]{2,1,0:T(8,128)(2,1)S(1)} %get-tuple-element.46.after), channel_id=1, source_target_pairs={{0,4},{1,5},{2,6},{3,7},{4,0},{5,1},{6,2},{7,3},{8,12},{9,13},{10,... | collective-permute-start | bytes 1966088 | tf_op jit(solution)/shard_map/ppermute | solution.py:631
  64.2 1.6 %collective-permute-start.6 = (bf16[4,192,256]{2,1,0:T(8,128)(2,1)S(1)}, bf16[4,192,256]{2,1,0:T(8,128)(2,1)S(1)}, u32[]{:S(2)}, u32[]{:S(2)}) collective-permute-start(bf16[4,192,256]{2,1,0:T(8,128)(2,1)S(1)} %get-tuple-element.36), channel_id=1, source_target_pairs={{0,1},{1,0},{2,3},{3,2},{4,5},{5,4},{6,7},{7,6},{8,9},{9,8},{10,11... | collective-permute-start | bytes 1179656 | tf_op jit(solution)/shard_map/ppermute | solution.py:631
  65.7 2.6 %collective-permute-start.11 = (bf16[96,1024]{1,0:T(8,128)(2,1)S(1)}, bf16[96,1024]{1,0:T(8,128)(2,1)S(1)}, u32[]{:S(2)}, u32[]{:S(2)}) collective-permute-start(bf16[96,1024]{1,0:T(8,128)(2,1)S(1)} %get-tuple-element.45.after), channel_id=1, source_target_pairs={{0,8},{1,9},{2,10},{3,11},{4,12},{5,13},{6,14},{7,15},{8,0},{9,1},... | collective-permute-start | bytes 589832 | tf_op jit(solution)/shard_map/ppermute | solution.py:631
  68.6 13.4 %collective-permute-done.17.got = bf16[2,160,1024]{2,1,0:T(8,128)(2,1)S(1)} collective-permute-done((bf16[2,160,1024]{2,1,0:T(8,128)(2,1)S(1)}, bf16[2,160,1024]{2,1,0:T(8,128)(2,1)S(1)}, u32[]{:S(2)}, u32[]{:S(2)}) %collective-permute-start.17) | collective-permute-done | bytes 655392 | tf_op jit(solution)/shard_map/ppermute | solution.py:631
  82.1 2.1 %collective-permute-start.18 = (bf16[160,1024]{1,0:T(8,128)(2,1)S(1)}, bf16[160,1024]{1,0:T(8,128)(2,1)S(1)}, u32[]{:S(2)}, u32[]{:S(2)}) collective-permute-start(bf16[160,1024]{1,0:T(8,128)(2,1)S(1)} %get-tuple-element.55), channel_id=1, source_target_pairs={{0,8},{1,9},{2,10},{3,11},{4,12},{5,13},{6,14},{7,15},{8,0},{9,1},... | collective-permute-start | bytes 983048 | tf_op jit(solution)/shard_map/ppermute | solution.py:631
  84.3 1.3 collective-permute-start.12
  85.5 3.3 %collective-permute-done.12.before.a1 = bf16[96,1024]{1,0:T(8,128)(2,1)S(1)} collective-permute-done((bf16[96,1024]{1,0:T(8,128)(2,1)S(1)}, bf16[96,1024]{1,0:T(8,128)(2,1)S(1)}, u32[]{:S(2)}, u32[]{:S(2)}) %collective-permute-start.12) | collective-permute-done | bytes 196640 | tf_op jit(solution)/shard_map/ppermute | solution.py:631
  88.8 5.8 %shard_map.109 = (bf16[192,1024]{1,0:T(8,128)(2,1)S(1)}, bf16[192,1024]{1,0:T(8,128)(2,1)S(1)}) custom-call(s32[6]{0:T(128)S(1)} %concatenate.6.place, bf16[4,192,256]{2,1,0:T(8,128)(2,1)S(1)} %get-tuple-element.33.own_a, bf16[4,192,256]{2,1,0:T(8,128)(2,1)S(1)} %collective-permute-done.4.got_a, bf16[4,192,256]{2,1,0:T(8,128)(2,1)S(1)} %get-tuple-element.35.own_b, ...), custom_call_target="tpu_custom_call" | custom-call | flops 1000 | bytes 1000 | tf_op jit(solution)/shard_map/pallas_call | solution.py:743
  94.7 6.8 %collective-permute-done.18.got = bf16[160,1024]{1,0:T(8,128)(2,1)S(1)} collective-permute-done((bf16[160,1024]{1,0:T(8,128)(2,1)S(1)}, bf16[160,1024]{1,0:T(8,128)(2,1)S(1)}, u32[]{:S(2)}, u32[]{:S(2)}) %collective-permute-start.18) | collective-permute-done | bytes 327712 | tf_op jit(solution)/shard_map/ppermute | solution.py:631
  101.6 1.3 collective-permute-start.19
  102.9 1.8 %collective-permute-start.14 = (bf16[192,1024]{1,0:T(8,128)(2,1)S(1)}, bf16[192,1024]{1,0:T(8,128)(2,1)S(1)}, u32[]{:S(2)}, u32[]{:S(2)}) collective-permute-start(bf16[192,1024]{1,0:T(8,128)(2,1)S(1)} %get-tuple-element.49), channel_id=1, source_target_pairs={{0,4},{1,12},{2,6},{3,14},{4,0},{5,8},{6,2},{7,10},{8,5},{9,13},{1... | collective-permute-start | bytes 1179656 | tf_op jit(solution)/shard_map/ppermute | solution.py:631
  104.6 1.9 %collective-permute-start.13 = (bf16[192,1024]{1,0:T(8,128)(2,1)S(1)}, bf16[192,1024]{1,0:T(8,128)(2,1)S(1)}, u32[]{:S(2)}, u32[]{:S(2)}) collective-permute-start(bf16[192,1024]{1,0:T(8,128)(2,1)S(1)} %get-tuple-element.48.refs_0_), channel_id=1, source_target_pairs={{0,0},{1,8},{2,2},{3,10},{4,4},{5,12},{6,6},{7,14},{8,1},{9,9},{10... | collective-permute-start | bytes 1179656 | tf_op jit(solution)/shard_map/ppermute | solution.py:631
  106.6 3.8 %collective-permute-done.19.b1 = bf16[160,1024]{1,0:T(8,128)(2,1)S(1)} collective-permute-done((bf16[160,1024]{1,0:T(8,128)(2,1)S(1)}, bf16[160,1024]{1,0:T(8,128)(2,1)S(1)}, u32[]{:S(2)}, u32[]{:S(2)}) %collective-permute-start.19) | collective-permute-done | bytes 327712 | tf_op jit(solution)/shard_map/ppermute | solution.py:631
  110.4 1.3 %collective-permute-start.21 = (bf16[160,1024]{1,0:T(8,128)(2,1)S(1)}, bf16[160,1024]{1,0:T(8,128)(2,1)S(1)}, u32[]{:S(2)}, u32[]{:S(2)}) collective-permute-start(bf16[160,1024]{1,0:T(8,128)(2,1)S(1)} %collective-permute-done.19.b1), channel_id=1, source_target_pairs={{0,1},{1,0},{2,3},{3,2},{4,5},{5,4},{6,7},{7,6},{8,9},{9,8},{10,11... | collective-permute-start | bytes 983048 | tf_op jit(solution)/shard_map/ppermute | solution.py:631
  111.8 1.7 %collective-permute-done.14.r1 = bf16[192,1024]{1,0:T(8,128)(2,1)S(1)} collective-permute-done((bf16[192,1024]{1,0:T(8,128)(2,1)S(1)}, bf16[192,1024]{1,0:T(8,128)(2,1)S(1)}, u32[]{:S(2)}, u32[]{:S(2)}) %collective-permute-start.14) | collective-permute-done | bytes 393248 | tf_op jit(solution)/shard_map/ppermute | solution.py:631
  113.5 2.3 %collective-permute-start.16 = (bf16[96,1024]{1,0:T(8,128)(2,1)S(1)}, bf16[96,1024]{1,0:T(8,128)(2,1)S(1)}, u32[]{:S(2)}, u32[]{:S(2)}) collective-permute-start(bf16[96,1024]{1,0:T(8,128)(2,1)S(1)} %collective-permute-done.12.before.a1), channel_id=1, source_target_pairs={{0,1},{1,0},{2,3},{3,2},{4,5},{5,4},{6,7},{7,6},{8,9},{9,8},{10,11... | collective-permute-start | bytes 589832 | tf_op jit(solution)/shard_map/ppermute | solution.py:631
  115.8 5.9 %collective-permute-done.13.r0 = bf16[192,1024]{1,0:T(8,128)(2,1)S(1)} collective-permute-done((bf16[192,1024]{1,0:T(8,128)(2,1)S(1)}, bf16[192,1024]{1,0:T(8,128)(2,1)S(1)}, u32[]{:S(2)}, u32[]{:S(2)}) %collective-permute-start.13) | collective-permute-done | bytes 393248 | tf_op jit(solution)/shard_map/ppermute | solution.py:631
  121.7 2.6 %shard_map.110 = (bf16[2,96,1024]{2,1,0:T(8,128)(2,1)}, bf16[2,96,1024]{2,1,0:T(8,128)(2,1)}) custom-call(s32[6]{0:T(128)S(1)} %concatenate.6.place, bf16[192,1024]{1,0:T(8,128)(2,1)S(1)} %collective-permute-done.13.r0, bf16[192,1024]{1,0:T(8,128)(2,1)S(1)} %collective-permute-done.14.r1, bf16[1024,1024]{1,0:T(8,128)(2,1)S(1)} %copy-done, ...), custom_call_target="tpu_custom_call" | custom-call | flops 1000 | bytes 1000 | tf_op jit(solution)/shard_map/pallas_call | solution.py:605
  124.3 3.0 %shard_map.113 = (f32[1024,768]{1,0:T(8,128)}, f32[1024,256]{1,0:T(8,128)}) custom-call(s32[6]{0:T(128)S(1)} %concatenate.6.place, bf16[96,1024]{1,0:T(8,128)(2,1)S(1)} %shard_map.108.a0, bf16[96,1024]{1,0:T(8,128)(2,1)S(1)} %collective-permute-done.12.before.a1, bf16[96,1024]{1,0:T(8,128)(2,1)S(1)} %collective-permute-done.15.a2, ...), custom_call_target="tpu_custom_call" | custom-call | flops 1000 | bytes 1000 | tf_op jit(solution)/shard_map/pallas_call | solution.py:605
  (32 shorter events, 5.4 us)
Async XLA Ops:
  3.6 19.5 %collective-permute-start = (bf16[192,1024]{1,0:T(8,128)(2,1)S(1)}, bf16[192,1024]{1,0:T(8,128)(2,1)S(1)}, u32[]{:S(2)}, u32[]{:S(2)}) collective-permute-start(bf16[192,1024]{1,0:T(8,128)(2,1)S(1)} %get-tuple-element.31.m0), channel_id=1, source_target_pairs={{0,0},{1,8},{2,2},{3,10},{4,4},{5,12},{6,6},{7,14},{8,1},{9,9},{10... | collective-permute-start | bytes 1179656 | tf_op jit(solution)/shard_map/ppermute | solution.py:631
  9.2 13.9 %collective-permute-start.1 = (bf16[192,1024]{1,0:T(8,128)(2,1)S(1)}, bf16[192,1024]{1,0:T(8,128)(2,1)S(1)}, u32[]{:S(2)}, u32[]{:S(2)}) collective-permute-start(bf16[192,1024]{1,0:T(8,128)(2,1)S(1)} %get-tuple-element.32.m1), channel_id=1, source_target_pairs={{0,4},{1,12},{2,6},{3,14},{4,0},{5,8},{6,2},{7,10},{8,5},{9,13},{1... | collective-permute-start | bytes 1179656 | tf_op jit(solution)/shard_map/ppermute | solution.py:631
  23.1 1.9 %collective-permute-start.2 = (bf16[192,1024]{1,0:T(8,128)(2,1)S(1)}, bf16[192,1024]{1,0:T(8,128)(2,1)S(1)}, u32[]{:S(2)}, u32[]{:S(2)}) collective-permute-start(bf16[192,1024]{1,0:T(8,128)(2,1)S(1)} %collective-permute-done.p0), channel_id=1, source_target_pairs={{0,1},{1,0},{2,3},{3,2},{4,5},{5,4},{6,7},{7,6},{8,9},{9,8},{10,11... | collective-permute-start | bytes 1179656 | tf_op jit(solution)/shard_map/ppermute | solution.py:631
  23.1 2.3 %collective-permute-start.3 = (bf16[192,1024]{1,0:T(8,128)(2,1)S(1)}, bf16[192,1024]{1,0:T(8,128)(2,1)S(1)}, u32[]{:S(2)}, u32[]{:S(2)}) collective-permute-start(bf16[192,1024]{1,0:T(8,128)(2,1)S(1)} %collective-permute-done.1.p1), channel_id=1, source_target_pairs={{0,1},{1,0},{2,3},{3,2},{4,5},{5,4},{6,7},{7,6},{8,9},{9,8},{10,11... | collective-permute-start | bytes 1179656 | tf_op jit(solution)/shard_map/ppermute | solution.py:631
  23.7 10.8 %collective-permute-start.5 = (bf16[192,1024]{1,0:T(8,128)(2,1)S(1)}, bf16[192,1024]{1,0:T(8,128)(2,1)S(1)}, u32[]{:S(2)}, u32[]{:S(2)}) collective-permute-start(bf16[192,1024]{1,0:T(8,128)(2,1)S(1)} %pad_maximum_fusion), channel_id=1, source_target_pairs={{0,2},{1,3},{2,0},{3,1},{4,6},{5,7},{6,4},{7,5},{8,10},{9,11},{10,... | collective-permute-start | bytes 1179656 | tf_op jit(solution)/shard_map/ppermute | solution.py:631
  32.2 14.2 %collective-permute-start.7 = (bf16[128,2176]{1,0:T(8,128)(2,1)S(1)}, bf16[128,2176]{1,0:T(8,128)(2,1)S(1)}, u32[]{:S(2)}, u32[]{:S(2)}) collective-permute-start(bf16[128,2176]{1,0:T(8,128)(2,1)S(1)} %get-tuple-element.38), channel_id=1, source_target_pairs={{0,2},{1,3},{2,0},{3,1},{4,6},{5,7},{6,4},{7,5},{8,10},{9,11},{10,... | collective-permute-start | bytes 1671176 | tf_op jit(solution)/shard_map/ppermute | solution.py:631
  34.5 8.9 %collective-permute-start.9 = (bf16[192,1024]{1,0:T(8,128)(2,1)S(1)}, bf16[192,1024]{1,0:T(8,128)(2,1)S(1)}, u32[]{:S(2)}, u32[]{:S(2)}) collective-permute-start(bf16[192,1024]{1,0:T(8,128)(2,1)S(1)} %collective-permute-done.5.after.n0), channel_id=1, source_target_pairs={{0,1},{1,0},{2,3},{3,2},{4,5},{5,4},{6,7},{7,6},{8,9},{9,8},{10,11... | collective-permute-start | bytes 1179656 | tf_op jit(solution)/shard_map/ppermute | solution.py:631
  42.1 16.9 %collective-permute-start.8 = (bf16[128,2176]{1,0:T(8,128)(2,1)S(1)}, bf16[128,2176]{1,0:T(8,128)(2,1)S(1)}, u32[]{:S(2)}, u32[]{:S(2)}) collective-permute-start(bf16[128,2176]{1,0:T(8,128)(2,1)S(1)} %get-tuple-element.41), channel_id=1, source_target_pairs={{0,2},{1,3},{2,0},{3,1},{4,6},{5,7},{6,4},{7,5},{8,10},{9,11},{10,... | collective-permute-start | bytes 1671176 | tf_op jit(solution)/shard_map/ppermute | solution.py:631
  47.7 11.2 %collective-permute-start.10 = (bf16[2,96,1024]{2,1,0:T(8,128)(2,1)S(1)}, bf16[2,96,1024]{2,1,0:T(8,128)(2,1)S(1)}, u32[]{:S(2)}, u32[]{:S(2)}) collective-permute-start(bf16[2,96,1024]{2,1,0:T(8,128)(2,1)S(1)} %get-tuple-element.44), channel_id=1, source_target_pairs={{0,4},{1,5},{2,6},{3,7},{4,0},{5,1},{6,2},{7,3},{8,12},{9,13},{10,... | collective-permute-start | bytes 1179656 | tf_op jit(solution)/shard_map/ppermute | solution.py:631
  61.0 21.0 %collective-permute-start.17 = (bf16[2,160,1024]{2,1,0:T(8,128)(2,1)S(1)}, bf16[2,160,1024]{2,1,0:T(8,128)(2,1)S(1)}, u32[]{:S(2)}, u32[]{:S(2)}) collective-permute-start(bf16[2,160,1024]{2,1,0:T(8,128)(2,1)S(1)} %get-tuple-element.46.after), channel_id=1, source_target_pairs={{0,4},{1,5},{2,6},{3,7},{4,0},{5,1},{6,2},{7,3},{8,12},{9,13},{10,... | collective-permute-start | bytes 1966088 | tf_op jit(solution)/shard_map/ppermute | solution.py:631
  64.2 21.3 %collective-permute-start.6 = (bf16[4,192,256]{2,1,0:T(8,128)(2,1)S(1)}, bf16[4,192,256]{2,1,0:T(8,128)(2,1)S(1)}, u32[]{:S(2)}, u32[]{:S(2)}) collective-permute-start(bf16[4,192,256]{2,1,0:T(8,128)(2,1)S(1)} %get-tuple-element.36), channel_id=1, source_target_pairs={{0,1},{1,0},{2,3},{3,2},{4,5},{5,4},{6,7},{7,6},{8,9},{9,8},{10,11... | collective-permute-start | bytes 1179656 | tf_op jit(solution)/shard_map/ppermute | solution.py:631
  65.7 18.5 %collective-permute-start.11 = (bf16[96,1024]{1,0:T(8,128)(2,1)S(1)}, bf16[96,1024]{1,0:T(8,128)(2,1)S(1)}, u32[]{:S(2)}, u32[]{:S(2)}) collective-permute-start(bf16[96,1024]{1,0:T(8,128)(2,1)S(1)} %get-tuple-element.45.after), channel_id=1, source_target_pairs={{0,8},{1,9},{2,10},{3,11},{4,12},{5,13},{6,14},{7,15},{8,0},{9,1},... | collective-permute-start | bytes 589832 | tf_op jit(solution)/shard_map/ppermute | solution.py:631
  68.3 17.2 %collective-permute-start.4 = (bf16[4,192,256]{2,1,0:T(8,128)(2,1)S(1)}, bf16[4,192,256]{2,1,0:T(8,128)(2,1)S(1)}, u32[]{:S(2)}, u32[]{:S(2)}) collective-permute-start(bf16[4,192,256]{2,1,0:T(8,128)(2,1)S(1)} %get-tuple-element.34), channel_id=1, source_target_pairs={{0,1},{1,0},{2,3},{3,2},{4,5},{5,4},{6,7},{7,6},{8,9},{9,8},{10,11... | collective-permute-start | bytes 1179656 | tf_op jit(solution)/shard_map/ppermute | solution.py:631
  82.1 19.4 %collective-permute-start.18 = (bf16[160,1024]{1,0:T(8,128)(2,1)S(1)}, bf16[160,1024]{1,0:T(8,128)(2,1)S(1)}, u32[]{:S(2)}, u32[]{:S(2)}) collective-permute-start(bf16[160,1024]{1,0:T(8,128)(2,1)S(1)} %get-tuple-element.55), channel_id=1, source_target_pairs={{0,8},{1,9},{2,10},{3,11},{4,12},{5,13},{6,14},{7,15},{8,0},{9,1},... | collective-permute-start | bytes 983048 | tf_op jit(solution)/shard_map/ppermute | solution.py:631
  84.3 4.6 %collective-permute-start.12 = (bf16[96,1024]{1,0:T(8,128)(2,1)S(1)}, bf16[96,1024]{1,0:T(8,128)(2,1)S(1)}, u32[]{:S(2)}, u32[]{:S(2)}) collective-permute-start(bf16[96,1024]{1,0:T(8,128)(2,1)S(1)} %shard_map.108.a0), channel_id=1, source_target_pairs={{0,2},{1,3},{2,0},{3,1},{4,6},{5,7},{6,4},{7,5},{8,10},{9,11},{10,... | collective-permute-start | bytes 589832 | tf_op jit(solution)/shard_map/ppermute | solution.py:631
  88.8 32.9 %copy-start = (bf16[1024,1024]{1,0:T(8,128)(2,1)S(1)}, bf16[1024,1024]{1,0:T(8,128)(2,1)}, u32[]{:S(2)}) copy-start(bf16[1024,1024]{1,0:T(8,128)(2,1)} %w_ref.3) | copy-start | bytes 6291460
  88.8 32.9 %copy-start.1 = (f32[1024]{0:T(1024)S(1)}, f32[1024]{0:T(1024)}, u32[]{:S(2)}) copy-start(f32[1024]{0:T(1024)} %param.13) | copy-start | bytes 12292
  101.6 8.9 %collective-permute-start.19 = (bf16[160,1024]{1,0:T(8,128)(2,1)S(1)}, bf16[160,1024]{1,0:T(8,128)(2,1)S(1)}, u32[]{:S(2)}, u32[]{:S(2)}) collective-permute-start(bf16[160,1024]{1,0:T(8,128)(2,1)S(1)} %shard_map.112.b0), channel_id=1, source_target_pairs={{0,2},{1,3},{2,0},{3,1},{4,6},{5,7},{6,4},{7,5},{8,10},{9,11},{10,... | collective-permute-start | bytes 983048 | tf_op jit(solution)/shard_map/ppermute | solution.py:631
  102.9 10.7 %collective-permute-start.14 = (bf16[192,1024]{1,0:T(8,128)(2,1)S(1)}, bf16[192,1024]{1,0:T(8,128)(2,1)S(1)}, u32[]{:S(2)}, u32[]{:S(2)}) collective-permute-start(bf16[192,1024]{1,0:T(8,128)(2,1)S(1)} %get-tuple-element.49), channel_id=1, source_target_pairs={{0,4},{1,12},{2,6},{3,14},{4,0},{5,8},{6,2},{7,10},{8,5},{9,13},{1... | collective-permute-start | bytes 1179656 | tf_op jit(solution)/shard_map/ppermute | solution.py:631
  104.6 17.1 %collective-permute-start.13 = (bf16[192,1024]{1,0:T(8,128)(2,1)S(1)}, bf16[192,1024]{1,0:T(8,128)(2,1)S(1)}, u32[]{:S(2)}, u32[]{:S(2)}) collective-permute-start(bf16[192,1024]{1,0:T(8,128)(2,1)S(1)} %get-tuple-element.48.refs_0_), channel_id=1, source_target_pairs={{0,0},{1,8},{2,2},{3,10},{4,4},{5,12},{6,6},{7,14},{8,1},{9,9},{10... | collective-permute-start | bytes 1179656 | tf_op jit(solution)/shard_map/ppermute | solution.py:631
  106.6 17.7 %collective-permute-start.20 = (bf16[160,1024]{1,0:T(8,128)(2,1)S(1)}, bf16[160,1024]{1,0:T(8,128)(2,1)S(1)}, u32[]{:S(2)}, u32[]{:S(2)}) collective-permute-start(bf16[160,1024]{1,0:T(8,128)(2,1)S(1)} %shard_map.112.b0), channel_id=1, source_target_pairs={{0,1},{1,0},{2,3},{3,2},{4,5},{5,4},{6,7},{7,6},{8,9},{9,8},{10,11... | collective-permute-start | bytes 983048 | tf_op jit(solution)/shard_map/ppermute | solution.py:631
  110.4 13.9 %collective-permute-start.21 = (bf16[160,1024]{1,0:T(8,128)(2,1)S(1)}, bf16[160,1024]{1,0:T(8,128)(2,1)S(1)}, u32[]{:S(2)}, u32[]{:S(2)}) collective-permute-start(bf16[160,1024]{1,0:T(8,128)(2,1)S(1)} %collective-permute-done.19.b1), channel_id=1, source_target_pairs={{0,1},{1,0},{2,3},{3,2},{4,5},{5,4},{6,7},{7,6},{8,9},{9,8},{10,11... | collective-permute-start | bytes 983048 | tf_op jit(solution)/shard_map/ppermute | solution.py:631
  111.8 12.5 %collective-permute-start.15 = (bf16[96,1024]{1,0:T(8,128)(2,1)S(1)}, bf16[96,1024]{1,0:T(8,128)(2,1)S(1)}, u32[]{:S(2)}, u32[]{:S(2)}) collective-permute-start(bf16[96,1024]{1,0:T(8,128)(2,1)S(1)} %shard_map.108.a0), channel_id=1, source_target_pairs={{0,1},{1,0},{2,3},{3,2},{4,5},{5,4},{6,7},{7,6},{8,9},{9,8},{10,11... | collective-permute-start | bytes 589832 | tf_op jit(solution)/shard_map/ppermute | solution.py:631
  113.5 10.8 %collective-permute-start.16 = (bf16[96,1024]{1,0:T(8,128)(2,1)S(1)}, bf16[96,1024]{1,0:T(8,128)(2,1)S(1)}, u32[]{:S(2)}, u32[]{:S(2)}) collective-permute-start(bf16[96,1024]{1,0:T(8,128)(2,1)S(1)} %collective-permute-done.12.before.a1), channel_id=1, source_target_pairs={{0,1},{1,0},{2,3},{3,2},{4,5},{5,4},{6,7},{7,6},{8,9},{9,8},{10,11... | collective-permute-start | bytes 589832 | tf_op jit(solution)/shard_map/ppermute | solution.py:631

commit v6 on v5

--- a/solution.py
+++ b/solution.py
@@ -285,8 +285,7 @@
 
 
 def norm_kernel(
-    place, patch_hbm, cot_hbm, index_hbm, gain_hbm, p0_ref, p1_ref, hidden_ref,
-    patch_ref, cot_ref, index_ref, gain_ref, sems,
+    place, patch_hbm, index_hbm, gain_hbm, n0_ref, n1_ref, hidden_ref, patch_ref, index_ref, gain_ref, sems,
 ):
     par = place[PAR]
     rows, width = patch_ref.shape[1:]
@@ -294,7 +293,7 @@
     copies = [
         pltpu.make_async_copy(src, dst, sems.at[i])
         for i, (src, dst) in enumerate(
-            ((index_hbm, index_ref), (patch_hbm, patch_ref), (gain_hbm, gain_ref), (cot_hbm, cot_ref))
+            ((index_hbm, index_ref), (patch_hbm, patch_ref), (gain_hbm, gain_ref))
         )
     ]
     for copy in copies:
@@ -316,7 +315,7 @@
         tables.append(jnp.concatenate(pieces, axis=1))
     copies[1].wait()
     copies[2].wait()
-    for k, out_ref in enumerate((p0_ref, p1_ref)):
+    for k, out_ref in enumerate((n0_ref, n1_ref)):
         s = k ^ par
         hidden = patch_ref[s].astype(jnp.float32) + tables[k]
         hidden_ref[k] = hidden
@@ -324,109 +323,135 @@
         spread = jnp.mean(center * center, axis=-1, keepdims=True)
         normed = center * lax.rsqrt(spread + epsilon) * gain_ref[...]
         live = live_column(place[KEPT + s], rows)
-        out_ref[:rows, :] = jnp.where(live, normed, MARK).astype(out_ref.dtype)
-    copies[3].wait()
-    for k, out_ref in enumerate((p0_ref, p1_ref)):
-        s = k ^ par
-        live = live_column(place[KEPT + s], rows)
+        out_ref[...] = jnp.where(live, normed, MARK).astype(out_ref.dtype)
+
+
+def grad_kernel(place, cot_hbm, after, g0_ref, g1_ref, cot_ref, sem):
+    del after
+    copy = pltpu.make_async_copy(cot_hbm, cot_ref, sem)
+    copy.start()
+    copy.wait()
+    for k, out_ref in enumerate((g0_ref, g1_ref)):
+        s = k ^ place[PAR]
         grad = cot_ref[s]
-        out_ref[rows:, :] = jnp.where(live, grad, jnp.zeros_like(grad))
-
-
-def load_weights(core, first_pair, w_in_hbm, w_out_hbm, wq, wk, wv, wo, sems):
-    width = w_out_hbm.shape[0]
+        live = live_column(place[KEPT + s], grad.shape[0])
+        out_ref[...] = jnp.where(live, grad, jnp.zeros_like(grad))
+
+
+def join_kernel(a, b, after, out):
+    del after
+    block = a.shape[0]
+    out[:block, :] = a[...]
+    out[block:, :] = b[...]
+
+
+def forward_kernel(
+    place, n0, n1, w_in_hbm, w_out_hbm, norm_out, q_out, k_out, v_out, wo, prob_out, att_out,
+    wq, wk, wv, sems,
+):
+    block, width = n0.shape
+    rows = 2 * block
+    pairs = width // 256
     copies = []
-    for j in range(wq.shape[1] // 128):
+    for j in range(pairs):
         to = pl.ds(128 * j, 128)
-        row = pl.multiple_of(256 * (first_pair + j) + 128 * core, 128)
-        pairs = [(w_out_hbm.at[pl.ds(row, 128), :], wo.at[to, :])]
+        row = pl.multiple_of(256 * j + 128 * place[CORE], 128)
+        moves = [(w_out_hbm.at[pl.ds(row, 128), :], wo.at[to, :])]
         for t, out in enumerate((wq, wk, wv)):
             at = pl.multiple_of(t * width + row, 128)
-            pairs.append((w_in_hbm.at[:, pl.ds(at, 128)], out.at[:, to]))
-        copies += [pltpu.make_async_copy(a, b, sems.at[4 * j + i]) for i, (a, b) in enumerate(pairs)]
+            moves.append((w_in_hbm.at[:, pl.ds(at, 128)], out.at[:, to]))
+        copies += [pltpu.make_async_copy(a, b, sems.at[4 * j + i]) for i, (a, b) in enumerate(moves)]
     for copy in copies:
         copy.start()
-    return copies
-
-
-def attend_pairs(
-    place, first_pair, payloads, w_in_hbm, w_out_hbm, own, oth, keep_t, out_keep, send,
-    norm_s, grad_s, att_s, wq, wk, wv, wo, sems,
-):
-    copies = load_weights(place[CORE], first_pair, w_in_hbm, w_out_hbm, wq, wk, wv, wo, sems)
-    block = payloads[0].shape[0] // 2
-    rows = 4 * block
-    half = 2 * block
     biases = []
-    for i, ref in enumerate(payloads):
-        at = slice(i * block, (i + 1) * block)
-        value = ref[:block, :]
+    for i, ref in enumerate((n0, n1)):
+        value = ref[...]
         live = value[:, 0:1].astype(jnp.float32) < MARK
-        norm_s[at, :] = jnp.where(live, value, jnp.zeros_like(value))
-        grad_s[at, :] = ref[block:, :]
+        norm_out[i * block : (i + 1) * block, :] = jnp.where(live, value, jnp.zeros_like(value))
         biases.append(jnp.where(live, 0.0, -1e30))
     bias = jnp.concatenate(biases, axis=0)
-    low = lax.broadcasted_iota(jnp.int32, (rows, 128), 1) < 64
-    scale = jnp.bfloat16(0.125)
-    zero = jnp.zeros((rows, 128), jnp.bfloat16)
-    first = place[SIDE] == 0
-    count = wq.shape[1] // 128
     for copy in copies:
         copy.wait()
-    normed = norm_s[...]
-    queries = dot_nn(normed, wq[...]).astype(jnp.bfloat16)
-    keys = dot_nn(normed, wk[...]).astype(jnp.bfloat16)
-    values = dot_nn(normed, wv[...]).astype(jnp.bfloat16)
-    d_att = dot_nt(grad_s[...], wo[...]).astype(jnp.bfloat16)
-    for j in range(count):
+    normed = norm_out[...]
+    q_out[...] = dot_nn(normed, wq[...]).astype(jnp.bfloat16) * jnp.bfloat16(0.125)
+    k_out[...] = dot_nn(normed, wk[...]).astype(jnp.bfloat16)
+    v_out[...] = dot_nn(normed, wv[...]).astype(jnp.bfloat16)
+    low = lax.broadcasted_iota(jnp.int32, (rows, 128), 1) < 64
+    zero = jnp.zeros((rows, 128), jnp.bfloat16)
+    for j in range(pairs):
         cols = slice(128 * j, 128 * j + 128)
-        q = queries[:, cols] * scale
-        k = keys[:, cols]
-        v = values[:, cols]
-        g = d_att[:, cols]
-        v_t = v.T
-        k_t = (k * scale).T
-        att_t, dq_t, dk, dv = [], [], [], []
+        q = q_out[:, cols]
+        k = k_out[:, cols]
+        v_t = v_out[:, cols].T
         for h in range(2):
             mine = low if h == 0 else jnp.logical_not(low)
             scores = dot_nt(k, jnp.where(mine, q, zero)) + bias
             raised = jnp.exp(scores - jnp.max(scores, axis=0, keepdims=True))
             prob = raised * (1.0 / jnp.sum(raised, axis=0, keepdims=True))
-            weights = prob.astype(jnp.bfloat16)
+            prob_out[2 * j + h] = prob
             part = slice(64 * h, 64 * h + 64)
-            att_t.append(dot_nn(v_t[part], weights))
-            dv.append(dot_nn(weights, g))
+            to = slice(128 * j + 64 * h, 128 * j + 64 * h + 64)
+            att_out[to, :] = dot_nn(v_t[part], prob.astype(jnp.bfloat16)).astype(jnp.bfloat16)
+
+
+def backward_pairs(
+    place, first_pair, grads, q_in, k_in, v_in, wo, prob_in, att_in, own, oth, keep_t, out_keep, send,
+    grad_s, att_s,
+):
+    half = grads[0].shape[0]
+    rows = 2 * half
+    for i, ref in enumerate(grads):
+        grad_s[i * half : (i + 1) * half, :] = ref[...]
+    low = lax.broadcasted_iota(jnp.int32, (rows, 128), 1) < 64
+    scale = jnp.bfloat16(0.125)
+    zero = jnp.zeros((rows, 128), jnp.bfloat16)
+    first = place[SIDE] == 0
+    count = own.shape[2] // 128
+    mine_rows = slice(128 * first_pair, 128 * (first_pair + count))
+    d_att = dot_nt(grad_s[...], wo[mine_rows, :]).astype(jnp.bfloat16)
+    for j in range(count):
+        cols = slice(128 * j, 128 * j + 128)
+        pair = slice(128 * (first_pair + j), 128 * (first_pair + j) + 128)
+        q = q_in[:, pair]
+        k = k_in[:, pair]
+        v = v_in[:, pair]
+        g = d_att[:, cols]
+        k_t = (k * scale).T
+        dq_t, dk, dv = [], [], []
+        for h in range(2):
+            mine = low if h == 0 else jnp.logical_not(low)
+            prob = prob_in[2 * (first_pair + j) + h]
+            dv.append(dot_nn(prob.astype(jnp.bfloat16), g))
             d_prob = dot_nt(v, jnp.where(mine, g, zero))
             total = jnp.sum(prob * d_prob, axis=0, keepdims=True)
             d_score = (prob * (d_prob - total)).astype(jnp.bfloat16)
-            dq_t.append(dot_nn(k_t[part], d_score))
+            dq_t.append(dot_nn(k_t[64 * h : 64 * h + 64], d_score))
             dk.append(dot_nn(d_score, q))
-        att_pair_t = jnp.concatenate(att_t, axis=0).astype(jnp.bfloat16)
+        att_pair_t = att_in[pair, :]
         dq_pair_t = jnp.concatenate(dq_t, axis=0).astype(jnp.bfloat16)
         dk_pair = jnp.where(low, dk[0], dk[1]).astype(jnp.bfloat16)
         dv_pair = jnp.where(low, dv[0], dv[1]).astype(jnp.bfloat16)
         for t, piece in enumerate((dq_pair_t.T, dk_pair, dv_pair, att_pair_t.T)):
             own[t, :, cols] = piece[:half]
             oth[t, :, cols] = piece[half:]
+        at = slice(64 * j, 64 * j + 64)
         for t, piece in enumerate((dq_pair_t, dk_pair.T, dv_pair.T)):
-            at = slice(64 * j, 64 * j + 64)
             part = slice(rows * t, rows * t + rows)
             keep_t[at, part] = jnp.where(first, piece[:64], piece[64:])
             send[at, part] = jnp.where(first, piece[64:], piece[:64])
-        at = slice(64 * j, 64 * j + 64)
         att_s[0, at, :] = jnp.where(first, att_pair_t[:64], att_pair_t[64:])
         att_s[1, at, :] = jnp.where(first, att_pair_t[64:], att_pair_t[:64])
     out_keep[...] = dot_nn(att_s[0], grad_s[...])
     send[:, 3 * rows :] = dot_nn(att_s[1], grad_s[...]).astype(send.dtype)
 
 
-def attend_first(place, p0, p1, p2, p3, *refs):
-    attend_pairs(place, 0, (p0, p1, p2, p3), *refs)
-
-
-def attend_second(place, p0, p1, p2, p3, w_in_hbm, w_out_hbm, after, *refs):
+def backward_second(place, g0, g1, *refs):
+    backward_pairs(place, 2, (g0, g1), *refs)
+
+
+def backward_first(place, g0, g1, q_in, k_in, v_in, wo, prob_in, att_in, after, *refs):
     del after
-    attend_pairs(place, 2, (p0, p1, p2, p3), w_in_hbm, w_out_hbm, *refs)
+    backward_pairs(place, 0, (g0, g1), q_in, k_in, v_in, wo, prob_in, att_in, *refs)
 
 
 def in_order(place, own, got):
@@ -438,8 +463,8 @@
     return jnp.concatenate(pieces, axis=1)
 
 
-def rows_kernel(place, own_a, got_a, own_b, got_b, w_ref, after, before, o0, o1, total):
-    del after, before
+def rows_kernel(place, own_a, got_a, own_b, got_b, w_ref, after, o0, o1, total):
+    del after
     step = pl.program_id(0)
     core = place[CORE]
     block = o0.shape[0] // 2
@@ -480,7 +505,7 @@
         inv_std = lax.rsqrt(spread + epsilon)
         unit = center * inv_std
         d_hidden = norm_backward(r_ref[rows:, :].astype(jnp.float32), gain_ref[...], unit, inv_std)
-        value = m_ref[rows:, :].astype(jnp.float32) + d_hidden
+        value = m_ref[...].astype(jnp.float32) + d_hidden
         d_patches[s] = jnp.where(live, value, 0.0).astype(d_patches.dtype)
 
 
@@ -505,43 +530,38 @@
 
 
 def weight_first(
-    place, keep, out_keep, got, p0, p1, p2, p3, n0, n1,
+    place, keep, out_keep, got, normed, n0, n1,
     part_keep, part_send, tokens, left, total, out_total,
 ):
-    block = p0.shape[0] // 2
-    rows = 4 * block
-    for i, ref in enumerate((p0, p1, p2, p3)):
-        tokens[i * block : (i + 1) * block, :] = ref[:block, :]
-    tokens[rows : rows + 2 * block, :] = n0[...]
-    tokens[rows + 2 * block :, :] = n1[...]
+    rows, half = normed.shape[0], n0.shape[0]
+    tokens[:half, :] = n0[...]
+    tokens[half:, :] = n1[...]
     for side, ref in enumerate((keep, got)):
         for i, at in enumerate((0, 2, 4, 5)):
             left[side, 64 * i : 64 * i + 64, :] = piece_of(ref, at, rows)
-    total[...] = dot_nn(left[0], tokens[:rows, :]) + dot_nn(left[1], tokens[rows:, :])
+    total[...] = dot_nn(left[0], normed[...]) + dot_nn(left[1], tokens[...])
     put_parts(place, total, out_keep, got, part_keep, part_send, out_total)
 
 
 def weight_second(
-    place, keep_a, got_a, keep_b, out_keep, got_b, p0, p1, p2, p3, n0, n1, after,
+    place, keep_a, got_a, keep_b, out_keep, got_b, normed, n0, n1, after, before,
     part_keep, part_send, tokens, left, total, out_total,
 ):
-    del after
-    block = p0.shape[0] // 2
-    rows = 4 * block
-    for i, ref in enumerate((p0, p1, p2, p3)):
-        tokens[i * block : (i + 1) * block, :] = ref[:block, :]
-    tokens[rows : rows + 2 * block, :] = n0[...]
-    tokens[rows + 2 * block :, :] = n1[...]
+    del after, before
+    rows, half = normed.shape[0], n0.shape[0]
+    tokens[:half, :] = n0[...]
+    tokens[half:, :] = n1[...]
     for side, (a, b) in enumerate(((keep_a, keep_b), (got_a, got_b))):
         for i, (ref, at) in enumerate(
             ((a, 1), (b, 0), (b, 1), (a, 3), (b, 2), (b, 3), (b, 4), (b, 5))
         ):
             left[side, 64 * i : 64 * i + 64, :] = piece_of(ref, at, rows)
-    total[...] = dot_nn(left[0], tokens[:rows, :]) + dot_nn(left[1], tokens[rows:, :])
+    total[...] = dot_nn(left[0], normed[...]) + dot_nn(left[1], tokens[...])
     put_parts(place, total, out_keep, got_b, part_keep, part_send, out_total)
 
 
-def pair_kernel(keep, got, mine, send):
+def pair_kernel(keep, got, *refs):
+    mine, send = refs[-2:]
     mine[...] = keep[0] + got[0].astype(jnp.float32)
     send[...] = (keep[1] + got[1].astype(jnp.float32)).astype(send.dtype)
 
@@ -647,69 +667,96 @@
 
     gain_row = gain.reshape(1, width)
     pay = struct((2 * slots, width))
-    hbm = pl.BlockSpec(memory_space=pl.ANY)
-    *mine, hidden = call(
+    block = struct((slots, width))
+    any_spec = pl.BlockSpec(memory_space=pl.ANY)
+    *normed, hidden = call(
         norm_kernel,
-        tuple(in_hbm(v) for v in (patches, cotangent, kept_index, gain_row)),
-        [pay, pay, struct(patches.shape, f32)],
+        tuple(in_hbm(v) for v in (patches, kept_index, gain_row)),
+        [block, block, struct(patches.shape, f32)],
         24,
         place,
         scratch=[
             pltpu.VMEM(patches.shape, bf16),
-            pltpu.VMEM(patches.shape, bf16),
             pltpu.VMEM(kept_index.shape, jnp.int32),
             pltpu.VMEM(gain_row.shape, f32),
-            pltpu.SemaphoreType.DMA((4,)),
+            pltpu.SemaphoreType.DMA((3,)),
         ],
-        specs=[hbm] * 4,
-    )
-    got = [to_chip(mine[k], k) for k in range(2)]
-    here = got + [to_core(v) for v in got]
-    from_x = to_x(jnp.concatenate([v[:slots] for v in got], axis=0))
+        specs=[any_spec] * 3,
+    )
+    mine = call(
+        grad_kernel,
+        (in_hbm(cotangent), normed[0]),
+        [block, block],
+        8,
+        place,
+        scratch=[pltpu.VMEM(patches.shape, bf16), pltpu.SemaphoreType.DMA(())],
+        specs=[any_spec] * 2,
+    )
+    got = [to_chip(normed[k], k) for k in range(2)]
+    got_g = [to_chip(mine[k], k) for k in range(2)]
+    joined = call(join_kernel, (*got, mine[0]), pay, 8, specs=[VMEM_SPEC] * 2 + [any_spec])
+    here = (joined, to_core(joined))
+    from_x = to_x(joined)
     there = (from_x, to_core(from_x))
 
-    any_spec = pl.BlockSpec(memory_space=pl.ANY)
     pairs = width // 512
+    own_cols = struct((rows, own_width))
+    normed, *saved = call(
+        forward_kernel,
+        (*here, in_hbm(w_qkv), in_hbm(w_out)),
+        [struct((rows, width))]
+        + [own_cols] * 3
+        + [struct((own_width, width)), struct((4 * pairs, rows, rows), f32), struct((own_width, rows))],
+        32,
+        place,
+        scratch=[pltpu.VMEM((width, own_width), bf16)] * 3 + [pltpu.SemaphoreType.DMA((8 * pairs,))],
+        specs=[VMEM_SPEC] * 2 + [any_spec] * 2,
+    )
+    joined = call(join_kernel, (*got_g, saved[0]), pay, 8, specs=[VMEM_SPEC] * 2 + [any_spec])
+    here_g = (joined, to_core(joined))
     half_rows = struct((4, 2 * slots, 128 * pairs))
     out_half = (64 * pairs, width)
     half_t = struct((64 * pairs, 3 * rows))
     half_send = struct((64 * pairs, 3 * rows + width))
 
-    def attend(kernel, extra):
+    def backward(kernel, extra):
         return call(
             kernel,
-            (*here, in_hbm(w_qkv), in_hbm(w_out), *extra),
+            (*here_g, *saved, *extra),
             [half_rows] * 2 + [half_t, struct(out_half, f32), half_send],
             32,
             place,
-            scratch=[pltpu.VMEM((rows, width), bf16)] * 2
-            + [pltpu.VMEM((2, 64 * pairs, rows), bf16)]
-            + [pltpu.VMEM((width, 128 * pairs), bf16)] * 3
-            + [pltpu.VMEM((128 * pairs, width), bf16), pltpu.SemaphoreType.DMA((4 * pairs,))],
-            specs=[VMEM_SPEC] * 4 + [any_spec] * (2 + len(extra)),
+            scratch=[pltpu.VMEM((rows, width), bf16), pltpu.VMEM((2, 64 * pairs, rows), bf16)],
+            specs=[VMEM_SPEC] * 8 + [any_spec] * len(extra),
         )
 
-    own_a, oth_a, keep_a, out_keep_a, send_a = attend(attend_first, ())
+    own_a, oth_a, keep_a, out_keep_a, send_a = backward(backward_first, (from_x,))
     got_a = to_x(send_a)
     core_a = to_core(oth_a)
-    own_b, oth_b, keep_b, out_keep_b, send_b = attend(attend_second, (from_x,))
+    own_b, oth_b, keep_b, out_keep_b, send_b = backward(backward_second, ())
     got_b = to_x(send_b)
     core_b = to_core(oth_b)
 
     def parts_of(kernel, args, tall, scratch, after=()):
         return call(
             kernel,
-            (*args, *here, *there, *after),
+            (*args, normed, *there, *after),
             [struct((2, tall, width), f32), struct((2, tall, width))],
             16,
             place,
-            scratch=[pltpu.VMEM((2 * rows, width), bf16)] + scratch + [pltpu.VMEM(out_half, f32)],
-            specs=[VMEM_SPEC] * (len(args) + 6) + [any_spec] * len(after),
+            scratch=[pltpu.VMEM((rows, width), bf16)] + scratch + [pltpu.VMEM(out_half, f32)],
+            specs=[VMEM_SPEC] * (len(args) + 3) + [any_spec] * len(after),
         )
 
-    def pair_sums(keep, part):
+    def pair_sums(keep, part, after=()):
         shape = keep.shape[1:]
-        mine, part = call(pair_kernel, (keep, along(part, 1)), [struct(shape, f32), struct(shape)], 8)
+        mine, part = call(
+            pair_kernel,
+            (keep, along(part, 1), *after),
+            [struct(shape, f32), struct(shape)],
+            8,
+            specs=[VMEM_SPEC] * 2 + [any_spec] * len(after),
+        )
         return mine, part, along(part, 2)
 
     def spread(mine, part, after=()):
@@ -730,32 +777,31 @@
         [pltpu.VMEM((2, 256, rows), bf16), pltpu.VMEM((256, width), f32)],
     )
     first_sum, paired, first_got = pair_sums(keep, part)
-    keep, part = parts_of(
-        weight_second,
-        (keep_a, got_a, keep_b, out_keep_b, got_b),
-        160,
-        [pltpu.VMEM((2, 512, rows), bf16), pltpu.VMEM((512, width), f32)],
-        (paired,),
-    )
-    started = part
-    second_sum, _, second_got = pair_sums(keep, part)
-    first = spread(first_sum, first_got)
     back = pl.pallas_call(
         rows_kernel,
         grid_spec=pltpu.PrefetchScalarGridSpec(
             num_scalar_prefetch=1,
             grid=(3,),
             in_specs=[pl.BlockSpec(half_rows.shape, lambda i, p: (0, 0, 0))] * 4
-            + [pl.BlockSpec((width, width), lambda i, p: (0, i)), any_spec, any_spec],
+            + [pl.BlockSpec((width, width), lambda i, p: (0, i)), any_spec],
             out_specs=[pl.BlockSpec(pay.shape, lambda i, p: (0, 0))] * 2,
             scratch_shapes=[pltpu.VMEM((2 * slots, width), f32)],
         ),
         out_shape=[pay] * 2,
         compiler_params=pltpu.CompilerParams(vmem_limit_bytes=20 * MIB),
         cost_estimate=COST,
-    )(place, own_a, core_a, own_b, core_b, in_hbm(w_qkv), started, first[1])
-    second = spread(second_sum, second_got, (back[0],))
+    )(place, own_a, core_a, own_b, core_b, in_hbm(w_qkv), part)
+    keep, part = parts_of(
+        weight_second,
+        (keep_a, got_a, keep_b, out_keep_b, got_b),
+        160,
+        [pltpu.VMEM((2, 512, rows), bf16), pltpu.VMEM((512, width), f32)],
+        (paired, back[0]),
+    )
     back = [to_rows(back[k], k, 0) for k in range(2)]
+    second_sum, _, second_got = pair_sums(keep, part, (back[0],))
+    first = spread(first_sum, first_got)
+    second = spread(second_sum, second_got, (back[1], first[1]))
     encoded, d_patches = call(
         return_kernel,
         (*back, w_out, hidden, *mine, gain_row),

time: 128 us -> 131 us (1.023)
  Pallas kernels: 30.9 us -> 34.3 us
  starting transfers between devices: 35.3 us -> 32.6 us
  waiting for transfers between devices: 59.5 us -> 61.9 us
    pallas_call x11 -> x15, Pallas kernels: 25.1 us -> 28.5 us  [call(): pl.pallas_call(kernel, in_specs=specs, out_specs=VMEM_SPEC if single else...]
    ppermute x22 -> x24, starting transfers between devices: 35.3 us -> 32.6 us  [send(): return lax.ppermute(value, AXES, line_perm(move, reps))]
    ppermute x22 -> x24, waiting for transfers between devices: 59.5 us -> 61.9 us  [send(): return lax.ppermute(value, AXES, line_perm(move, reps))]
  transfers between devices with their start and end apart: 22 -> 24, of which waited for: 11 -> 11; matrix products, arithmetic and copies ran while one was open for 0% -> 0% of each run, Pallas kernels for 19% -> 18%
where the time goes in v6:
time: 131 us; the launch traced here: 130 us
  waiting for transfers between devices  61.9 us (47%)
  Pallas kernels  34.3 us (26%)
  starting transfers between devices  32.6 us (25%)
    ppermute x24, waiting for transfers between devices, send(): return lax.ppermute(value, AXES, line_perm(move, reps))  61.9 us
    ppermute x24, starting transfers between devices, send(): return lax.ppermute(value, AXES, line_perm(move, reps))  32.6 us
    pallas_call x15, Pallas kernels, call(): pl.pallas_call(kernel, in_specs=specs, out_specs=VMEM_SPEC if single else...  28.5 us
    pallas_call x1, Pallas kernels, chip_shards(): pl.pallas_call(rows_kernel, grid_spec=pltpu.PrefetchScalarGridSpec(num_sc...  5.82 us
  transfers between devices with their start and end apart: 24, of which 11 were waited for; matrix products, arithmetic and copies ran while one was open for 0% of the time, Pallas kernels for 18%

profile of v6, /device:TPU:1, one launch (start us, length us, event | category | flops | bytes accessed | tf_op | source)
XLA Modules:
  0.0 130.4 jit_solution(17316616409747635148)
XLA Ops:
  0.6 0.7 concatenate.3.place
  1.4 2.2 %shard_map.102 = (bf16[96,1024]{1,0:T(8,128)(2,1)S(1)}, bf16[96,1024]{1,0:T(8,128)(2,1)S(1)}, f32[2,96,1024]{2,1,0:T(8,128)S(1)}) custom-call(s32[6]{0:T(128)S(1)} %concatenate.3.place, bf16[2,96,1024]{2,1,0:T(8,128)(2,1)} %patch_hbm.1, s32[2,96]{1,0:T(2,128)} %index_hbm.1, f32[1,1024]{1,0:T(1,128)} %bitcast.6), custom_call_target="tpu_custom_call" | custom-call | flops 1000 | bytes 1000 | tf_op jit(solution)/shard_map/pallas_call | solution.py:625
  3.5 5.6 %collective-permute-start.2 = (bf16[96,1024]{1,0:T(8,128)(2,1)S(1)}, bf16[96,1024]{1,0:T(8,128)(2,1)S(1)}, u32[]{:S(2)}, u32[]{:S(2)}) collective-permute-start(bf16[96,1024]{1,0:T(8,128)(2,1)S(1)} %get-tuple-element.40.after), channel_id=1, source_target_pairs={{0,0},{1,8},{2,2},{3,10},{4,4},{5,12},{6,6},{7,14},{8,1},{9,9},{10... | collective-permute-start | bytes 589832 | tf_op jit(solution)/shard_map/ppermute | solution.py:651
  9.1 1.1 collective-permute-start.3
  10.2 1.6 %shard_map.103 = (bf16[96,1024]{1,0:T(8,128)(2,1)S(1)}, bf16[96,1024]{1,0:T(8,128)(2,1)S(1)}) custom-call(s32[6]{0:T(128)S(1)} %concatenate.3.place, bf16[2,96,1024]{2,1,0:T(8,128)(2,1)} %cot_hbm.1, bf16[96,1024]{1,0:T(8,128)(2,1)S(1)} %get-tuple-element.40.after), custom_call_target="tpu_custom_call" | custom-call | flops 1000 | bytes 1000 | tf_op jit(solution)/shard_map/pallas_call | solution.py:625
  11.8 4.9 %collective-permute-done.2.a = bf16[96,1024]{1,0:T(8,128)(2,1)S(1)} collective-permute-done((bf16[96,1024]{1,0:T(8,128)(2,1)S(1)}, bf16[96,1024]{1,0:T(8,128)(2,1)S(1)}, u32[]{:S(2)}, u32[]{:S(2)}) %collective-permute-start.2) | collective-permute-done | bytes 196640 | tf_op jit(solution)/shard_map/ppermute | solution.py:651
  16.8 6.7 %collective-permute-start = (bf16[96,1024]{1,0:T(8,128)(2,1)S(1)}, bf16[96,1024]{1,0:T(8,128)(2,1)S(1)}, u32[]{:S(2)}, u32[]{:S(2)}) collective-permute-start(bf16[96,1024]{1,0:T(8,128)(2,1)S(1)} %get-tuple-element.41.after.m0), channel_id=1, source_target_pairs={{0,0},{1,8},{2,2},{3,10},{4,4},{5,12},{6,6},{7,14},{8,1},{9,9},{10... | collective-permute-start | bytes 589832 | tf_op jit(solution)/shard_map/ppermute | solution.py:651
  23.8 1.2 collective-permute-start.6
  25.0 8.0 %shard_map.105 = (bf16[384,1024]{1,0:T(8,128)(2,1)S(1)}, bf16[384,512]{1,0:T(8,128)(2,1)S(1)}, bf16[384,512]{1,0:T(8,128)(2,1)S(1)}, bf16[384,512]{1,0:T(8,128)(...) custom-call(s32[6]{0:T(128)S(1)} %concatenate.3.place, ...), custom_call_target="tpu_custom_call" | custom-call | flops 1000 | bytes 1000 | tf_op jit(solution)/shard_map/pallas_call | solution.py:625
  33.1 1.7 %collective-permute-done.5.g1 = bf16[192,1024]{1,0:T(8,128)(2,1)S(1)} collective-permute-done((bf16[192,1024]{1,0:T(8,128)(2,1)S(1)}, bf16[192,1024]{1,0:T(8,128)(2,1)S(1)}, u32[]{:S(2)}, u32[]{:S(2)}) %collective-permute-start.5) | collective-permute-done | bytes 393248 | tf_op jit(solution)/shard_map/ppermute | solution.py:651
  34.8 3.7 %shard_map.107 = (bf16[4,192,256]{2,1,0:T(8,128)(2,1)S(1)}, bf16[4,192,256]{2,1,0:T(8,128)(2,1)S(1)}, bf16[128,1152]{1,0:T(8,128)(2,1)S(1)}, f32[128,1024]{1,0:T(8,128)S(1)}, bf16[128,2176]{1,0:T(8,128)(2,1)S(1)}) custom-call(s32[6]{0:T(128)S(1)} %concatenate.3.place, bf16[192,1024]{1,0:T(8,128)(2,1)S(1)} %shard_map.106.g0, ...), custom_call_target="tpu_custom_call" | custom-call | flops 1000 | bytes 1000 | tf_op jit(solution)/shard_map/pallas_call | solution.py:625
  39.3 3.7 %shard_map.108 = (bf16[4,192,256]{2,1,0:T(8,128)(2,1)S(1)}, bf16[4,192,256]{2,1,0:T(8,128)(2,1)S(1)}, bf16[128,1152]{1,0:T(8,128)(2,1)S(1)}, f32[128,1024]{1,0:T(8,128)S(1)}, bf16[128,2176]{1,0:T(8,128)(2,1)S(1)}) custom-call(s32[6]{0:T(128)S(1)} %concatenate.3.place, bf16[192,1024]{1,0:T(8,128)(2,1)S(1)} %shard_map.106.g0, ...), custom_call_target="tpu_custom_call" | custom-call | flops 1000 | bytes 1000 | tf_op jit(solution)/shard_map/pallas_call | solution.py:625
  43.0 1.3 collective-permute-start.18
  44.8 7.9 %collective-permute-done.9.got.got_a = bf16[128,2176]{1,0:T(8,128)(2,1)S(1)} collective-permute-done((bf16[128,2176]{1,0:T(8,128)(2,1)S(1)}, bf16[128,2176]{1,0:T(8,128)(2,1)S(1)}, u32[]{:S(2)}, u32[]{:S(2)}) %collective-permute-start.9) | collective-permute-done | bytes 557088 | tf_op jit(solution)/shard_map/ppermute | solution.py:651
  52.7 1.4 %shard_map.109 = (f32[2,96,1024]{2,1,0:T(8,128)S(1)}, bf16[2,96,1024]{2,1,0:T(8,128)(2,1)S(1)}) custom-call(s32[6]{0:T(128)S(1)} %concatenate.3.place, bf16[128,1152]{1,0:T(8,128)(2,1)S(1)} %get-tuple-element.54.keep.keep_a, f32[128,1024]{1,0:T(8,128)S(1)} %get-tuple-element.55.out_keep, bf16[128,2176]{1,0:T(8,128)(2,1)S(1)} %collective-permute-done.9.got.got_a, ...), custom_call_target="tpu_custom_call" | custom-call | flops 1000 | bytes 1000 | tf_op jit(solution)/shard_map/pallas_call | solution.py:625
  54.6 5.8 %shard_map.110 = (bf16[192,1024]{1,0:T(8,128)(2,1)S(1)}, bf16[192,1024]{1,0:T(8,128)(2,1)S(1)}) custom-call(s32[6]{0:T(128)S(1)} %concatenate.3.place, bf16[4,192,256]{2,1,0:T(8,128)(2,1)S(1)} %get-tuple-element.50.own_a, bf16[4,192,256]{2,1,0:T(8,128)(2,1)S(1)} %collective-permute-done.7.got_a, bf16[4,192,256]{2,1,0:T(8,128)(2,1)S(1)} %get-tuple-element.52.own_b, ...), custom_call_target="tpu_custom_call" | custom-call | flops 1000 | bytes 1000 | tf_op jit(solution)/shard_map/pallas_call | solution.py:780
  60.5 2.8 %collective-permute-done.13.got = bf16[2,96,1024]{2,1,0:T(8,128)(2,1)S(1)} collective-permute-done((bf16[2,96,1024]{2,1,0:T(8,128)(2,1)S(1)}, bf16[2,96,1024]{2,1,0:T(8,128)(2,1)S(1)}, u32[]{:S(2)}, u32[]{:S(2)}) %collective-permute-start.13) | collective-permute-done | bytes 393248 | tf_op jit(solution)/shard_map/ppermute | solution.py:651
  63.3 1.3 collective-permute-done.18.got_b
  64.6 2.0 %shard_map.114 = (f32[2,160,1024]{2,1,0:T(8,128)S(1)}, bf16[2,160,1024]{2,1,0:T(8,128)(2,1)S(1)}) custom-call(s32[6]{0:T(128)S(1)} %concatenate.3.place, bf16[128,1152]{1,0:T(8,128)(2,1)S(1)} %get-tuple-element.54.keep.keep_a, bf16[128,2176]{1,0:T(8,128)(2,1)S(1)} %collective-permute-done.9.got.got_a, bf16[128,1152]{1,0:T(8,128)(2,1)S(1)} %get-tuple-element.67.keep_b, ...), custom_call_target="tpu_custom_call" | custom-call | flops 1000 | bytes 1000 | tf_op jit(solution)/shard_map/pallas_call | solution.py:625
  67.2 6.2 %collective-permute-start.11 = (bf16[192,1024]{1,0:T(8,128)(2,1)S(1)}, bf16[192,1024]{1,0:T(8,128)(2,1)S(1)}, u32[]{:S(2)}, u32[]{:S(2)}) collective-permute-start(bf16[192,1024]{1,0:T(8,128)(2,1)S(1)} %get-tuple-element.59.before), channel_id=1, source_target_pairs={{0,0},{1,8},{2,2},{3,10},{4,4},{5,12},{6,6},{7,14},{8,1},{9,9},{10... | collective-permute-start | bytes 1179656 | tf_op jit(solution)/shard_map/ppermute | solution.py:651
  73.6 15.0 %collective-permute-done.11.r0.refs_0_ = bf16[192,1024]{1,0:T(8,128)(2,1)S(1)} collective-permute-done((bf16[192,1024]{1,0:T(8,128)(2,1)S(1)}, bf16[192,1024]{1,0:T(8,128)(2,1)S(1)}, u32[]{:S(2)}, u32[]{:S(2)}) %collective-permute-start.11) | collective-permute-done | bytes 393248 | tf_op jit(solution)/shard_map/ppermute | solution.py:651
  88.6 1.7 %collective-permute-done.19.got = bf16[2,160,1024]{2,1,0:T(8,128)(2,1)S(1)} collective-permute-done((bf16[2,160,1024]{2,1,0:T(8,128)(2,1)S(1)}, bf16[2,160,1024]{2,1,0:T(8,128)(2,1)S(1)}, u32[]{:S(2)}, u32[]{:S(2)}) %collective-permute-start.19) | collective-permute-done | bytes 655392 | tf_op jit(solution)/shard_map/ppermute | solution.py:651
  90.4 1.2 collective-permute-start.20
  91.6 1.2 collective-permute-done.14.got
  92.8 1.3 collective-permute-start.15
  94.1 10.8 %collective-permute-done.12.r1.refs_0_ = bf16[192,1024]{1,0:T(8,128)(2,1)S(1)} collective-permute-done((bf16[192,1024]{1,0:T(8,128)(2,1)S(1)}, bf16[192,1024]{1,0:T(8,128)(2,1)S(1)}, u32[]{:S(2)}, u32[]{:S(2)}) %collective-permute-start.12) | collective-permute-done | bytes 393248 | tf_op jit(solution)/shard_map/ppermute | solution.py:651
  104.9 9.0 %collective-permute-done.20.got = bf16[160,1024]{1,0:T(8,128)(2,1)S(1)} collective-permute-done((bf16[160,1024]{1,0:T(8,128)(2,1)S(1)}, bf16[160,1024]{1,0:T(8,128)(2,1)S(1)}, u32[]{:S(2)}, u32[]{:S(2)}) %collective-permute-start.20) | collective-permute-done | bytes 327712 | tf_op jit(solution)/shard_map/ppermute | solution.py:651
  114.3 1.8 %collective-permute-start.22 = (bf16[160,1024]{1,0:T(8,128)(2,1)S(1)}, bf16[160,1024]{1,0:T(8,128)(2,1)S(1)}, u32[]{:S(2)}, u32[]{:S(2)}) collective-permute-start(bf16[160,1024]{1,0:T(8,128)(2,1)S(1)} %shard_map.116.b0), channel_id=1, source_target_pairs={{0,1},{1,0},{2,3},{3,2},{4,5},{5,4},{6,7},{7,6},{8,9},{9,8},{10,11... | collective-permute-start | bytes 983048 | tf_op jit(solution)/shard_map/ppermute | solution.py:651
  116.1 5.7 %collective-permute-done.21.b1 = bf16[160,1024]{1,0:T(8,128)(2,1)S(1)} collective-permute-done((bf16[160,1024]{1,0:T(8,128)(2,1)S(1)}, bf16[160,1024]{1,0:T(8,128)(2,1)S(1)}, u32[]{:S(2)}, u32[]{:S(2)}) %collective-permute-start.21) | collective-permute-done | bytes 327712 | tf_op jit(solution)/shard_map/ppermute | solution.py:651
  121.7 2.4 %collective-permute-start.23 = (bf16[160,1024]{1,0:T(8,128)(2,1)S(1)}, bf16[160,1024]{1,0:T(8,128)(2,1)S(1)}, u32[]{:S(2)}, u32[]{:S(2)}) collective-permute-start(bf16[160,1024]{1,0:T(8,128)(2,1)S(1)} %collective-permute-done.21.b1), channel_id=1, source_target_pairs={{0,1},{1,0},{2,3},{3,2},{4,5},{5,4},{6,7},{7,6},{8,9},{9,8},{10,11... | collective-permute-start | bytes 983048 | tf_op jit(solution)/shard_map/ppermute | solution.py:651
  124.7 2.6 %shard_map.111 = (bf16[2,96,1024]{2,1,0:T(8,128)(2,1)}, bf16[2,96,1024]{2,1,0:T(8,128)(2,1)}) custom-call(s32[6]{0:T(128)S(1)} %concatenate.3.place, bf16[192,1024]{1,0:T(8,128)(2,1)S(1)} %collective-permute-done.11.r0.refs_0_, bf16[192,1024]{1,0:T(8,128)(2,1)S(1)} %collective-permute-done.12.r1.refs_0_, bf16[1024,1024]{1,0:T(8,128)(2,1)S(1)} %copy-done, ...), custom_call_target="tpu_custom_call" | custom-call | flops 1000 | bytes 1000 | tf_op jit(solution)/shard_map/pallas_call | solution.py:625
  127.3 3.0 %shard_map.117 = (f32[1024,768]{1,0:T(8,128)}, f32[1024,256]{1,0:T(8,128)}) custom-call(s32[6]{0:T(128)S(1)} %concatenate.3.place, bf16[96,1024]{1,0:T(8,128)(2,1)S(1)} %shard_map.113.a0, bf16[96,1024]{1,0:T(8,128)(2,1)S(1)} %collective-permute-done.15.refs_1_.a1, bf16[96,1024]{1,0:T(8,128)(2,1)S(1)} %collective-permute-done.16.a2, ...), custom_call_target="tpu_custom_call" | custom-call | flops 1000 | bytes 1000 | tf_op jit(solution)/shard_map/pallas_call | solution.py:625
  (37 shorter events, 4.1 us)
Async XLA Ops:
  3.5 13.2 %collective-permute-start.2 = (bf16[96,1024]{1,0:T(8,128)(2,1)S(1)}, bf16[96,1024]{1,0:T(8,128)(2,1)S(1)}, u32[]{:S(2)}, u32[]{:S(2)}) collective-permute-start(bf16[96,1024]{1,0:T(8,128)(2,1)S(1)} %get-tuple-element.40.after), channel_id=1, source_target_pairs={{0,0},{1,8},{2,2},{3,10},{4,4},{5,12},{6,6},{7,14},{8,1},{9,9},{10... | collective-permute-start | bytes 589832 | tf_op jit(solution)/shard_map/ppermute | solution.py:651
  9.1 7.6 %collective-permute-start.3 = (bf16[96,1024]{1,0:T(8,128)(2,1)S(1)}, bf16[96,1024]{1,0:T(8,128)(2,1)S(1)}, u32[]{:S(2)}, u32[]{:S(2)}) collective-permute-start(bf16[96,1024]{1,0:T(8,128)(2,1)S(1)} %get-tuple-element.43), channel_id=1, source_target_pairs={{0,4},{1,12},{2,6},{3,14},{4,0},{5,8},{6,2},{7,10},{8,5},{9,13},{1... | collective-permute-start | bytes 589832 | tf_op jit(solution)/shard_map/ppermute | solution.py:651
  16.7 8.3 %collective-permute-start.4 = (bf16[192,1024]{1,0:T(8,128)(2,1)S(1)}, bf16[192,1024]{1,0:T(8,128)(2,1)S(1)}, u32[]{:S(2)}, u32[]{:S(2)}) collective-permute-start(bf16[192,1024]{1,0:T(8,128)(2,1)S(1)} %shard_map.104.n0), channel_id=1, source_target_pairs={{0,1},{1,0},{2,3},{3,2},{4,5},{5,4},{6,7},{7,6},{8,9},{9,8},{10,11... | collective-permute-start | bytes 1179656 | tf_op jit(solution)/shard_map/ppermute | solution.py:651
  16.8 16.2 %collective-permute-start = (bf16[96,1024]{1,0:T(8,128)(2,1)S(1)}, bf16[96,1024]{1,0:T(8,128)(2,1)S(1)}, u32[]{:S(2)}, u32[]{:S(2)}) collective-permute-start(bf16[96,1024]{1,0:T(8,128)(2,1)S(1)} %get-tuple-element.41.after.m0), channel_id=1, source_target_pairs={{0,0},{1,8},{2,2},{3,10},{4,4},{5,12},{6,6},{7,14},{8,1},{9,9},{10... | collective-permute-start | bytes 589832 | tf_op jit(solution)/shard_map/ppermute | solution.py:651
  23.6 9.4 %collective-permute-start.1 = (bf16[96,1024]{1,0:T(8,128)(2,1)S(1)}, bf16[96,1024]{1,0:T(8,128)(2,1)S(1)}, u32[]{:S(2)}, u32[]{:S(2)}) collective-permute-start(bf16[96,1024]{1,0:T(8,128)(2,1)S(1)} %get-tuple-element.42.m1), channel_id=1, source_target_pairs={{0,4},{1,12},{2,6},{3,14},{4,0},{5,8},{6,2},{7,10},{8,5},{9,13},{1... | collective-permute-start | bytes 589832 | tf_op jit(solution)/shard_map/ppermute | solution.py:651
  23.8 9.3 %collective-permute-start.6 = (bf16[192,1024]{1,0:T(8,128)(2,1)S(1)}, bf16[192,1024]{1,0:T(8,128)(2,1)S(1)}, u32[]{:S(2)}, u32[]{:S(2)}) collective-permute-start(bf16[192,1024]{1,0:T(8,128)(2,1)S(1)} %shard_map.104.n0), channel_id=1, source_target_pairs={{0,2},{1,3},{2,0},{3,1},{4,6},{5,7},{6,4},{7,5},{8,10},{9,11},{10,... | collective-permute-start | bytes 1179656 | tf_op jit(solution)/shard_map/ppermute | solution.py:651
  33.0 1.8 %collective-permute-start.5 = (bf16[192,1024]{1,0:T(8,128)(2,1)S(1)}, bf16[192,1024]{1,0:T(8,128)(2,1)S(1)}, u32[]{:S(2)}, u32[]{:S(2)}) collective-permute-start(bf16[192,1024]{1,0:T(8,128)(2,1)S(1)} %shard_map.106.g0), channel_id=1, source_target_pairs={{0,1},{1,0},{2,3},{3,2},{4,5},{5,4},{6,7},{7,6},{8,9},{9,8},{10,11... | collective-permute-start | bytes 1179656 | tf_op jit(solution)/shard_map/ppermute | solution.py:651
  38.5 14.2 %collective-permute-start.9 = (bf16[128,2176]{1,0:T(8,128)(2,1)S(1)}, bf16[128,2176]{1,0:T(8,128)(2,1)S(1)}, u32[]{:S(2)}, u32[]{:S(2)}) collective-permute-start(bf16[128,2176]{1,0:T(8,128)(2,1)S(1)} %get-tuple-element.56), channel_id=1, source_target_pairs={{0,2},{1,3},{2,0},{3,1},{4,6},{5,7},{6,4},{7,5},{8,10},{9,11},{10,... | collective-permute-start | bytes 1671176 | tf_op jit(solution)/shard_map/ppermute | solution.py:651
  38.8 5.9 %collective-permute-start.10 = (bf16[192,1024]{1,0:T(8,128)(2,1)S(1)}, bf16[192,1024]{1,0:T(8,128)(2,1)S(1)}, u32[]{:S(2)}, u32[]{:S(2)}) collective-permute-start(bf16[192,1024]{1,0:T(8,128)(2,1)S(1)} %collective-permute-done.6.after.n0), channel_id=1, source_target_pairs={{0,1},{1,0},{2,3},{3,2},{4,5},{5,4},{6,7},{7,6},{8,9},{9,8},{10,11... | collective-permute-start | bytes 1179656 | tf_op jit(solution)/shard_map/ppermute | solution.py:651
  43.0 21.7 %collective-permute-start.18 = (bf16[128,2176]{1,0:T(8,128)(2,1)S(1)}, bf16[128,2176]{1,0:T(8,128)(2,1)S(1)}, u32[]{:S(2)}, u32[]{:S(2)}) collective-permute-start(bf16[128,2176]{1,0:T(8,128)(2,1)S(1)} %get-tuple-element.69), channel_id=1, source_target_pairs={{0,2},{1,3},{2,0},{3,1},{4,6},{5,7},{6,4},{7,5},{8,10},{9,11},{10,... | collective-permute-start | bytes 1671176 | tf_op jit(solution)/shard_map/ppermute | solution.py:651
  44.3 10.4 %collective-permute-start.7 = (bf16[4,192,256]{2,1,0:T(8,128)(2,1)S(1)}, bf16[4,192,256]{2,1,0:T(8,128)(2,1)S(1)}, u32[]{:S(2)}, u32[]{:S(2)}) collective-permute-start(bf16[4,192,256]{2,1,0:T(8,128)(2,1)S(1)} %get-tuple-element.51), channel_id=1, source_target_pairs={{0,1},{1,0},{2,3},{3,2},{4,5},{5,4},{6,7},{7,6},{8,9},{9,8},{10,11... | collective-permute-start | bytes 1179656 | tf_op jit(solution)/shard_map/ppermute | solution.py:651
  44.6 10.0 %collective-permute-start.8 = (bf16[4,192,256]{2,1,0:T(8,128)(2,1)S(1)}, bf16[4,192,256]{2,1,0:T(8,128)(2,1)S(1)}, u32[]{:S(2)}, u32[]{:S(2)}) collective-permute-start(bf16[4,192,256]{2,1,0:T(8,128)(2,1)S(1)} %get-tuple-element.53), channel_id=1, source_target_pairs={{0,1},{1,0},{2,3},{3,2},{4,5},{5,4},{6,7},{7,6},{8,9},{9,8},{10,11... | collective-permute-start | bytes 1179656 | tf_op jit(solution)/shard_map/ppermute | solution.py:651
  54.1 9.2 %collective-permute-start.13 = (bf16[2,96,1024]{2,1,0:T(8,128)(2,1)S(1)}, bf16[2,96,1024]{2,1,0:T(8,128)(2,1)S(1)}, u32[]{:S(2)}, u32[]{:S(2)}) collective-permute-start(bf16[2,96,1024]{2,1,0:T(8,128)(2,1)S(1)} %get-tuple-element.58.after), channel_id=1, source_target_pairs={{0,4},{1,5},{2,6},{3,7},{4,0},{5,1},{6,2},{7,3},{8,12},{9,13},{10,... | collective-permute-start | bytes 1179656 | tf_op jit(solution)/shard_map/ppermute | solution.py:651
  66.6 58.0 %copy-start = (bf16[1024,1024]{1,0:T(8,128)(2,1)S(1)}, bf16[1024,1024]{1,0:T(8,128)(2,1)}, u32[]{:S(2)}) copy-start(bf16[1024,1024]{1,0:T(8,128)(2,1)} %w_ref.3) | copy-start | bytes 6291460
  66.6 58.0 %copy-start.1 = (f32[1024]{0:T(1024)S(1)}, f32[1024]{0:T(1024)}, u32[]{:S(2)}) copy-start(f32[1024]{0:T(1024)} %param.13) | copy-start | bytes 12292
  66.7 23.6 %collective-permute-start.19 = (bf16[2,160,1024]{2,1,0:T(8,128)(2,1)S(1)}, bf16[2,160,1024]{2,1,0:T(8,128)(2,1)S(1)}, u32[]{:S(2)}, u32[]{:S(2)}) collective-permute-start(bf16[2,160,1024]{2,1,0:T(8,128)(2,1)S(1)} %get-tuple-element.71), channel_id=1, source_target_pairs={{0,4},{1,5},{2,6},{3,7},{4,0},{5,1},{6,2},{7,3},{8,12},{9,13},{10,... | collective-permute-start | bytes 1966088 | tf_op jit(solution)/shard_map/ppermute | solution.py:651
  67.2 21.4 %collective-permute-start.11 = (bf16[192,1024]{1,0:T(8,128)(2,1)S(1)}, bf16[192,1024]{1,0:T(8,128)(2,1)S(1)}, u32[]{:S(2)}, u32[]{:S(2)}) collective-permute-start(bf16[192,1024]{1,0:T(8,128)(2,1)S(1)} %get-tuple-element.59.before), channel_id=1, source_target_pairs={{0,0},{1,8},{2,2},{3,10},{4,4},{5,12},{6,6},{7,14},{8,1},{9,9},{10... | collective-permute-start | bytes 1179656 | tf_op jit(solution)/shard_map/ppermute | solution.py:651
  73.4 19.3 %collective-permute-start.14 = (bf16[96,1024]{1,0:T(8,128)(2,1)S(1)}, bf16[96,1024]{1,0:T(8,128)(2,1)S(1)}, u32[]{:S(2)}, u32[]{:S(2)}) collective-permute-start(bf16[96,1024]{1,0:T(8,128)(2,1)S(1)} %get-tuple-element.66.after), channel_id=1, source_target_pairs={{0,8},{1,9},{2,10},{3,11},{4,12},{5,13},{6,14},{7,15},{8,0},{9,1},... | collective-permute-start | bytes 589832 | tf_op jit(solution)/shard_map/ppermute | solution.py:651
  73.5 31.4 %collective-permute-start.12 = (bf16[192,1024]{1,0:T(8,128)(2,1)S(1)}, bf16[192,1024]{1,0:T(8,128)(2,1)S(1)}, u32[]{:S(2)}, u32[]{:S(2)}) collective-permute-start(bf16[192,1024]{1,0:T(8,128)(2,1)S(1)} %get-tuple-element.60), channel_id=1, source_target_pairs={{0,4},{1,12},{2,6},{3,14},{4,0},{5,8},{6,2},{7,10},{8,5},{9,13},{1... | collective-permute-start | bytes 1179656 | tf_op jit(solution)/shard_map/ppermute | solution.py:651
  90.4 23.5 %collective-permute-start.20 = (bf16[160,1024]{1,0:T(8,128)(2,1)S(1)}, bf16[160,1024]{1,0:T(8,128)(2,1)S(1)}, u32[]{:S(2)}, u32[]{:S(2)}) collective-permute-start(bf16[160,1024]{1,0:T(8,128)(2,1)S(1)} %get-tuple-element.73), channel_id=1, source_target_pairs={{0,8},{1,9},{2,10},{3,11},{4,12},{5,13},{6,14},{7,15},{8,0},{9,1},... | collective-permute-start | bytes 983048 | tf_op jit(solution)/shard_map/ppermute | solution.py:651
  92.8 12.1 %collective-permute-start.15 = (bf16[96,1024]{1,0:T(8,128)(2,1)S(1)}, bf16[96,1024]{1,0:T(8,128)(2,1)S(1)}, u32[]{:S(2)}, u32[]{:S(2)}) collective-permute-start(bf16[96,1024]{1,0:T(8,128)(2,1)S(1)} %shard_map.113.a0), channel_id=1, source_target_pairs={{0,2},{1,3},{2,0},{3,1},{4,6},{5,7},{6,4},{7,5},{8,10},{9,11},{10,... | collective-permute-start | bytes 589832 | tf_op jit(solution)/shard_map/ppermute | solution.py:651
  114.0 7.8 %collective-permute-start.21 = (bf16[160,1024]{1,0:T(8,128)(2,1)S(1)}, bf16[160,1024]{1,0:T(8,128)(2,1)S(1)}, u32[]{:S(2)}, u32[]{:S(2)}) collective-permute-start(bf16[160,1024]{1,0:T(8,128)(2,1)S(1)} %shard_map.116.b0), channel_id=1, source_target_pairs={{0,2},{1,3},{2,0},{3,1},{4,6},{5,7},{6,4},{7,5},{8,10},{9,11},{10,... | collective-permute-start | bytes 983048 | tf_op jit(solution)/shard_map/ppermute | solution.py:651
  114.3 13.0 %collective-permute-start.22 = (bf16[160,1024]{1,0:T(8,128)(2,1)S(1)}, bf16[160,1024]{1,0:T(8,128)(2,1)S(1)}, u32[]{:S(2)}, u32[]{:S(2)}) collective-permute-start(bf16[160,1024]{1,0:T(8,128)(2,1)S(1)} %shard_map.116.b0), channel_id=1, source_target_pairs={{0,1},{1,0},{2,3},{3,2},{4,5},{5,4},{6,7},{7,6},{8,9},{9,8},{10,11... | collective-permute-start | bytes 983048 | tf_op jit(solution)/shard_map/ppermute | solution.py:651
  121.7 5.6 %collective-permute-start.23 = (bf16[160,1024]{1,0:T(8,128)(2,1)S(1)}, bf16[160,1024]{1,0:T(8,128)(2,1)S(1)}, u32[]{:S(2)}, u32[]{:S(2)}) collective-permute-start(bf16[160,1024]{1,0:T(8,128)(2,1)S(1)} %collective-permute-done.21.b1), channel_id=1, source_target_pairs={{0,1},{1,0},{2,3},{3,2},{4,5},{5,4},{6,7},{7,6},{8,9},{9,8},{10,11... | collective-permute-start | bytes 983048 | tf_op jit(solution)/shard_map/ppermute | solution.py:651
  124.2 3.1 %collective-permute-start.16 = (bf16[96,1024]{1,0:T(8,128)(2,1)S(1)}, bf16[96,1024]{1,0:T(8,128)(2,1)S(1)}, u32[]{:S(2)}, u32[]{:S(2)}) collective-permute-start(bf16[96,1024]{1,0:T(8,128)(2,1)S(1)} %shard_map.113.a0), channel_id=1, source_target_pairs={{0,1},{1,0},{2,3},{3,2},{4,5},{5,4},{6,7},{7,6},{8,9},{9,8},{10,11... | collective-permute-start | bytes 589832 | tf_op jit(solution)/shard_map/ppermute | solution.py:651
  124.2 3.1 %collective-permute-start.17 = (bf16[96,1024]{1,0:T(8,128)(2,1)S(1)}, bf16[96,1024]{1,0:T(8,128)(2,1)S(1)}, u32[]{:S(2)}, u32[]{:S(2)}) collective-permute-start(bf16[96,1024]{1,0:T(8,128)(2,1)S(1)} %collective-permute-done.15.refs_1_.a1), channel_id=1, source_target_pairs={{0,1},{1,0},{2,3},{3,2},{4,5},{5,4},{6,7},{7,6},{8,9},{9,8},{10,11... | collective-permute-start | bytes 589832 | tf_op jit(solution)/shard_map/ppermute | solution.py:651

commit v7 on v5

--- a/solution.py
+++ b/solution.py
@@ -350,7 +350,7 @@
 
 
 def attend_pairs(
-    place, first_pair, payloads, w_in_hbm, w_out_hbm, own, oth, keep_t, out_keep, send,
+    place, first_pair, payloads, w_in_hbm, w_out_hbm, own, oth, att_own, att_oth, keep_t, out_keep, send,
     norm_s, grad_s, att_s, wq, wk, wv, wo, sems,
 ):
     copies = load_weights(place[CORE], first_pair, w_in_hbm, w_out_hbm, wq, wk, wv, wo, sems)
@@ -405,9 +405,13 @@
         dq_pair_t = jnp.concatenate(dq_t, axis=0).astype(jnp.bfloat16)
         dk_pair = jnp.where(low, dk[0], dk[1]).astype(jnp.bfloat16)
         dv_pair = jnp.where(low, dv[0], dv[1]).astype(jnp.bfloat16)
-        for t, piece in enumerate((dq_pair_t.T, dk_pair, dv_pair, att_pair_t.T)):
+        for t, piece in enumerate((dq_pair_t.T, dk_pair, dv_pair)):
             own[t, :, cols] = piece[:half]
             oth[t, :, cols] = piece[half:]
+        att_pair = att_pair_t.T
+        to = slice(128 * (first_pair + j), 128 * (first_pair + j) + 128)
+        att_own[:, to] = att_pair[:half]
+        att_oth[:, to] = att_pair[half:]
         for t, piece in enumerate((dq_pair_t, dk_pair.T, dv_pair.T)):
             at = slice(64 * j, 64 * j + 64)
             part = slice(rows * t, rows * t + rows)
@@ -424,9 +428,19 @@
     attend_pairs(place, 0, (p0, p1, p2, p3), *refs)
 
 
-def attend_second(place, p0, p1, p2, p3, w_in_hbm, w_out_hbm, after, *refs):
+def attend_second(place, p0, p1, p2, p3, w_in_hbm, w_out_hbm, att_own, att_oth, after, own, oth, all_own, all_oth, *refs):
     del after
-    attend_pairs(place, 2, (p0, p1, p2, p3), w_in_hbm, w_out_hbm, *refs)
+    width = att_own.shape[1] // 2
+    all_own[:, :width] = att_own[:, :width]
+    all_oth[:, :width] = att_oth[:, :width]
+    attend_pairs(place, 2, (p0, p1, p2, p3), w_in_hbm, w_out_hbm, own, oth, all_own, all_oth, *refs)
+
+
+def att_kernel(place, own, got, o0, o1):
+    block = o0.shape[0]
+    att = in_order(place[CORE], own[...], got[...])
+    o0[...] = att[:block]
+    o1[...] = att[block:]
 
 
 def in_order(place, own, got):
@@ -438,11 +452,11 @@
     return jnp.concatenate(pieces, axis=1)
 
 
-def rows_kernel(place, own_a, got_a, own_b, got_b, w_ref, after, before, o0, o1, total):
-    del after, before
+def rows_kernel(place, own_a, got_a, own_b, got_b, w_ref, after, o0, o1, total):
+    del after
     step = pl.program_id(0)
     core = place[CORE]
-    block = o0.shape[0] // 2
+    block = o0.shape[0]
 
     def rows_of(t):
         return jnp.concatenate([in_order(core, own_a[t], got_a[t]), in_order(core, own_b[t], got_b[t])], axis=1)
@@ -452,9 +466,6 @@
     @pl.when(step == 0)
     def _():
         total[...] = term
-        att = rows_of(3)
-        o0[:block, :] = att[:block]
-        o1[:block, :] = att[block:]
 
     @pl.when(step > 0)
     def _():
@@ -462,41 +473,51 @@
 
     @pl.when(step == pl.num_programs(0) - 1)
     def _():
-        o0[block:, :] = total[:block].astype(o0.dtype)
-        o1[block:, :] = total[block:].astype(o1.dtype)
-
-
-def return_kernel(place, r0, r1, w_ref, hidden_ref, m0, m1, gain_ref, encoded, d_patches):
-    par = place[PAR]
-    rows = r0.shape[0] // 2
+        o0[...] = total[:block].astype(o0.dtype)
+        o1[...] = total[block:].astype(o1.dtype)
+
+
+def encode_kernel(place, r0, r1, w_ref, hidden_ref, after, encoded):
+    del after
+    for k, ref in enumerate((r0, r1)):
+        s = k ^ place[PAR]
+        live = live_column(place[KEPT + s], ref.shape[0])
+        projected = dot_nn(ref[...], w_ref[...])
+        encoded[s] = jnp.where(live, hidden_ref[k] + projected, 0.0).astype(encoded.dtype)
+
+
+def patch_grad_kernel(place, r0, r1, hidden_ref, m0, m1, gain_ref, d_patches):
+    rows = r0.shape[0]
     for k, (r_ref, m_ref) in enumerate(((r0, m0), (r1, m1))):
-        s = k ^ par
+        s = k ^ place[PAR]
         live = live_column(place[KEPT + s], rows)
         hidden = hidden_ref[k]
-        projected = dot_nn(r_ref[:rows, :], w_ref[...])
-        encoded[s] = jnp.where(live, hidden + projected, 0.0).astype(encoded.dtype)
         center = hidden - jnp.mean(hidden, axis=-1, keepdims=True)
         spread = jnp.mean(center * center, axis=-1, keepdims=True)
         inv_std = lax.rsqrt(spread + epsilon)
         unit = center * inv_std
-        d_hidden = norm_backward(r_ref[rows:, :].astype(jnp.float32), gain_ref[...], unit, inv_std)
+        d_hidden = norm_backward(r_ref[...].astype(jnp.float32), gain_ref[...], unit, inv_std)
         value = m_ref[rows:, :].astype(jnp.float32) + d_hidden
         d_patches[s] = jnp.where(live, value, 0.0).astype(d_patches.dtype)
 
 
-def put_parts(place, total, out_keep, got, keep, send, out_total):
-    out_total[...] = out_keep[...] + got[:, got.shape[1] - out_total.shape[1] :].astype(jnp.float32)
+def put_parts(place, total, first, out_total, out_first, keep, send):
     columns = out_total.shape[1] // 4
-    tall = out_total.shape[0] // 4
-    count = total.shape[0] // 4
+    count = 64
+    tall = keep.shape[1] - count
     for k in range(4):
         ref, spot = (keep, send)[k % 2], k // 2
-        at = pl.multiple_of((place[LINE] ^ k) * count, 64)
+        slab = place[LINE] ^ k
+        at = pl.multiple_of(first + slab * count, 64)
         ref[spot, :count, :] = total[pl.ds(at, count), :].astype(ref.dtype)
-        at = pl.multiple_of((place[LINE] ^ k) * columns, 128)
-        value = out_total[:, pl.ds(at, columns)].astype(ref.dtype)
+        at = pl.ds(pl.multiple_of(slab * columns, 128), columns)
         for j in range(4):
-            ref[spot, count:, columns * j : columns * j + columns] = value[tall * j : tall * j + tall, :]
+            rows = slice(out_first + tall * j, out_first + tall * j + tall)
+            ref[spot, count:, columns * j : columns * j + columns] = out_total[rows, at].astype(ref.dtype)
+
+
+def sum_out_part(out_keep, got, out_total):
+    out_total[...] = out_keep[...] + got[:, got.shape[1] - out_total.shape[1] :].astype(jnp.float32)
 
 
 def piece_of(ref, at, rows):
@@ -505,9 +526,10 @@
 
 
 def weight_first(
-    place, keep, out_keep, got, p0, p1, p2, p3, n0, n1,
+    place, keep, out_keep, got, p0, p1, p2, p3, n0, n1, after,
     part_keep, part_send, tokens, left, total, out_total,
 ):
+    del after
     block = p0.shape[0] // 2
     rows = 4 * block
     for i, ref in enumerate((p0, p1, p2, p3)):
@@ -518,14 +540,15 @@
         for i, at in enumerate((0, 2, 4, 5)):
             left[side, 64 * i : 64 * i + 64, :] = piece_of(ref, at, rows)
     total[...] = dot_nn(left[0], tokens[:rows, :]) + dot_nn(left[1], tokens[rows:, :])
-    put_parts(place, total, out_keep, got, part_keep, part_send, out_total)
+    sum_out_part(out_keep, got, out_total)
+    put_parts(place, total, 0, out_total, 0, part_keep, part_send)
 
 
 def weight_second(
-    place, keep_a, got_a, keep_b, out_keep, got_b, p0, p1, p2, p3, n0, n1, after,
-    part_keep, part_send, tokens, left, total, out_total,
+    place, keep_a, got_a, keep_b, out_keep, got_b, p0, p1, p2, p3, n0, n1, after, before, early,
+    part_keep, part_send, last_keep, last_send, tokens, left, total, out_total,
 ):
-    del after
+    del after, before, early
     block = p0.shape[0] // 2
     rows = 4 * block
     for i, ref in enumerate((p0, p1, p2, p3)):
@@ -534,21 +557,28 @@
     tokens[rows + 2 * block :, :] = n1[...]
     for side, (a, b) in enumerate(((keep_a, keep_b), (got_a, got_b))):
         for i, (ref, at) in enumerate(
-            ((a, 1), (b, 0), (b, 1), (a, 3), (b, 2), (b, 3), (b, 4), (b, 5))
+            ((a, 1), (b, 1), (b, 2), (b, 4), (b, 0), (a, 3), (b, 3), (b, 5))
         ):
             left[side, 64 * i : 64 * i + 64, :] = piece_of(ref, at, rows)
     total[...] = dot_nn(left[0], tokens[:rows, :]) + dot_nn(left[1], tokens[rows:, :])
-    put_parts(place, total, out_keep, got_b, part_keep, part_send, out_total)
-
-
-def pair_kernel(keep, got, mine, send):
+    sum_out_part(out_keep, got_b, out_total)
+    put_parts(place, total, 0, out_total, 0, part_keep, part_send)
+    put_parts(place, total, 256, out_total, 64, last_keep, last_send)
+
+
+def pair_kernel(keep, got, *refs):
+    mine, send = refs[-2:]
     mine[...] = keep[0] + got[0].astype(jnp.float32)
     send[...] = (keep[1] + got[1].astype(jnp.float32)).astype(send.dtype)
 
 
-def sum_kernel(mine, got, *refs):
+def sum_kernel(*refs):
     out = refs[-1]
-    out[...] = (mine[...] + got[...].astype(jnp.float32)).astype(out.dtype)
+    at = 0
+    for mine, got in zip(refs[:-1:2], refs[1:-1:2]):
+        count = mine.shape[0]
+        out[at : at + count, :] = (mine[...] + got[...].astype(jnp.float32)).astype(out.dtype)
+        at += count
 
 
 def finish_kernel(place, a0, a1, a2, a3, b0, b1, b2, b3, wide, narrow):
@@ -567,19 +597,18 @@
     every = slice(None)
     first, second = (a0, a1, a2, a3), (b0, b1, b2, b3)
     for c in range(2):
-        for i, (refs, row) in enumerate(((first, 0), (second, 0), (second, 64))):
+        for i, (refs, row) in enumerate(((first, 0), (first, 96), (second, 0))):
             at = slice(row, row + 64)
             both = jnp.concatenate([pick(refs, c, x, at, every) for x in range(2)], axis=0)
             col = pl.multiple_of(128 * (2 * spots[i] + c), 128)
             wide[:, pl.ds(col, 128)] = both.T.astype(wide.dtype)
-        for half, (refs, base) in enumerate(((first, 64), (second, 128))):
+        for refs, base, tall, pair in ((first, 64, 32, 0), (first, 160, 16, 2), (second, 64, 16, 3)):
             for j in range(4):
-                at = slice(base, base + 32)
+                at = slice(base, base + tall)
                 part = slice(columns * j, columns * j + columns)
                 for x in range(2):
-                    pair, row = 2 * half + j // 2, 32 * (j % 2)
-                    row += 128 * (2 * pair + c) + 64 * x
-                    narrow[row : row + 32, :] = pick(refs, c, x, at, part).astype(narrow.dtype)
+                    row = 128 * (2 * (pair + tall * j // 64) + c) + 64 * x + tall * j % 64
+                    narrow[row : row + tall, :] = pick(refs, c, x, at, part).astype(narrow.dtype)
 
 
 SMEM_SPEC = pl.BlockSpec(memory_space=pltpu.SMEM)
@@ -670,96 +699,112 @@
 
     any_spec = pl.BlockSpec(memory_space=pl.ANY)
     pairs = width // 512
-    half_rows = struct((4, 2 * slots, 128 * pairs))
+    half_rows = struct((3, 2 * slots, 128 * pairs))
+    att_rows = struct((2 * slots, own_width))
     out_half = (64 * pairs, width)
     half_t = struct((64 * pairs, 3 * rows))
     half_send = struct((64 * pairs, 3 * rows + width))
 
-    def attend(kernel, extra):
+    def attend(kernel, extra, specs=()):
         return call(
             kernel,
             (*here, in_hbm(w_qkv), in_hbm(w_out), *extra),
-            [half_rows] * 2 + [half_t, struct(out_half, f32), half_send],
+            [half_rows] * 2 + [att_rows] * 2 + [half_t, struct(out_half, f32), half_send],
             32,
             place,
             scratch=[pltpu.VMEM((rows, width), bf16)] * 2
             + [pltpu.VMEM((2, 64 * pairs, rows), bf16)]
             + [pltpu.VMEM((width, 128 * pairs), bf16)] * 3
             + [pltpu.VMEM((128 * pairs, width), bf16), pltpu.SemaphoreType.DMA((4 * pairs,))],
-            specs=[VMEM_SPEC] * 4 + [any_spec] * (2 + len(extra)),
+            specs=[VMEM_SPEC] * 4 + [any_spec] * 2 + list(specs),
         )
 
-    own_a, oth_a, keep_a, out_keep_a, send_a = attend(attend_first, ())
+    own_a, oth_a, *att_a, keep_a, out_keep_a, send_a = attend(attend_first, ())
     got_a = to_x(send_a)
     core_a = to_core(oth_a)
-    own_b, oth_b, keep_b, out_keep_b, send_b = attend(attend_second, (from_x,))
+    own_b, oth_b, att_own, att_oth, keep_b, out_keep_b, send_b = attend(
+        attend_second, (*att_a, from_x), [VMEM_SPEC] * 2 + [any_spec]
+    )
     got_b = to_x(send_b)
     core_b = to_core(oth_b)
-
-    def parts_of(kernel, args, tall, scratch, after=()):
+    block = struct((slots, width))
+    att = call(att_kernel, (att_own, to_core(att_oth)), [block] * 2, 8, place)
+    back_att = [to_rows(att[k], k, 0) for k in range(2)]
+
+    def parts_of(kernel, args, chunks, scratch, after=()):
         return call(
             kernel,
             (*args, *here, *there, *after),
-            [struct((2, tall, width), f32), struct((2, tall, width))],
+            [struct((2, tall, width), kind) for tall in chunks for kind in (f32, bf16)],
             16,
             place,
             scratch=[pltpu.VMEM((2 * rows, width), bf16)] + scratch + [pltpu.VMEM(out_half, f32)],
             specs=[VMEM_SPEC] * (len(args) + 6) + [any_spec] * len(after),
         )
 
-    def pair_sums(keep, part):
+    def pair_sums(keep, part, after=()):
         shape = keep.shape[1:]
-        mine, part = call(pair_kernel, (keep, along(part, 1)), [struct(shape, f32), struct(shape)], 8)
-        return mine, part, along(part, 2)
-
-    def spread(mine, part, after=()):
-        sums = call(
-            sum_kernel,
-            (mine, part, *after),
-            struct(part.shape),
+        mine, part = call(
+            pair_kernel,
+            (keep, along(part, 1), *after),
+            [struct(shape, f32), struct(shape)],
             8,
             specs=[VMEM_SPEC] * 2 + [any_spec] * len(after),
         )
+        return mine, part, along(part, 2)
+
+    def spread(*parts):
+        count = sum(part.shape[0] for part in parts[::2])
+        sums = call(sum_kernel, parts, struct((count, width)), 8)
         by_x = to_x(sums)
         return (sums, by_x, to_core(sums), to_core(by_x))
 
     keep, part = parts_of(
         weight_first,
         (keep_a, out_keep_a, got_a),
-        96,
+        (96,),
         [pltpu.VMEM((2, 256, rows), bf16), pltpu.VMEM((256, width), f32)],
-    )
-    first_sum, paired, first_got = pair_sums(keep, part)
-    keep, part = parts_of(
-        weight_second,
-        (keep_a, got_a, keep_b, out_keep_b, got_b),
-        160,
-        [pltpu.VMEM((2, 512, rows), bf16), pltpu.VMEM((512, width), f32)],
-        (paired,),
-    )
-    started = part
-    second_sum, _, second_got = pair_sums(keep, part)
-    first = spread(first_sum, first_got)
-    back = pl.pallas_call(
+        (att[0],),
+    )
+    d_normed = pl.pallas_call(
         rows_kernel,
         grid_spec=pltpu.PrefetchScalarGridSpec(
             num_scalar_prefetch=1,
             grid=(3,),
             in_specs=[pl.BlockSpec(half_rows.shape, lambda i, p: (0, 0, 0))] * 4
-            + [pl.BlockSpec((width, width), lambda i, p: (0, i)), any_spec, any_spec],
-            out_specs=[pl.BlockSpec(pay.shape, lambda i, p: (0, 0))] * 2,
+            + [pl.BlockSpec((width, width), lambda i, p: (0, i)), any_spec],
+            out_specs=[pl.BlockSpec(block.shape, lambda i, p: (0, 0))] * 2,
             scratch_shapes=[pltpu.VMEM((2 * slots, width), f32)],
         ),
-        out_shape=[pay] * 2,
+        out_shape=[block] * 2,
         compiler_params=pltpu.CompilerParams(vmem_limit_bytes=20 * MIB),
         cost_estimate=COST,
-    )(place, own_a, core_a, own_b, core_b, in_hbm(w_qkv), started, first[1])
-    second = spread(second_sum, second_got, (back[0],))
-    back = [to_rows(back[k], k, 0) for k in range(2)]
-    encoded, d_patches = call(
-        return_kernel,
-        (*back, w_out, hidden, *mine, gain_row),
-        [struct(patches.shape)] * 2,
+    )(place, own_a, core_a, own_b, core_b, in_hbm(w_qkv), part)
+    encoded = call(
+        encode_kernel,
+        (*back_att, w_out, hidden, d_normed[0]),
+        struct(patches.shape),
+        12,
+        place,
+        specs=[VMEM_SPEC] * 4 + [any_spec],
+    )
+    first_sum, paired, first_got = pair_sums(keep, part)
+    keep, part, last_keep, last_part = parts_of(
+        weight_second,
+        (keep_a, got_a, keep_b, out_keep_b, got_b),
+        (80, 80),
+        [pltpu.VMEM((2, 512, rows), bf16), pltpu.VMEM((512, width), f32)],
+        (paired, d_normed[0], encoded),
+    )
+    second_sum, paired, second_got = pair_sums(keep, part)
+    last_sum, paired, last_got = pair_sums(last_keep, last_part)
+    first = spread(first_sum, first_got, second_sum, second_got)
+    second = spread(last_sum, last_got)
+    back_dn = [to_rows(d_normed[k], k, 0) for k in range(2)]
+    d_patches = call(
+        patch_grad_kernel,
+        (*back_dn, hidden, *mine, gain_row),
+        struct(patches.shape),
         12,
         place,
     )

time: 128 us -> 129 us (level)
  waiting for transfers between devices: 59.5 us -> 51.2 us
  starting transfers between devices: 35.3 us -> 42.3 us
  Pallas kernels: 30.9 us -> 32.8 us
    ppermute x22 -> x27, waiting for transfers between devices: 59.5 us -> 51.2 us  [send(): return lax.ppermute(value, AXES, line_perm(move, reps))]
    ppermute x22 -> x27, starting transfers between devices: 35.3 us -> 42.3 us  [send(): return lax.ppermute(value, AXES, line_perm(move, reps))]
    pallas_call x11 -> x14, Pallas kernels: 25.1 us -> 27.1 us  [call(): pl.pallas_call(kernel, in_specs=specs, out_specs=VMEM_SPEC if single else...]
  transfers between devices with their start and end apart: 22 -> 27, of which waited for: 11 -> 12; matrix products, arithmetic and copies ran while one was open for 0% -> 0% of each run, Pallas kernels for 19% -> 20%
where the time goes in v7:
time: 129 us
  waiting for transfers between devices  51.2 us (40%)
  starting transfers between devices  42.3 us (33%)
  Pallas kernels  32.8 us (25%)
  local copies, waits for them, and re-layouts  1.77 us (1%)
    ppermute x27, waiting for transfers between devices, send(): return lax.ppermute(value, AXES, line_perm(move, reps))  51.2 us
    ppermute x27, starting transfers between devices, send(): return lax.ppermute(value, AXES, line_perm(move, reps))  42.3 us
    pallas_call x14, Pallas kernels, call(): pl.pallas_call(kernel, in_specs=specs, out_specs=VMEM_SPEC if single else...  27.1 us
    pallas_call x1, Pallas kernels, chip_shards(): pl.pallas_call(rows_kernel, grid_spec=pltpu.PrefetchScalarGridSpec(num_sc...  5.67 us
  transfers between devices with their start and end apart: 27, of which 12 were waited for; matrix products, arithmetic and copies ran while one was open for 0% of the time, Pallas kernels for 20%

profile of v7, /device:TPU:1, one launch (start us, length us, event | category | flops | bytes accessed | tf_op | source)
XLA Modules:
  0.0 128.9 jit_solution(14477449248673826715)
XLA Ops:
  1.4 2.2 %shard_map.102 = (bf16[192,1024]{1,0:T(8,128)(2,1)S(1)}, bf16[192,1024]{1,0:T(8,128)(2,1)S(1)}, f32[2,96,1024]{2,1,0:T(8,128)S(1)}) custom-call(s32[6]{0:T(128)S(1)} %concatenate.6.place, bf16[2,96,1024]{2,1,0:T(8,128)(2,1)} %patch_hbm.1, bf16[2,96,1024]{2,1,0:T(8,128)(2,1)} %cot_hbm.1, s32[2,96]{1,0:T(2,128)} %index_hbm.1, f32[1,1024]{1,0:T(1,128)} %bitcast.6), custom_call_target="tpu_custom_call" | custom-call | flops 1000 | bytes 1000 | tf_op jit(solution)/shard_map/pallas_call | solution.py:634
  3.6 5.6 %collective-permute-start = (bf16[192,1024]{1,0:T(8,128)(2,1)S(1)}, bf16[192,1024]{1,0:T(8,128)(2,1)S(1)}, u32[]{:S(2)}, u32[]{:S(2)}) collective-permute-start(bf16[192,1024]{1,0:T(8,128)(2,1)S(1)} %get-tuple-element.39.m0), channel_id=1, source_target_pairs={{0,0},{1,8},{2,2},{3,10},{4,4},{5,12},{6,6},{7,14},{8,1},{9,9},{10... | collective-permute-start | bytes 1179656 | tf_op jit(solution)/shard_map/ppermute | solution.py:660
  10.3 12.8 %collective-permute-done.p0 = bf16[192,1024]{1,0:T(8,128)(2,1)S(1)} collective-permute-done((bf16[192,1024]{1,0:T(8,128)(2,1)S(1)}, bf16[192,1024]{1,0:T(8,128)(2,1)S(1)}, u32[]{:S(2)}, u32[]{:S(2)}) %collective-permute-start) | collective-permute-done | bytes 393248 | tf_op jit(solution)/shard_map/ppermute | solution.py:660
  25.4 6.8 %shard_map.103 = (bf16[3,192,256]{2,1,0:T(8,128)(2,1)S(1)}, bf16[3,192,256]{2,1,0:T(8,128)(2,1)S(1)}, bf16[192,512]{1,0:T(8,128)(2,1)S(1)}, bf16[192,512]{1,0:T(...) custom-call(s32[6]{0:T(128)S(1)} %concatenate.6.place, ...), custom_call_target="tpu_custom_call" | custom-call | flops 1000 | bytes 1000 | tf_op jit(solution)/shard_map/pallas_call | solution.py:634
  32.2 1.3 collective-permute-start.10
  35.3 6.8 %shard_map.104 = (bf16[3,192,256]{2,1,0:T(8,128)(2,1)S(1)}, bf16[3,192,256]{2,1,0:T(8,128)(2,1)S(1)}, bf16[192,512]{1,0:T(8,128)(2,1)S(1)}, bf16[192,512]{1,0:T(...) custom-call(s32[6]{0:T(128)S(1)} %concatenate.6.place, ...), custom_call_target="tpu_custom_call" | custom-call | flops 1000 | bytes 1000 | tf_op jit(solution)/shard_map/pallas_call | solution.py:634
  44.8 1.6 %collective-permute-done.10.got.got_a = bf16[128,2176]{1,0:T(8,128)(2,1)S(1)} collective-permute-done((bf16[128,2176]{1,0:T(8,128)(2,1)S(1)}, bf16[128,2176]{1,0:T(8,128)(2,1)S(1)}, u32[]{:S(2)}, u32[]{:S(2)}) %collective-permute-start.10) | collective-permute-done | bytes 557088 | tf_op jit(solution)/shard_map/ppermute | solution.py:660
  46.3 1.4 %shard_map.106 = (f32[2,96,1024]{2,1,0:T(8,128)S(1)}, bf16[2,96,1024]{2,1,0:T(8,128)(2,1)S(1)}) custom-call(s32[6]{0:T(128)S(1)} %concatenate.6.place, bf16[128,1152]{1,0:T(8,128)(2,1)S(1)} %get-tuple-element.52.keep.keep_a, f32[128,1024]{1,0:T(8,128)S(1)} %get-tuple-element.53.out_keep, bf16[128,2176]{1,0:T(8,128)(2,1)S(1)} %collective-permute-done.10.got.got_a, ...), custom_call_target="tpu_custom_call" | custom-call | flops 1000 | bytes 1000 | tf_op jit(solution)/shard_map/pallas_call | solution.py:634
  47.7 3.9 %collective-permute-start.14 = (bf16[2,96,1024]{2,1,0:T(8,128)(2,1)S(1)}, bf16[2,96,1024]{2,1,0:T(8,128)(2,1)S(1)}, u32[]{:S(2)}, u32[]{:S(2)}) collective-permute-start(bf16[2,96,1024]{2,1,0:T(8,128)(2,1)S(1)} %get-tuple-element.55.after), channel_id=1, source_target_pairs={{0,4},{1,5},{2,6},{3,7},{4,0},{5,1},{6,2},{7,3},{8,12},{9,13},{10,... | collective-permute-start | bytes 1179656 | tf_op jit(solution)/shard_map/ppermute | solution.py:660
  51.6 2.4 %collective-permute-start.9 = (bf16[3,192,256]{2,1,0:T(8,128)(2,1)S(1)}, bf16[3,192,256]{2,1,0:T(8,128)(2,1)S(1)}, u32[]{:S(2)}, u32[]{:S(2)}) collective-permute-start(bf16[3,192,256]{2,1,0:T(8,128)(2,1)S(1)} %get-tuple-element.51), channel_id=1, source_target_pairs={{0,1},{1,0},{2,3},{3,2},{4,5},{5,4},{6,7},{7,6},{8,9},{9,8},{10,11... | collective-permute-start | bytes 884744 | tf_op jit(solution)/shard_map/ppermute | solution.py:660
  54.0 2.9 %collective-permute-start.7 = (bf16[96,1024]{1,0:T(8,128)(2,1)S(1)}, bf16[96,1024]{1,0:T(8,128)(2,1)S(1)}, u32[]{:S(2)}, u32[]{:S(2)}) collective-permute-start(bf16[96,1024]{1,0:T(8,128)(2,1)S(1)} %get-tuple-element.46), channel_id=1, source_target_pairs={{0,4},{1,12},{2,6},{3,14},{4,0},{5,8},{6,2},{7,10},{8,5},{9,13},{1... | collective-permute-start | bytes 589832 | tf_op jit(solution)/shard_map/ppermute | solution.py:660
  57.0 2.1 %collective-permute-start.6 = (bf16[96,1024]{1,0:T(8,128)(2,1)S(1)}, bf16[96,1024]{1,0:T(8,128)(2,1)S(1)}, u32[]{:S(2)}, u32[]{:S(2)}) collective-permute-start(bf16[96,1024]{1,0:T(8,128)(2,1)S(1)} %get-tuple-element.45.after), channel_id=1, source_target_pairs={{0,0},{1,8},{2,2},{3,10},{4,4},{5,12},{6,6},{7,14},{8,1},{9,9},{10... | collective-permute-start | bytes 589832 | tf_op jit(solution)/shard_map/ppermute | solution.py:660
  59.1 5.7 %shard_map.107 = (bf16[96,1024]{1,0:T(8,128)(2,1)S(1)}, bf16[96,1024]{1,0:T(8,128)(2,1)S(1)}) custom-call(s32[6]{0:T(128)S(1)} %concatenate.6.place, bf16[3,192,256]{2,1,0:T(8,128)(2,1)S(1)} %get-tuple-element.48.own_a, bf16[3,192,256]{2,1,0:T(8,128)(2,1)S(1)} %collective-permute-done.8.got_a, bf16[3,192,256]{2,1,0:T(8,128)(2,1)S(1)} %get-tuple-element.50.own_b, ...), custom_call_target="tpu_custom_call" | custom-call | flops 1000 | bytes 1000 | tf_op jit(solution)/shard_map/pallas_call | solution.py:769
  64.8 4.3 %collective-permute-done.7.r1 = bf16[96,1024]{1,0:T(8,128)(2,1)S(1)} collective-permute-done((bf16[96,1024]{1,0:T(8,128)(2,1)S(1)}, bf16[96,1024]{1,0:T(8,128)(2,1)S(1)}, u32[]{:S(2)}, u32[]{:S(2)}) %collective-permute-start.7) | collective-permute-done | bytes 196640 | tf_op jit(solution)/shard_map/ppermute | solution.py:660
  69.1 2.1 %shard_map.108.early = bf16[2,96,1024]{2,1,0:T(8,128)(2,1)} custom-call(s32[6]{0:T(128)S(1)} %concatenate.6.place, bf16[96,1024]{1,0:T(8,128)(2,1)S(1)} %collective-permute-done.6.r0, bf16[96,1024]{1,0:T(8,128)(2,1)S(1)} %collective-permute-done.7.r1, bf16[1024,1024]{1,0:T(8,128)(2,1)S(1)} %copy-done, f32[2,96,1024]{2,1,0:T(8,128)S(1)} %get-tuple-element.47.hidden_ref, ...), custom_call_target="tpu_custom_call" | custom-call | flops 1000 | bytes 1000 | tf_op jit(solution)/shard_map/pallas_call | solution.py:634
  72.3 2.0 %shard_map.111 = (f32[2,80,1024]{2,1,0:T(8,128)S(1)}, bf16[2,80,1024]{2,1,0:T(8,128)(2,1)S(1)}, f32[2,80,1024]{2,1,0:T(8,128)S(1)}, bf16[2,80,1024]{2,1,0:T(8,128)(2,1)S(1)}) custom-call(s32[6]{0:T(128)S(1)} %concatenate.6.place, bf16[128,1152]{1,0:T(8,128)(2,1)S(1)} %get-tuple-element.52.keep.keep_a, ...), custom_call_target="tpu_custom_call" | custom-call | flops 1000 | bytes 1000 | tf_op jit(solution)/shard_map/pallas_call | solution.py:634
  74.3 2.4 %collective-permute-start.17 = (bf16[2,80,1024]{2,1,0:T(8,128)(2,1)S(1)}, bf16[2,80,1024]{2,1,0:T(8,128)(2,1)S(1)}, u32[]{:S(2)}, u32[]{:S(2)}) collective-permute-start(bf16[2,80,1024]{2,1,0:T(8,128)(2,1)S(1)} %get-tuple-element.65), channel_id=1, source_target_pairs={{0,4},{1,5},{2,6},{3,7},{4,0},{5,1},{6,2},{7,3},{8,12},{9,13},{10,... | collective-permute-start | bytes 983048 | tf_op jit(solution)/shard_map/ppermute | solution.py:660
  76.8 10.3 %collective-permute-done.17.got = bf16[2,80,1024]{2,1,0:T(8,128)(2,1)S(1)} collective-permute-done((bf16[2,80,1024]{2,1,0:T(8,128)(2,1)S(1)}, bf16[2,80,1024]{2,1,0:T(8,128)(2,1)S(1)}, u32[]{:S(2)}, u32[]{:S(2)}) %collective-permute-start.17) | collective-permute-done | bytes 327712 | tf_op jit(solution)/shard_map/ppermute | solution.py:660
  88.3 2.2 %collective-permute-start.22 = (bf16[2,80,1024]{2,1,0:T(8,128)(2,1)S(1)}, bf16[2,80,1024]{2,1,0:T(8,128)(2,1)S(1)}, u32[]{:S(2)}, u32[]{:S(2)}) collective-permute-start(bf16[2,80,1024]{2,1,0:T(8,128)(2,1)S(1)} %get-tuple-element.69), channel_id=1, source_target_pairs={{0,4},{1,5},{2,6},{3,7},{4,0},{5,1},{6,2},{7,3},{8,12},{9,13},{10,... | collective-permute-start | bytes 983048 | tf_op jit(solution)/shard_map/ppermute | solution.py:660
  90.5 6.8 %collective-permute-done.18.refs_3_ = bf16[80,1024]{1,0:T(8,128)(2,1)S(1)} collective-permute-done((bf16[80,1024]{1,0:T(8,128)(2,1)S(1)}, bf16[80,1024]{1,0:T(8,128)(2,1)S(1)}, u32[]{:S(2)}, u32[]{:S(2)}) %collective-permute-start.18) | collective-permute-done | bytes 163872 | tf_op jit(solution)/shard_map/ppermute | solution.py:660
  97.4 1.4 %collective-permute-start.19 = (bf16[176,1024]{1,0:T(8,128)(2,1)S(1)}, bf16[176,1024]{1,0:T(8,128)(2,1)S(1)}, u32[]{:S(2)}, u32[]{:S(2)}) collective-permute-start(bf16[176,1024]{1,0:T(8,128)(2,1)S(1)} %shard_map.113.a0), channel_id=1, source_target_pairs={{0,2},{1,3},{2,0},{3,1},{4,6},{5,7},{6,4},{7,5},{8,10},{9,11},{10,... | collective-permute-start | bytes 1081352 | tf_op jit(solution)/shard_map/ppermute | solution.py:660
  100.0 1.5 %collective-permute-start.23 = (bf16[80,1024]{1,0:T(8,128)(2,1)S(1)}, bf16[80,1024]{1,0:T(8,128)(2,1)S(1)}, u32[]{:S(2)}, u32[]{:S(2)}) collective-permute-start(bf16[80,1024]{1,0:T(8,128)(2,1)S(1)} %get-tuple-element.71), channel_id=1, source_target_pairs={{0,8},{1,9},{2,10},{3,11},{4,12},{5,13},{6,14},{7,15},{8,0},{9,1},... | collective-permute-start | bytes 491528 | tf_op jit(solution)/shard_map/ppermute | solution.py:660
  101.6 2.8 %collective-permute-start.13 = (bf16[96,1024]{1,0:T(8,128)(2,1)S(1)}, bf16[96,1024]{1,0:T(8,128)(2,1)S(1)}, u32[]{:S(2)}, u32[]{:S(2)}) collective-permute-start(bf16[96,1024]{1,0:T(8,128)(2,1)S(1)} %get-tuple-element.57), channel_id=1, source_target_pairs={{0,4},{1,12},{2,6},{3,14},{4,0},{5,8},{6,2},{7,10},{8,5},{9,13},{1... | collective-permute-start | bytes 589832 | tf_op jit(solution)/shard_map/ppermute | solution.py:660
  104.9 2.1 %collective-permute-done.19.a1 = bf16[176,1024]{1,0:T(8,128)(2,1)S(1)} collective-permute-done((bf16[176,1024]{1,0:T(8,128)(2,1)S(1)}, bf16[176,1024]{1,0:T(8,128)(2,1)S(1)}, u32[]{:S(2)}, u32[]{:S(2)}) %collective-permute-start.19) | collective-permute-done | bytes 360480 | tf_op jit(solution)/shard_map/ppermute | solution.py:660
  108.3 4.3 %collective-permute-done.23.refs_1_ = bf16[80,1024]{1,0:T(8,128)(2,1)S(1)} collective-permute-done((bf16[80,1024]{1,0:T(8,128)(2,1)S(1)}, bf16[80,1024]{1,0:T(8,128)(2,1)S(1)}, u32[]{:S(2)}, u32[]{:S(2)}) %collective-permute-start.23) | collective-permute-done | bytes 163872 | tf_op jit(solution)/shard_map/ppermute | solution.py:660
  112.6 1.4 %collective-permute-start.24 = (bf16[80,1024]{1,0:T(8,128)(2,1)S(1)}, bf16[80,1024]{1,0:T(8,128)(2,1)S(1)}, u32[]{:S(2)}, u32[]{:S(2)}) collective-permute-start(bf16[80,1024]{1,0:T(8,128)(2,1)S(1)} %shard_map.115.b0), channel_id=1, source_target_pairs={{0,2},{1,3},{2,0},{3,1},{4,6},{5,7},{6,4},{7,5},{8,10},{9,11},{10,... | collective-permute-start | bytes 491528 | tf_op jit(solution)/shard_map/ppermute | solution.py:660
  114.0 2.0 %collective-permute-start.12 = (bf16[96,1024]{1,0:T(8,128)(2,1)S(1)}, bf16[96,1024]{1,0:T(8,128)(2,1)S(1)}, u32[]{:S(2)}, u32[]{:S(2)}) collective-permute-start(bf16[96,1024]{1,0:T(8,128)(2,1)S(1)} %get-tuple-element.56.after.before), channel_id=1, source_target_pairs={{0,0},{1,8},{2,2},{3,10},{4,4},{5,12},{6,6},{7,14},{8,1},{9,9},{10... | collective-permute-start | bytes 589832 | tf_op jit(solution)/shard_map/ppermute | solution.py:660
  116.1 1.5 %collective-permute-done.24.b1 = bf16[80,1024]{1,0:T(8,128)(2,1)S(1)} collective-permute-done((bf16[80,1024]{1,0:T(8,128)(2,1)S(1)}, bf16[80,1024]{1,0:T(8,128)(2,1)S(1)}, u32[]{:S(2)}, u32[]{:S(2)}) %collective-permute-start.24) | collective-permute-done | bytes 163872 | tf_op jit(solution)/shard_map/ppermute | solution.py:660
  117.7 1.7 %collective-permute-start.26 = (bf16[80,1024]{1,0:T(8,128)(2,1)S(1)}, bf16[80,1024]{1,0:T(8,128)(2,1)S(1)}, u32[]{:S(2)}, u32[]{:S(2)}) collective-permute-start(bf16[80,1024]{1,0:T(8,128)(2,1)S(1)} %collective-permute-done.24.b1), channel_id=1, source_target_pairs={{0,1},{1,0},{2,3},{3,2},{4,5},{5,4},{6,7},{7,6},{8,9},{9,8},{10,11... | collective-permute-start | bytes 491528 | tf_op jit(solution)/shard_map/ppermute | solution.py:660
  119.3 4.7 %collective-permute-done.12.r0 = bf16[96,1024]{1,0:T(8,128)(2,1)S(1)} collective-permute-done((bf16[96,1024]{1,0:T(8,128)(2,1)S(1)}, bf16[96,1024]{1,0:T(8,128)(2,1)S(1)}, u32[]{:S(2)}, u32[]{:S(2)}) %collective-permute-start.12) | collective-permute-done | bytes 196640 | tf_op jit(solution)/shard_map/ppermute | solution.py:660
  124.0 1.9 %shard_map.109 = bf16[2,96,1024]{2,1,0:T(8,128)(2,1)} custom-call(s32[6]{0:T(128)S(1)} %concatenate.6.place, bf16[96,1024]{1,0:T(8,128)(2,1)S(1)} %collective-permute-done.12.r0, bf16[96,1024]{1,0:T(8,128)(2,1)S(1)} %collective-permute-done.13.r1, f32[2,96,1024]{2,1,0:T(8,128)S(1)} %get-tuple-element.47.hidden_ref, ...), custom_call_target="tpu_custom_call" | custom-call | flops 1000 | bytes 1000 | tf_op jit(solution)/shard_map/pallas_call | solution.py:634
  125.9 3.0 %shard_map.116 = (f32[1024,768]{1,0:T(8,128)}, f32[1024,256]{1,0:T(8,128)}) custom-call(s32[6]{0:T(128)S(1)} %concatenate.6.place, bf16[176,1024]{1,0:T(8,128)(2,1)S(1)} %shard_map.113.a0, bf16[176,1024]{1,0:T(8,128)(2,1)S(1)} %collective-permute-done.19.a1, bf16[176,1024]{1,0:T(8,128)(2,1)S(1)} %collective-permute-done.20.a2, ...), custom_call_target="tpu_custom_call" | custom-call | flops 1000 | bytes 1000 | tf_op jit(solution)/shard_map/pallas_call | solution.py:634
  (47 shorter events, 14.2 us)
Async XLA Ops:
  3.6 19.5 %collective-permute-start = (bf16[192,1024]{1,0:T(8,128)(2,1)S(1)}, bf16[192,1024]{1,0:T(8,128)(2,1)S(1)}, u32[]{:S(2)}, u32[]{:S(2)}) collective-permute-start(bf16[192,1024]{1,0:T(8,128)(2,1)S(1)} %get-tuple-element.39.m0), channel_id=1, source_target_pairs={{0,0},{1,8},{2,2},{3,10},{4,4},{5,12},{6,6},{7,14},{8,1},{9,9},{10... | collective-permute-start | bytes 1179656 | tf_op jit(solution)/shard_map/ppermute | solution.py:660
  9.2 13.9 %collective-permute-start.1 = (bf16[192,1024]{1,0:T(8,128)(2,1)S(1)}, bf16[192,1024]{1,0:T(8,128)(2,1)S(1)}, u32[]{:S(2)}, u32[]{:S(2)}) collective-permute-start(bf16[192,1024]{1,0:T(8,128)(2,1)S(1)} %get-tuple-element.40.m1), channel_id=1, source_target_pairs={{0,4},{1,12},{2,6},{3,14},{4,0},{5,8},{6,2},{7,10},{8,5},{9,13},{1... | collective-permute-start | bytes 1179656 | tf_op jit(solution)/shard_map/ppermute | solution.py:660
  23.1 1.9 %collective-permute-start.2 = (bf16[192,1024]{1,0:T(8,128)(2,1)S(1)}, bf16[192,1024]{1,0:T(8,128)(2,1)S(1)}, u32[]{:S(2)}, u32[]{:S(2)}) collective-permute-start(bf16[192,1024]{1,0:T(8,128)(2,1)S(1)} %collective-permute-done.p0), channel_id=1, source_target_pairs={{0,1},{1,0},{2,3},{3,2},{4,5},{5,4},{6,7},{7,6},{8,9},{9,8},{10,11... | collective-permute-start | bytes 1179656 | tf_op jit(solution)/shard_map/ppermute | solution.py:660
  23.1 2.3 %collective-permute-start.3 = (bf16[192,1024]{1,0:T(8,128)(2,1)S(1)}, bf16[192,1024]{1,0:T(8,128)(2,1)S(1)}, u32[]{:S(2)}, u32[]{:S(2)}) collective-permute-start(bf16[192,1024]{1,0:T(8,128)(2,1)S(1)} %collective-permute-done.1.p1), channel_id=1, source_target_pairs={{0,1},{1,0},{2,3},{3,2},{4,5},{5,4},{6,7},{7,6},{8,9},{9,8},{10,11... | collective-permute-start | bytes 1179656 | tf_op jit(solution)/shard_map/ppermute | solution.py:660
  23.7 10.8 %collective-permute-start.4 = (bf16[192,1024]{1,0:T(8,128)(2,1)S(1)}, bf16[192,1024]{1,0:T(8,128)(2,1)S(1)}, u32[]{:S(2)}, u32[]{:S(2)}) collective-permute-start(bf16[192,1024]{1,0:T(8,128)(2,1)S(1)} %pad_maximum_fusion), channel_id=1, source_target_pairs={{0,2},{1,3},{2,0},{3,1},{4,6},{5,7},{6,4},{7,5},{8,10},{9,11},{10,... | collective-permute-start | bytes 1179656 | tf_op jit(solution)/shard_map/ppermute | solution.py:660
  32.2 14.2 %collective-permute-start.10 = (bf16[128,2176]{1,0:T(8,128)(2,1)S(1)}, bf16[128,2176]{1,0:T(8,128)(2,1)S(1)}, u32[]{:S(2)}, u32[]{:S(2)}) collective-permute-start(bf16[128,2176]{1,0:T(8,128)(2,1)S(1)} %get-tuple-element.54), channel_id=1, source_target_pairs={{0,2},{1,3},{2,0},{3,1},{4,6},{5,7},{6,4},{7,5},{8,10},{9,11},{10,... | collective-permute-start | bytes 1671176 | tf_op jit(solution)/shard_map/ppermute | solution.py:660
  34.5 10.3 %collective-permute-start.11 = (bf16[192,1024]{1,0:T(8,128)(2,1)S(1)}, bf16[192,1024]{1,0:T(8,128)(2,1)S(1)}, u32[]{:S(2)}, u32[]{:S(2)}) collective-permute-start(bf16[192,1024]{1,0:T(8,128)(2,1)S(1)} %collective-permute-done.4.after.n0), channel_id=1, source_target_pairs={{0,1},{1,0},{2,3},{3,2},{4,5},{5,4},{6,7},{7,6},{8,9},{9,8},{10,11... | collective-permute-start | bytes 1179656 | tf_op jit(solution)/shard_map/ppermute | solution.py:660
  42.1 2.1 %collective-permute-start.5 = (bf16[192,512]{1,0:T(8,128)(2,1)S(1)}, bf16[192,512]{1,0:T(8,128)(2,1)S(1)}, u32[]{:S(2)}, u32[]{:S(2)}) collective-permute-start(bf16[192,512]{1,0:T(8,128)(2,1)S(1)} %get-tuple-element.44), channel_id=1, source_target_pairs={{0,1},{1,0},{2,3},{3,2},{4,5},{5,4},{6,7},{7,6},{8,9},{9,8},{10,11... | collective-permute-start | bytes 589832 | tf_op jit(solution)/shard_map/ppermute | solution.py:660
  42.2 29.1 %collective-permute-start.16 = (bf16[128,2176]{1,0:T(8,128)(2,1)S(1)}, bf16[128,2176]{1,0:T(8,128)(2,1)S(1)}, u32[]{:S(2)}, u32[]{:S(2)}) collective-permute-start(bf16[128,2176]{1,0:T(8,128)(2,1)S(1)} %get-tuple-element.63), channel_id=1, source_target_pairs={{0,2},{1,3},{2,0},{3,1},{4,6},{5,7},{6,4},{7,5},{8,10},{9,11},{10,... | collective-permute-start | bytes 1671176 | tf_op jit(solution)/shard_map/ppermute | solution.py:660
  43.5 13.5 %collective-permute-start.8 = (bf16[3,192,256]{2,1,0:T(8,128)(2,1)S(1)}, bf16[3,192,256]{2,1,0:T(8,128)(2,1)S(1)}, u32[]{:S(2)}, u32[]{:S(2)}) collective-permute-start(bf16[3,192,256]{2,1,0:T(8,128)(2,1)S(1)} %get-tuple-element.49), channel_id=1, source_target_pairs={{0,1},{1,0},{2,3},{3,2},{4,5},{5,4},{6,7},{7,6},{8,9},{9,8},{10,11... | collective-permute-start | bytes 884744 | tf_op jit(solution)/shard_map/ppermute | solution.py:660
  47.7 23.5 %collective-permute-start.14 = (bf16[2,96,1024]{2,1,0:T(8,128)(2,1)S(1)}, bf16[2,96,1024]{2,1,0:T(8,128)(2,1)S(1)}, u32[]{:S(2)}, u32[]{:S(2)}) collective-permute-start(bf16[2,96,1024]{2,1,0:T(8,128)(2,1)S(1)} %get-tuple-element.55.after), channel_id=1, source_target_pairs={{0,4},{1,5},{2,6},{3,7},{4,0},{5,1},{6,2},{7,3},{8,12},{9,13},{10,... | collective-permute-start | bytes 1179656 | tf_op jit(solution)/shard_map/ppermute | solution.py:660
  51.6 7.5 %collective-permute-start.9 = (bf16[3,192,256]{2,1,0:T(8,128)(2,1)S(1)}, bf16[3,192,256]{2,1,0:T(8,128)(2,1)S(1)}, u32[]{:S(2)}, u32[]{:S(2)}) collective-permute-start(bf16[3,192,256]{2,1,0:T(8,128)(2,1)S(1)} %get-tuple-element.51), channel_id=1, source_target_pairs={{0,1},{1,0},{2,3},{3,2},{4,5},{5,4},{6,7},{7,6},{8,9},{9,8},{10,11... | collective-permute-start | bytes 884744 | tf_op jit(solution)/shard_map/ppermute | solution.py:660
  54.0 15.1 %collective-permute-start.7 = (bf16[96,1024]{1,0:T(8,128)(2,1)S(1)}, bf16[96,1024]{1,0:T(8,128)(2,1)S(1)}, u32[]{:S(2)}, u32[]{:S(2)}) collective-permute-start(bf16[96,1024]{1,0:T(8,128)(2,1)S(1)} %get-tuple-element.46), channel_id=1, source_target_pairs={{0,4},{1,12},{2,6},{3,14},{4,0},{5,8},{6,2},{7,10},{8,5},{9,13},{1... | collective-permute-start | bytes 589832 | tf_op jit(solution)/shard_map/ppermute | solution.py:660
  57.0 12.1 %collective-permute-start.6 = (bf16[96,1024]{1,0:T(8,128)(2,1)S(1)}, bf16[96,1024]{1,0:T(8,128)(2,1)S(1)}, u32[]{:S(2)}, u32[]{:S(2)}) collective-permute-start(bf16[96,1024]{1,0:T(8,128)(2,1)S(1)} %get-tuple-element.45.after), channel_id=1, source_target_pairs={{0,0},{1,8},{2,2},{3,10},{4,4},{5,12},{6,6},{7,14},{8,1},{9,9},{10... | collective-permute-start | bytes 589832 | tf_op jit(solution)/shard_map/ppermute | solution.py:660
  59.1 10.0 %copy-start = (bf16[1024,1024]{1,0:T(8,128)(2,1)S(1)}, bf16[1024,1024]{1,0:T(8,128)(2,1)}, u32[]{:S(2)}) copy-start(bf16[1024,1024]{1,0:T(8,128)(2,1)} %w_ref.3) | copy-start | bytes 6291460
  71.3 1.0 copy-start.1
  74.3 49.7 %copy-start.2 = (f32[1024]{0:T(1024)S(1)}, f32[1024]{0:T(1024)}, u32[]{:S(2)}) copy-start(f32[1024]{0:T(1024)} %param.13) | copy-start | bytes 12292
  74.3 12.8 %collective-permute-start.17 = (bf16[2,80,1024]{2,1,0:T(8,128)(2,1)S(1)}, bf16[2,80,1024]{2,1,0:T(8,128)(2,1)S(1)}, u32[]{:S(2)}, u32[]{:S(2)}) collective-permute-start(bf16[2,80,1024]{2,1,0:T(8,128)(2,1)S(1)} %get-tuple-element.65), channel_id=1, source_target_pairs={{0,4},{1,5},{2,6},{3,7},{4,0},{5,1},{6,2},{7,3},{8,12},{9,13},{10,... | collective-permute-start | bytes 983048 | tf_op jit(solution)/shard_map/ppermute | solution.py:660
  76.8 13.8 %collective-permute-start.15 = (bf16[96,1024]{1,0:T(8,128)(2,1)S(1)}, bf16[96,1024]{1,0:T(8,128)(2,1)S(1)}, u32[]{:S(2)}, u32[]{:S(2)}) collective-permute-start(bf16[96,1024]{1,0:T(8,128)(2,1)S(1)} %get-tuple-element.60.after), channel_id=1, source_target_pairs={{0,8},{1,9},{2,10},{3,11},{4,12},{5,13},{6,14},{7,15},{8,0},{9,1},... | collective-permute-start | bytes 589832 | tf_op jit(solution)/shard_map/ppermute | solution.py:660
  87.2 10.1 %collective-permute-start.18 = (bf16[80,1024]{1,0:T(8,128)(2,1)S(1)}, bf16[80,1024]{1,0:T(8,128)(2,1)S(1)}, u32[]{:S(2)}, u32[]{:S(2)}) collective-permute-start(bf16[80,1024]{1,0:T(8,128)(2,1)S(1)} %get-tuple-element.67), channel_id=1, source_target_pairs={{0,8},{1,9},{2,10},{3,11},{4,12},{5,13},{6,14},{7,15},{8,0},{9,1},... | collective-permute-start | bytes 491528 | tf_op jit(solution)/shard_map/ppermute | solution.py:660
  88.3 11.7 %collective-permute-start.22 = (bf16[2,80,1024]{2,1,0:T(8,128)(2,1)S(1)}, bf16[2,80,1024]{2,1,0:T(8,128)(2,1)S(1)}, u32[]{:S(2)}, u32[]{:S(2)}) collective-permute-start(bf16[2,80,1024]{2,1,0:T(8,128)(2,1)S(1)} %get-tuple-element.69), channel_id=1, source_target_pairs={{0,4},{1,5},{2,6},{3,7},{4,0},{5,1},{6,2},{7,3},{8,12},{9,13},{10,... | collective-permute-start | bytes 983048 | tf_op jit(solution)/shard_map/ppermute | solution.py:660
  97.4 9.7 %collective-permute-start.19 = (bf16[176,1024]{1,0:T(8,128)(2,1)S(1)}, bf16[176,1024]{1,0:T(8,128)(2,1)S(1)}, u32[]{:S(2)}, u32[]{:S(2)}) collective-permute-start(bf16[176,1024]{1,0:T(8,128)(2,1)S(1)} %shard_map.113.a0), channel_id=1, source_target_pairs={{0,2},{1,3},{2,0},{3,1},{4,6},{5,7},{6,4},{7,5},{8,10},{9,11},{10,... | collective-permute-start | bytes 1081352 | tf_op jit(solution)/shard_map/ppermute | solution.py:660
  100.0 12.5 %collective-permute-start.23 = (bf16[80,1024]{1,0:T(8,128)(2,1)S(1)}, bf16[80,1024]{1,0:T(8,128)(2,1)S(1)}, u32[]{:S(2)}, u32[]{:S(2)}) collective-permute-start(bf16[80,1024]{1,0:T(8,128)(2,1)S(1)} %get-tuple-element.71), channel_id=1, source_target_pairs={{0,8},{1,9},{2,10},{3,11},{4,12},{5,13},{6,14},{7,15},{8,0},{9,1},... | collective-permute-start | bytes 491528 | tf_op jit(solution)/shard_map/ppermute | solution.py:660
  101.6 14.4 %collective-permute-start.13 = (bf16[96,1024]{1,0:T(8,128)(2,1)S(1)}, bf16[96,1024]{1,0:T(8,128)(2,1)S(1)}, u32[]{:S(2)}, u32[]{:S(2)}) collective-permute-start(bf16[96,1024]{1,0:T(8,128)(2,1)S(1)} %get-tuple-element.57), channel_id=1, source_target_pairs={{0,4},{1,12},{2,6},{3,14},{4,0},{5,8},{6,2},{7,10},{8,5},{9,13},{1... | collective-permute-start | bytes 589832 | tf_op jit(solution)/shard_map/ppermute | solution.py:660
  104.3 21.5 %collective-permute-start.20 = (bf16[176,1024]{1,0:T(8,128)(2,1)S(1)}, bf16[176,1024]{1,0:T(8,128)(2,1)S(1)}, u32[]{:S(2)}, u32[]{:S(2)}) collective-permute-start(bf16[176,1024]{1,0:T(8,128)(2,1)S(1)} %shard_map.113.a0), channel_id=1, source_target_pairs={{0,1},{1,0},{2,3},{3,2},{4,5},{5,4},{6,7},{7,6},{8,9},{9,8},{10,11... | collective-permute-start | bytes 1081352 | tf_op jit(solution)/shard_map/ppermute | solution.py:660
  107.0 18.8 %collective-permute-start.21 = (bf16[176,1024]{1,0:T(8,128)(2,1)S(1)}, bf16[176,1024]{1,0:T(8,128)(2,1)S(1)}, u32[]{:S(2)}, u32[]{:S(2)}) collective-permute-start(bf16[176,1024]{1,0:T(8,128)(2,1)S(1)} %collective-permute-done.19.a1), channel_id=1, source_target_pairs={{0,1},{1,0},{2,3},{3,2},{4,5},{5,4},{6,7},{7,6},{8,9},{9,8},{10,11... | collective-permute-start | bytes 1081352 | tf_op jit(solution)/shard_map/ppermute | solution.py:660
  112.6 5.0 %collective-permute-start.24 = (bf16[80,1024]{1,0:T(8,128)(2,1)S(1)}, bf16[80,1024]{1,0:T(8,128)(2,1)S(1)}, u32[]{:S(2)}, u32[]{:S(2)}) collective-permute-start(bf16[80,1024]{1,0:T(8,128)(2,1)S(1)} %shard_map.115.b0), channel_id=1, source_target_pairs={{0,2},{1,3},{2,0},{3,1},{4,6},{5,7},{6,4},{7,5},{8,10},{9,11},{10,... | collective-permute-start | bytes 491528 | tf_op jit(solution)/shard_map/ppermute | solution.py:660
  114.0 10.0 %collective-permute-start.12 = (bf16[96,1024]{1,0:T(8,128)(2,1)S(1)}, bf16[96,1024]{1,0:T(8,128)(2,1)S(1)}, u32[]{:S(2)}, u32[]{:S(2)}) collective-permute-start(bf16[96,1024]{1,0:T(8,128)(2,1)S(1)} %get-tuple-element.56.after.before), channel_id=1, source_target_pairs={{0,0},{1,8},{2,2},{3,10},{4,4},{5,12},{6,6},{7,14},{8,1},{9,9},{10... | collective-permute-start | bytes 589832 | tf_op jit(solution)/shard_map/ppermute | solution.py:660
  116.0 9.8 %collective-permute-start.25 = (bf16[80,1024]{1,0:T(8,128)(2,1)S(1)}, bf16[80,1024]{1,0:T(8,128)(2,1)S(1)}, u32[]{:S(2)}, u32[]{:S(2)}) collective-permute-start(bf16[80,1024]{1,0:T(8,128)(2,1)S(1)} %shard_map.115.b0), channel_id=1, source_target_pairs={{0,1},{1,0},{2,3},{3,2},{4,5},{5,4},{6,7},{7,6},{8,9},{9,8},{10,11... | collective-permute-start | bytes 491528 | tf_op jit(solution)/shard_map/ppermute | solution.py:660
  117.7 8.2 %collective-permute-start.26 = (bf16[80,1024]{1,0:T(8,128)(2,1)S(1)}, bf16[80,1024]{1,0:T(8,128)(2,1)S(1)}, u32[]{:S(2)}, u32[]{:S(2)}) collective-permute-start(bf16[80,1024]{1,0:T(8,128)(2,1)S(1)} %collective-permute-done.24.b1), channel_id=1, source_target_pairs={{0,1},{1,0},{2,3},{3,2},{4,5},{5,4},{6,7},{7,6},{8,9},{9,8},{10,11... | collective-permute-start | bytes 491528 | tf_op jit(solution)/shard_map/ppermute | solution.py:660

commit v8 on v7

--- a/solution.py
+++ b/solution.py
@@ -284,8 +284,25 @@
 PAR, CORE, LINE, SIDE, KEPT = range(5)
 
 
+def load_weights(core, w_in_hbm, w_out_hbm, wq, wk, wv, wo, sems):
+    width = w_out_hbm.shape[0]
+    copies = []
+    for j in range(width // 256):
+        to = pl.ds(128 * j, 128)
+        row = pl.multiple_of(256 * j + 128 * core, 128)
+        pairs = [(w_out_hbm.at[pl.ds(row, 128), :], wo.at[to, :])]
+        for t, out in enumerate((wq, wk, wv)):
+            at = pl.multiple_of(t * width + row, 128)
+            pairs.append((w_in_hbm.at[:, pl.ds(at, 128)], out.at[:, to]))
+        copies += [pltpu.make_async_copy(a, b, sems.at[4 + 4 * j + i]) for i, (a, b) in enumerate(pairs)]
+    for copy in copies:
+        copy.start()
+    return copies
+
+
 def norm_kernel(
-    place, patch_hbm, cot_hbm, index_hbm, gain_hbm, p0_ref, p1_ref, hidden_ref,
+    place, patch_hbm, cot_hbm, index_hbm, gain_hbm, w_in_hbm, w_out_hbm,
+    p0_ref, p1_ref, hidden_ref, wq, wk, wv, wo,
     patch_ref, cot_ref, index_ref, gain_ref, sems,
 ):
     par = place[PAR]
@@ -299,6 +316,7 @@
     ]
     for copy in copies:
         copy.start()
+    staged = load_weights(place[CORE], w_in_hbm, w_out_hbm, wq, wk, wv, wo, sems)
     order = lax.broadcasted_iota(jnp.int32, (1, quarter), 1).astype(jnp.float32)
     freq = jnp.exp(-np.log(np.float32(10000.0)) * order / quarter)
     diagonal = lax.broadcasted_iota(jnp.int32, (rows, rows), 0) == lax.broadcasted_iota(
@@ -331,29 +349,14 @@
         live = live_column(place[KEPT + s], rows)
         grad = cot_ref[s]
         out_ref[rows:, :] = jnp.where(live, grad, jnp.zeros_like(grad))
-
-
-def load_weights(core, first_pair, w_in_hbm, w_out_hbm, wq, wk, wv, wo, sems):
-    width = w_out_hbm.shape[0]
-    copies = []
-    for j in range(wq.shape[1] // 128):
-        to = pl.ds(128 * j, 128)
-        row = pl.multiple_of(256 * (first_pair + j) + 128 * core, 128)
-        pairs = [(w_out_hbm.at[pl.ds(row, 128), :], wo.at[to, :])]
-        for t, out in enumerate((wq, wk, wv)):
-            at = pl.multiple_of(t * width + row, 128)
-            pairs.append((w_in_hbm.at[:, pl.ds(at, 128)], out.at[:, to]))
-        copies += [pltpu.make_async_copy(a, b, sems.at[4 * j + i]) for i, (a, b) in enumerate(pairs)]
-    for copy in copies:
-        copy.start()
-    return copies
+    for copy in staged:
+        copy.wait()
 
 
 def attend_pairs(
-    place, first_pair, payloads, w_in_hbm, w_out_hbm, own, oth, att_own, att_oth, keep_t, out_keep, send,
-    norm_s, grad_s, att_s, wq, wk, wv, wo, sems,
+    place, first_pair, payloads, wq, wk, wv, wo, own, oth, att_own, att_oth, keep_t, out_keep, send,
+    norm_s, grad_s, att_s,
 ):
-    copies = load_weights(place[CORE], first_pair, w_in_hbm, w_out_hbm, wq, wk, wv, wo, sems)
     block = payloads[0].shape[0] // 2
     rows = 4 * block
     half = 2 * block
@@ -370,14 +373,13 @@
     scale = jnp.bfloat16(0.125)
     zero = jnp.zeros((rows, 128), jnp.bfloat16)
     first = place[SIDE] == 0
-    count = wq.shape[1] // 128
-    for copy in copies:
-        copy.wait()
+    count = own.shape[2] // 128
+    here = slice(128 * first_pair, 128 * (first_pair + count))
     normed = norm_s[...]
-    queries = dot_nn(normed, wq[...]).astype(jnp.bfloat16)
-    keys = dot_nn(normed, wk[...]).astype(jnp.bfloat16)
-    values = dot_nn(normed, wv[...]).astype(jnp.bfloat16)
-    d_att = dot_nt(grad_s[...], wo[...]).astype(jnp.bfloat16)
+    queries = dot_nn(normed, wq[:, here]).astype(jnp.bfloat16)
+    keys = dot_nn(normed, wk[:, here]).astype(jnp.bfloat16)
+    values = dot_nn(normed, wv[:, here]).astype(jnp.bfloat16)
+    d_att = dot_nt(grad_s[...], wo[here, :]).astype(jnp.bfloat16)
     for j in range(count):
         cols = slice(128 * j, 128 * j + 128)
         q = queries[:, cols] * scale
@@ -428,12 +430,14 @@
     attend_pairs(place, 0, (p0, p1, p2, p3), *refs)
 
 
-def attend_second(place, p0, p1, p2, p3, w_in_hbm, w_out_hbm, att_own, att_oth, after, own, oth, all_own, all_oth, *refs):
+def attend_second(
+    place, p0, p1, p2, p3, wq, wk, wv, wo, att_own, att_oth, after, own, oth, all_own, all_oth, *refs
+):
     del after
     width = att_own.shape[1] // 2
     all_own[:, :width] = att_own[:, :width]
     all_oth[:, :width] = att_oth[:, :width]
-    attend_pairs(place, 2, (p0, p1, p2, p3), w_in_hbm, w_out_hbm, own, oth, all_own, all_oth, *refs)
+    attend_pairs(place, 2, (p0, p1, p2, p3), wq, wk, wv, wo, own, oth, all_own, all_oth, *refs)
 
 
 def att_kernel(place, own, got, o0, o1):
@@ -477,8 +481,7 @@
         o1[...] = total[block:].astype(o1.dtype)
 
 
-def encode_kernel(place, r0, r1, w_ref, hidden_ref, after, encoded):
-    del after
+def encode_kernel(place, r0, r1, w_ref, hidden_ref, encoded):
     for k, ref in enumerate((r0, r1)):
         s = k ^ place[PAR]
         live = live_column(place[KEPT + s], ref.shape[0])
@@ -501,18 +504,18 @@
         d_patches[s] = jnp.where(live, value, 0.0).astype(d_patches.dtype)
 
 
-def put_parts(place, total, first, out_total, out_first, keep, send):
+def put_parts(place, total, out_total, keep, send):
     columns = out_total.shape[1] // 4
-    count = 64
-    tall = keep.shape[1] - count
+    count = total.shape[0] // 4
+    tall = out_total.shape[0] // 4
     for k in range(4):
         ref, spot = (keep, send)[k % 2], k // 2
         slab = place[LINE] ^ k
-        at = pl.multiple_of(first + slab * count, 64)
+        at = pl.multiple_of(slab * count, 64)
         ref[spot, :count, :] = total[pl.ds(at, count), :].astype(ref.dtype)
         at = pl.ds(pl.multiple_of(slab * columns, 128), columns)
         for j in range(4):
-            rows = slice(out_first + tall * j, out_first + tall * j + tall)
+            rows = slice(tall * j, tall * j + tall)
             ref[spot, count:, columns * j : columns * j + columns] = out_total[rows, at].astype(ref.dtype)
 
 
@@ -541,14 +544,14 @@
             left[side, 64 * i : 64 * i + 64, :] = piece_of(ref, at, rows)
     total[...] = dot_nn(left[0], tokens[:rows, :]) + dot_nn(left[1], tokens[rows:, :])
     sum_out_part(out_keep, got, out_total)
-    put_parts(place, total, 0, out_total, 0, part_keep, part_send)
+    put_parts(place, total, out_total, part_keep, part_send)
 
 
 def weight_second(
-    place, keep_a, got_a, keep_b, out_keep, got_b, p0, p1, p2, p3, n0, n1, after, before, early,
-    part_keep, part_send, last_keep, last_send, tokens, left, total, out_total,
+    place, keep_a, got_a, keep_b, out_keep, got_b, p0, p1, p2, p3, n0, n1, after, before,
+    part_keep, part_send, tokens, left, total, out_total,
 ):
-    del after, before, early
+    del after, before
     block = p0.shape[0] // 2
     rows = 4 * block
     for i, ref in enumerate((p0, p1, p2, p3)):
@@ -557,13 +560,12 @@
     tokens[rows + 2 * block :, :] = n1[...]
     for side, (a, b) in enumerate(((keep_a, keep_b), (got_a, got_b))):
         for i, (ref, at) in enumerate(
-            ((a, 1), (b, 1), (b, 2), (b, 4), (b, 0), (a, 3), (b, 3), (b, 5))
+            ((a, 1), (b, 0), (b, 1), (a, 3), (b, 2), (b, 3), (b, 4), (b, 5))
         ):
             left[side, 64 * i : 64 * i + 64, :] = piece_of(ref, at, rows)
     total[...] = dot_nn(left[0], tokens[:rows, :]) + dot_nn(left[1], tokens[rows:, :])
     sum_out_part(out_keep, got_b, out_total)
-    put_parts(place, total, 0, out_total, 0, part_keep, part_send)
-    put_parts(place, total, 256, out_total, 64, last_keep, last_send)
+    put_parts(place, total, out_total, part_keep, part_send)
 
 
 def pair_kernel(keep, got, *refs):
@@ -572,13 +574,9 @@
     send[...] = (keep[1] + got[1].astype(jnp.float32)).astype(send.dtype)
 
 
-def sum_kernel(*refs):
+def sum_kernel(mine, got, *refs):
     out = refs[-1]
-    at = 0
-    for mine, got in zip(refs[:-1:2], refs[1:-1:2]):
-        count = mine.shape[0]
-        out[at : at + count, :] = (mine[...] + got[...].astype(jnp.float32)).astype(out.dtype)
-        at += count
+    out[...] = (mine[...] + got[...].astype(jnp.float32)).astype(out.dtype)
 
 
 def finish_kernel(place, a0, a1, a2, a3, b0, b1, b2, b3, wide, narrow):
@@ -597,12 +595,12 @@
     every = slice(None)
     first, second = (a0, a1, a2, a3), (b0, b1, b2, b3)
     for c in range(2):
-        for i, (refs, row) in enumerate(((first, 0), (first, 96), (second, 0))):
+        for i, (refs, row) in enumerate(((first, 0), (second, 0), (second, 64))):
             at = slice(row, row + 64)
             both = jnp.concatenate([pick(refs, c, x, at, every) for x in range(2)], axis=0)
             col = pl.multiple_of(128 * (2 * spots[i] + c), 128)
             wide[:, pl.ds(col, 128)] = both.T.astype(wide.dtype)
-        for refs, base, tall, pair in ((first, 64, 32, 0), (first, 160, 16, 2), (second, 64, 16, 3)):
+        for refs, base, tall, pair in ((first, 64, 32, 0), (second, 128, 32, 2)):
             for j in range(4):
                 at = slice(base, base + tall)
                 part = slice(columns * j, columns * j + columns)
@@ -677,10 +675,12 @@
     gain_row = gain.reshape(1, width)
     pay = struct((2 * slots, width))
     hbm = pl.BlockSpec(memory_space=pl.ANY)
-    *mine, hidden = call(
+    any_spec = pl.BlockSpec(memory_space=pl.ANY)
+    own_cols = struct((width, own_width))
+    *outs, wq, wk, wv, wo = call(
         norm_kernel,
-        tuple(in_hbm(v) for v in (patches, cotangent, kept_index, gain_row)),
-        [pay, pay, struct(patches.shape, f32)],
+        tuple(in_hbm(v) for v in (patches, cotangent, kept_index, gain_row, w_qkv, w_out)),
+        [pay, pay, struct(patches.shape, f32)] + [own_cols] * 3 + [struct((own_width, width))],
         24,
         place,
         scratch=[
@@ -688,10 +688,12 @@
             pltpu.VMEM(patches.shape, bf16),
             pltpu.VMEM(kept_index.shape, jnp.int32),
             pltpu.VMEM(gain_row.shape, f32),
-            pltpu.SemaphoreType.DMA((4,)),
+            pltpu.SemaphoreType.DMA((4 + 4 * (width // 256),)),
         ],
-        specs=[hbm] * 4,
-    )
+        specs=[any_spec] * 6,
+    )
+    *mine, hidden = outs
+    staged = (wq, wk, wv, wo)
     got = [to_chip(mine[k], k) for k in range(2)]
     here = got + [to_core(v) for v in got]
     from_x = to_x(jnp.concatenate([v[:slots] for v in got], axis=0))
@@ -708,15 +710,13 @@
     def attend(kernel, extra, specs=()):
         return call(
             kernel,
-            (*here, in_hbm(w_qkv), in_hbm(w_out), *extra),
+            (*here, *staged, *extra),
             [half_rows] * 2 + [att_rows] * 2 + [half_t, struct(out_half, f32), half_send],
             32,
             place,
             scratch=[pltpu.VMEM((rows, width), bf16)] * 2
-            + [pltpu.VMEM((2, 64 * pairs, rows), bf16)]
-            + [pltpu.VMEM((width, 128 * pairs), bf16)] * 3
-            + [pltpu.VMEM((128 * pairs, width), bf16), pltpu.SemaphoreType.DMA((4 * pairs,))],
-            specs=[VMEM_SPEC] * 4 + [any_spec] * 2 + list(specs),
+            + [pltpu.VMEM((2, 64 * pairs, rows), bf16)],
+            specs=[VMEM_SPEC] * 8 + list(specs),
         )
 
     own_a, oth_a, *att_a, keep_a, out_keep_a, send_a = attend(attend_first, ())
@@ -753,9 +753,14 @@
         )
         return mine, part, along(part, 2)
 
-    def spread(*parts):
-        count = sum(part.shape[0] for part in parts[::2])
-        sums = call(sum_kernel, parts, struct((count, width)), 8)
+    def spread(mine, part, after=()):
+        sums = call(
+            sum_kernel,
+            (mine, part, *after),
+            struct(part.shape),
+            8,
+            specs=[VMEM_SPEC] * 2 + [any_spec] * len(after),
+        )
         by_x = to_x(sums)
         return (sums, by_x, to_core(sums), to_core(by_x))
 
@@ -780,38 +785,36 @@
         compiler_params=pltpu.CompilerParams(vmem_limit_bytes=20 * MIB),
         cost_estimate=COST,
     )(place, own_a, core_a, own_b, core_b, in_hbm(w_qkv), part)
+    first_sum, paired, first_got = pair_sums(keep, part)
+    keep, part = parts_of(
+        weight_second,
+        (keep_a, got_a, keep_b, out_keep_b, got_b),
+        (160,),
+        [pltpu.VMEM((2, 512, rows), bf16), pltpu.VMEM((512, width), f32)],
+        (paired, d_normed[0]),
+    )
+    second_sum, _, second_got = pair_sums(keep, part, back_att)
+    first = spread(first_sum, first_got)
     encoded = call(
         encode_kernel,
-        (*back_att, w_out, hidden, d_normed[0]),
+        (*back_att, w_out, hidden),
         struct(patches.shape),
         12,
         place,
-        specs=[VMEM_SPEC] * 4 + [any_spec],
-    )
-    first_sum, paired, first_got = pair_sums(keep, part)
-    keep, part, last_keep, last_part = parts_of(
-        weight_second,
-        (keep_a, got_a, keep_b, out_keep_b, got_b),
-        (80, 80),
-        [pltpu.VMEM((2, 512, rows), bf16), pltpu.VMEM((512, width), f32)],
-        (paired, d_normed[0], encoded),
-    )
-    second_sum, paired, second_got = pair_sums(keep, part)
-    last_sum, paired, last_got = pair_sums(last_keep, last_part)
-    first = spread(first_sum, first_got, second_sum, second_got)
-    second = spread(last_sum, last_got)
+    )
+    second = spread(second_sum, second_got, (*first[1:], encoded))
     back_dn = [to_rows(d_normed[k], k, 0) for k in range(2)]
+    qkv_grad, out_grad = call(
+        finish_kernel,
+        (*first, *second),
+        [struct((width, 3 * quarter), f32), struct((width, quarter), f32)],
+        12,
+        place,
+    )
     d_patches = call(
         patch_grad_kernel,
         (*back_dn, hidden, *mine, gain_row),
         struct(patches.shape),
-        12,
-        place,
-    )
-    qkv_grad, out_grad = call(
-        finish_kernel,
-        (*first, *second),
-        [struct((width, 3 * quarter), f32), struct((width, quarter), f32)],
         12,
         place,
     )

time: 129 us -> 137 us (1.062)
  the two profiles are of different devices: /device:TPU:1 before, /device:TPU:9 now
where the time goes in v8:
time: 137 us; the launch traced here: 136 us
  waiting for transfers between devices  68.1 us (50%)
  starting transfers between devices  35 us (26%)
  Pallas kernels  30.6 us (22%)
  local copies, waits for them, and re-layouts  1.77 us (1%)
    ppermute x25, waiting for transfers between devices, send(): return lax.ppermute(value, AXES, line_perm(move, reps))  68.1 us
    ppermute x25, starting transfers between devices, send(): return lax.ppermute(value, AXES, line_perm(move, reps))  35 us
    pallas_call x13, Pallas kernels, call(): pl.pallas_call(kernel, in_specs=specs, out_specs=VMEM_SPEC if single else...  25 us
    pallas_call x1, Pallas kernels, chip_shards(): pl.pallas_call(rows_kernel, grid_spec=pltpu.PrefetchScalarGridSpec(num_sc...  5.59 us
  transfers between devices with their start and end apart: 25, of which 15 were waited for; matrix products, arithmetic and copies ran while one was open for 0% of the time, Pallas kernels for 16%

profile of v8, /device:TPU:9, one launch (start us, length us, event | category | flops | bytes accessed | tf_op | source)
XLA Modules:
  0.0 136.4 jit_solution(11506820568154346484)
XLA Ops:
  1.4 3.2 %shard_map.102 = (bf16[192,1024]{1,0:T(8,128)(2,1)S(1)}, bf16[192,1024]{1,0:T(8,128)(2,1)S(1)}, f32[2,96,1024]{2,1,0:T(8,128)S(1)}, bf16[1024,512]{1,0:T(8,128)(...) custom-call(s32[6]{0:T(128)S(1)} %concatenate.6.place, ...), custom_call_target="tpu_custom_call" | custom-call | flops 1000 | bytes 1000 | tf_op jit(solution)/shard_map/pallas_call | solution.py:632
  4.6 4.8 %collective-permute-start = (bf16[192,1024]{1,0:T(8,128)(2,1)S(1)}, bf16[192,1024]{1,0:T(8,128)(2,1)S(1)}, u32[]{:S(2)}, u32[]{:S(2)}) collective-permute-start(bf16[192,1024]{1,0:T(8,128)(2,1)S(1)} %get-tuple-element.39.m0), channel_id=1, source_target_pairs={{0,0},{1,8},{2,2},{3,10},{4,4},{5,12},{6,6},{7,14},{8,1},{9,9},{10... | collective-permute-start | bytes 1179656 | tf_op jit(solution)/shard_map/ppermute | solution.py:658
  9.5 13.0 %collective-permute-done.p0 = bf16[192,1024]{1,0:T(8,128)(2,1)S(1)} collective-permute-done((bf16[192,1024]{1,0:T(8,128)(2,1)S(1)}, bf16[192,1024]{1,0:T(8,128)(2,1)S(1)}, u32[]{:S(2)}, u32[]{:S(2)}) %collective-permute-start) | collective-permute-done | bytes 393248 | tf_op jit(solution)/shard_map/ppermute | solution.py:658
  22.5 4.2 %collective-permute-done.1.p1 = bf16[192,1024]{1,0:T(8,128)(2,1)S(1)} collective-permute-done((bf16[192,1024]{1,0:T(8,128)(2,1)S(1)}, bf16[192,1024]{1,0:T(8,128)(2,1)S(1)}, u32[]{:S(2)}, u32[]{:S(2)}) %collective-permute-start.1) | collective-permute-done | bytes 393248 | tf_op jit(solution)/shard_map/ppermute | solution.py:658
  26.8 1.3 collective-permute-start.4
  28.4 5.2 %shard_map.103 = (bf16[3,192,256]{2,1,0:T(8,128)(2,1)S(1)}, bf16[3,192,256]{2,1,0:T(8,128)(2,1)S(1)}, bf16[192,512]{1,0:T(8,128)(2,1)S(1)}, bf16[192,512]{1,0:T(...) custom-call(s32[6]{0:T(128)S(1)} %concatenate.6.place, ...), custom_call_target="tpu_custom_call" | custom-call | flops 1000 | bytes 1000 | tf_op jit(solution)/shard_map/pallas_call | solution.py:632
  33.7 1.3 collective-permute-start.10
  34.9 2.1 %collective-permute-done.4.after.n0 = bf16[192,1024]{1,0:T(8,128)(2,1)S(1)} collective-permute-done((bf16[192,1024]{1,0:T(8,128)(2,1)S(1)}, bf16[192,1024]{1,0:T(8,128)(2,1)S(1)}, u32[]{:S(2)}, u32[]{:S(2)}) %collective-permute-start.4) | collective-permute-done | bytes 393248 | tf_op jit(solution)/shard_map/ppermute | solution.py:658
  37.0 2.3 %collective-permute-start.11 = (bf16[192,1024]{1,0:T(8,128)(2,1)S(1)}, bf16[192,1024]{1,0:T(8,128)(2,1)S(1)}, u32[]{:S(2)}, u32[]{:S(2)}) collective-permute-start(bf16[192,1024]{1,0:T(8,128)(2,1)S(1)} %collective-permute-done.4.after.n0), channel_id=1, source_target_pairs={{0,1},{1,0},{2,3},{3,2},{4,5},{5,4},{6,7},{7,6},{8,9},{9,8},{10,11... | collective-permute-start | bytes 1179656 | tf_op jit(solution)/shard_map/ppermute | solution.py:658
  39.3 5.2 %shard_map.104 = (bf16[3,192,256]{2,1,0:T(8,128)(2,1)S(1)}, bf16[3,192,256]{2,1,0:T(8,128)(2,1)S(1)}, bf16[192,512]{1,0:T(8,128)(2,1)S(1)}, bf16[192,512]{1,0:T(...) custom-call(s32[6]{0:T(128)S(1)} %concatenate.6.place, ...), custom_call_target="tpu_custom_call" | custom-call | flops 1000 | bytes 1000 | tf_op jit(solution)/shard_map/pallas_call | solution.py:632
  44.7 1.3 collective-permute-start.19
  46.7 2.2 %collective-permute-done.10.got.got_a = bf16[128,2176]{1,0:T(8,128)(2,1)S(1)} collective-permute-done((bf16[128,2176]{1,0:T(8,128)(2,1)S(1)}, bf16[128,2176]{1,0:T(8,128)(2,1)S(1)}, u32[]{:S(2)}, u32[]{:S(2)}) %collective-permute-start.10) | collective-permute-done | bytes 557088 | tf_op jit(solution)/shard_map/ppermute | solution.py:658
  48.9 1.4 %shard_map.107 = (f32[2,96,1024]{2,1,0:T(8,128)S(1)}, bf16[2,96,1024]{2,1,0:T(8,128)(2,1)S(1)}) custom-call(s32[6]{0:T(128)S(1)} %concatenate.6.place, bf16[128,1152]{1,0:T(8,128)(2,1)S(1)} %get-tuple-element.56.keep.keep_a, f32[128,1024]{1,0:T(8,128)S(1)} %get-tuple-element.57.out_keep, bf16[128,2176]{1,0:T(8,128)(2,1)S(1)} %collective-permute-done.10.got.got_a, ...), custom_call_target="tpu_custom_call" | custom-call | flops 1000 | bytes 1000 | tf_op jit(solution)/shard_map/pallas_call | solution.py:632
  50.4 2.4 %collective-permute-start.9 = (bf16[3,192,256]{2,1,0:T(8,128)(2,1)S(1)}, bf16[3,192,256]{2,1,0:T(8,128)(2,1)S(1)}, u32[]{:S(2)}, u32[]{:S(2)}) collective-permute-start(bf16[3,192,256]{2,1,0:T(8,128)(2,1)S(1)} %get-tuple-element.55), channel_id=1, source_target_pairs={{0,1},{1,0},{2,3},{3,2},{4,5},{5,4},{6,7},{7,6},{8,9},{9,8},{10,11... | collective-permute-start | bytes 884744 | tf_op jit(solution)/shard_map/ppermute | solution.py:658
  54.4 5.6 %shard_map.108 = (bf16[96,1024]{1,0:T(8,128)(2,1)S(1)}, bf16[96,1024]{1,0:T(8,128)(2,1)S(1)}) custom-call(s32[6]{0:T(128)S(1)} %concatenate.6.place, bf16[3,192,256]{2,1,0:T(8,128)(2,1)S(1)} %get-tuple-element.52.own_a, bf16[3,192,256]{2,1,0:T(8,128)(2,1)S(1)} %collective-permute-done.8.got_a, bf16[3,192,256]{2,1,0:T(8,128)(2,1)S(1)} %get-tuple-element.54.own_b, ...), custom_call_target="tpu_custom_call" | custom-call | flops 1000 | bytes 1000 | tf_op jit(solution)/shard_map/pallas_call | solution.py:774
  60.9 2.0 %shard_map.112 = (f32[2,160,1024]{2,1,0:T(8,128)S(1)}, bf16[2,160,1024]{2,1,0:T(8,128)(2,1)S(1)}) custom-call(s32[6]{0:T(128)S(1)} %concatenate.6.place, bf16[128,1152]{1,0:T(8,128)(2,1)S(1)} %get-tuple-element.56.keep.keep_a, bf16[128,2176]{1,0:T(8,128)(2,1)S(1)} %collective-permute-done.10.got.got_a, bf16[128,1152]{1,0:T(8,128)(2,1)S(1)} %get-tuple-element.65.keep_b, ...), custom_call_target="tpu_custom_call" | custom-call | flops 1000 | bytes 1000 | tf_op jit(solution)/shard_map/pallas_call | solution.py:632
  63.9 3.4 %collective-permute-start.15 = (bf16[96,1024]{1,0:T(8,128)(2,1)S(1)}, bf16[96,1024]{1,0:T(8,128)(2,1)S(1)}, u32[]{:S(2)}, u32[]{:S(2)}) collective-permute-start(bf16[96,1024]{1,0:T(8,128)(2,1)S(1)} %get-tuple-element.64.after), channel_id=1, source_target_pairs={{0,8},{1,9},{2,10},{3,11},{4,12},{5,13},{6,14},{7,15},{8,0},{9,1},... | collective-permute-start | bytes 589832 | tf_op jit(solution)/shard_map/ppermute | solution.py:658
  67.3 3.4 %collective-permute-start.6 = (bf16[96,1024]{1,0:T(8,128)(2,1)S(1)}, bf16[96,1024]{1,0:T(8,128)(2,1)S(1)}, u32[]{:S(2)}, u32[]{:S(2)}) collective-permute-start(bf16[96,1024]{1,0:T(8,128)(2,1)S(1)} %get-tuple-element.49.after), channel_id=1, source_target_pairs={{0,0},{1,8},{2,2},{3,10},{4,4},{5,12},{6,6},{7,14},{8,1},{9,9},{10... | collective-permute-start | bytes 589832 | tf_op jit(solution)/shard_map/ppermute | solution.py:658
  71.0 14.1 %collective-permute-done.15.got = bf16[96,1024]{1,0:T(8,128)(2,1)S(1)} collective-permute-done((bf16[96,1024]{1,0:T(8,128)(2,1)S(1)}, bf16[96,1024]{1,0:T(8,128)(2,1)S(1)}, u32[]{:S(2)}, u32[]{:S(2)}) %collective-permute-start.15) | collective-permute-done | bytes 196640 | tf_op jit(solution)/shard_map/ppermute | solution.py:658
  85.1 1.3 collective-permute-start.16
  86.4 4.3 %collective-permute-done.6.r0.refs_0_ = bf16[96,1024]{1,0:T(8,128)(2,1)S(1)} collective-permute-done((bf16[96,1024]{1,0:T(8,128)(2,1)S(1)}, bf16[96,1024]{1,0:T(8,128)(2,1)S(1)}, u32[]{:S(2)}, u32[]{:S(2)}) %collective-permute-start.6) | collective-permute-done | bytes 196640 | tf_op jit(solution)/shard_map/ppermute | solution.py:658
  90.9 2.5 %collective-permute-start.21 = (bf16[160,1024]{1,0:T(8,128)(2,1)S(1)}, bf16[160,1024]{1,0:T(8,128)(2,1)S(1)}, u32[]{:S(2)}, u32[]{:S(2)}) collective-permute-start(bf16[160,1024]{1,0:T(8,128)(2,1)S(1)} %get-tuple-element.71), channel_id=1, source_target_pairs={{0,8},{1,9},{2,10},{3,11},{4,12},{5,13},{6,14},{7,15},{8,0},{9,1},... | collective-permute-start | bytes 983048 | tf_op jit(solution)/shard_map/ppermute | solution.py:658
  94.7 2.1 %shard_map.106.refs_3_ = bf16[2,96,1024]{2,1,0:T(8,128)(2,1)} custom-call(s32[6]{0:T(128)S(1)} %concatenate.6.place, bf16[96,1024]{1,0:T(8,128)(2,1)S(1)} %collective-permute-done.6.r0.refs_0_, bf16[96,1024]{1,0:T(8,128)(2,1)S(1)} %collective-permute-done.7.r1.refs_1_, bf16[1024,1024]{1,0:T(8,128)(2,1)S(1)} %copy-done, ...), custom_call_target="tpu_custom_call" | custom-call | flops 1000 | bytes 1000 | tf_op jit(solution)/shard_map/pallas_call | solution.py:632
  96.8 10.2 %collective-permute-done.21.got = bf16[160,1024]{1,0:T(8,128)(2,1)S(1)} collective-permute-done((bf16[160,1024]{1,0:T(8,128)(2,1)S(1)}, bf16[160,1024]{1,0:T(8,128)(2,1)S(1)}, u32[]{:S(2)}, u32[]{:S(2)}) %collective-permute-start.21) | collective-permute-done | bytes 327712 | tf_op jit(solution)/shard_map/ppermute | solution.py:658
  108.0 1.2 collective-permute-start.22
  110.0 6.9 %collective-permute-done.22.b1 = bf16[160,1024]{1,0:T(8,128)(2,1)S(1)} collective-permute-done((bf16[160,1024]{1,0:T(8,128)(2,1)S(1)}, bf16[160,1024]{1,0:T(8,128)(2,1)S(1)}, u32[]{:S(2)}, u32[]{:S(2)}) %collective-permute-start.22) | collective-permute-done | bytes 327712 | tf_op jit(solution)/shard_map/ppermute | solution.py:658
  116.9 1.3 collective-permute-start.24
  118.2 4.9 %collective-permute-start.12 = (bf16[96,1024]{1,0:T(8,128)(2,1)S(1)}, bf16[96,1024]{1,0:T(8,128)(2,1)S(1)}, u32[]{:S(2)}, u32[]{:S(2)}) collective-permute-start(bf16[96,1024]{1,0:T(8,128)(2,1)S(1)} %get-tuple-element.60.before), channel_id=1, source_target_pairs={{0,0},{1,8},{2,2},{3,10},{4,4},{5,12},{6,6},{7,14},{8,1},{9,9},{10... | collective-permute-start | bytes 589832 | tf_op jit(solution)/shard_map/ppermute | solution.py:658
  123.2 4.9 %collective-permute-done.12.r0 = bf16[96,1024]{1,0:T(8,128)(2,1)S(1)} collective-permute-done((bf16[96,1024]{1,0:T(8,128)(2,1)S(1)}, bf16[96,1024]{1,0:T(8,128)(2,1)S(1)}, u32[]{:S(2)}, u32[]{:S(2)}) %collective-permute-start.12) | collective-permute-done | bytes 196640 | tf_op jit(solution)/shard_map/ppermute | solution.py:658
  128.1 3.3 %collective-permute-done.13.r1 = bf16[96,1024]{1,0:T(8,128)(2,1)S(1)} collective-permute-done((bf16[96,1024]{1,0:T(8,128)(2,1)S(1)}, bf16[96,1024]{1,0:T(8,128)(2,1)S(1)}, u32[]{:S(2)}, u32[]{:S(2)}) %collective-permute-start.13) | collective-permute-done | bytes 196640 | tf_op jit(solution)/shard_map/ppermute | solution.py:658
  131.5 1.9 %shard_map.109 = bf16[2,96,1024]{2,1,0:T(8,128)(2,1)} custom-call(s32[6]{0:T(128)S(1)} %concatenate.6.place, bf16[96,1024]{1,0:T(8,128)(2,1)S(1)} %collective-permute-done.12.r0, bf16[96,1024]{1,0:T(8,128)(2,1)S(1)} %collective-permute-done.13.r1, f32[2,96,1024]{2,1,0:T(8,128)S(1)} %get-tuple-element.51.hidden_ref, ...), custom_call_target="tpu_custom_call" | custom-call | flops 1000 | bytes 1000 | tf_op jit(solution)/shard_map/pallas_call | solution.py:632
  133.3 3.0 %shard_map.115 = (f32[1024,768]{1,0:T(8,128)}, f32[1024,256]{1,0:T(8,128)}) custom-call(s32[6]{0:T(128)S(1)} %concatenate.6.place, bf16[96,1024]{1,0:T(8,128)(2,1)S(1)} %shard_map.111.a0, bf16[96,1024]{1,0:T(8,128)(2,1)S(1)} %collective-permute-done.16.refs_0_.a1, bf16[96,1024]{1,0:T(8,128)(2,1)S(1)} %collective-permute-done.17.refs_1_.a2, ...), custom_call_target="tpu_custom_call" | custom-call | flops 1000 | bytes 1000 | tf_op jit(solution)/shard_map/pallas_call | solution.py:632
  (42 shorter events, 9.3 us)
Async XLA Ops:
  4.6 17.9 %collective-permute-start = (bf16[192,1024]{1,0:T(8,128)(2,1)S(1)}, bf16[192,1024]{1,0:T(8,128)(2,1)S(1)}, u32[]{:S(2)}, u32[]{:S(2)}) collective-permute-start(bf16[192,1024]{1,0:T(8,128)(2,1)S(1)} %get-tuple-element.39.m0), channel_id=1, source_target_pairs={{0,0},{1,8},{2,2},{3,10},{4,4},{5,12},{6,6},{7,14},{8,1},{9,9},{10... | collective-permute-start | bytes 1179656 | tf_op jit(solution)/shard_map/ppermute | solution.py:658
  9.4 17.3 %collective-permute-start.1 = (bf16[192,1024]{1,0:T(8,128)(2,1)S(1)}, bf16[192,1024]{1,0:T(8,128)(2,1)S(1)}, u32[]{:S(2)}, u32[]{:S(2)}) collective-permute-start(bf16[192,1024]{1,0:T(8,128)(2,1)S(1)} %get-tuple-element.40.m1), channel_id=1, source_target_pairs={{0,4},{1,12},{2,6},{3,14},{4,0},{5,8},{6,2},{7,10},{8,5},{9,13},{1... | collective-permute-start | bytes 1179656 | tf_op jit(solution)/shard_map/ppermute | solution.py:658
  22.5 5.6 %collective-permute-start.2 = (bf16[192,1024]{1,0:T(8,128)(2,1)S(1)}, bf16[192,1024]{1,0:T(8,128)(2,1)S(1)}, u32[]{:S(2)}, u32[]{:S(2)}) collective-permute-start(bf16[192,1024]{1,0:T(8,128)(2,1)S(1)} %collective-permute-done.p0), channel_id=1, source_target_pairs={{0,1},{1,0},{2,3},{3,2},{4,5},{5,4},{6,7},{7,6},{8,9},{9,8},{10,11... | collective-permute-start | bytes 1179656 | tf_op jit(solution)/shard_map/ppermute | solution.py:658
  26.7 1.7 %collective-permute-start.3 = (bf16[192,1024]{1,0:T(8,128)(2,1)S(1)}, bf16[192,1024]{1,0:T(8,128)(2,1)S(1)}, u32[]{:S(2)}, u32[]{:S(2)}) collective-permute-start(bf16[192,1024]{1,0:T(8,128)(2,1)S(1)} %collective-permute-done.1.p1), channel_id=1, source_target_pairs={{0,1},{1,0},{2,3},{3,2},{4,5},{5,4},{6,7},{7,6},{8,9},{9,8},{10,11... | collective-permute-start | bytes 1179656 | tf_op jit(solution)/shard_map/ppermute | solution.py:658
  26.8 10.2 %collective-permute-start.4 = (bf16[192,1024]{1,0:T(8,128)(2,1)S(1)}, bf16[192,1024]{1,0:T(8,128)(2,1)S(1)}, u32[]{:S(2)}, u32[]{:S(2)}) collective-permute-start(bf16[192,1024]{1,0:T(8,128)(2,1)S(1)} %pad_maximum_fusion), channel_id=1, source_target_pairs={{0,2},{1,3},{2,0},{3,1},{4,6},{5,7},{6,4},{7,5},{8,10},{9,11},{10,... | collective-permute-start | bytes 1179656 | tf_op jit(solution)/shard_map/ppermute | solution.py:658
  33.7 15.3 %collective-permute-start.10 = (bf16[128,2176]{1,0:T(8,128)(2,1)S(1)}, bf16[128,2176]{1,0:T(8,128)(2,1)S(1)}, u32[]{:S(2)}, u32[]{:S(2)}) collective-permute-start(bf16[128,2176]{1,0:T(8,128)(2,1)S(1)} %get-tuple-element.58), channel_id=1, source_target_pairs={{0,2},{1,3},{2,0},{3,1},{4,6},{5,7},{6,4},{7,5},{8,10},{9,11},{10,... | collective-permute-start | bytes 1671176 | tf_op jit(solution)/shard_map/ppermute | solution.py:658
  37.0 9.7 %collective-permute-start.11 = (bf16[192,1024]{1,0:T(8,128)(2,1)S(1)}, bf16[192,1024]{1,0:T(8,128)(2,1)S(1)}, u32[]{:S(2)}, u32[]{:S(2)}) collective-permute-start(bf16[192,1024]{1,0:T(8,128)(2,1)S(1)} %collective-permute-done.4.after.n0), channel_id=1, source_target_pairs={{0,1},{1,0},{2,3},{3,2},{4,5},{5,4},{6,7},{7,6},{8,9},{9,8},{10,11... | collective-permute-start | bytes 1179656 | tf_op jit(solution)/shard_map/ppermute | solution.py:658
  44.6 1.5 %collective-permute-start.5 = (bf16[192,512]{1,0:T(8,128)(2,1)S(1)}, bf16[192,512]{1,0:T(8,128)(2,1)S(1)}, u32[]{:S(2)}, u32[]{:S(2)}) collective-permute-start(bf16[192,512]{1,0:T(8,128)(2,1)S(1)} %get-tuple-element.48), channel_id=1, source_target_pairs={{0,1},{1,0},{2,3},{3,2},{4,5},{5,4},{6,7},{7,6},{8,9},{9,8},{10,11... | collective-permute-start | bytes 589832 | tf_op jit(solution)/shard_map/ppermute | solution.py:658
  44.7 16.2 %collective-permute-start.19 = (bf16[128,2176]{1,0:T(8,128)(2,1)S(1)}, bf16[128,2176]{1,0:T(8,128)(2,1)S(1)}, u32[]{:S(2)}, u32[]{:S(2)}) collective-permute-start(bf16[128,2176]{1,0:T(8,128)(2,1)S(1)} %get-tuple-element.67), channel_id=1, source_target_pairs={{0,2},{1,3},{2,0},{3,1},{4,6},{5,7},{6,4},{7,5},{8,10},{9,11},{10,... | collective-permute-start | bytes 1671176 | tf_op jit(solution)/shard_map/ppermute | solution.py:658
  50.3 9.7 %collective-permute-start.14 = (bf16[2,96,1024]{2,1,0:T(8,128)(2,1)S(1)}, bf16[2,96,1024]{2,1,0:T(8,128)(2,1)S(1)}, u32[]{:S(2)}, u32[]{:S(2)}) collective-permute-start(bf16[2,96,1024]{2,1,0:T(8,128)(2,1)S(1)} %get-tuple-element.59.after), channel_id=1, source_target_pairs={{0,4},{1,5},{2,6},{3,7},{4,0},{5,1},{6,2},{7,3},{8,12},{9,13},{10,... | collective-permute-start | bytes 1179656 | tf_op jit(solution)/shard_map/ppermute | solution.py:658
  50.4 3.6 %collective-permute-start.9 = (bf16[3,192,256]{2,1,0:T(8,128)(2,1)S(1)}, bf16[3,192,256]{2,1,0:T(8,128)(2,1)S(1)}, u32[]{:S(2)}, u32[]{:S(2)}) collective-permute-start(bf16[3,192,256]{2,1,0:T(8,128)(2,1)S(1)} %get-tuple-element.55), channel_id=1, source_target_pairs={{0,1},{1,0},{2,3},{3,2},{4,5},{5,4},{6,7},{7,6},{8,9},{9,8},{10,11... | collective-permute-start | bytes 884744 | tf_op jit(solution)/shard_map/ppermute | solution.py:658
  52.8 1.6 %collective-permute-start.8 = (bf16[3,192,256]{2,1,0:T(8,128)(2,1)S(1)}, bf16[3,192,256]{2,1,0:T(8,128)(2,1)S(1)}, u32[]{:S(2)}, u32[]{:S(2)}) collective-permute-start(bf16[3,192,256]{2,1,0:T(8,128)(2,1)S(1)} %get-tuple-element.53), channel_id=1, source_target_pairs={{0,1},{1,0},{2,3},{3,2},{4,5},{5,4},{6,7},{7,6},{8,9},{9,8},{10,11... | collective-permute-start | bytes 884744 | tf_op jit(solution)/shard_map/ppermute | solution.py:658
  60.9 33.8 %copy-start = (bf16[1024,1024]{1,0:T(8,128)(2,1)S(1)}, bf16[1024,1024]{1,0:T(8,128)(2,1)}, u32[]{:S(2)}) copy-start(bf16[1024,1024]{1,0:T(8,128)(2,1)} %w_ref.2) | copy-start | bytes 6291460
  62.9 27.8 %collective-permute-start.20 = (bf16[2,160,1024]{2,1,0:T(8,128)(2,1)S(1)}, bf16[2,160,1024]{2,1,0:T(8,128)(2,1)S(1)}, u32[]{:S(2)}, u32[]{:S(2)}) collective-permute-start(bf16[2,160,1024]{2,1,0:T(8,128)(2,1)S(1)} %get-tuple-element.69), channel_id=1, source_target_pairs={{0,4},{1,5},{2,6},{3,7},{4,0},{5,1},{6,2},{7,3},{8,12},{9,13},{10,... | collective-permute-start | bytes 1966088 | tf_op jit(solution)/shard_map/ppermute | solution.py:658
  63.9 21.2 %collective-permute-start.15 = (bf16[96,1024]{1,0:T(8,128)(2,1)S(1)}, bf16[96,1024]{1,0:T(8,128)(2,1)S(1)}, u32[]{:S(2)}, u32[]{:S(2)}) collective-permute-start(bf16[96,1024]{1,0:T(8,128)(2,1)S(1)} %get-tuple-element.64.after), channel_id=1, source_target_pairs={{0,8},{1,9},{2,10},{3,11},{4,12},{5,13},{6,14},{7,15},{8,0},{9,1},... | collective-permute-start | bytes 589832 | tf_op jit(solution)/shard_map/ppermute | solution.py:658
  67.3 23.4 %collective-permute-start.6 = (bf16[96,1024]{1,0:T(8,128)(2,1)S(1)}, bf16[96,1024]{1,0:T(8,128)(2,1)S(1)}, u32[]{:S(2)}, u32[]{:S(2)}) collective-permute-start(bf16[96,1024]{1,0:T(8,128)(2,1)S(1)} %get-tuple-element.49.after), channel_id=1, source_target_pairs={{0,0},{1,8},{2,2},{3,10},{4,4},{5,12},{6,6},{7,14},{8,1},{9,9},{10... | collective-permute-start | bytes 589832 | tf_op jit(solution)/shard_map/ppermute | solution.py:658
  70.7 20.0 %collective-permute-start.7 = (bf16[96,1024]{1,0:T(8,128)(2,1)S(1)}, bf16[96,1024]{1,0:T(8,128)(2,1)S(1)}, u32[]{:S(2)}, u32[]{:S(2)}) collective-permute-start(bf16[96,1024]{1,0:T(8,128)(2,1)S(1)} %get-tuple-element.50), channel_id=1, source_target_pairs={{0,4},{1,12},{2,6},{3,14},{4,0},{5,8},{6,2},{7,10},{8,5},{9,13},{1... | collective-permute-start | bytes 589832 | tf_op jit(solution)/shard_map/ppermute | solution.py:658
  85.1 8.5 %collective-permute-start.16 = (bf16[96,1024]{1,0:T(8,128)(2,1)S(1)}, bf16[96,1024]{1,0:T(8,128)(2,1)S(1)}, u32[]{:S(2)}, u32[]{:S(2)}) collective-permute-start(bf16[96,1024]{1,0:T(8,128)(2,1)S(1)} %shard_map.111.a0), channel_id=1, source_target_pairs={{0,2},{1,3},{2,0},{3,1},{4,6},{5,7},{6,4},{7,5},{8,10},{9,11},{10,... | collective-permute-start | bytes 589832 | tf_op jit(solution)/shard_map/ppermute | solution.py:658
  90.9 40.6 %copy-start.2 = (f32[1024]{0:T(1024)S(1)}, f32[1024]{0:T(1024)}, u32[]{:S(2)}) copy-start(f32[1024]{0:T(1024)} %param.13) | copy-start | bytes 12292
  90.9 16.0 %collective-permute-start.21 = (bf16[160,1024]{1,0:T(8,128)(2,1)S(1)}, bf16[160,1024]{1,0:T(8,128)(2,1)S(1)}, u32[]{:S(2)}, u32[]{:S(2)}) collective-permute-start(bf16[160,1024]{1,0:T(8,128)(2,1)S(1)} %get-tuple-element.71), channel_id=1, source_target_pairs={{0,8},{1,9},{2,10},{3,11},{4,12},{5,13},{6,14},{7,15},{8,0},{9,1},... | collective-permute-start | bytes 983048 | tf_op jit(solution)/shard_map/ppermute | solution.py:658
  93.4 3.4 %collective-permute-start.17 = (bf16[96,1024]{1,0:T(8,128)(2,1)S(1)}, bf16[96,1024]{1,0:T(8,128)(2,1)S(1)}, u32[]{:S(2)}, u32[]{:S(2)}) collective-permute-start(bf16[96,1024]{1,0:T(8,128)(2,1)S(1)} %shard_map.111.a0), channel_id=1, source_target_pairs={{0,1},{1,0},{2,3},{3,2},{4,5},{5,4},{6,7},{7,6},{8,9},{9,8},{10,11... | collective-permute-start | bytes 589832 | tf_op jit(solution)/shard_map/ppermute | solution.py:658
  93.6 3.2 %collective-permute-start.18 = (bf16[96,1024]{1,0:T(8,128)(2,1)S(1)}, bf16[96,1024]{1,0:T(8,128)(2,1)S(1)}, u32[]{:S(2)}, u32[]{:S(2)}) collective-permute-start(bf16[96,1024]{1,0:T(8,128)(2,1)S(1)} %collective-permute-done.16.refs_0_.a1), channel_id=1, source_target_pairs={{0,1},{1,0},{2,3},{3,2},{4,5},{5,4},{6,7},{7,6},{8,9},{9,8},{10,11... | collective-permute-start | bytes 589832 | tf_op jit(solution)/shard_map/ppermute | solution.py:658
  106.9 1.0 copy-start.1
  108.0 8.9 %collective-permute-start.22 = (bf16[160,1024]{1,0:T(8,128)(2,1)S(1)}, bf16[160,1024]{1,0:T(8,128)(2,1)S(1)}, u32[]{:S(2)}, u32[]{:S(2)}) collective-permute-start(bf16[160,1024]{1,0:T(8,128)(2,1)S(1)} %shard_map.114.b0), channel_id=1, source_target_pairs={{0,2},{1,3},{2,0},{3,1},{4,6},{5,7},{6,4},{7,5},{8,10},{9,11},{10,... | collective-permute-start | bytes 983048 | tf_op jit(solution)/shard_map/ppermute | solution.py:658
  109.2 24.1 %collective-permute-start.23 = (bf16[160,1024]{1,0:T(8,128)(2,1)S(1)}, bf16[160,1024]{1,0:T(8,128)(2,1)S(1)}, u32[]{:S(2)}, u32[]{:S(2)}) collective-permute-start(bf16[160,1024]{1,0:T(8,128)(2,1)S(1)} %shard_map.114.b0), channel_id=1, source_target_pairs={{0,1},{1,0},{2,3},{3,2},{4,5},{5,4},{6,7},{7,6},{8,9},{9,8},{10,11... | collective-permute-start | bytes 983048 | tf_op jit(solution)/shard_map/ppermute | solution.py:658
  116.9 16.5 %collective-permute-start.24 = (bf16[160,1024]{1,0:T(8,128)(2,1)S(1)}, bf16[160,1024]{1,0:T(8,128)(2,1)S(1)}, u32[]{:S(2)}, u32[]{:S(2)}) collective-permute-start(bf16[160,1024]{1,0:T(8,128)(2,1)S(1)} %collective-permute-done.22.b1), channel_id=1, source_target_pairs={{0,1},{1,0},{2,3},{3,2},{4,5},{5,4},{6,7},{7,6},{8,9},{9,8},{10,11... | collective-permute-start | bytes 983048 | tf_op jit(solution)/shard_map/ppermute | solution.py:658
  118.2 9.9 %collective-permute-start.12 = (bf16[96,1024]{1,0:T(8,128)(2,1)S(1)}, bf16[96,1024]{1,0:T(8,128)(2,1)S(1)}, u32[]{:S(2)}, u32[]{:S(2)}) collective-permute-start(bf16[96,1024]{1,0:T(8,128)(2,1)S(1)} %get-tuple-element.60.before), channel_id=1, source_target_pairs={{0,0},{1,8},{2,2},{3,10},{4,4},{5,12},{6,6},{7,14},{8,1},{9,9},{10... | collective-permute-start | bytes 589832 | tf_op jit(solution)/shard_map/ppermute | solution.py:658
  123.1 8.4 %collective-permute-start.13 = (bf16[96,1024]{1,0:T(8,128)(2,1)S(1)}, bf16[96,1024]{1,0:T(8,128)(2,1)S(1)}, u32[]{:S(2)}, u32[]{:S(2)}) collective-permute-start(bf16[96,1024]{1,0:T(8,128)(2,1)S(1)} %get-tuple-element.61), channel_id=1, source_target_pairs={{0,4},{1,12},{2,6},{3,14},{4,0},{5,8},{6,2},{7,10},{8,5},{9,13},{1... | collective-permute-start | bytes 589832 | tf_op jit(solution)/shard_map/ppermute | solution.py:658

commit v9 on v5

--- a/solution.py
+++ b/solution.py
@@ -284,9 +284,26 @@
 PAR, CORE, LINE, SIDE, KEPT = range(5)
 
 
+def load_weights(core, first_pair, w_in_hbm, w_out_hbm, wq, wk, wv, wo, sems):
+    width = w_out_hbm.shape[0]
+    copies = []
+    for j in range(wq.shape[1] // 128):
+        to = pl.ds(128 * j, 128)
+        row = pl.multiple_of(256 * (first_pair + j) + 128 * core, 128)
+        pairs = [(w_out_hbm.at[pl.ds(row, 128), :], wo.at[to, :])]
+        for t, out in enumerate((wq, wk, wv)):
+            at = pl.multiple_of(t * width + row, 128)
+            pairs.append((w_in_hbm.at[:, pl.ds(at, 128)], out.at[:, to]))
+        copies += [pltpu.make_async_copy(a, b, sems.at[4 * j + i]) for i, (a, b) in enumerate(pairs)]
+    for copy in copies:
+        copy.start()
+    return copies
+
+
 def norm_kernel(
-    place, patch_hbm, cot_hbm, index_hbm, gain_hbm, p0_ref, p1_ref, hidden_ref,
-    patch_ref, cot_ref, index_ref, gain_ref, sems,
+    place, patch_hbm, cot_hbm, index_hbm, gain_hbm, w_in_hbm, w_out_hbm,
+    p0_ref, p1_ref, hidden_ref, wq, wk, wv, wo,
+    patch_ref, cot_ref, index_ref, gain_ref, sems, w_sems,
 ):
     par = place[PAR]
     rows, width = patch_ref.shape[1:]
@@ -299,6 +316,7 @@
     ]
     for copy in copies:
         copy.start()
+    staged = load_weights(place[CORE], 0, w_in_hbm, w_out_hbm, wq, wk, wv, wo, w_sems)
     order = lax.broadcasted_iota(jnp.int32, (1, quarter), 1).astype(jnp.float32)
     freq = jnp.exp(-np.log(np.float32(10000.0)) * order / quarter)
     diagonal = lax.broadcasted_iota(jnp.int32, (rows, rows), 0) == lax.broadcasted_iota(
@@ -331,29 +349,13 @@
         live = live_column(place[KEPT + s], rows)
         grad = cot_ref[s]
         out_ref[rows:, :] = jnp.where(live, grad, jnp.zeros_like(grad))
-
-
-def load_weights(core, first_pair, w_in_hbm, w_out_hbm, wq, wk, wv, wo, sems):
-    width = w_out_hbm.shape[0]
-    copies = []
-    for j in range(wq.shape[1] // 128):
-        to = pl.ds(128 * j, 128)
-        row = pl.multiple_of(256 * (first_pair + j) + 128 * core, 128)
-        pairs = [(w_out_hbm.at[pl.ds(row, 128), :], wo.at[to, :])]
-        for t, out in enumerate((wq, wk, wv)):
-            at = pl.multiple_of(t * width + row, 128)
-            pairs.append((w_in_hbm.at[:, pl.ds(at, 128)], out.at[:, to]))
-        copies += [pltpu.make_async_copy(a, b, sems.at[4 * j + i]) for i, (a, b) in enumerate(pairs)]
-    for copy in copies:
-        copy.start()
-    return copies
+    for copy in staged:
+        copy.wait()
 
 
 def attend_pairs(
-    place, first_pair, payloads, w_in_hbm, w_out_hbm, own, oth, keep_t, out_keep, send,
-    norm_s, grad_s, att_s, wq, wk, wv, wo, sems,
+    place, payloads, wq, wk, wv, wo, own, oth, keep_t, out_keep, send, norm_s, grad_s, att_s,
 ):
-    copies = load_weights(place[CORE], first_pair, w_in_hbm, w_out_hbm, wq, wk, wv, wo, sems)
     block = payloads[0].shape[0] // 2
     rows = 4 * block
     half = 2 * block
@@ -371,8 +373,6 @@
     zero = jnp.zeros((rows, 128), jnp.bfloat16)
     first = place[SIDE] == 0
     count = wq.shape[1] // 128
-    for copy in copies:
-        copy.wait()
     normed = norm_s[...]
     queries = dot_nn(normed, wq[...]).astype(jnp.bfloat16)
     keys = dot_nn(normed, wk[...]).astype(jnp.bfloat16)
@@ -420,13 +420,21 @@
     send[:, 3 * rows :] = dot_nn(att_s[1], grad_s[...]).astype(send.dtype)
 
 
-def attend_first(place, p0, p1, p2, p3, *refs):
-    attend_pairs(place, 0, (p0, p1, p2, p3), *refs)
-
-
-def attend_second(place, p0, p1, p2, p3, w_in_hbm, w_out_hbm, after, *refs):
+def attend_first(
+    place, p0, p1, p2, p3, wq, wk, wv, wo, w_in_hbm, w_out_hbm,
+    own, oth, keep_t, out_keep, send, wq2, wk2, wv2, wo2, norm_s, grad_s, att_s, sems,
+):
+    copies = load_weights(place[CORE], 2, w_in_hbm, w_out_hbm, wq2, wk2, wv2, wo2, sems)
+    attend_pairs(
+        place, (p0, p1, p2, p3), wq, wk, wv, wo, own, oth, keep_t, out_keep, send, norm_s, grad_s, att_s
+    )
+    for copy in copies:
+        copy.wait()
+
+
+def attend_second(place, p0, p1, p2, p3, wq, wk, wv, wo, after, *refs):
     del after
-    attend_pairs(place, 2, (p0, p1, p2, p3), w_in_hbm, w_out_hbm, *refs)
+    attend_pairs(place, (p0, p1, p2, p3), wq, wk, wv, wo, *refs)
 
 
 def in_order(place, own, got):
@@ -466,7 +474,8 @@
         o1[block:, :] = total[block:].astype(o1.dtype)
 
 
-def return_kernel(place, r0, r1, w_ref, hidden_ref, m0, m1, gain_ref, encoded, d_patches):
+def return_kernel(place, r0, r1, w_ref, hidden_ref, m0, m1, gain_ref, after, encoded, d_patches):
+    del after
     par = place[PAR]
     rows = r0.shape[0] // 2
     for k, (r_ref, m_ref) in enumerate(((r0, m0), (r1, m1))):
@@ -648,10 +657,13 @@
     gain_row = gain.reshape(1, width)
     pay = struct((2 * slots, width))
     hbm = pl.BlockSpec(memory_space=pl.ANY)
-    *mine, hidden = call(
+    any_spec = pl.BlockSpec(memory_space=pl.ANY)
+    pairs = width // 512
+    half_w = [struct((width, 128 * pairs))] * 3 + [struct((128 * pairs, width))]
+    *outs, wq, wk, wv, wo = call(
         norm_kernel,
-        tuple(in_hbm(v) for v in (patches, cotangent, kept_index, gain_row)),
-        [pay, pay, struct(patches.shape, f32)],
+        tuple(in_hbm(v) for v in (patches, cotangent, kept_index, gain_row, w_qkv, w_out)),
+        [pay, pay, struct(patches.shape, f32)] + half_w,
         24,
         place,
         scratch=[
@@ -660,39 +672,43 @@
             pltpu.VMEM(kept_index.shape, jnp.int32),
             pltpu.VMEM(gain_row.shape, f32),
             pltpu.SemaphoreType.DMA((4,)),
+            pltpu.SemaphoreType.DMA((4 * pairs,)),
         ],
-        specs=[hbm] * 4,
-    )
+        specs=[any_spec] * 6,
+    )
+    *mine, hidden = outs
     got = [to_chip(mine[k], k) for k in range(2)]
     here = got + [to_core(v) for v in got]
     from_x = to_x(jnp.concatenate([v[:slots] for v in got], axis=0))
     there = (from_x, to_core(from_x))
 
-    any_spec = pl.BlockSpec(memory_space=pl.ANY)
-    pairs = width // 512
     half_rows = struct((4, 2 * slots, 128 * pairs))
     out_half = (64 * pairs, width)
     half_t = struct((64 * pairs, 3 * rows))
     half_send = struct((64 * pairs, 3 * rows + width))
 
-    def attend(kernel, extra):
+    def attend(kernel, args, outs=(), scratch=()):
         return call(
             kernel,
-            (*here, in_hbm(w_qkv), in_hbm(w_out), *extra),
-            [half_rows] * 2 + [half_t, struct(out_half, f32), half_send],
+            (*here, *args),
+            [half_rows] * 2 + [half_t, struct(out_half, f32), half_send] + list(outs),
             32,
             place,
             scratch=[pltpu.VMEM((rows, width), bf16)] * 2
             + [pltpu.VMEM((2, 64 * pairs, rows), bf16)]
-            + [pltpu.VMEM((width, 128 * pairs), bf16)] * 3
-            + [pltpu.VMEM((128 * pairs, width), bf16), pltpu.SemaphoreType.DMA((4 * pairs,))],
-            specs=[VMEM_SPEC] * 4 + [any_spec] * (2 + len(extra)),
+            + list(scratch),
+            specs=[VMEM_SPEC] * 8 + [any_spec] * (len(args) - 4),
         )
 
-    own_a, oth_a, keep_a, out_keep_a, send_a = attend(attend_first, ())
+    own_a, oth_a, keep_a, out_keep_a, send_a, *staged = attend(
+        attend_first,
+        (wq, wk, wv, wo, in_hbm(w_qkv), in_hbm(w_out)),
+        half_w,
+        [pltpu.SemaphoreType.DMA((4 * pairs,))],
+    )
     got_a = to_x(send_a)
     core_a = to_core(oth_a)
-    own_b, oth_b, keep_b, out_keep_b, send_b = attend(attend_second, (from_x,))
+    own_b, oth_b, keep_b, out_keep_b, send_b = attend(attend_second, (*staged, from_x))
     got_b = to_x(send_b)
     core_b = to_core(oth_b)
 
@@ -754,21 +770,22 @@
         compiler_params=pltpu.CompilerParams(vmem_limit_bytes=20 * MIB),
         cost_estimate=COST,
     )(place, own_a, core_a, own_b, core_b, in_hbm(w_qkv), started, first[1])
-    second = spread(second_sum, second_got, (back[0],))
+    second = spread(second_sum, second_got, (back[0], *first[1:]))
     back = [to_rows(back[k], k, 0) for k in range(2)]
-    encoded, d_patches = call(
-        return_kernel,
-        (*back, w_out, hidden, *mine, gain_row),
-        [struct(patches.shape)] * 2,
-        12,
-        place,
-    )
     qkv_grad, out_grad = call(
         finish_kernel,
         (*first, *second),
         [struct((width, 3 * quarter), f32), struct((width, quarter), f32)],
         12,
         place,
+    )
+    encoded, d_patches = call(
+        return_kernel,
+        (*back, w_out, hidden, *mine, gain_row, qkv_grad),
+        [struct(patches.shape)] * 2,
+        12,
+        place,
+        specs=[VMEM_SPEC] * 7 + [any_spec],
     )
     return (encoded, d_patches, qkv_grad, out_grad)
 

time: 128 us -> 128 us (level)
  the two profiles are of different devices: /device:TPU:1 before, /device:TPU:9 now
where the time goes in v9:
time: 128 us
  waiting for transfers between devices  63.7 us (50%)
  starting transfers between devices  30.4 us (24%)
  Pallas kernels  29.9 us (23%)
  local copies, waits for them, and re-layouts  2.67 us (2%)
    ppermute x22, waiting for transfers between devices, send(): return lax.ppermute(value, AXES, line_perm(move, reps))  63.7 us
    ppermute x22, starting transfers between devices, send(): return lax.ppermute(value, AXES, line_perm(move, reps))  30.4 us
    pallas_call x11, Pallas kernels, call(): pl.pallas_call(kernel, in_specs=specs, out_specs=VMEM_SPEC if single else...  24.1 us
    pallas_call x1, Pallas kernels, chip_shards(): pl.pallas_call(rows_kernel, grid_spec=pltpu.PrefetchScalarGridSpec(num_sc...  5.83 us
  transfers between devices with their start and end apart: 22, of which 14 were waited for; matrix products, arithmetic and copies ran while one was open for 0% of the time, Pallas kernels for 18%

profile of v9, /device:TPU:9, one launch (start us, length us, event | category | flops | bytes accessed | tf_op | source)
XLA Modules:
  0.0 127.5 jit_solution(1111090523740319902)
XLA Ops:
  1.4 2.6 %shard_map.102 = (bf16[192,1024]{1,0:T(8,128)(2,1)S(1)}, bf16[192,1024]{1,0:T(8,128)(2,1)S(1)}, f32[2,96,1024]{2,1,0:T(8,128)S(1)}, bf16[1024,256]{1,0:T(8,128)(...) custom-call(s32[6]{0:T(128)S(1)} %concatenate.6.place, ...), custom_call_target="tpu_custom_call" | custom-call | flops 1000 | bytes 1000 | tf_op jit(solution)/shard_map/pallas_call | solution.py:614
  4.0 4.8 %collective-permute-start = (bf16[192,1024]{1,0:T(8,128)(2,1)S(1)}, bf16[192,1024]{1,0:T(8,128)(2,1)S(1)}, u32[]{:S(2)}, u32[]{:S(2)}) collective-permute-start(bf16[192,1024]{1,0:T(8,128)(2,1)S(1)} %get-tuple-element.39.m0), channel_id=1, source_target_pairs={{0,0},{1,8},{2,2},{3,10},{4,4},{5,12},{6,6},{7,14},{8,1},{9,9},{10... | collective-permute-start | bytes 1179656 | tf_op jit(solution)/shard_map/ppermute | solution.py:640
  8.9 13.0 %collective-permute-done.p0 = bf16[192,1024]{1,0:T(8,128)(2,1)S(1)} collective-permute-done((bf16[192,1024]{1,0:T(8,128)(2,1)S(1)}, bf16[192,1024]{1,0:T(8,128)(2,1)S(1)}, u32[]{:S(2)}, u32[]{:S(2)}) %collective-permute-start) | collective-permute-done | bytes 393248 | tf_op jit(solution)/shard_map/ppermute | solution.py:640
  21.9 4.2 %collective-permute-done.1.p1 = bf16[192,1024]{1,0:T(8,128)(2,1)S(1)} collective-permute-done((bf16[192,1024]{1,0:T(8,128)(2,1)S(1)}, bf16[192,1024]{1,0:T(8,128)(2,1)S(1)}, u32[]{:S(2)}, u32[]{:S(2)}) %collective-permute-start.1) | collective-permute-done | bytes 393248 | tf_op jit(solution)/shard_map/ppermute | solution.py:640
  26.2 1.3 %collective-permute-start.5 = (bf16[192,1024]{1,0:T(8,128)(2,1)S(1)}, bf16[192,1024]{1,0:T(8,128)(2,1)S(1)}, u32[]{:S(2)}, u32[]{:S(2)}) collective-permute-start(bf16[192,1024]{1,0:T(8,128)(2,1)S(1)} %pad_maximum_fusion), channel_id=1, source_target_pairs={{0,2},{1,3},{2,0},{3,1},{4,6},{5,7},{6,4},{7,5},{8,10},{9,11},{10,... | collective-permute-start | bytes 1179656 | tf_op jit(solution)/shard_map/ppermute | solution.py:640
  27.8 6.8 %shard_map.103 = (bf16[4,192,256]{2,1,0:T(8,128)(2,1)S(1)}, bf16[4,192,256]{2,1,0:T(8,128)(2,1)S(1)}, bf16[128,1152]{1,0:T(8,128)(2,1)S(1)}, f32[128,1024]{1,0:T...) custom-call(s32[6]{0:T(128)S(1)} %concatenate.6.place, ...), custom_call_target="tpu_custom_call" | custom-call | flops 1000 | bytes 1000 | tf_op jit(solution)/shard_map/pallas_call | solution.py:614
  34.6 1.3 %collective-permute-start.7 = (bf16[128,2176]{1,0:T(8,128)(2,1)S(1)}, bf16[128,2176]{1,0:T(8,128)(2,1)S(1)}, u32[]{:S(2)}, u32[]{:S(2)}) collective-permute-start(bf16[128,2176]{1,0:T(8,128)(2,1)S(1)} %get-tuple-element.54), channel_id=1, source_target_pairs={{0,2},{1,3},{2,0},{3,1},{4,6},{5,7},{6,4},{7,5},{8,10},{9,11},{10,... | collective-permute-start | bytes 1671176 | tf_op jit(solution)/shard_map/ppermute | solution.py:640
  36.4 1.4 %collective-permute-start.9 = (bf16[192,1024]{1,0:T(8,128)(2,1)S(1)}, bf16[192,1024]{1,0:T(8,128)(2,1)S(1)}, u32[]{:S(2)}, u32[]{:S(2)}) collective-permute-start(bf16[192,1024]{1,0:T(8,128)(2,1)S(1)} %collective-permute-done.5.after.n0), channel_id=1, source_target_pairs={{0,1},{1,0},{2,3},{3,2},{4,5},{5,4},{6,7},{7,6},{8,9},{9,8},{10,11... | collective-permute-start | bytes 1179656 | tf_op jit(solution)/shard_map/ppermute | solution.py:640
  37.8 5.2 %shard_map.104 = (bf16[4,192,256]{2,1,0:T(8,128)(2,1)S(1)}, bf16[4,192,256]{2,1,0:T(8,128)(2,1)S(1)}, bf16[128,1152]{1,0:T(8,128)(2,1)S(1)}, f32[128,1024]{1,0:T(8,128)S(1)}, bf16[128,2176]{1,0:T(8,128)(2,1)S(1)}) custom-call(s32[6]{0:T(128)S(1)} %concatenate.6.place, bf16[192,1024]{1,0:T(8,128)(2,1)S(1)} %collective-permute-done.p0, ...), custom_call_target="tpu_custom_call" | custom-call | flops 1000 | bytes 1000 | tf_op jit(solution)/shard_map/pallas_call | solution.py:614
  43.0 1.3 collective-permute-start.8
  44.3 4.2 %collective-permute-done.7.got.got_a = bf16[128,2176]{1,0:T(8,128)(2,1)S(1)} collective-permute-done((bf16[128,2176]{1,0:T(8,128)(2,1)S(1)}, bf16[128,2176]{1,0:T(8,128)(2,1)S(1)}, u32[]{:S(2)}, u32[]{:S(2)}) %collective-permute-start.7) | collective-permute-done | bytes 557088 | tf_op jit(solution)/shard_map/ppermute | solution.py:640
  48.5 1.4 %shard_map.105 = (f32[2,96,1024]{2,1,0:T(8,128)S(1)}, bf16[2,96,1024]{2,1,0:T(8,128)(2,1)S(1)}) custom-call(s32[6]{0:T(128)S(1)} %concatenate.6.place, bf16[128,1152]{1,0:T(8,128)(2,1)S(1)} %get-tuple-element.53.keep.keep_a, f32[128,1024]{1,0:T(8,128)S(1)} %get-tuple-element.58.out_keep, bf16[128,2176]{1,0:T(8,128)(2,1)S(1)} %collective-permute-done.7.got.got_a, ...), custom_call_target="tpu_custom_call" | custom-call | flops 1000 | bytes 1000 | tf_op jit(solution)/shard_map/pallas_call | solution.py:614
  49.9 8.4 %collective-permute-done.10.got = bf16[2,96,1024]{2,1,0:T(8,128)(2,1)S(1)} collective-permute-done((bf16[2,96,1024]{2,1,0:T(8,128)(2,1)S(1)}, bf16[2,96,1024]{2,1,0:T(8,128)(2,1)S(1)}, u32[]{:S(2)}, u32[]{:S(2)}) %collective-permute-start.10) | collective-permute-done | bytes 393248 | tf_op jit(solution)/shard_map/ppermute | solution.py:640
  58.5 1.9 %collective-permute-done.8.got_b = bf16[128,2176]{1,0:T(8,128)(2,1)S(1)} collective-permute-done((bf16[128,2176]{1,0:T(8,128)(2,1)S(1)}, bf16[128,2176]{1,0:T(8,128)(2,1)S(1)}, u32[]{:S(2)}, u32[]{:S(2)}) %collective-permute-start.8) | collective-permute-done | bytes 557088 | tf_op jit(solution)/shard_map/ppermute | solution.py:640
  60.4 2.0 %shard_map.107 = (f32[2,160,1024]{2,1,0:T(8,128)S(1)}, bf16[2,160,1024]{2,1,0:T(8,128)(2,1)S(1)}) custom-call(s32[6]{0:T(128)S(1)} %concatenate.6.place, bf16[128,1152]{1,0:T(8,128)(2,1)S(1)} %get-tuple-element.53.keep.keep_a, bf16[128,2176]{1,0:T(8,128)(2,1)S(1)} %collective-permute-done.7.got.got_a, bf16[128,1152]{1,0:T(8,128)(2,1)S(1)} %get-tuple-element.55.keep_b, ...), custom_call_target="tpu_custom_call" | custom-call | flops 1000 | bytes 1000 | tf_op jit(solution)/shard_map/pallas_call | solution.py:614
  62.5 4.2 %collective-permute-start.11 = (bf16[96,1024]{1,0:T(8,128)(2,1)S(1)}, bf16[96,1024]{1,0:T(8,128)(2,1)S(1)}, u32[]{:S(2)}, u32[]{:S(2)}) collective-permute-start(bf16[96,1024]{1,0:T(8,128)(2,1)S(1)} %get-tuple-element.61.after), channel_id=1, source_target_pairs={{0,8},{1,9},{2,10},{3,11},{4,12},{5,13},{6,14},{7,15},{8,0},{9,1},... | collective-permute-start | bytes 589832 | tf_op jit(solution)/shard_map/ppermute | solution.py:640
  66.7 1.7 %collective-permute-start.4 = (bf16[4,192,256]{2,1,0:T(8,128)(2,1)S(1)}, bf16[4,192,256]{2,1,0:T(8,128)(2,1)S(1)}, u32[]{:S(2)}, u32[]{:S(2)}) collective-permute-start(bf16[4,192,256]{2,1,0:T(8,128)(2,1)S(1)} %get-tuple-element.46), channel_id=1, source_target_pairs={{0,1},{1,0},{2,3},{3,2},{4,5},{5,4},{6,7},{7,6},{8,9},{9,8},{10,11... | collective-permute-start | bytes 1179656 | tf_op jit(solution)/shard_map/ppermute | solution.py:640
  68.4 16.1 %collective-permute-done.11.got = bf16[96,1024]{1,0:T(8,128)(2,1)S(1)} collective-permute-done((bf16[96,1024]{1,0:T(8,128)(2,1)S(1)}, bf16[96,1024]{1,0:T(8,128)(2,1)S(1)}, u32[]{:S(2)}, u32[]{:S(2)}) %collective-permute-start.11) | collective-permute-done | bytes 196640 | tf_op jit(solution)/shard_map/ppermute | solution.py:640
  84.5 1.3 collective-permute-start.12
  86.0 2.5 %collective-permute-start.15 = (bf16[96,1024]{1,0:T(8,128)(2,1)S(1)}, bf16[96,1024]{1,0:T(8,128)(2,1)S(1)}, u32[]{:S(2)}, u32[]{:S(2)}) collective-permute-start(bf16[96,1024]{1,0:T(8,128)(2,1)S(1)} %shard_map.108.a0), channel_id=1, source_target_pairs={{0,1},{1,0},{2,3},{3,2},{4,5},{5,4},{6,7},{7,6},{8,9},{9,8},{10,11... | collective-permute-start | bytes 589832 | tf_op jit(solution)/shard_map/ppermute | solution.py:640
  89.1 3.2 %collective-permute-start.16 = (bf16[96,1024]{1,0:T(8,128)(2,1)S(1)}, bf16[96,1024]{1,0:T(8,128)(2,1)S(1)}, u32[]{:S(2)}, u32[]{:S(2)}) collective-permute-start(bf16[96,1024]{1,0:T(8,128)(2,1)S(1)} %collective-permute-done.12.before.refs_1_.a1), channel_id=1, source_target_pairs={{0,1},{1,0},{2,3},{3,2},{4,5},{5,4},{6,7},{7,6},{8,9},{9,8},{10,11... | collective-permute-start | bytes 589832 | tf_op jit(solution)/shard_map/ppermute | solution.py:640
  92.4 5.8 %shard_map.109 = (bf16[192,1024]{1,0:T(8,128)(2,1)S(1)}, bf16[192,1024]{1,0:T(8,128)(2,1)S(1)}) custom-call(s32[6]{0:T(128)S(1)} %concatenate.6.place, bf16[4,192,256]{2,1,0:T(8,128)(2,1)S(1)} %get-tuple-element.45.own_a, bf16[4,192,256]{2,1,0:T(8,128)(2,1)S(1)} %collective-permute-done.4.got_a, bf16[4,192,256]{2,1,0:T(8,128)(2,1)S(1)} %get-tuple-element.51.own_b, ...), custom_call_target="tpu_custom_call" | custom-call | flops 1000 | bytes 1000 | tf_op jit(solution)/shard_map/pallas_call | solution.py:759
  98.2 1.9 %collective-permute-done.18.got = bf16[160,1024]{1,0:T(8,128)(2,1)S(1)} collective-permute-done((bf16[160,1024]{1,0:T(8,128)(2,1)S(1)}, bf16[160,1024]{1,0:T(8,128)(2,1)S(1)}, u32[]{:S(2)}, u32[]{:S(2)}) %collective-permute-start.18) | collective-permute-done | bytes 327712 | tf_op jit(solution)/shard_map/ppermute | solution.py:640
  100.3 5.7 %collective-permute-start.13 = (bf16[192,1024]{1,0:T(8,128)(2,1)S(1)}, bf16[192,1024]{1,0:T(8,128)(2,1)S(1)}, u32[]{:S(2)}, u32[]{:S(2)}) collective-permute-start(bf16[192,1024]{1,0:T(8,128)(2,1)S(1)} %get-tuple-element.64.refs_0_), channel_id=1, source_target_pairs={{0,0},{1,8},{2,2},{3,10},{4,4},{5,12},{6,6},{7,14},{8,1},{9,9},{10... | collective-permute-start | bytes 1179656 | tf_op jit(solution)/shard_map/ppermute | solution.py:640
  106.1 2.9 %collective-permute-done.19.b1 = bf16[160,1024]{1,0:T(8,128)(2,1)S(1)} collective-permute-done((bf16[160,1024]{1,0:T(8,128)(2,1)S(1)}, bf16[160,1024]{1,0:T(8,128)(2,1)S(1)}, u32[]{:S(2)}, u32[]{:S(2)}) %collective-permute-start.19) | collective-permute-done | bytes 327712 | tf_op jit(solution)/shard_map/ppermute | solution.py:640
  109.1 1.3 %collective-permute-start.21 = (bf16[160,1024]{1,0:T(8,128)(2,1)S(1)}, bf16[160,1024]{1,0:T(8,128)(2,1)S(1)}, u32[]{:S(2)}, u32[]{:S(2)}) collective-permute-start(bf16[160,1024]{1,0:T(8,128)(2,1)S(1)} %collective-permute-done.19.b1), channel_id=1, source_target_pairs={{0,1},{1,0},{2,3},{3,2},{4,5},{5,4},{6,7},{7,6},{8,9},{9,8},{10,11... | collective-permute-start | bytes 983048 | tf_op jit(solution)/shard_map/ppermute | solution.py:640
  110.4 1.3 collective-permute-done.21.b3
  111.7 3.0 %shard_map.112 = (f32[1024,768]{1,0:T(8,128)}, f32[1024,256]{1,0:T(8,128)}) custom-call(s32[6]{0:T(128)S(1)} %concatenate.6.place, bf16[96,1024]{1,0:T(8,128)(2,1)S(1)} %shard_map.108.a0, bf16[96,1024]{1,0:T(8,128)(2,1)S(1)} %collective-permute-done.12.before.refs_1_.a1, bf16[96,1024]{1,0:T(8,128)(2,1)S(1)} %collective-permute-done.15.refs_2_.a2, ...), custom_call_target="tpu_custom_call" | custom-call | flops 1000 | bytes 1000 | tf_op jit(solution)/shard_map/pallas_call | solution.py:614
  114.7 3.5 %collective-permute-done.13.r0 = bf16[192,1024]{1,0:T(8,128)(2,1)S(1)} collective-permute-done((bf16[192,1024]{1,0:T(8,128)(2,1)S(1)}, bf16[192,1024]{1,0:T(8,128)(2,1)S(1)}, u32[]{:S(2)}, u32[]{:S(2)}) %collective-permute-start.13) | collective-permute-done | bytes 393248 | tf_op jit(solution)/shard_map/ppermute | solution.py:640
  118.2 4.8 %collective-permute-done.14.r1 = bf16[192,1024]{1,0:T(8,128)(2,1)S(1)} collective-permute-done((bf16[192,1024]{1,0:T(8,128)(2,1)S(1)}, bf16[192,1024]{1,0:T(8,128)(2,1)S(1)}, u32[]{:S(2)}, u32[]{:S(2)}) %collective-permute-start.14) | collective-permute-done | bytes 393248 | tf_op jit(solution)/shard_map/ppermute | solution.py:640
  123.0 1.9 %copy-done.1 = f32[1024,768]{1,0:T(8,128)S(1)} copy-done((f32[1024,768]{1,0:T(8,128)S(1)}, f32[1024,768]{1,0:T(8,128)}, u32[]{:S(2)}) %copy-start.1) | copy-done | bytes 3145752
  124.9 2.6 %shard_map.113 = (bf16[2,96,1024]{2,1,0:T(8,128)(2,1)}, bf16[2,96,1024]{2,1,0:T(8,128)(2,1)}) custom-call(s32[6]{0:T(128)S(1)} %concatenate.6.place, bf16[192,1024]{1,0:T(8,128)(2,1)S(1)} %collective-permute-done.13.r0, bf16[192,1024]{1,0:T(8,128)(2,1)S(1)} %collective-permute-done.14.r1, bf16[1024,1024]{1,0:T(8,128)(2,1)S(1)} %copy-done, ...), custom_call_target="tpu_custom_call" | custom-call | flops 1000 | bytes 1000 | tf_op jit(solution)/shard_map/pallas_call | solution.py:614
  (34 shorter events, 3.2 us)
Async XLA Ops:
  4.0 17.9 %collective-permute-start = (bf16[192,1024]{1,0:T(8,128)(2,1)S(1)}, bf16[192,1024]{1,0:T(8,128)(2,1)S(1)}, u32[]{:S(2)}, u32[]{:S(2)}) collective-permute-start(bf16[192,1024]{1,0:T(8,128)(2,1)S(1)} %get-tuple-element.39.m0), channel_id=1, source_target_pairs={{0,0},{1,8},{2,2},{3,10},{4,4},{5,12},{6,6},{7,14},{8,1},{9,9},{10... | collective-permute-start | bytes 1179656 | tf_op jit(solution)/shard_map/ppermute | solution.py:640
  8.8 17.3 %collective-permute-start.1 = (bf16[192,1024]{1,0:T(8,128)(2,1)S(1)}, bf16[192,1024]{1,0:T(8,128)(2,1)S(1)}, u32[]{:S(2)}, u32[]{:S(2)}) collective-permute-start(bf16[192,1024]{1,0:T(8,128)(2,1)S(1)} %get-tuple-element.40.m1), channel_id=1, source_target_pairs={{0,4},{1,12},{2,6},{3,14},{4,0},{5,8},{6,2},{7,10},{8,5},{9,13},{1... | collective-permute-start | bytes 1179656 | tf_op jit(solution)/shard_map/ppermute | solution.py:640
  21.9 5.6 %collective-permute-start.2 = (bf16[192,1024]{1,0:T(8,128)(2,1)S(1)}, bf16[192,1024]{1,0:T(8,128)(2,1)S(1)}, u32[]{:S(2)}, u32[]{:S(2)}) collective-permute-start(bf16[192,1024]{1,0:T(8,128)(2,1)S(1)} %collective-permute-done.p0), channel_id=1, source_target_pairs={{0,1},{1,0},{2,3},{3,2},{4,5},{5,4},{6,7},{7,6},{8,9},{9,8},{10,11... | collective-permute-start | bytes 1179656 | tf_op jit(solution)/shard_map/ppermute | solution.py:640
  26.1 1.7 %collective-permute-start.3 = (bf16[192,1024]{1,0:T(8,128)(2,1)S(1)}, bf16[192,1024]{1,0:T(8,128)(2,1)S(1)}, u32[]{:S(2)}, u32[]{:S(2)}) collective-permute-start(bf16[192,1024]{1,0:T(8,128)(2,1)S(1)} %collective-permute-done.1.p1), channel_id=1, source_target_pairs={{0,1},{1,0},{2,3},{3,2},{4,5},{5,4},{6,7},{7,6},{8,9},{9,8},{10,11... | collective-permute-start | bytes 1179656 | tf_op jit(solution)/shard_map/ppermute | solution.py:640
  26.2 10.2 %collective-permute-start.5 = (bf16[192,1024]{1,0:T(8,128)(2,1)S(1)}, bf16[192,1024]{1,0:T(8,128)(2,1)S(1)}, u32[]{:S(2)}, u32[]{:S(2)}) collective-permute-start(bf16[192,1024]{1,0:T(8,128)(2,1)S(1)} %pad_maximum_fusion), channel_id=1, source_target_pairs={{0,2},{1,3},{2,0},{3,1},{4,6},{5,7},{6,4},{7,5},{8,10},{9,11},{10,... | collective-permute-start | bytes 1179656 | tf_op jit(solution)/shard_map/ppermute | solution.py:640
  34.6 13.8 %collective-permute-start.7 = (bf16[128,2176]{1,0:T(8,128)(2,1)S(1)}, bf16[128,2176]{1,0:T(8,128)(2,1)S(1)}, u32[]{:S(2)}, u32[]{:S(2)}) collective-permute-start(bf16[128,2176]{1,0:T(8,128)(2,1)S(1)} %get-tuple-element.54), channel_id=1, source_target_pairs={{0,2},{1,3},{2,0},{3,1},{4,6},{5,7},{6,4},{7,5},{8,10},{9,11},{10,... | collective-permute-start | bytes 1671176 | tf_op jit(solution)/shard_map/ppermute | solution.py:640
  36.4 7.9 %collective-permute-start.9 = (bf16[192,1024]{1,0:T(8,128)(2,1)S(1)}, bf16[192,1024]{1,0:T(8,128)(2,1)S(1)}, u32[]{:S(2)}, u32[]{:S(2)}) collective-permute-start(bf16[192,1024]{1,0:T(8,128)(2,1)S(1)} %collective-permute-done.5.after.n0), channel_id=1, source_target_pairs={{0,1},{1,0},{2,3},{3,2},{4,5},{5,4},{6,7},{7,6},{8,9},{9,8},{10,11... | collective-permute-start | bytes 1179656 | tf_op jit(solution)/shard_map/ppermute | solution.py:640
  43.0 17.4 %collective-permute-start.8 = (bf16[128,2176]{1,0:T(8,128)(2,1)S(1)}, bf16[128,2176]{1,0:T(8,128)(2,1)S(1)}, u32[]{:S(2)}, u32[]{:S(2)}) collective-permute-start(bf16[128,2176]{1,0:T(8,128)(2,1)S(1)} %get-tuple-element.57), channel_id=1, source_target_pairs={{0,2},{1,3},{2,0},{3,1},{4,6},{5,7},{6,4},{7,5},{8,10},{9,11},{10,... | collective-permute-start | bytes 1671176 | tf_op jit(solution)/shard_map/ppermute | solution.py:640
  49.9 8.5 %collective-permute-start.10 = (bf16[2,96,1024]{2,1,0:T(8,128)(2,1)S(1)}, bf16[2,96,1024]{2,1,0:T(8,128)(2,1)S(1)}, u32[]{:S(2)}, u32[]{:S(2)}) collective-permute-start(bf16[2,96,1024]{2,1,0:T(8,128)(2,1)S(1)} %get-tuple-element.60), channel_id=1, source_target_pairs={{0,4},{1,5},{2,6},{3,7},{4,0},{5,1},{6,2},{7,3},{8,12},{9,13},{10,... | collective-permute-start | bytes 1179656 | tf_op jit(solution)/shard_map/ppermute | solution.py:640
  62.4 23.4 %collective-permute-start.17 = (bf16[2,160,1024]{2,1,0:T(8,128)(2,1)S(1)}, bf16[2,160,1024]{2,1,0:T(8,128)(2,1)S(1)}, u32[]{:S(2)}, u32[]{:S(2)}) collective-permute-start(bf16[2,160,1024]{2,1,0:T(8,128)(2,1)S(1)} %get-tuple-element.62.after), channel_id=1, source_target_pairs={{0,4},{1,5},{2,6},{3,7},{4,0},{5,1},{6,2},{7,3},{8,12},{9,13},{10,... | collective-permute-start | bytes 1966088 | tf_op jit(solution)/shard_map/ppermute | solution.py:640
  62.5 22.0 %collective-permute-start.11 = (bf16[96,1024]{1,0:T(8,128)(2,1)S(1)}, bf16[96,1024]{1,0:T(8,128)(2,1)S(1)}, u32[]{:S(2)}, u32[]{:S(2)}) collective-permute-start(bf16[96,1024]{1,0:T(8,128)(2,1)S(1)} %get-tuple-element.61.after), channel_id=1, source_target_pairs={{0,8},{1,9},{2,10},{3,11},{4,12},{5,13},{6,14},{7,15},{8,0},{9,1},... | collective-permute-start | bytes 589832 | tf_op jit(solution)/shard_map/ppermute | solution.py:640
  66.7 25.7 %collective-permute-start.4 = (bf16[4,192,256]{2,1,0:T(8,128)(2,1)S(1)}, bf16[4,192,256]{2,1,0:T(8,128)(2,1)S(1)}, u32[]{:S(2)}, u32[]{:S(2)}) collective-permute-start(bf16[4,192,256]{2,1,0:T(8,128)(2,1)S(1)} %get-tuple-element.46), channel_id=1, source_target_pairs={{0,1},{1,0},{2,3},{3,2},{4,5},{5,4},{6,7},{7,6},{8,9},{9,8},{10,11... | collective-permute-start | bytes 1179656 | tf_op jit(solution)/shard_map/ppermute | solution.py:640
  68.4 24.0 %collective-permute-start.6 = (bf16[4,192,256]{2,1,0:T(8,128)(2,1)S(1)}, bf16[4,192,256]{2,1,0:T(8,128)(2,1)S(1)}, u32[]{:S(2)}, u32[]{:S(2)}) collective-permute-start(bf16[4,192,256]{2,1,0:T(8,128)(2,1)S(1)} %get-tuple-element.52), channel_id=1, source_target_pairs={{0,1},{1,0},{2,3},{3,2},{4,5},{5,4},{6,7},{7,6},{8,9},{9,8},{10,11... | collective-permute-start | bytes 1179656 | tf_op jit(solution)/shard_map/ppermute | solution.py:640
  84.5 4.6 %collective-permute-start.12 = (bf16[96,1024]{1,0:T(8,128)(2,1)S(1)}, bf16[96,1024]{1,0:T(8,128)(2,1)S(1)}, u32[]{:S(2)}, u32[]{:S(2)}) collective-permute-start(bf16[96,1024]{1,0:T(8,128)(2,1)S(1)} %shard_map.108.a0), channel_id=1, source_target_pairs={{0,2},{1,3},{2,0},{3,1},{4,6},{5,7},{6,4},{7,5},{8,10},{9,11},{10,... | collective-permute-start | bytes 589832 | tf_op jit(solution)/shard_map/ppermute | solution.py:640
  86.0 14.2 %collective-permute-start.18 = (bf16[160,1024]{1,0:T(8,128)(2,1)S(1)}, bf16[160,1024]{1,0:T(8,128)(2,1)S(1)}, u32[]{:S(2)}, u32[]{:S(2)}) collective-permute-start(bf16[160,1024]{1,0:T(8,128)(2,1)S(1)} %get-tuple-element.69), channel_id=1, source_target_pairs={{0,8},{1,9},{2,10},{3,11},{4,12},{5,13},{6,14},{7,15},{8,0},{9,1},... | collective-permute-start | bytes 983048 | tf_op jit(solution)/shard_map/ppermute | solution.py:640
  86.0 12.2 %collective-permute-start.15 = (bf16[96,1024]{1,0:T(8,128)(2,1)S(1)}, bf16[96,1024]{1,0:T(8,128)(2,1)S(1)}, u32[]{:S(2)}, u32[]{:S(2)}) collective-permute-start(bf16[96,1024]{1,0:T(8,128)(2,1)S(1)} %shard_map.108.a0), channel_id=1, source_target_pairs={{0,1},{1,0},{2,3},{3,2},{4,5},{5,4},{6,7},{7,6},{8,9},{9,8},{10,11... | collective-permute-start | bytes 589832 | tf_op jit(solution)/shard_map/ppermute | solution.py:640
  89.1 9.1 %collective-permute-start.16 = (bf16[96,1024]{1,0:T(8,128)(2,1)S(1)}, bf16[96,1024]{1,0:T(8,128)(2,1)S(1)}, u32[]{:S(2)}, u32[]{:S(2)}) collective-permute-start(bf16[96,1024]{1,0:T(8,128)(2,1)S(1)} %collective-permute-done.12.before.refs_1_.a1), channel_id=1, source_target_pairs={{0,1},{1,0},{2,3},{3,2},{4,5},{5,4},{6,7},{7,6},{8,9},{9,8},{10,11... | collective-permute-start | bytes 589832 | tf_op jit(solution)/shard_map/ppermute | solution.py:640
  98.2 24.8 %copy-start = (bf16[1024,1024]{1,0:T(8,128)(2,1)S(1)}, bf16[1024,1024]{1,0:T(8,128)(2,1)}, u32[]{:S(2)}) copy-start(bf16[1024,1024]{1,0:T(8,128)(2,1)} %w_ref.3) | copy-start | bytes 6291460
  98.2 24.8 %copy-start.2 = (f32[1024]{0:T(1024)S(1)}, f32[1024]{0:T(1024)}, u32[]{:S(2)}) copy-start(f32[1024]{0:T(1024)} %param.13) | copy-start | bytes 12292
  100.2 8.9 %collective-permute-start.19 = (bf16[160,1024]{1,0:T(8,128)(2,1)S(1)}, bf16[160,1024]{1,0:T(8,128)(2,1)S(1)}, u32[]{:S(2)}, u32[]{:S(2)}) collective-permute-start(bf16[160,1024]{1,0:T(8,128)(2,1)S(1)} %shard_map.111.b0), channel_id=1, source_target_pairs={{0,2},{1,3},{2,0},{3,1},{4,6},{5,7},{6,4},{7,5},{8,10},{9,11},{10,... | collective-permute-start | bytes 983048 | tf_op jit(solution)/shard_map/ppermute | solution.py:640
  100.3 17.9 %collective-permute-start.13 = (bf16[192,1024]{1,0:T(8,128)(2,1)S(1)}, bf16[192,1024]{1,0:T(8,128)(2,1)S(1)}, u32[]{:S(2)}, u32[]{:S(2)}) collective-permute-start(bf16[192,1024]{1,0:T(8,128)(2,1)S(1)} %get-tuple-element.64.refs_0_), channel_id=1, source_target_pairs={{0,0},{1,8},{2,2},{3,10},{4,4},{5,12},{6,6},{7,14},{8,1},{9,9},{10... | collective-permute-start | bytes 1179656 | tf_op jit(solution)/shard_map/ppermute | solution.py:640
  106.0 17.0 %collective-permute-start.14 = (bf16[192,1024]{1,0:T(8,128)(2,1)S(1)}, bf16[192,1024]{1,0:T(8,128)(2,1)S(1)}, u32[]{:S(2)}, u32[]{:S(2)}) collective-permute-start(bf16[192,1024]{1,0:T(8,128)(2,1)S(1)} %get-tuple-element.65), channel_id=1, source_target_pairs={{0,4},{1,12},{2,6},{3,14},{4,0},{5,8},{6,2},{7,10},{8,5},{9,13},{1... | collective-permute-start | bytes 1179656 | tf_op jit(solution)/shard_map/ppermute | solution.py:640
  106.1 4.4 %collective-permute-start.20 = (bf16[160,1024]{1,0:T(8,128)(2,1)S(1)}, bf16[160,1024]{1,0:T(8,128)(2,1)S(1)}, u32[]{:S(2)}, u32[]{:S(2)}) collective-permute-start(bf16[160,1024]{1,0:T(8,128)(2,1)S(1)} %shard_map.111.b0), channel_id=1, source_target_pairs={{0,1},{1,0},{2,3},{3,2},{4,5},{5,4},{6,7},{7,6},{8,9},{9,8},{10,11... | collective-permute-start | bytes 983048 | tf_op jit(solution)/shard_map/ppermute | solution.py:640
  109.1 2.6 %collective-permute-start.21 = (bf16[160,1024]{1,0:T(8,128)(2,1)S(1)}, bf16[160,1024]{1,0:T(8,128)(2,1)S(1)}, u32[]{:S(2)}, u32[]{:S(2)}) collective-permute-start(bf16[160,1024]{1,0:T(8,128)(2,1)S(1)} %collective-permute-done.19.b1), channel_id=1, source_target_pairs={{0,1},{1,0},{2,3},{3,2},{4,5},{5,4},{6,7},{7,6},{8,9},{9,8},{10,11... | collective-permute-start | bytes 983048 | tf_op jit(solution)/shard_map/ppermute | solution.py:640
  123.0 1.9 %copy-start.1 = (f32[1024,768]{1,0:T(8,128)S(1)}, f32[1024,768]{1,0:T(8,128)}, u32[]{:S(2)}) copy-start(f32[1024,768]{1,0:T(8,128)} %get-tuple-element.37.after) | copy-start | bytes 9437188

commit v10 on v9

--- a/solution.py
+++ b/solution.py
@@ -284,12 +284,12 @@
 PAR, CORE, LINE, SIDE, KEPT = range(5)
 
 
-def load_weights(core, first_pair, w_in_hbm, w_out_hbm, wq, wk, wv, wo, sems):
+def load_weights(core, w_in_hbm, w_out_hbm, wq, wk, wv, wo, sems):
     width = w_out_hbm.shape[0]
     copies = []
     for j in range(wq.shape[1] // 128):
         to = pl.ds(128 * j, 128)
-        row = pl.multiple_of(256 * (first_pair + j) + 128 * core, 128)
+        row = pl.multiple_of(256 * j + 128 * core, 128)
         pairs = [(w_out_hbm.at[pl.ds(row, 128), :], wo.at[to, :])]
         for t, out in enumerate((wq, wk, wv)):
             at = pl.multiple_of(t * width + row, 128)
@@ -316,7 +316,7 @@
     ]
     for copy in copies:
         copy.start()
-    staged = load_weights(place[CORE], 0, w_in_hbm, w_out_hbm, wq, wk, wv, wo, w_sems)
+    staged = load_weights(place[CORE], w_in_hbm, w_out_hbm, wq, wk, wv, wo, w_sems)
     order = lax.broadcasted_iota(jnp.int32, (1, quarter), 1).astype(jnp.float32)
     freq = jnp.exp(-np.log(np.float32(10000.0)) * order / quarter)
     diagonal = lax.broadcasted_iota(jnp.int32, (rows, rows), 0) == lax.broadcasted_iota(
@@ -354,7 +354,7 @@
 
 
 def attend_pairs(
-    place, payloads, wq, wk, wv, wo, own, oth, keep_t, out_keep, send, norm_s, grad_s, att_s,
+    place, first_pair, payloads, wq, wk, wv, wo, own, oth, keep_t, out_keep, send, norm_s, grad_s, att_s,
 ):
     block = payloads[0].shape[0] // 2
     rows = 4 * block
@@ -372,12 +372,13 @@
     scale = jnp.bfloat16(0.125)
     zero = jnp.zeros((rows, 128), jnp.bfloat16)
     first = place[SIDE] == 0
-    count = wq.shape[1] // 128
+    count = own.shape[2] // 128
+    here = slice(128 * first_pair, 128 * (first_pair + count))
     normed = norm_s[...]
-    queries = dot_nn(normed, wq[...]).astype(jnp.bfloat16)
-    keys = dot_nn(normed, wk[...]).astype(jnp.bfloat16)
-    values = dot_nn(normed, wv[...]).astype(jnp.bfloat16)
-    d_att = dot_nt(grad_s[...], wo[...]).astype(jnp.bfloat16)
+    queries = dot_nn(normed, wq[:, here]).astype(jnp.bfloat16)
+    keys = dot_nn(normed, wk[:, here]).astype(jnp.bfloat16)
+    values = dot_nn(normed, wv[:, here]).astype(jnp.bfloat16)
+    d_att = dot_nt(grad_s[...], wo[here, :]).astype(jnp.bfloat16)
     for j in range(count):
         cols = slice(128 * j, 128 * j + 128)
         q = queries[:, cols] * scale
@@ -420,21 +421,13 @@
     send[:, 3 * rows :] = dot_nn(att_s[1], grad_s[...]).astype(send.dtype)
 
 
-def attend_first(
-    place, p0, p1, p2, p3, wq, wk, wv, wo, w_in_hbm, w_out_hbm,
-    own, oth, keep_t, out_keep, send, wq2, wk2, wv2, wo2, norm_s, grad_s, att_s, sems,
-):
-    copies = load_weights(place[CORE], 2, w_in_hbm, w_out_hbm, wq2, wk2, wv2, wo2, sems)
-    attend_pairs(
-        place, (p0, p1, p2, p3), wq, wk, wv, wo, own, oth, keep_t, out_keep, send, norm_s, grad_s, att_s
-    )
-    for copy in copies:
-        copy.wait()
+def attend_first(place, p0, p1, p2, p3, *refs):
+    attend_pairs(place, 0, (p0, p1, p2, p3), *refs)
 
 
 def attend_second(place, p0, p1, p2, p3, wq, wk, wv, wo, after, *refs):
     del after
-    attend_pairs(place, (p0, p1, p2, p3), wq, wk, wv, wo, *refs)
+    attend_pairs(place, 2, (p0, p1, p2, p3), wq, wk, wv, wo, *refs)
 
 
 def in_order(place, own, got):
@@ -446,7 +439,7 @@
     return jnp.concatenate(pieces, axis=1)
 
 
-def rows_kernel(place, own_a, got_a, own_b, got_b, w_ref, after, before, o0, o1, total):
+def rows_kernel(place, own_a, got_a, own_b, got_b, w_ref, w_out_ref, after, before, o0, o1, total):
     del after, before
     step = pl.program_id(0)
     core = place[CORE]
@@ -460,9 +453,9 @@
     @pl.when(step == 0)
     def _():
         total[...] = term
-        att = rows_of(3)
-        o0[:block, :] = att[:block]
-        o1[:block, :] = att[block:]
+        projected = dot_nn(rows_of(3), w_out_ref[...]).astype(o0.dtype)
+        o0[:block, :] = projected[:block]
+        o1[:block, :] = projected[block:]
 
     @pl.when(step > 0)
     def _():
@@ -474,7 +467,7 @@
         o1[block:, :] = total[block:].astype(o1.dtype)
 
 
-def return_kernel(place, r0, r1, w_ref, hidden_ref, m0, m1, gain_ref, after, encoded, d_patches):
+def return_kernel(place, r0, r1, hidden_ref, m0, m1, gain_ref, after, encoded, d_patches):
     del after
     par = place[PAR]
     rows = r0.shape[0] // 2
@@ -482,7 +475,7 @@
         s = k ^ par
         live = live_column(place[KEPT + s], rows)
         hidden = hidden_ref[k]
-        projected = dot_nn(r_ref[:rows, :], w_ref[...])
+        projected = r_ref[:rows, :].astype(jnp.float32)
         encoded[s] = jnp.where(live, hidden + projected, 0.0).astype(encoded.dtype)
         center = hidden - jnp.mean(hidden, axis=-1, keepdims=True)
         spread = jnp.mean(center * center, axis=-1, keepdims=True)
@@ -659,11 +652,11 @@
     hbm = pl.BlockSpec(memory_space=pl.ANY)
     any_spec = pl.BlockSpec(memory_space=pl.ANY)
     pairs = width // 512
-    half_w = [struct((width, 128 * pairs))] * 3 + [struct((128 * pairs, width))]
+    own_w = [struct((width, own_width))] * 3 + [struct((own_width, width))]
     *outs, wq, wk, wv, wo = call(
         norm_kernel,
         tuple(in_hbm(v) for v in (patches, cotangent, kept_index, gain_row, w_qkv, w_out)),
-        [pay, pay, struct(patches.shape, f32)] + half_w,
+        [pay, pay, struct(patches.shape, f32)] + own_w,
         24,
         place,
         scratch=[
@@ -672,7 +665,7 @@
             pltpu.VMEM(kept_index.shape, jnp.int32),
             pltpu.VMEM(gain_row.shape, f32),
             pltpu.SemaphoreType.DMA((4,)),
-            pltpu.SemaphoreType.DMA((4 * pairs,)),
+            pltpu.SemaphoreType.DMA((8 * pairs,)),
         ],
         specs=[any_spec] * 6,
     )
@@ -687,28 +680,23 @@
     half_t = struct((64 * pairs, 3 * rows))
     half_send = struct((64 * pairs, 3 * rows + width))
 
-    def attend(kernel, args, outs=(), scratch=()):
+    staged = (wq, wk, wv, wo)
+
+    def attend(kernel, after):
         return call(
             kernel,
-            (*here, *args),
-            [half_rows] * 2 + [half_t, struct(out_half, f32), half_send] + list(outs),
+            (*here, *staged, *after),
+            [half_rows] * 2 + [half_t, struct(out_half, f32), half_send],
             32,
             place,
-            scratch=[pltpu.VMEM((rows, width), bf16)] * 2
-            + [pltpu.VMEM((2, 64 * pairs, rows), bf16)]
-            + list(scratch),
-            specs=[VMEM_SPEC] * 8 + [any_spec] * (len(args) - 4),
+            scratch=[pltpu.VMEM((rows, width), bf16)] * 2 + [pltpu.VMEM((2, 64 * pairs, rows), bf16)],
+            specs=[VMEM_SPEC] * 8 + [any_spec] * len(after),
         )
 
-    own_a, oth_a, keep_a, out_keep_a, send_a, *staged = attend(
-        attend_first,
-        (wq, wk, wv, wo, in_hbm(w_qkv), in_hbm(w_out)),
-        half_w,
-        [pltpu.SemaphoreType.DMA((4 * pairs,))],
-    )
+    own_a, oth_a, keep_a, out_keep_a, send_a = attend(attend_first, ())
     got_a = to_x(send_a)
     core_a = to_core(oth_a)
-    own_b, oth_b, keep_b, out_keep_b, send_b = attend(attend_second, (*staged, from_x))
+    own_b, oth_b, keep_b, out_keep_b, send_b = attend(attend_second, (from_x,))
     got_b = to_x(send_b)
     core_b = to_core(oth_b)
 
@@ -756,20 +744,21 @@
     started = part
     second_sum, _, second_got = pair_sums(keep, part)
     first = spread(first_sum, first_got)
+    whole_w = pl.BlockSpec((width, width), lambda i, p: (0, 0))
     back = pl.pallas_call(
         rows_kernel,
         grid_spec=pltpu.PrefetchScalarGridSpec(
             num_scalar_prefetch=1,
             grid=(3,),
             in_specs=[pl.BlockSpec(half_rows.shape, lambda i, p: (0, 0, 0))] * 4
-            + [pl.BlockSpec((width, width), lambda i, p: (0, i)), any_spec, any_spec],
+            + [pl.BlockSpec((width, width), lambda i, p: (0, i)), whole_w, any_spec, any_spec],
             out_specs=[pl.BlockSpec(pay.shape, lambda i, p: (0, 0))] * 2,
             scratch_shapes=[pltpu.VMEM((2 * slots, width), f32)],
         ),
         out_shape=[pay] * 2,
         compiler_params=pltpu.CompilerParams(vmem_limit_bytes=20 * MIB),
         cost_estimate=COST,
-    )(place, own_a, core_a, own_b, core_b, in_hbm(w_qkv), started, first[1])
+    )(place, own_a, core_a, own_b, core_b, in_hbm(w_qkv), in_hbm(w_out), started, first[1])
     second = spread(second_sum, second_got, (back[0], *first[1:]))
     back = [to_rows(back[k], k, 0) for k in range(2)]
     qkv_grad, out_grad = call(
@@ -781,11 +770,11 @@
     )
     encoded, d_patches = call(
         return_kernel,
-        (*back, w_out, hidden, *mine, gain_row, qkv_grad),
+        (*back, hidden, *mine, gain_row, qkv_grad),
         [struct(patches.shape)] * 2,
         12,
         place,
-        specs=[VMEM_SPEC] * 7 + [any_spec],
+        specs=[VMEM_SPEC] * 6 + [any_spec],
     )
     return (encoded, d_patches, qkv_grad, out_grad)
 

time: 128 us -> 128 us (level)
  starting transfers between devices: 30.4 us -> 31.7 us
    pallas_call x11, Pallas kernels: 24.1 us -> 22.5 us  [call(): pl.pallas_call(kernel, in_specs=specs, out_specs=VMEM_SPEC if single else...]
    ppermute x22, starting transfers between devices: 30.4 us -> 31.7 us  [send(): return lax.ppermute(value, AXES, line_perm(move, reps))]
  transfers between devices with their start and end apart: 22 -> 22, of which waited for: 14 -> 13; matrix products, arithmetic and copies ran while one was open for 0% -> 0% of each run, Pallas kernels for 18% -> 17%
where the time goes in v10:
time: 128 us
  waiting for transfers between devices  63 us (49%)
  starting transfers between devices  31.7 us (25%)
  Pallas kernels  29.6 us (23%)
  local copies, waits for them, and re-layouts  2.66 us (2%)
    ppermute x22, waiting for transfers between devices, send(): return lax.ppermute(value, AXES, line_perm(move, reps))  63 us
    ppermute x22, starting transfers between devices, send(): return lax.ppermute(value, AXES, line_perm(move, reps))  31.7 us
    pallas_call x11, Pallas kernels, call(): pl.pallas_call(kernel, in_specs=specs, out_specs=VMEM_SPEC if single else...  22.5 us
    pallas_call x1, Pallas kernels, chip_shards(): pl.pallas_call(rows_kernel, grid_spec=pltpu.PrefetchScalarGridSpec(num_sc...  7.06 us
  transfers between devices with their start and end apart: 22, of which 13 were waited for; matrix products, arithmetic and copies ran while one was open for 0% of the time, Pallas kernels for 17%

profile of v10, /device:TPU:9, one launch (start us, length us, event | category | flops | bytes accessed | tf_op | source)
XLA Modules:
  0.0 127.7 jit_solution(14116651166491452667)
XLA Ops:
  1.4 3.4 %shard_map.102 = (bf16[192,1024]{1,0:T(8,128)(2,1)S(1)}, bf16[192,1024]{1,0:T(8,128)(2,1)S(1)}, f32[2,96,1024]{2,1,0:T(8,128)S(1)}, bf16[1024,512]{1,0:T(8,128)(...) custom-call(s32[6]{0:T(128)S(1)} %concatenate.6.place, ...), custom_call_target="tpu_custom_call" | custom-call | flops 1000 | bytes 1000 | tf_op jit(solution)/shard_map/pallas_call | solution.py:607
  4.8 4.8 %collective-permute-start = (bf16[192,1024]{1,0:T(8,128)(2,1)S(1)}, bf16[192,1024]{1,0:T(8,128)(2,1)S(1)}, u32[]{:S(2)}, u32[]{:S(2)}) collective-permute-start(bf16[192,1024]{1,0:T(8,128)(2,1)S(1)} %get-tuple-element.35.m0), channel_id=1, source_target_pairs={{0,0},{1,8},{2,2},{3,10},{4,4},{5,12},{6,6},{7,14},{8,1},{9,9},{10... | collective-permute-start | bytes 1179656 | tf_op jit(solution)/shard_map/ppermute | solution.py:633
  9.6 13.0 %collective-permute-done.p0 = bf16[192,1024]{1,0:T(8,128)(2,1)S(1)} collective-permute-done((bf16[192,1024]{1,0:T(8,128)(2,1)S(1)}, bf16[192,1024]{1,0:T(8,128)(2,1)S(1)}, u32[]{:S(2)}, u32[]{:S(2)}) %collective-permute-start) | collective-permute-done | bytes 393248 | tf_op jit(solution)/shard_map/ppermute | solution.py:633
  22.7 4.2 %collective-permute-done.1.p1 = bf16[192,1024]{1,0:T(8,128)(2,1)S(1)} collective-permute-done((bf16[192,1024]{1,0:T(8,128)(2,1)S(1)}, bf16[192,1024]{1,0:T(8,128)(2,1)S(1)}, u32[]{:S(2)}, u32[]{:S(2)}) %collective-permute-start.1) | collective-permute-done | bytes 393248 | tf_op jit(solution)/shard_map/ppermute | solution.py:633
  26.9 1.3 collective-permute-start.5
  28.6 5.2 %shard_map.103 = (bf16[4,192,256]{2,1,0:T(8,128)(2,1)S(1)}, bf16[4,192,256]{2,1,0:T(8,128)(2,1)S(1)}, bf16[128,1152]{1,0:T(8,128)(2,1)S(1)}, f32[128,1024]{1,0:T(8,128)S(1)}, bf16[128,2176]{1,0:T(8,128)(2,1)S(1)}) custom-call(s32[6]{0:T(128)S(1)} %concatenate.6.place, bf16[192,1024]{1,0:T(8,128)(2,1)S(1)} %collective-permute-done.p0, ...), custom_call_target="tpu_custom_call" | custom-call | flops 1000 | bytes 1000 | tf_op jit(solution)/shard_map/pallas_call | solution.py:607
  33.8 1.3 %collective-permute-start.7 = (bf16[128,2176]{1,0:T(8,128)(2,1)S(1)}, bf16[128,2176]{1,0:T(8,128)(2,1)S(1)}, u32[]{:S(2)}, u32[]{:S(2)}) collective-permute-start(bf16[128,2176]{1,0:T(8,128)(2,1)S(1)} %get-tuple-element.46), channel_id=1, source_target_pairs={{0,2},{1,3},{2,0},{3,1},{4,6},{5,7},{6,4},{7,5},{8,10},{9,11},{10,... | collective-permute-start | bytes 1671176 | tf_op jit(solution)/shard_map/ppermute | solution.py:633
  35.1 2.1 %collective-permute-done.5.after.n0 = bf16[192,1024]{1,0:T(8,128)(2,1)S(1)} collective-permute-done((bf16[192,1024]{1,0:T(8,128)(2,1)S(1)}, bf16[192,1024]{1,0:T(8,128)(2,1)S(1)}, u32[]{:S(2)}, u32[]{:S(2)}) %collective-permute-start.5) | collective-permute-done | bytes 393248 | tf_op jit(solution)/shard_map/ppermute | solution.py:633
  37.2 2.3 %collective-permute-start.9 = (bf16[192,1024]{1,0:T(8,128)(2,1)S(1)}, bf16[192,1024]{1,0:T(8,128)(2,1)S(1)}, u32[]{:S(2)}, u32[]{:S(2)}) collective-permute-start(bf16[192,1024]{1,0:T(8,128)(2,1)S(1)} %collective-permute-done.5.after.n0), channel_id=1, source_target_pairs={{0,1},{1,0},{2,3},{3,2},{4,5},{5,4},{6,7},{7,6},{8,9},{9,8},{10,11... | collective-permute-start | bytes 1179656 | tf_op jit(solution)/shard_map/ppermute | solution.py:633
  39.5 5.2 %shard_map.104 = (bf16[4,192,256]{2,1,0:T(8,128)(2,1)S(1)}, bf16[4,192,256]{2,1,0:T(8,128)(2,1)S(1)}, bf16[128,1152]{1,0:T(8,128)(2,1)S(1)}, f32[128,1024]{1,0:T(8,128)S(1)}, bf16[128,2176]{1,0:T(8,128)(2,1)S(1)}) custom-call(s32[6]{0:T(128)S(1)} %concatenate.6.place, bf16[192,1024]{1,0:T(8,128)(2,1)S(1)} %collective-permute-done.p0, ...), custom_call_target="tpu_custom_call" | custom-call | flops 1000 | bytes 1000 | tf_op jit(solution)/shard_map/pallas_call | solution.py:607
  44.8 1.3 %collective-permute-start.8 = (bf16[128,2176]{1,0:T(8,128)(2,1)S(1)}, bf16[128,2176]{1,0:T(8,128)(2,1)S(1)}, u32[]{:S(2)}, u32[]{:S(2)}) collective-permute-start(bf16[128,2176]{1,0:T(8,128)(2,1)S(1)} %get-tuple-element.49), channel_id=1, source_target_pairs={{0,2},{1,3},{2,0},{3,1},{4,6},{5,7},{6,4},{7,5},{8,10},{9,11},{10,... | collective-permute-start | bytes 1671176 | tf_op jit(solution)/shard_map/ppermute | solution.py:633
  46.0 3.1 %collective-permute-done.7.got.got_a = bf16[128,2176]{1,0:T(8,128)(2,1)S(1)} collective-permute-done((bf16[128,2176]{1,0:T(8,128)(2,1)S(1)}, bf16[128,2176]{1,0:T(8,128)(2,1)S(1)}, u32[]{:S(2)}, u32[]{:S(2)}) %collective-permute-start.7) | collective-permute-done | bytes 557088 | tf_op jit(solution)/shard_map/ppermute | solution.py:633
  49.1 1.4 %shard_map.105 = (f32[2,96,1024]{2,1,0:T(8,128)S(1)}, bf16[2,96,1024]{2,1,0:T(8,128)(2,1)S(1)}) custom-call(s32[6]{0:T(128)S(1)} %concatenate.6.place, bf16[128,1152]{1,0:T(8,128)(2,1)S(1)} %get-tuple-element.45.keep.keep_a, f32[128,1024]{1,0:T(8,128)S(1)} %get-tuple-element.50.out_keep, bf16[128,2176]{1,0:T(8,128)(2,1)S(1)} %collective-permute-done.7.got.got_a, ...), custom_call_target="tpu_custom_call" | custom-call | flops 1000 | bytes 1000 | tf_op jit(solution)/shard_map/pallas_call | solution.py:607
  50.6 8.3 %collective-permute-done.10.got = bf16[2,96,1024]{2,1,0:T(8,128)(2,1)S(1)} collective-permute-done((bf16[2,96,1024]{2,1,0:T(8,128)(2,1)S(1)}, bf16[2,96,1024]{2,1,0:T(8,128)(2,1)S(1)}, u32[]{:S(2)}, u32[]{:S(2)}) %collective-permute-start.10) | collective-permute-done | bytes 393248 | tf_op jit(solution)/shard_map/ppermute | solution.py:633
  59.0 2.1 %collective-permute-done.8.got_b = bf16[128,2176]{1,0:T(8,128)(2,1)S(1)} collective-permute-done((bf16[128,2176]{1,0:T(8,128)(2,1)S(1)}, bf16[128,2176]{1,0:T(8,128)(2,1)S(1)}, u32[]{:S(2)}, u32[]{:S(2)}) %collective-permute-start.8) | collective-permute-done | bytes 557088 | tf_op jit(solution)/shard_map/ppermute | solution.py:633
  61.1 2.0 %shard_map.107 = (f32[2,160,1024]{2,1,0:T(8,128)S(1)}, bf16[2,160,1024]{2,1,0:T(8,128)(2,1)S(1)}) custom-call(s32[6]{0:T(128)S(1)} %concatenate.6.place, bf16[128,1152]{1,0:T(8,128)(2,1)S(1)} %get-tuple-element.45.keep.keep_a, bf16[128,2176]{1,0:T(8,128)(2,1)S(1)} %collective-permute-done.7.got.got_a, bf16[128,1152]{1,0:T(8,128)(2,1)S(1)} %get-tuple-element.47.keep_b, ...), custom_call_target="tpu_custom_call" | custom-call | flops 1000 | bytes 1000 | tf_op jit(solution)/shard_map/pallas_call | solution.py:607
  63.1 4.3 %collective-permute-start.11 = (bf16[96,1024]{1,0:T(8,128)(2,1)S(1)}, bf16[96,1024]{1,0:T(8,128)(2,1)S(1)}, u32[]{:S(2)}, u32[]{:S(2)}) collective-permute-start(bf16[96,1024]{1,0:T(8,128)(2,1)S(1)} %get-tuple-element.53.after), channel_id=1, source_target_pairs={{0,8},{1,9},{2,10},{3,11},{4,12},{5,13},{6,14},{7,15},{8,0},{9,1},... | collective-permute-start | bytes 589832 | tf_op jit(solution)/shard_map/ppermute | solution.py:633
  67.5 1.7 %collective-permute-start.4 = (bf16[4,192,256]{2,1,0:T(8,128)(2,1)S(1)}, bf16[4,192,256]{2,1,0:T(8,128)(2,1)S(1)}, u32[]{:S(2)}, u32[]{:S(2)}) collective-permute-start(bf16[4,192,256]{2,1,0:T(8,128)(2,1)S(1)} %get-tuple-element.42), channel_id=1, source_target_pairs={{0,1},{1,0},{2,3},{3,2},{4,5},{5,4},{6,7},{7,6},{8,9},{9,8},{10,11... | collective-permute-start | bytes 1179656 | tf_op jit(solution)/shard_map/ppermute | solution.py:633
  69.2 16.1 %collective-permute-done.11.got = bf16[96,1024]{1,0:T(8,128)(2,1)S(1)} collective-permute-done((bf16[96,1024]{1,0:T(8,128)(2,1)S(1)}, bf16[96,1024]{1,0:T(8,128)(2,1)S(1)}, u32[]{:S(2)}, u32[]{:S(2)}) %collective-permute-start.11) | collective-permute-done | bytes 196640 | tf_op jit(solution)/shard_map/ppermute | solution.py:633
  85.4 1.3 collective-permute-start.12
  86.9 2.5 %collective-permute-start.15 = (bf16[96,1024]{1,0:T(8,128)(2,1)S(1)}, bf16[96,1024]{1,0:T(8,128)(2,1)S(1)}, u32[]{:S(2)}, u32[]{:S(2)}) collective-permute-start(bf16[96,1024]{1,0:T(8,128)(2,1)S(1)} %shard_map.108.a0), channel_id=1, source_target_pairs={{0,1},{1,0},{2,3},{3,2},{4,5},{5,4},{6,7},{7,6},{8,9},{9,8},{10,11... | collective-permute-start | bytes 589832 | tf_op jit(solution)/shard_map/ppermute | solution.py:633
  89.9 3.3 %collective-permute-start.16 = (bf16[96,1024]{1,0:T(8,128)(2,1)S(1)}, bf16[96,1024]{1,0:T(8,128)(2,1)S(1)}, u32[]{:S(2)}, u32[]{:S(2)}) collective-permute-start(bf16[96,1024]{1,0:T(8,128)(2,1)S(1)} %collective-permute-done.12.before.refs_1_.a1), channel_id=1, source_target_pairs={{0,1},{1,0},{2,3},{3,2},{4,5},{5,4},{6,7},{7,6},{8,9},{9,8},{10,11... | collective-permute-start | bytes 589832 | tf_op jit(solution)/shard_map/ppermute | solution.py:633
  93.3 7.1 %shard_map.109 = (bf16[192,1024]{1,0:T(8,128)(2,1)S(1)}, bf16[192,1024]{1,0:T(8,128)(2,1)S(1)}) custom-call(s32[6]{0:T(128)S(1)} %concatenate.6.place, bf16[4,192,256]{2,1,0:T(8,128)(2,1)S(1)} %get-tuple-element.41.own_a, bf16[4,192,256]{2,1,0:T(8,128)(2,1)S(1)} %collective-permute-done.4.got_a, bf16[4,192,256]{2,1,0:T(8,128)(2,1)S(1)} %get-tuple-element.43.own_b, ...), custom_call_target="tpu_custom_call" | custom-call | flops 1000 | bytes 1000 | tf_op jit(solution)/shard_map/pallas_call | solution.py:748
  100.4 1.3 %collective-permute-start.19 = (bf16[160,1024]{1,0:T(8,128)(2,1)S(1)}, bf16[160,1024]{1,0:T(8,128)(2,1)S(1)}, u32[]{:S(2)}, u32[]{:S(2)}) collective-permute-start(bf16[160,1024]{1,0:T(8,128)(2,1)S(1)} %shard_map.111.b0), channel_id=1, source_target_pairs={{0,2},{1,3},{2,0},{3,1},{4,6},{5,7},{6,4},{7,5},{8,10},{9,11},{10,... | collective-permute-start | bytes 983048 | tf_op jit(solution)/shard_map/ppermute | solution.py:633
  101.7 4.6 %collective-permute-start.13 = (bf16[192,1024]{1,0:T(8,128)(2,1)S(1)}, bf16[192,1024]{1,0:T(8,128)(2,1)S(1)}, u32[]{:S(2)}, u32[]{:S(2)}) collective-permute-start(bf16[192,1024]{1,0:T(8,128)(2,1)S(1)} %get-tuple-element.56.refs_0_), channel_id=1, source_target_pairs={{0,0},{1,8},{2,2},{3,10},{4,4},{5,12},{6,6},{7,14},{8,1},{9,9},{10... | collective-permute-start | bytes 1179656 | tf_op jit(solution)/shard_map/ppermute | solution.py:633
  106.5 2.9 %collective-permute-done.19.b1 = bf16[160,1024]{1,0:T(8,128)(2,1)S(1)} collective-permute-done((bf16[160,1024]{1,0:T(8,128)(2,1)S(1)}, bf16[160,1024]{1,0:T(8,128)(2,1)S(1)}, u32[]{:S(2)}, u32[]{:S(2)}) %collective-permute-start.19) | collective-permute-done | bytes 327712 | tf_op jit(solution)/shard_map/ppermute | solution.py:633
  109.4 1.3 collective-permute-start.21
  111.9 3.0 %shard_map.112 = (f32[1024,768]{1,0:T(8,128)}, f32[1024,256]{1,0:T(8,128)}) custom-call(s32[6]{0:T(128)S(1)} %concatenate.6.place, bf16[96,1024]{1,0:T(8,128)(2,1)S(1)} %shard_map.108.a0, bf16[96,1024]{1,0:T(8,128)(2,1)S(1)} %collective-permute-done.12.before.refs_1_.a1, bf16[96,1024]{1,0:T(8,128)(2,1)S(1)} %collective-permute-done.15.refs_2_.a2, ...), custom_call_target="tpu_custom_call" | custom-call | flops 1000 | bytes 1000 | tf_op jit(solution)/shard_map/pallas_call | solution.py:607
  114.9 3.9 %collective-permute-done.13.r0 = bf16[192,1024]{1,0:T(8,128)(2,1)S(1)} collective-permute-done((bf16[192,1024]{1,0:T(8,128)(2,1)S(1)}, bf16[192,1024]{1,0:T(8,128)(2,1)S(1)}, u32[]{:S(2)}, u32[]{:S(2)}) %collective-permute-start.13) | collective-permute-done | bytes 393248 | tf_op jit(solution)/shard_map/ppermute | solution.py:633
  118.8 5.1 %collective-permute-done.14.r1 = bf16[192,1024]{1,0:T(8,128)(2,1)S(1)} collective-permute-done((bf16[192,1024]{1,0:T(8,128)(2,1)S(1)}, bf16[192,1024]{1,0:T(8,128)(2,1)S(1)}, u32[]{:S(2)}, u32[]{:S(2)}) %collective-permute-start.14) | collective-permute-done | bytes 393248 | tf_op jit(solution)/shard_map/ppermute | solution.py:633
  123.9 1.9 %copy-done = f32[1024,768]{1,0:T(8,128)S(1)} copy-done((f32[1024,768]{1,0:T(8,128)S(1)}, f32[1024,768]{1,0:T(8,128)}, u32[]{:S(2)}) %copy-start) | copy-done | bytes 3145752
  125.8 1.9 %shard_map.113 = (bf16[2,96,1024]{2,1,0:T(8,128)(2,1)}, bf16[2,96,1024]{2,1,0:T(8,128)(2,1)}) custom-call(s32[6]{0:T(128)S(1)} %concatenate.6.place, bf16[192,1024]{1,0:T(8,128)(2,1)S(1)} %collective-permute-done.13.r0, bf16[192,1024]{1,0:T(8,128)(2,1)S(1)} %collective-permute-done.14.r1, f32[2,96,1024]{2,1,0:T(8,128)S(1)} %get-tuple-element.58.hidden_ref, ...), custom_call_target="tpu_custom_call" | custom-call | flops 1000 | bytes 1000 | tf_op jit(solution)/shard_map/pallas_call | solution.py:607
  (32 shorter events, 3.8 us)
Async XLA Ops:
  4.8 17.9 %collective-permute-start = (bf16[192,1024]{1,0:T(8,128)(2,1)S(1)}, bf16[192,1024]{1,0:T(8,128)(2,1)S(1)}, u32[]{:S(2)}, u32[]{:S(2)}) collective-permute-start(bf16[192,1024]{1,0:T(8,128)(2,1)S(1)} %get-tuple-element.35.m0), channel_id=1, source_target_pairs={{0,0},{1,8},{2,2},{3,10},{4,4},{5,12},{6,6},{7,14},{8,1},{9,9},{10... | collective-permute-start | bytes 1179656 | tf_op jit(solution)/shard_map/ppermute | solution.py:633
  9.6 17.3 %collective-permute-start.1 = (bf16[192,1024]{1,0:T(8,128)(2,1)S(1)}, bf16[192,1024]{1,0:T(8,128)(2,1)S(1)}, u32[]{:S(2)}, u32[]{:S(2)}) collective-permute-start(bf16[192,1024]{1,0:T(8,128)(2,1)S(1)} %get-tuple-element.36.m1), channel_id=1, source_target_pairs={{0,4},{1,12},{2,6},{3,14},{4,0},{5,8},{6,2},{7,10},{8,5},{9,13},{1... | collective-permute-start | bytes 1179656 | tf_op jit(solution)/shard_map/ppermute | solution.py:633
  22.7 5.6 %collective-permute-start.2 = (bf16[192,1024]{1,0:T(8,128)(2,1)S(1)}, bf16[192,1024]{1,0:T(8,128)(2,1)S(1)}, u32[]{:S(2)}, u32[]{:S(2)}) collective-permute-start(bf16[192,1024]{1,0:T(8,128)(2,1)S(1)} %collective-permute-done.p0), channel_id=1, source_target_pairs={{0,1},{1,0},{2,3},{3,2},{4,5},{5,4},{6,7},{7,6},{8,9},{9,8},{10,11... | collective-permute-start | bytes 1179656 | tf_op jit(solution)/shard_map/ppermute | solution.py:633
  26.9 1.7 %collective-permute-start.3 = (bf16[192,1024]{1,0:T(8,128)(2,1)S(1)}, bf16[192,1024]{1,0:T(8,128)(2,1)S(1)}, u32[]{:S(2)}, u32[]{:S(2)}) collective-permute-start(bf16[192,1024]{1,0:T(8,128)(2,1)S(1)} %collective-permute-done.1.p1), channel_id=1, source_target_pairs={{0,1},{1,0},{2,3},{3,2},{4,5},{5,4},{6,7},{7,6},{8,9},{9,8},{10,11... | collective-permute-start | bytes 1179656 | tf_op jit(solution)/shard_map/ppermute | solution.py:633
  26.9 10.2 %collective-permute-start.5 = (bf16[192,1024]{1,0:T(8,128)(2,1)S(1)}, bf16[192,1024]{1,0:T(8,128)(2,1)S(1)}, u32[]{:S(2)}, u32[]{:S(2)}) collective-permute-start(bf16[192,1024]{1,0:T(8,128)(2,1)S(1)} %pad_maximum_fusion), channel_id=1, source_target_pairs={{0,2},{1,3},{2,0},{3,1},{4,6},{5,7},{6,4},{7,5},{8,10},{9,11},{10,... | collective-permute-start | bytes 1179656 | tf_op jit(solution)/shard_map/ppermute | solution.py:633
  33.8 15.3 %collective-permute-start.7 = (bf16[128,2176]{1,0:T(8,128)(2,1)S(1)}, bf16[128,2176]{1,0:T(8,128)(2,1)S(1)}, u32[]{:S(2)}, u32[]{:S(2)}) collective-permute-start(bf16[128,2176]{1,0:T(8,128)(2,1)S(1)} %get-tuple-element.46), channel_id=1, source_target_pairs={{0,2},{1,3},{2,0},{3,1},{4,6},{5,7},{6,4},{7,5},{8,10},{9,11},{10,... | collective-permute-start | bytes 1671176 | tf_op jit(solution)/shard_map/ppermute | solution.py:633
  37.2 8.9 %collective-permute-start.9 = (bf16[192,1024]{1,0:T(8,128)(2,1)S(1)}, bf16[192,1024]{1,0:T(8,128)(2,1)S(1)}, u32[]{:S(2)}, u32[]{:S(2)}) collective-permute-start(bf16[192,1024]{1,0:T(8,128)(2,1)S(1)} %collective-permute-done.5.after.n0), channel_id=1, source_target_pairs={{0,1},{1,0},{2,3},{3,2},{4,5},{5,4},{6,7},{7,6},{8,9},{9,8},{10,11... | collective-permute-start | bytes 1179656 | tf_op jit(solution)/shard_map/ppermute | solution.py:633
  44.8 16.3 %collective-permute-start.8 = (bf16[128,2176]{1,0:T(8,128)(2,1)S(1)}, bf16[128,2176]{1,0:T(8,128)(2,1)S(1)}, u32[]{:S(2)}, u32[]{:S(2)}) collective-permute-start(bf16[128,2176]{1,0:T(8,128)(2,1)S(1)} %get-tuple-element.49), channel_id=1, source_target_pairs={{0,2},{1,3},{2,0},{3,1},{4,6},{5,7},{6,4},{7,5},{8,10},{9,11},{10,... | collective-permute-start | bytes 1671176 | tf_op jit(solution)/shard_map/ppermute | solution.py:633
  50.5 8.4 %collective-permute-start.10 = (bf16[2,96,1024]{2,1,0:T(8,128)(2,1)S(1)}, bf16[2,96,1024]{2,1,0:T(8,128)(2,1)S(1)}, u32[]{:S(2)}, u32[]{:S(2)}) collective-permute-start(bf16[2,96,1024]{2,1,0:T(8,128)(2,1)S(1)} %get-tuple-element.52), channel_id=1, source_target_pairs={{0,4},{1,5},{2,6},{3,7},{4,0},{5,1},{6,2},{7,3},{8,12},{9,13},{10,... | collective-permute-start | bytes 1179656 | tf_op jit(solution)/shard_map/ppermute | solution.py:633
  63.1 23.6 %collective-permute-start.17 = (bf16[2,160,1024]{2,1,0:T(8,128)(2,1)S(1)}, bf16[2,160,1024]{2,1,0:T(8,128)(2,1)S(1)}, u32[]{:S(2)}, u32[]{:S(2)}) collective-permute-start(bf16[2,160,1024]{2,1,0:T(8,128)(2,1)S(1)} %get-tuple-element.54.after), channel_id=1, source_target_pairs={{0,4},{1,5},{2,6},{3,7},{4,0},{5,1},{6,2},{7,3},{8,12},{9,13},{10,... | collective-permute-start | bytes 1966088 | tf_op jit(solution)/shard_map/ppermute | solution.py:633
  63.1 22.2 %collective-permute-start.11 = (bf16[96,1024]{1,0:T(8,128)(2,1)S(1)}, bf16[96,1024]{1,0:T(8,128)(2,1)S(1)}, u32[]{:S(2)}, u32[]{:S(2)}) collective-permute-start(bf16[96,1024]{1,0:T(8,128)(2,1)S(1)} %get-tuple-element.53.after), channel_id=1, source_target_pairs={{0,8},{1,9},{2,10},{3,11},{4,12},{5,13},{6,14},{7,15},{8,0},{9,1},... | collective-permute-start | bytes 589832 | tf_op jit(solution)/shard_map/ppermute | solution.py:633
  67.5 25.8 %collective-permute-start.4 = (bf16[4,192,256]{2,1,0:T(8,128)(2,1)S(1)}, bf16[4,192,256]{2,1,0:T(8,128)(2,1)S(1)}, u32[]{:S(2)}, u32[]{:S(2)}) collective-permute-start(bf16[4,192,256]{2,1,0:T(8,128)(2,1)S(1)} %get-tuple-element.42), channel_id=1, source_target_pairs={{0,1},{1,0},{2,3},{3,2},{4,5},{5,4},{6,7},{7,6},{8,9},{9,8},{10,11... | collective-permute-start | bytes 1179656 | tf_op jit(solution)/shard_map/ppermute | solution.py:633
  69.2 24.1 %collective-permute-start.6 = (bf16[4,192,256]{2,1,0:T(8,128)(2,1)S(1)}, bf16[4,192,256]{2,1,0:T(8,128)(2,1)S(1)}, u32[]{:S(2)}, u32[]{:S(2)}) collective-permute-start(bf16[4,192,256]{2,1,0:T(8,128)(2,1)S(1)} %get-tuple-element.44), channel_id=1, source_target_pairs={{0,1},{1,0},{2,3},{3,2},{4,5},{5,4},{6,7},{7,6},{8,9},{9,8},{10,11... | collective-permute-start | bytes 1179656 | tf_op jit(solution)/shard_map/ppermute | solution.py:633
  85.4 4.6 %collective-permute-start.12 = (bf16[96,1024]{1,0:T(8,128)(2,1)S(1)}, bf16[96,1024]{1,0:T(8,128)(2,1)S(1)}, u32[]{:S(2)}, u32[]{:S(2)}) collective-permute-start(bf16[96,1024]{1,0:T(8,128)(2,1)S(1)} %shard_map.108.a0), channel_id=1, source_target_pairs={{0,2},{1,3},{2,0},{3,1},{4,6},{5,7},{6,4},{7,5},{8,10},{9,11},{10,... | collective-permute-start | bytes 589832 | tf_op jit(solution)/shard_map/ppermute | solution.py:633
  86.8 13.6 %collective-permute-start.18 = (bf16[160,1024]{1,0:T(8,128)(2,1)S(1)}, bf16[160,1024]{1,0:T(8,128)(2,1)S(1)}, u32[]{:S(2)}, u32[]{:S(2)}) collective-permute-start(bf16[160,1024]{1,0:T(8,128)(2,1)S(1)} %get-tuple-element.61), channel_id=1, source_target_pairs={{0,8},{1,9},{2,10},{3,11},{4,12},{5,13},{6,14},{7,15},{8,0},{9,1},... | collective-permute-start | bytes 983048 | tf_op jit(solution)/shard_map/ppermute | solution.py:633
  86.9 13.5 %collective-permute-start.15 = (bf16[96,1024]{1,0:T(8,128)(2,1)S(1)}, bf16[96,1024]{1,0:T(8,128)(2,1)S(1)}, u32[]{:S(2)}, u32[]{:S(2)}) collective-permute-start(bf16[96,1024]{1,0:T(8,128)(2,1)S(1)} %shard_map.108.a0), channel_id=1, source_target_pairs={{0,1},{1,0},{2,3},{3,2},{4,5},{5,4},{6,7},{7,6},{8,9},{9,8},{10,11... | collective-permute-start | bytes 589832 | tf_op jit(solution)/shard_map/ppermute | solution.py:633
  89.9 10.4 %collective-permute-start.16 = (bf16[96,1024]{1,0:T(8,128)(2,1)S(1)}, bf16[96,1024]{1,0:T(8,128)(2,1)S(1)}, u32[]{:S(2)}, u32[]{:S(2)}) collective-permute-start(bf16[96,1024]{1,0:T(8,128)(2,1)S(1)} %collective-permute-done.12.before.refs_1_.a1), channel_id=1, source_target_pairs={{0,1},{1,0},{2,3},{3,2},{4,5},{5,4},{6,7},{7,6},{8,9},{9,8},{10,11... | collective-permute-start | bytes 589832 | tf_op jit(solution)/shard_map/ppermute | solution.py:633
  100.3 23.6 %copy-start.1 = (f32[1024]{0:T(1024)S(1)}, f32[1024]{0:T(1024)}, u32[]{:S(2)}) copy-start(f32[1024]{0:T(1024)} %param.13) | copy-start | bytes 12292
  100.4 8.9 %collective-permute-start.19 = (bf16[160,1024]{1,0:T(8,128)(2,1)S(1)}, bf16[160,1024]{1,0:T(8,128)(2,1)S(1)}, u32[]{:S(2)}, u32[]{:S(2)}) collective-permute-start(bf16[160,1024]{1,0:T(8,128)(2,1)S(1)} %shard_map.111.b0), channel_id=1, source_target_pairs={{0,2},{1,3},{2,0},{3,1},{4,6},{5,7},{6,4},{7,5},{8,10},{9,11},{10,... | collective-permute-start | bytes 983048 | tf_op jit(solution)/shard_map/ppermute | solution.py:633
  101.7 17.1 %collective-permute-start.13 = (bf16[192,1024]{1,0:T(8,128)(2,1)S(1)}, bf16[192,1024]{1,0:T(8,128)(2,1)S(1)}, u32[]{:S(2)}, u32[]{:S(2)}) collective-permute-start(bf16[192,1024]{1,0:T(8,128)(2,1)S(1)} %get-tuple-element.56.refs_0_), channel_id=1, source_target_pairs={{0,0},{1,8},{2,2},{3,10},{4,4},{5,12},{6,6},{7,14},{8,1},{9,9},{10... | collective-permute-start | bytes 1179656 | tf_op jit(solution)/shard_map/ppermute | solution.py:633
  106.3 17.6 %collective-permute-start.14 = (bf16[192,1024]{1,0:T(8,128)(2,1)S(1)}, bf16[192,1024]{1,0:T(8,128)(2,1)S(1)}, u32[]{:S(2)}, u32[]{:S(2)}) collective-permute-start(bf16[192,1024]{1,0:T(8,128)(2,1)S(1)} %get-tuple-element.57), channel_id=1, source_target_pairs={{0,4},{1,12},{2,6},{3,14},{4,0},{5,8},{6,2},{7,10},{8,5},{9,13},{1... | collective-permute-start | bytes 1179656 | tf_op jit(solution)/shard_map/ppermute | solution.py:633
  106.4 4.2 %collective-permute-start.20 = (bf16[160,1024]{1,0:T(8,128)(2,1)S(1)}, bf16[160,1024]{1,0:T(8,128)(2,1)S(1)}, u32[]{:S(2)}, u32[]{:S(2)}) collective-permute-start(bf16[160,1024]{1,0:T(8,128)(2,1)S(1)} %shard_map.111.b0), channel_id=1, source_target_pairs={{0,1},{1,0},{2,3},{3,2},{4,5},{5,4},{6,7},{7,6},{8,9},{9,8},{10,11... | collective-permute-start | bytes 983048 | tf_op jit(solution)/shard_map/ppermute | solution.py:633
  109.4 2.5 %collective-permute-start.21 = (bf16[160,1024]{1,0:T(8,128)(2,1)S(1)}, bf16[160,1024]{1,0:T(8,128)(2,1)S(1)}, u32[]{:S(2)}, u32[]{:S(2)}) collective-permute-start(bf16[160,1024]{1,0:T(8,128)(2,1)S(1)} %collective-permute-done.19.b1), channel_id=1, source_target_pairs={{0,1},{1,0},{2,3},{3,2},{4,5},{5,4},{6,7},{7,6},{8,9},{9,8},{10,11... | collective-permute-start | bytes 983048 | tf_op jit(solution)/shard_map/ppermute | solution.py:633
  123.9 1.9 %copy-start = (f32[1024,768]{1,0:T(8,128)S(1)}, f32[1024,768]{1,0:T(8,128)}, u32[]{:S(2)}) copy-start(f32[1024,768]{1,0:T(8,128)} %get-tuple-element.33.after) | copy-start | bytes 9437188

commit v11 on v10

--- a/solution.py
+++ b/solution.py
@@ -770,7 +770,7 @@
     )
     encoded, d_patches = call(
         return_kernel,
-        (*back, hidden, *mine, gain_row, qkv_grad),
+        (*back, hidden, *mine, gain_row, in_hbm(qkv_grad)),
         [struct(patches.shape)] * 2,
         12,
         place,

time: 128 us -> 126 us (0.984)
  local copies, waits for them, and re-layouts: 2.66 us -> 0.77 us
    unnamed x4 -> x2, local copies, waits for them, and re-layouts: 1.9 us -> 0.01 us
  transfers between devices with their start and end apart: 22 -> 22, of which waited for: 13 -> 13; matrix products, arithmetic and copies ran while one was open for 0% -> 0% of each run, Pallas kernels for 17% -> 18%
where the time goes in v11:
time: 126 us
  waiting for transfers between devices  63 us (50%)
  starting transfers between devices  31.7 us (25%)
  Pallas kernels  29.6 us (23%)
    ppermute x22, waiting for transfers between devices, send(): return lax.ppermute(value, AXES, line_perm(move, reps))  63 us
    ppermute x22, starting transfers between devices, send(): return lax.ppermute(value, AXES, line_perm(move, reps))  31.7 us
    pallas_call x11, Pallas kernels, call(): pl.pallas_call(kernel, in_specs=specs, out_specs=VMEM_SPEC if single else...  22.5 us
    pallas_call x1, Pallas kernels, chip_shards(): pl.pallas_call(rows_kernel, grid_spec=pltpu.PrefetchScalarGridSpec(num_sc...  7.06 us
  transfers between devices with their start and end apart: 22, of which 13 were waited for; matrix products, arithmetic and copies ran while one was open for 0% of the time, Pallas kernels for 18%

profile of v11, /device:TPU:9, one launch (start us, length us, event | category | flops | bytes accessed | tf_op | source)
XLA Modules:
  0.0 125.8 jit_solution(7430589505977217738)
XLA Ops:
  1.4 3.4 %shard_map.102 = (bf16[192,1024]{1,0:T(8,128)(2,1)S(1)}, bf16[192,1024]{1,0:T(8,128)(2,1)S(1)}, f32[2,96,1024]{2,1,0:T(8,128)S(1)}, bf16[1024,512]{1,0:T(8,128)(...) custom-call(s32[6]{0:T(128)S(1)} %concatenate.6.place, ...), custom_call_target="tpu_custom_call" | custom-call | flops 1000 | bytes 1000 | tf_op jit(solution)/shard_map/pallas_call | solution.py:607
  4.8 4.8 %collective-permute-start = (bf16[192,1024]{1,0:T(8,128)(2,1)S(1)}, bf16[192,1024]{1,0:T(8,128)(2,1)S(1)}, u32[]{:S(2)}, u32[]{:S(2)}) collective-permute-start(bf16[192,1024]{1,0:T(8,128)(2,1)S(1)} %get-tuple-element.35.m0), channel_id=1, source_target_pairs={{0,0},{1,8},{2,2},{3,10},{4,4},{5,12},{6,6},{7,14},{8,1},{9,9},{10... | collective-permute-start | bytes 1179656 | tf_op jit(solution)/shard_map/ppermute | solution.py:633
  9.6 13.0 %collective-permute-done.p0 = bf16[192,1024]{1,0:T(8,128)(2,1)S(1)} collective-permute-done((bf16[192,1024]{1,0:T(8,128)(2,1)S(1)}, bf16[192,1024]{1,0:T(8,128)(2,1)S(1)}, u32[]{:S(2)}, u32[]{:S(2)}) %collective-permute-start) | collective-permute-done | bytes 393248 | tf_op jit(solution)/shard_map/ppermute | solution.py:633
  22.7 4.2 %collective-permute-done.1.p1 = bf16[192,1024]{1,0:T(8,128)(2,1)S(1)} collective-permute-done((bf16[192,1024]{1,0:T(8,128)(2,1)S(1)}, bf16[192,1024]{1,0:T(8,128)(2,1)S(1)}, u32[]{:S(2)}, u32[]{:S(2)}) %collective-permute-start.1) | collective-permute-done | bytes 393248 | tf_op jit(solution)/shard_map/ppermute | solution.py:633
  26.9 1.3 %collective-permute-start.5 = (bf16[192,1024]{1,0:T(8,128)(2,1)S(1)}, bf16[192,1024]{1,0:T(8,128)(2,1)S(1)}, u32[]{:S(2)}, u32[]{:S(2)}) collective-permute-start(bf16[192,1024]{1,0:T(8,128)(2,1)S(1)} %pad_maximum_fusion), channel_id=1, source_target_pairs={{0,2},{1,3},{2,0},{3,1},{4,6},{5,7},{6,4},{7,5},{8,10},{9,11},{10,... | collective-permute-start | bytes 1179656 | tf_op jit(solution)/shard_map/ppermute | solution.py:633
  28.6 5.2 %shard_map.103 = (bf16[4,192,256]{2,1,0:T(8,128)(2,1)S(1)}, bf16[4,192,256]{2,1,0:T(8,128)(2,1)S(1)}, bf16[128,1152]{1,0:T(8,128)(2,1)S(1)}, f32[128,1024]{1,0:T(8,128)S(1)}, bf16[128,2176]{1,0:T(8,128)(2,1)S(1)}) custom-call(s32[6]{0:T(128)S(1)} %concatenate.6.place, bf16[192,1024]{1,0:T(8,128)(2,1)S(1)} %collective-permute-done.p0, ...), custom_call_target="tpu_custom_call" | custom-call | flops 1000 | bytes 1000 | tf_op jit(solution)/shard_map/pallas_call | solution.py:607
  33.8 1.3 %collective-permute-start.7 = (bf16[128,2176]{1,0:T(8,128)(2,1)S(1)}, bf16[128,2176]{1,0:T(8,128)(2,1)S(1)}, u32[]{:S(2)}, u32[]{:S(2)}) collective-permute-start(bf16[128,2176]{1,0:T(8,128)(2,1)S(1)} %get-tuple-element.46), channel_id=1, source_target_pairs={{0,2},{1,3},{2,0},{3,1},{4,6},{5,7},{6,4},{7,5},{8,10},{9,11},{10,... | collective-permute-start | bytes 1671176 | tf_op jit(solution)/shard_map/ppermute | solution.py:633
  35.1 2.1 %collective-permute-done.5.after.n0 = bf16[192,1024]{1,0:T(8,128)(2,1)S(1)} collective-permute-done((bf16[192,1024]{1,0:T(8,128)(2,1)S(1)}, bf16[192,1024]{1,0:T(8,128)(2,1)S(1)}, u32[]{:S(2)}, u32[]{:S(2)}) %collective-permute-start.5) | collective-permute-done | bytes 393248 | tf_op jit(solution)/shard_map/ppermute | solution.py:633
  37.2 2.3 %collective-permute-start.9 = (bf16[192,1024]{1,0:T(8,128)(2,1)S(1)}, bf16[192,1024]{1,0:T(8,128)(2,1)S(1)}, u32[]{:S(2)}, u32[]{:S(2)}) collective-permute-start(bf16[192,1024]{1,0:T(8,128)(2,1)S(1)} %collective-permute-done.5.after.n0), channel_id=1, source_target_pairs={{0,1},{1,0},{2,3},{3,2},{4,5},{5,4},{6,7},{7,6},{8,9},{9,8},{10,11... | collective-permute-start | bytes 1179656 | tf_op jit(solution)/shard_map/ppermute | solution.py:633
  39.5 5.2 %shard_map.104 = (bf16[4,192,256]{2,1,0:T(8,128)(2,1)S(1)}, bf16[4,192,256]{2,1,0:T(8,128)(2,1)S(1)}, bf16[128,1152]{1,0:T(8,128)(2,1)S(1)}, f32[128,1024]{1,0:T(8,128)S(1)}, bf16[128,2176]{1,0:T(8,128)(2,1)S(1)}) custom-call(s32[6]{0:T(128)S(1)} %concatenate.6.place, bf16[192,1024]{1,0:T(8,128)(2,1)S(1)} %collective-permute-done.p0, ...), custom_call_target="tpu_custom_call" | custom-call | flops 1000 | bytes 1000 | tf_op jit(solution)/shard_map/pallas_call | solution.py:607
  44.8 1.3 %collective-permute-start.8 = (bf16[128,2176]{1,0:T(8,128)(2,1)S(1)}, bf16[128,2176]{1,0:T(8,128)(2,1)S(1)}, u32[]{:S(2)}, u32[]{:S(2)}) collective-permute-start(bf16[128,2176]{1,0:T(8,128)(2,1)S(1)} %get-tuple-element.49), channel_id=1, source_target_pairs={{0,2},{1,3},{2,0},{3,1},{4,6},{5,7},{6,4},{7,5},{8,10},{9,11},{10,... | collective-permute-start | bytes 1671176 | tf_op jit(solution)/shard_map/ppermute | solution.py:633
  46.0 3.1 %collective-permute-done.7.got.got_a = bf16[128,2176]{1,0:T(8,128)(2,1)S(1)} collective-permute-done((bf16[128,2176]{1,0:T(8,128)(2,1)S(1)}, bf16[128,2176]{1,0:T(8,128)(2,1)S(1)}, u32[]{:S(2)}, u32[]{:S(2)}) %collective-permute-start.7) | collective-permute-done | bytes 557088 | tf_op jit(solution)/shard_map/ppermute | solution.py:633
  49.1 1.4 %shard_map.105 = (f32[2,96,1024]{2,1,0:T(8,128)S(1)}, bf16[2,96,1024]{2,1,0:T(8,128)(2,1)S(1)}) custom-call(s32[6]{0:T(128)S(1)} %concatenate.6.place, bf16[128,1152]{1,0:T(8,128)(2,1)S(1)} %get-tuple-element.45.keep.keep_a, f32[128,1024]{1,0:T(8,128)S(1)} %get-tuple-element.50.out_keep, bf16[128,2176]{1,0:T(8,128)(2,1)S(1)} %collective-permute-done.7.got.got_a, ...), custom_call_target="tpu_custom_call" | custom-call | flops 1000 | bytes 1000 | tf_op jit(solution)/shard_map/pallas_call | solution.py:607
  50.6 8.3 %collective-permute-done.10.got = bf16[2,96,1024]{2,1,0:T(8,128)(2,1)S(1)} collective-permute-done((bf16[2,96,1024]{2,1,0:T(8,128)(2,1)S(1)}, bf16[2,96,1024]{2,1,0:T(8,128)(2,1)S(1)}, u32[]{:S(2)}, u32[]{:S(2)}) %collective-permute-start.10) | collective-permute-done | bytes 393248 | tf_op jit(solution)/shard_map/ppermute | solution.py:633
  59.0 2.1 %collective-permute-done.8.got_b = bf16[128,2176]{1,0:T(8,128)(2,1)S(1)} collective-permute-done((bf16[128,2176]{1,0:T(8,128)(2,1)S(1)}, bf16[128,2176]{1,0:T(8,128)(2,1)S(1)}, u32[]{:S(2)}, u32[]{:S(2)}) %collective-permute-start.8) | collective-permute-done | bytes 557088 | tf_op jit(solution)/shard_map/ppermute | solution.py:633
  61.1 2.0 %shard_map.107 = (f32[2,160,1024]{2,1,0:T(8,128)S(1)}, bf16[2,160,1024]{2,1,0:T(8,128)(2,1)S(1)}) custom-call(s32[6]{0:T(128)S(1)} %concatenate.6.place, bf16[128,1152]{1,0:T(8,128)(2,1)S(1)} %get-tuple-element.45.keep.keep_a, bf16[128,2176]{1,0:T(8,128)(2,1)S(1)} %collective-permute-done.7.got.got_a, bf16[128,1152]{1,0:T(8,128)(2,1)S(1)} %get-tuple-element.47.keep_b, ...), custom_call_target="tpu_custom_call" | custom-call | flops 1000 | bytes 1000 | tf_op jit(solution)/shard_map/pallas_call | solution.py:607
  63.1 4.3 %collective-permute-start.11 = (bf16[96,1024]{1,0:T(8,128)(2,1)S(1)}, bf16[96,1024]{1,0:T(8,128)(2,1)S(1)}, u32[]{:S(2)}, u32[]{:S(2)}) collective-permute-start(bf16[96,1024]{1,0:T(8,128)(2,1)S(1)} %get-tuple-element.53.after), channel_id=1, source_target_pairs={{0,8},{1,9},{2,10},{3,11},{4,12},{5,13},{6,14},{7,15},{8,0},{9,1},... | collective-permute-start | bytes 589832 | tf_op jit(solution)/shard_map/ppermute | solution.py:633
  67.5 1.7 %collective-permute-start.4 = (bf16[4,192,256]{2,1,0:T(8,128)(2,1)S(1)}, bf16[4,192,256]{2,1,0:T(8,128)(2,1)S(1)}, u32[]{:S(2)}, u32[]{:S(2)}) collective-permute-start(bf16[4,192,256]{2,1,0:T(8,128)(2,1)S(1)} %get-tuple-element.42), channel_id=1, source_target_pairs={{0,1},{1,0},{2,3},{3,2},{4,5},{5,4},{6,7},{7,6},{8,9},{9,8},{10,11... | collective-permute-start | bytes 1179656 | tf_op jit(solution)/shard_map/ppermute | solution.py:633
  69.2 16.1 %collective-permute-done.11.got = bf16[96,1024]{1,0:T(8,128)(2,1)S(1)} collective-permute-done((bf16[96,1024]{1,0:T(8,128)(2,1)S(1)}, bf16[96,1024]{1,0:T(8,128)(2,1)S(1)}, u32[]{:S(2)}, u32[]{:S(2)}) %collective-permute-start.11) | collective-permute-done | bytes 196640 | tf_op jit(solution)/shard_map/ppermute | solution.py:633
  85.4 1.3 %collective-permute-start.12 = (bf16[96,1024]{1,0:T(8,128)(2,1)S(1)}, bf16[96,1024]{1,0:T(8,128)(2,1)S(1)}, u32[]{:S(2)}, u32[]{:S(2)}) collective-permute-start(bf16[96,1024]{1,0:T(8,128)(2,1)S(1)} %shard_map.108.a0), channel_id=1, source_target_pairs={{0,2},{1,3},{2,0},{3,1},{4,6},{5,7},{6,4},{7,5},{8,10},{9,11},{10,... | collective-permute-start | bytes 589832 | tf_op jit(solution)/shard_map/ppermute | solution.py:633
  86.9 2.5 %collective-permute-start.15 = (bf16[96,1024]{1,0:T(8,128)(2,1)S(1)}, bf16[96,1024]{1,0:T(8,128)(2,1)S(1)}, u32[]{:S(2)}, u32[]{:S(2)}) collective-permute-start(bf16[96,1024]{1,0:T(8,128)(2,1)S(1)} %shard_map.108.a0), channel_id=1, source_target_pairs={{0,1},{1,0},{2,3},{3,2},{4,5},{5,4},{6,7},{7,6},{8,9},{9,8},{10,11... | collective-permute-start | bytes 589832 | tf_op jit(solution)/shard_map/ppermute | solution.py:633
  89.9 3.3 %collective-permute-start.16 = (bf16[96,1024]{1,0:T(8,128)(2,1)S(1)}, bf16[96,1024]{1,0:T(8,128)(2,1)S(1)}, u32[]{:S(2)}, u32[]{:S(2)}) collective-permute-start(bf16[96,1024]{1,0:T(8,128)(2,1)S(1)} %collective-permute-done.12.before.refs_1_.a1), channel_id=1, source_target_pairs={{0,1},{1,0},{2,3},{3,2},{4,5},{5,4},{6,7},{7,6},{8,9},{9,8},{10,11... | collective-permute-start | bytes 589832 | tf_op jit(solution)/shard_map/ppermute | solution.py:633
  93.3 7.1 %shard_map.109 = (bf16[192,1024]{1,0:T(8,128)(2,1)S(1)}, bf16[192,1024]{1,0:T(8,128)(2,1)S(1)}) custom-call(s32[6]{0:T(128)S(1)} %concatenate.6.place, bf16[4,192,256]{2,1,0:T(8,128)(2,1)S(1)} %get-tuple-element.41.own_a, bf16[4,192,256]{2,1,0:T(8,128)(2,1)S(1)} %collective-permute-done.4.got_a, bf16[4,192,256]{2,1,0:T(8,128)(2,1)S(1)} %get-tuple-element.43.own_b, ...), custom_call_target="tpu_custom_call" | custom-call | flops 1000 | bytes 1000 | tf_op jit(solution)/shard_map/pallas_call | solution.py:748
  100.4 1.3 %collective-permute-start.19 = (bf16[160,1024]{1,0:T(8,128)(2,1)S(1)}, bf16[160,1024]{1,0:T(8,128)(2,1)S(1)}, u32[]{:S(2)}, u32[]{:S(2)}) collective-permute-start(bf16[160,1024]{1,0:T(8,128)(2,1)S(1)} %shard_map.111.b0), channel_id=1, source_target_pairs={{0,2},{1,3},{2,0},{3,1},{4,6},{5,7},{6,4},{7,5},{8,10},{9,11},{10,... | collective-permute-start | bytes 983048 | tf_op jit(solution)/shard_map/ppermute | solution.py:633
  101.7 4.6 %collective-permute-start.13 = (bf16[192,1024]{1,0:T(8,128)(2,1)S(1)}, bf16[192,1024]{1,0:T(8,128)(2,1)S(1)}, u32[]{:S(2)}, u32[]{:S(2)}) collective-permute-start(bf16[192,1024]{1,0:T(8,128)(2,1)S(1)} %get-tuple-element.56.refs_0_), channel_id=1, source_target_pairs={{0,0},{1,8},{2,2},{3,10},{4,4},{5,12},{6,6},{7,14},{8,1},{9,9},{10... | collective-permute-start | bytes 1179656 | tf_op jit(solution)/shard_map/ppermute | solution.py:633
  106.5 2.9 %collective-permute-done.19.b1 = bf16[160,1024]{1,0:T(8,128)(2,1)S(1)} collective-permute-done((bf16[160,1024]{1,0:T(8,128)(2,1)S(1)}, bf16[160,1024]{1,0:T(8,128)(2,1)S(1)}, u32[]{:S(2)}, u32[]{:S(2)}) %collective-permute-start.19) | collective-permute-done | bytes 327712 | tf_op jit(solution)/shard_map/ppermute | solution.py:633
  109.4 1.3 %collective-permute-start.21 = (bf16[160,1024]{1,0:T(8,128)(2,1)S(1)}, bf16[160,1024]{1,0:T(8,128)(2,1)S(1)}, u32[]{:S(2)}, u32[]{:S(2)}) collective-permute-start(bf16[160,1024]{1,0:T(8,128)(2,1)S(1)} %collective-permute-done.19.b1), channel_id=1, source_target_pairs={{0,1},{1,0},{2,3},{3,2},{4,5},{5,4},{6,7},{7,6},{8,9},{9,8},{10,11... | collective-permute-start | bytes 983048 | tf_op jit(solution)/shard_map/ppermute | solution.py:633
  110.6 1.3 collective-permute-done.21.b3
  111.9 3.0 %shard_map.112 = (f32[1024,768]{1,0:T(8,128)}, f32[1024,256]{1,0:T(8,128)}) custom-call(s32[6]{0:T(128)S(1)} %concatenate.6.place, bf16[96,1024]{1,0:T(8,128)(2,1)S(1)} %shard_map.108.a0, bf16[96,1024]{1,0:T(8,128)(2,1)S(1)} %collective-permute-done.12.before.refs_1_.a1, bf16[96,1024]{1,0:T(8,128)(2,1)S(1)} %collective-permute-done.15.refs_2_.a2, ...), custom_call_target="tpu_custom_call" | custom-call | flops 1000 | bytes 1000 | tf_op jit(solution)/shard_map/pallas_call | solution.py:607
  114.9 3.9 %collective-permute-done.13.r0 = bf16[192,1024]{1,0:T(8,128)(2,1)S(1)} collective-permute-done((bf16[192,1024]{1,0:T(8,128)(2,1)S(1)}, bf16[192,1024]{1,0:T(8,128)(2,1)S(1)}, u32[]{:S(2)}, u32[]{:S(2)}) %collective-permute-start.13) | collective-permute-done | bytes 393248 | tf_op jit(solution)/shard_map/ppermute | solution.py:633
  118.8 5.1 %collective-permute-done.14.r1 = bf16[192,1024]{1,0:T(8,128)(2,1)S(1)} collective-permute-done((bf16[192,1024]{1,0:T(8,128)(2,1)S(1)}, bf16[192,1024]{1,0:T(8,128)(2,1)S(1)}, u32[]{:S(2)}, u32[]{:S(2)}) %collective-permute-start.14) | collective-permute-done | bytes 393248 | tf_op jit(solution)/shard_map/ppermute | solution.py:633
  123.9 1.9 %shard_map.113 = (bf16[2,96,1024]{2,1,0:T(8,128)(2,1)}, bf16[2,96,1024]{2,1,0:T(8,128)(2,1)}) custom-call(s32[6]{0:T(128)S(1)} %concatenate.6.place, bf16[192,1024]{1,0:T(8,128)(2,1)S(1)} %collective-permute-done.13.r0, bf16[192,1024]{1,0:T(8,128)(2,1)S(1)} %collective-permute-done.14.r1, f32[2,96,1024]{2,1,0:T(8,128)S(1)} %get-tuple-element.58.hidden_ref, ...), custom_call_target="tpu_custom_call" | custom-call | flops 1000 | bytes 1000 | tf_op jit(solution)/shard_map/pallas_call | solution.py:607
  (30 shorter events, 2.5 us)
Async XLA Ops:
  4.8 17.9 %collective-permute-start = (bf16[192,1024]{1,0:T(8,128)(2,1)S(1)}, bf16[192,1024]{1,0:T(8,128)(2,1)S(1)}, u32[]{:S(2)}, u32[]{:S(2)}) collective-permute-start(bf16[192,1024]{1,0:T(8,128)(2,1)S(1)} %get-tuple-element.35.m0), channel_id=1, source_target_pairs={{0,0},{1,8},{2,2},{3,10},{4,4},{5,12},{6,6},{7,14},{8,1},{9,9},{10... | collective-permute-start | bytes 1179656 | tf_op jit(solution)/shard_map/ppermute | solution.py:633
  9.6 17.3 %collective-permute-start.1 = (bf16[192,1024]{1,0:T(8,128)(2,1)S(1)}, bf16[192,1024]{1,0:T(8,128)(2,1)S(1)}, u32[]{:S(2)}, u32[]{:S(2)}) collective-permute-start(bf16[192,1024]{1,0:T(8,128)(2,1)S(1)} %get-tuple-element.36.m1), channel_id=1, source_target_pairs={{0,4},{1,12},{2,6},{3,14},{4,0},{5,8},{6,2},{7,10},{8,5},{9,13},{1... | collective-permute-start | bytes 1179656 | tf_op jit(solution)/shard_map/ppermute | solution.py:633
  22.7 5.6 %collective-permute-start.2 = (bf16[192,1024]{1,0:T(8,128)(2,1)S(1)}, bf16[192,1024]{1,0:T(8,128)(2,1)S(1)}, u32[]{:S(2)}, u32[]{:S(2)}) collective-permute-start(bf16[192,1024]{1,0:T(8,128)(2,1)S(1)} %collective-permute-done.p0), channel_id=1, source_target_pairs={{0,1},{1,0},{2,3},{3,2},{4,5},{5,4},{6,7},{7,6},{8,9},{9,8},{10,11... | collective-permute-start | bytes 1179656 | tf_op jit(solution)/shard_map/ppermute | solution.py:633
  26.9 1.7 %collective-permute-start.3 = (bf16[192,1024]{1,0:T(8,128)(2,1)S(1)}, bf16[192,1024]{1,0:T(8,128)(2,1)S(1)}, u32[]{:S(2)}, u32[]{:S(2)}) collective-permute-start(bf16[192,1024]{1,0:T(8,128)(2,1)S(1)} %collective-permute-done.1.p1), channel_id=1, source_target_pairs={{0,1},{1,0},{2,3},{3,2},{4,5},{5,4},{6,7},{7,6},{8,9},{9,8},{10,11... | collective-permute-start | bytes 1179656 | tf_op jit(solution)/shard_map/ppermute | solution.py:633
  26.9 10.2 %collective-permute-start.5 = (bf16[192,1024]{1,0:T(8,128)(2,1)S(1)}, bf16[192,1024]{1,0:T(8,128)(2,1)S(1)}, u32[]{:S(2)}, u32[]{:S(2)}) collective-permute-start(bf16[192,1024]{1,0:T(8,128)(2,1)S(1)} %pad_maximum_fusion), channel_id=1, source_target_pairs={{0,2},{1,3},{2,0},{3,1},{4,6},{5,7},{6,4},{7,5},{8,10},{9,11},{10,... | collective-permute-start | bytes 1179656 | tf_op jit(solution)/shard_map/ppermute | solution.py:633
  33.8 15.3 %collective-permute-start.7 = (bf16[128,2176]{1,0:T(8,128)(2,1)S(1)}, bf16[128,2176]{1,0:T(8,128)(2,1)S(1)}, u32[]{:S(2)}, u32[]{:S(2)}) collective-permute-start(bf16[128,2176]{1,0:T(8,128)(2,1)S(1)} %get-tuple-element.46), channel_id=1, source_target_pairs={{0,2},{1,3},{2,0},{3,1},{4,6},{5,7},{6,4},{7,5},{8,10},{9,11},{10,... | collective-permute-start | bytes 1671176 | tf_op jit(solution)/shard_map/ppermute | solution.py:633
  37.2 8.9 %collective-permute-start.9 = (bf16[192,1024]{1,0:T(8,128)(2,1)S(1)}, bf16[192,1024]{1,0:T(8,128)(2,1)S(1)}, u32[]{:S(2)}, u32[]{:S(2)}) collective-permute-start(bf16[192,1024]{1,0:T(8,128)(2,1)S(1)} %collective-permute-done.5.after.n0), channel_id=1, source_target_pairs={{0,1},{1,0},{2,3},{3,2},{4,5},{5,4},{6,7},{7,6},{8,9},{9,8},{10,11... | collective-permute-start | bytes 1179656 | tf_op jit(solution)/shard_map/ppermute | solution.py:633
  44.8 16.3 %collective-permute-start.8 = (bf16[128,2176]{1,0:T(8,128)(2,1)S(1)}, bf16[128,2176]{1,0:T(8,128)(2,1)S(1)}, u32[]{:S(2)}, u32[]{:S(2)}) collective-permute-start(bf16[128,2176]{1,0:T(8,128)(2,1)S(1)} %get-tuple-element.49), channel_id=1, source_target_pairs={{0,2},{1,3},{2,0},{3,1},{4,6},{5,7},{6,4},{7,5},{8,10},{9,11},{10,... | collective-permute-start | bytes 1671176 | tf_op jit(solution)/shard_map/ppermute | solution.py:633
  50.5 8.4 %collective-permute-start.10 = (bf16[2,96,1024]{2,1,0:T(8,128)(2,1)S(1)}, bf16[2,96,1024]{2,1,0:T(8,128)(2,1)S(1)}, u32[]{:S(2)}, u32[]{:S(2)}) collective-permute-start(bf16[2,96,1024]{2,1,0:T(8,128)(2,1)S(1)} %get-tuple-element.52), channel_id=1, source_target_pairs={{0,4},{1,5},{2,6},{3,7},{4,0},{5,1},{6,2},{7,3},{8,12},{9,13},{10,... | collective-permute-start | bytes 1179656 | tf_op jit(solution)/shard_map/ppermute | solution.py:633
  63.1 23.6 %collective-permute-start.17 = (bf16[2,160,1024]{2,1,0:T(8,128)(2,1)S(1)}, bf16[2,160,1024]{2,1,0:T(8,128)(2,1)S(1)}, u32[]{:S(2)}, u32[]{:S(2)}) collective-permute-start(bf16[2,160,1024]{2,1,0:T(8,128)(2,1)S(1)} %get-tuple-element.54.after), channel_id=1, source_target_pairs={{0,4},{1,5},{2,6},{3,7},{4,0},{5,1},{6,2},{7,3},{8,12},{9,13},{10,... | collective-permute-start | bytes 1966088 | tf_op jit(solution)/shard_map/ppermute | solution.py:633
  63.1 22.2 %collective-permute-start.11 = (bf16[96,1024]{1,0:T(8,128)(2,1)S(1)}, bf16[96,1024]{1,0:T(8,128)(2,1)S(1)}, u32[]{:S(2)}, u32[]{:S(2)}) collective-permute-start(bf16[96,1024]{1,0:T(8,128)(2,1)S(1)} %get-tuple-element.53.after), channel_id=1, source_target_pairs={{0,8},{1,9},{2,10},{3,11},{4,12},{5,13},{6,14},{7,15},{8,0},{9,1},... | collective-permute-start | bytes 589832 | tf_op jit(solution)/shard_map/ppermute | solution.py:633
  67.5 25.8 %collective-permute-start.4 = (bf16[4,192,256]{2,1,0:T(8,128)(2,1)S(1)}, bf16[4,192,256]{2,1,0:T(8,128)(2,1)S(1)}, u32[]{:S(2)}, u32[]{:S(2)}) collective-permute-start(bf16[4,192,256]{2,1,0:T(8,128)(2,1)S(1)} %get-tuple-element.42), channel_id=1, source_target_pairs={{0,1},{1,0},{2,3},{3,2},{4,5},{5,4},{6,7},{7,6},{8,9},{9,8},{10,11... | collective-permute-start | bytes 1179656 | tf_op jit(solution)/shard_map/ppermute | solution.py:633
  69.2 24.1 %collective-permute-start.6 = (bf16[4,192,256]{2,1,0:T(8,128)(2,1)S(1)}, bf16[4,192,256]{2,1,0:T(8,128)(2,1)S(1)}, u32[]{:S(2)}, u32[]{:S(2)}) collective-permute-start(bf16[4,192,256]{2,1,0:T(8,128)(2,1)S(1)} %get-tuple-element.44), channel_id=1, source_target_pairs={{0,1},{1,0},{2,3},{3,2},{4,5},{5,4},{6,7},{7,6},{8,9},{9,8},{10,11... | collective-permute-start | bytes 1179656 | tf_op jit(solution)/shard_map/ppermute | solution.py:633
  85.4 4.6 %collective-permute-start.12 = (bf16[96,1024]{1,0:T(8,128)(2,1)S(1)}, bf16[96,1024]{1,0:T(8,128)(2,1)S(1)}, u32[]{:S(2)}, u32[]{:S(2)}) collective-permute-start(bf16[96,1024]{1,0:T(8,128)(2,1)S(1)} %shard_map.108.a0), channel_id=1, source_target_pairs={{0,2},{1,3},{2,0},{3,1},{4,6},{5,7},{6,4},{7,5},{8,10},{9,11},{10,... | collective-permute-start | bytes 589832 | tf_op jit(solution)/shard_map/ppermute | solution.py:633
  86.8 13.6 %collective-permute-start.18 = (bf16[160,1024]{1,0:T(8,128)(2,1)S(1)}, bf16[160,1024]{1,0:T(8,128)(2,1)S(1)}, u32[]{:S(2)}, u32[]{:S(2)}) collective-permute-start(bf16[160,1024]{1,0:T(8,128)(2,1)S(1)} %get-tuple-element.61), channel_id=1, source_target_pairs={{0,8},{1,9},{2,10},{3,11},{4,12},{5,13},{6,14},{7,15},{8,0},{9,1},... | collective-permute-start | bytes 983048 | tf_op jit(solution)/shard_map/ppermute | solution.py:633
  86.9 13.5 %collective-permute-start.15 = (bf16[96,1024]{1,0:T(8,128)(2,1)S(1)}, bf16[96,1024]{1,0:T(8,128)(2,1)S(1)}, u32[]{:S(2)}, u32[]{:S(2)}) collective-permute-start(bf16[96,1024]{1,0:T(8,128)(2,1)S(1)} %shard_map.108.a0), channel_id=1, source_target_pairs={{0,1},{1,0},{2,3},{3,2},{4,5},{5,4},{6,7},{7,6},{8,9},{9,8},{10,11... | collective-permute-start | bytes 589832 | tf_op jit(solution)/shard_map/ppermute | solution.py:633
  89.9 10.4 %collective-permute-start.16 = (bf16[96,1024]{1,0:T(8,128)(2,1)S(1)}, bf16[96,1024]{1,0:T(8,128)(2,1)S(1)}, u32[]{:S(2)}, u32[]{:S(2)}) collective-permute-start(bf16[96,1024]{1,0:T(8,128)(2,1)S(1)} %collective-permute-done.12.before.refs_1_.a1), channel_id=1, source_target_pairs={{0,1},{1,0},{2,3},{3,2},{4,5},{5,4},{6,7},{7,6},{8,9},{9,8},{10,11... | collective-permute-start | bytes 589832 | tf_op jit(solution)/shard_map/ppermute | solution.py:633
  100.3 23.6 %copy-start = (f32[1024]{0:T(1024)S(1)}, f32[1024]{0:T(1024)}, u32[]{:S(2)}) copy-start(f32[1024]{0:T(1024)} %param.13) | copy-start | bytes 12292
  100.4 8.9 %collective-permute-start.19 = (bf16[160,1024]{1,0:T(8,128)(2,1)S(1)}, bf16[160,1024]{1,0:T(8,128)(2,1)S(1)}, u32[]{:S(2)}, u32[]{:S(2)}) collective-permute-start(bf16[160,1024]{1,0:T(8,128)(2,1)S(1)} %shard_map.111.b0), channel_id=1, source_target_pairs={{0,2},{1,3},{2,0},{3,1},{4,6},{5,7},{6,4},{7,5},{8,10},{9,11},{10,... | collective-permute-start | bytes 983048 | tf_op jit(solution)/shard_map/ppermute | solution.py:633
  101.7 17.1 %collective-permute-start.13 = (bf16[192,1024]{1,0:T(8,128)(2,1)S(1)}, bf16[192,1024]{1,0:T(8,128)(2,1)S(1)}, u32[]{:S(2)}, u32[]{:S(2)}) collective-permute-start(bf16[192,1024]{1,0:T(8,128)(2,1)S(1)} %get-tuple-element.56.refs_0_), channel_id=1, source_target_pairs={{0,0},{1,8},{2,2},{3,10},{4,4},{5,12},{6,6},{7,14},{8,1},{9,9},{10... | collective-permute-start | bytes 1179656 | tf_op jit(solution)/shard_map/ppermute | solution.py:633
  106.3 17.6 %collective-permute-start.14 = (bf16[192,1024]{1,0:T(8,128)(2,1)S(1)}, bf16[192,1024]{1,0:T(8,128)(2,1)S(1)}, u32[]{:S(2)}, u32[]{:S(2)}) collective-permute-start(bf16[192,1024]{1,0:T(8,128)(2,1)S(1)} %get-tuple-element.57), channel_id=1, source_target_pairs={{0,4},{1,12},{2,6},{3,14},{4,0},{5,8},{6,2},{7,10},{8,5},{9,13},{1... | collective-permute-start | bytes 1179656 | tf_op jit(solution)/shard_map/ppermute | solution.py:633
  106.4 4.2 %collective-permute-start.20 = (bf16[160,1024]{1,0:T(8,128)(2,1)S(1)}, bf16[160,1024]{1,0:T(8,128)(2,1)S(1)}, u32[]{:S(2)}, u32[]{:S(2)}) collective-permute-start(bf16[160,1024]{1,0:T(8,128)(2,1)S(1)} %shard_map.111.b0), channel_id=1, source_target_pairs={{0,1},{1,0},{2,3},{3,2},{4,5},{5,4},{6,7},{7,6},{8,9},{9,8},{10,11... | collective-permute-start | bytes 983048 | tf_op jit(solution)/shard_map/ppermute | solution.py:633
  109.4 2.5 %collective-permute-start.21 = (bf16[160,1024]{1,0:T(8,128)(2,1)S(1)}, bf16[160,1024]{1,0:T(8,128)(2,1)S(1)}, u32[]{:S(2)}, u32[]{:S(2)}) collective-permute-start(bf16[160,1024]{1,0:T(8,128)(2,1)S(1)} %collective-permute-done.19.b1), channel_id=1, source_target_pairs={{0,1},{1,0},{2,3},{3,2},{4,5},{5,4},{6,7},{7,6},{8,9},{9,8},{10,11... | collective-permute-start | bytes 983048 | tf_op jit(solution)/shard_map/ppermute | solution.py:633

commit v12 on v11

--- a/solution.py
+++ b/solution.py
@@ -300,55 +300,63 @@
     return copies
 
 
-def norm_kernel(
-    place, patch_hbm, cot_hbm, index_hbm, gain_hbm, w_in_hbm, w_out_hbm,
-    p0_ref, p1_ref, hidden_ref, wq, wk, wv, wo,
-    patch_ref, cot_ref, index_ref, gain_ref, sems, w_sems,
+def norm_block(
+    k, place, patch_hbm, cot_hbm, index_hbm, gain_hbm, out_ref, hidden_ref,
+    patch_ref, cot_ref, index_ref, gain_ref, sems,
 ):
-    par = place[PAR]
-    rows, width = patch_ref.shape[1:]
+    s = k ^ place[PAR]
+    rows, width = patch_ref.shape
     quarter = width // 4
     copies = [
         pltpu.make_async_copy(src, dst, sems.at[i])
         for i, (src, dst) in enumerate(
-            ((index_hbm, index_ref), (patch_hbm, patch_ref), (gain_hbm, gain_ref), (cot_hbm, cot_ref))
+            (
+                (index_hbm, index_ref),
+                (patch_hbm.at[s], patch_ref),
+                (gain_hbm, gain_ref),
+                (cot_hbm.at[s], cot_ref),
+            )
         )
     ]
     for copy in copies:
         copy.start()
-    staged = load_weights(place[CORE], w_in_hbm, w_out_hbm, wq, wk, wv, wo, w_sems)
     order = lax.broadcasted_iota(jnp.int32, (1, quarter), 1).astype(jnp.float32)
     freq = jnp.exp(-np.log(np.float32(10000.0)) * order / quarter)
     diagonal = lax.broadcasted_iota(jnp.int32, (rows, rows), 0) == lax.broadcasted_iota(
         jnp.int32, (rows, rows), 1
     )
     copies[0].wait()
-    tables = []
-    for k in range(2):
-        position = index_ref[pl.ds(k ^ par, 1), :]
-        grid_row = (position // GRID_COLS).astype(jnp.float32)
-        grid_col = (position % GRID_COLS).astype(jnp.float32)
-        grid_row = jnp.sum(jnp.where(diagonal, grid_row, 0.0), axis=1, keepdims=True)
-        grid_col = jnp.sum(jnp.where(diagonal, grid_col, 0.0), axis=1, keepdims=True)
-        pieces = sine_cosine(grid_row * freq) + sine_cosine(grid_col * freq)
-        tables.append(jnp.concatenate(pieces, axis=1))
+    position = index_ref[pl.ds(s, 1), :]
+    grid_row = (position // GRID_COLS).astype(jnp.float32)
+    grid_col = (position % GRID_COLS).astype(jnp.float32)
+    grid_row = jnp.sum(jnp.where(diagonal, grid_row, 0.0), axis=1, keepdims=True)
+    grid_col = jnp.sum(jnp.where(diagonal, grid_col, 0.0), axis=1, keepdims=True)
+    table = jnp.concatenate(sine_cosine(grid_row * freq) + sine_cosine(grid_col * freq), axis=1)
     copies[1].wait()
     copies[2].wait()
-    for k, out_ref in enumerate((p0_ref, p1_ref)):
-        s = k ^ par
-        hidden = patch_ref[s].astype(jnp.float32) + tables[k]
-        hidden_ref[k] = hidden
-        center = hidden - jnp.mean(hidden, axis=-1, keepdims=True)
-        spread = jnp.mean(center * center, axis=-1, keepdims=True)
-        normed = center * lax.rsqrt(spread + epsilon) * gain_ref[...]
-        live = live_column(place[KEPT + s], rows)
-        out_ref[:rows, :] = jnp.where(live, normed, MARK).astype(out_ref.dtype)
+    hidden = patch_ref[...].astype(jnp.float32) + table
+    hidden_ref[...] = hidden
+    center = hidden - jnp.mean(hidden, axis=-1, keepdims=True)
+    spread = jnp.mean(center * center, axis=-1, keepdims=True)
+    normed = center * lax.rsqrt(spread + epsilon) * gain_ref[...]
+    live = live_column(place[KEPT + s], rows)
+    out_ref[:rows, :] = jnp.where(live, normed, MARK).astype(out_ref.dtype)
     copies[3].wait()
-    for k, out_ref in enumerate((p0_ref, p1_ref)):
-        s = k ^ par
-        live = live_column(place[KEPT + s], rows)
-        grad = cot_ref[s]
-        out_ref[rows:, :] = jnp.where(live, grad, jnp.zeros_like(grad))
+    grad = cot_ref[...]
+    out_ref[rows:, :] = jnp.where(live, grad, jnp.zeros_like(grad))
+
+
+def norm_first(place, patch_hbm, cot_hbm, index_hbm, gain_hbm, *refs):
+    norm_block(0, place, patch_hbm, cot_hbm, index_hbm, gain_hbm, *refs)
+
+
+def norm_second(
+    place, patch_hbm, cot_hbm, index_hbm, gain_hbm, w_in_hbm, w_out_hbm, after,
+    out_ref, hidden_ref, wq, wk, wv, wo, *refs,
+):
+    del after
+    staged = load_weights(place[CORE], w_in_hbm, w_out_hbm, wq, wk, wv, wo, refs[-1])
+    norm_block(1, place, patch_hbm, cot_hbm, index_hbm, gain_hbm, out_ref, hidden_ref, *refs[:-1])
     for copy in staged:
         copy.wait()
 
@@ -467,14 +475,14 @@
         o1[block:, :] = total[block:].astype(o1.dtype)
 
 
-def return_kernel(place, r0, r1, hidden_ref, m0, m1, gain_ref, after, encoded, d_patches):
+def return_kernel(place, r0, r1, h0, h1, m0, m1, gain_ref, after, encoded, d_patches):
     del after
     par = place[PAR]
     rows = r0.shape[0] // 2
-    for k, (r_ref, m_ref) in enumerate(((r0, m0), (r1, m1))):
+    for k, (r_ref, m_ref, hidden_ref) in enumerate(((r0, m0, h0), (r1, m1, h1))):
         s = k ^ par
         live = live_column(place[KEPT + s], rows)
-        hidden = hidden_ref[k]
+        hidden = hidden_ref[...]
         projected = r_ref[:rows, :].astype(jnp.float32)
         encoded[s] = jnp.where(live, hidden + projected, 0.0).astype(encoded.dtype)
         center = hidden - jnp.mean(hidden, axis=-1, keepdims=True)
@@ -653,23 +661,28 @@
     any_spec = pl.BlockSpec(memory_space=pl.ANY)
     pairs = width // 512
     own_w = [struct((width, own_width))] * 3 + [struct((own_width, width))]
-    *outs, wq, wk, wv, wo = call(
-        norm_kernel,
-        tuple(in_hbm(v) for v in (patches, cotangent, kept_index, gain_row, w_qkv, w_out)),
-        [pay, pay, struct(patches.shape, f32)] + own_w,
+    rows_in = tuple(in_hbm(v) for v in (patches, cotangent, kept_index, gain_row))
+    held = struct((slots, width), f32)
+    scratch = [
+        pltpu.VMEM((slots, width), bf16),
+        pltpu.VMEM((slots, width), bf16),
+        pltpu.VMEM(kept_index.shape, jnp.int32),
+        pltpu.VMEM(gain_row.shape, f32),
+        pltpu.SemaphoreType.DMA((4,)),
+    ]
+    first_in, first_hidden = call(
+        norm_first, rows_in, [pay, held], 24, place, scratch=scratch, specs=[any_spec] * 4
+    )
+    second_in, second_hidden, wq, wk, wv, wo = call(
+        norm_second,
+        (*rows_in, in_hbm(w_qkv), in_hbm(w_out), first_in),
+        [pay, held] + own_w,
         24,
         place,
-        scratch=[
-            pltpu.VMEM(patches.shape, bf16),
-            pltpu.VMEM(patches.shape, bf16),
-            pltpu.VMEM(kept_index.shape, jnp.int32),
-            pltpu.VMEM(gain_row.shape, f32),
-            pltpu.SemaphoreType.DMA((4,)),
-            pltpu.SemaphoreType.DMA((8 * pairs,)),
-        ],
-        specs=[any_spec] * 6,
-    )
-    *mine, hidden = outs
+        scratch=scratch + [pltpu.SemaphoreType.DMA((8 * pairs,))],
+        specs=[any_spec] * 7,
+    )
+    mine = (first_in, second_in)
     got = [to_chip(mine[k], k) for k in range(2)]
     here = got + [to_core(v) for v in got]
     from_x = to_x(jnp.concatenate([v[:slots] for v in got], axis=0))
@@ -770,11 +783,11 @@
     )
     encoded, d_patches = call(
         return_kernel,
-        (*back, hidden, *mine, gain_row, in_hbm(qkv_grad)),
+        (*back, first_hidden, second_hidden, *mine, gain_row, in_hbm(qkv_grad)),
         [struct(patches.shape)] * 2,
         12,
         place,
-        specs=[VMEM_SPEC] * 6 + [any_spec],
+        specs=[VMEM_SPEC] * 7 + [any_spec],
     )
     return (encoded, d_patches, qkv_grad, out_grad)
 

time: 126 us -> 124 us (0.984)
  waiting for transfers between devices: 63 us -> 59.5 us
  Pallas kernels: 29.6 us -> 31.1 us
    ppermute x22, waiting for transfers between devices: 63 us -> 59.5 us  [send(): return lax.ppermute(value, AXES, line_perm(move, reps))]
    pallas_call x11 -> x12, Pallas kernels: 22.5 us -> 24.3 us  [call(): pl.pallas_call(kernel, in_specs=specs, out_specs=VMEM_SPEC if single else...]
  transfers between devices with their start and end apart: 22 -> 22, of which waited for: 13 -> 14; matrix products, arithmetic and copies ran while one was open for 0% -> 0% of each run, Pallas kernels for 18% -> 20%
where the time goes in v12:
time: 124 us
  waiting for transfers between devices  59.5 us (48%)
  starting transfers between devices  32 us (26%)
  Pallas kernels  31.1 us (25%)
    ppermute x22, waiting for transfers between devices, send(): return lax.ppermute(value, AXES, line_perm(move, reps))  59.5 us
    ppermute x22, starting transfers between devices, send(): return lax.ppermute(value, AXES, line_perm(move, reps))  32 us
    pallas_call x12, Pallas kernels, call(): pl.pallas_call(kernel, in_specs=specs, out_specs=VMEM_SPEC if single else...  24.3 us
    pallas_call x1, Pallas kernels, chip_shards(): pl.pallas_call(rows_kernel, grid_spec=pltpu.PrefetchScalarGridSpec(num_sc...  6.88 us
  transfers between devices with their start and end apart: 22, of which 14 were waited for; matrix products, arithmetic and copies ran while one was open for 0% of the time, Pallas kernels for 20%

profile of v12, /device:TPU:9, one launch (start us, length us, event | category | flops | bytes accessed | tf_op | source)
XLA Modules:
  0.0 124.3 jit_solution(1826377956224445982)
XLA Ops:
  1.4 1.9 %shard_map.102 = (bf16[192,1024]{1,0:T(8,128)(2,1)S(1)}, f32[96,1024]{1,0:T(8,128)S(1)}) custom-call(s32[6]{0:T(128)S(1)} %concatenate.6.place, bf16[2,96,1024]{2,1,0:T(8,128)(2,1)} %patch_hbm.3, bf16[2,96,1024]{2,1,0:T(8,128)(2,1)} %cot_hbm.3, s32[2,96]{1,0:T(2,128)} %index_hbm.3, f32[1,1024]{1,0:T(1,128)} %bitcast.6), custom_call_target="tpu_custom_call" | custom-call | flops 1000 | bytes 1000 | tf_op jit(solution)/shard_map/pallas_call | solution.py:615
  3.2 4.8 %collective-permute-start = (bf16[192,1024]{1,0:T(8,128)(2,1)S(1)}, bf16[192,1024]{1,0:T(8,128)(2,1)S(1)}, u32[]{:S(2)}, u32[]{:S(2)}) collective-permute-start(bf16[192,1024]{1,0:T(8,128)(2,1)S(1)} %get-tuple-element.36.after.m0), channel_id=1, source_target_pairs={{0,0},{1,8},{2,2},{3,10},{4,4},{5,12},{6,6},{7,14},{8,1},{9,9},{10... | collective-permute-start | bytes 1179656 | tf_op jit(solution)/shard_map/ppermute | solution.py:641
  8.0 3.2 %shard_map.103 = (bf16[192,1024]{1,0:T(8,128)(2,1)S(1)}, f32[96,1024]{1,0:T(8,128)S(1)}, bf16[1024,512]{1,0:T(8,128)(2,1)S(1)}, bf16[1024,512]{1,0:T(8,128)(2,1)...) custom-call(s32[6]{0:T(128)S(1)} %concatenate.6.place, bf16[2,96,1024]{2,1,0:T(8,128)(2,1)} %patch_hbm.3, ...), custom_call_target="tpu_custom_call" | custom-call | flops 1000 | bytes 1000 | tf_op jit(solution)/shard_map/pallas_call | solution.py:615
  11.3 7.1 %collective-permute-done.p0 = bf16[192,1024]{1,0:T(8,128)(2,1)S(1)} collective-permute-done((bf16[192,1024]{1,0:T(8,128)(2,1)S(1)}, bf16[192,1024]{1,0:T(8,128)(2,1)S(1)}, u32[]{:S(2)}, u32[]{:S(2)}) %collective-permute-start) | collective-permute-done | bytes 393248 | tf_op jit(solution)/shard_map/ppermute | solution.py:641
  18.5 6.8 %collective-permute-done.1.p1 = bf16[192,1024]{1,0:T(8,128)(2,1)S(1)} collective-permute-done((bf16[192,1024]{1,0:T(8,128)(2,1)S(1)}, bf16[192,1024]{1,0:T(8,128)(2,1)S(1)}, u32[]{:S(2)}, u32[]{:S(2)}) %collective-permute-start.1) | collective-permute-done | bytes 393248 | tf_op jit(solution)/shard_map/ppermute | solution.py:641
  25.4 1.3 %collective-permute-start.5 = (bf16[192,1024]{1,0:T(8,128)(2,1)S(1)}, bf16[192,1024]{1,0:T(8,128)(2,1)S(1)}, u32[]{:S(2)}, u32[]{:S(2)}) collective-permute-start(bf16[192,1024]{1,0:T(8,128)(2,1)S(1)} %pad_maximum_fusion), channel_id=1, source_target_pairs={{0,2},{1,3},{2,0},{3,1},{4,6},{5,7},{6,4},{7,5},{8,10},{9,11},{10,... | collective-permute-start | bytes 1179656 | tf_op jit(solution)/shard_map/ppermute | solution.py:641
  27.0 5.2 %shard_map.104 = (bf16[4,192,256]{2,1,0:T(8,128)(2,1)S(1)}, bf16[4,192,256]{2,1,0:T(8,128)(2,1)S(1)}, bf16[128,1152]{1,0:T(8,128)(2,1)S(1)}, f32[128,1024]{1,0:T(8,128)S(1)}, bf16[128,2176]{1,0:T(8,128)(2,1)S(1)}) custom-call(s32[6]{0:T(128)S(1)} %concatenate.6.place, bf16[192,1024]{1,0:T(8,128)(2,1)S(1)} %collective-permute-done.p0, ...), custom_call_target="tpu_custom_call" | custom-call | flops 1000 | bytes 1000 | tf_op jit(solution)/shard_map/pallas_call | solution.py:615
  32.3 1.3 %collective-permute-start.7 = (bf16[128,2176]{1,0:T(8,128)(2,1)S(1)}, bf16[128,2176]{1,0:T(8,128)(2,1)S(1)}, u32[]{:S(2)}, u32[]{:S(2)}) collective-permute-start(bf16[128,2176]{1,0:T(8,128)(2,1)S(1)} %get-tuple-element.47), channel_id=1, source_target_pairs={{0,2},{1,3},{2,0},{3,1},{4,6},{5,7},{6,4},{7,5},{8,10},{9,11},{10,... | collective-permute-start | bytes 1671176 | tf_op jit(solution)/shard_map/ppermute | solution.py:641
  33.6 2.1 %collective-permute-done.5.after.n0 = bf16[192,1024]{1,0:T(8,128)(2,1)S(1)} collective-permute-done((bf16[192,1024]{1,0:T(8,128)(2,1)S(1)}, bf16[192,1024]{1,0:T(8,128)(2,1)S(1)}, u32[]{:S(2)}, u32[]{:S(2)}) %collective-permute-start.5) | collective-permute-done | bytes 393248 | tf_op jit(solution)/shard_map/ppermute | solution.py:641
  35.6 2.3 %collective-permute-start.9 = (bf16[192,1024]{1,0:T(8,128)(2,1)S(1)}, bf16[192,1024]{1,0:T(8,128)(2,1)S(1)}, u32[]{:S(2)}, u32[]{:S(2)}) collective-permute-start(bf16[192,1024]{1,0:T(8,128)(2,1)S(1)} %collective-permute-done.5.after.n0), channel_id=1, source_target_pairs={{0,1},{1,0},{2,3},{3,2},{4,5},{5,4},{6,7},{7,6},{8,9},{9,8},{10,11... | collective-permute-start | bytes 1179656 | tf_op jit(solution)/shard_map/ppermute | solution.py:641
  37.9 5.3 %shard_map.105 = (bf16[4,192,256]{2,1,0:T(8,128)(2,1)S(1)}, bf16[4,192,256]{2,1,0:T(8,128)(2,1)S(1)}, bf16[128,1152]{1,0:T(8,128)(2,1)S(1)}, f32[128,1024]{1,0:T(8,128)S(1)}, bf16[128,2176]{1,0:T(8,128)(2,1)S(1)}) custom-call(s32[6]{0:T(128)S(1)} %concatenate.6.place, bf16[192,1024]{1,0:T(8,128)(2,1)S(1)} %collective-permute-done.p0, ...), custom_call_target="tpu_custom_call" | custom-call | flops 1000 | bytes 1000 | tf_op jit(solution)/shard_map/pallas_call | solution.py:615
  43.2 1.3 %collective-permute-start.8 = (bf16[128,2176]{1,0:T(8,128)(2,1)S(1)}, bf16[128,2176]{1,0:T(8,128)(2,1)S(1)}, u32[]{:S(2)}, u32[]{:S(2)}) collective-permute-start(bf16[128,2176]{1,0:T(8,128)(2,1)S(1)} %get-tuple-element.50), channel_id=1, source_target_pairs={{0,2},{1,3},{2,0},{3,1},{4,6},{5,7},{6,4},{7,5},{8,10},{9,11},{10,... | collective-permute-start | bytes 1671176 | tf_op jit(solution)/shard_map/ppermute | solution.py:641
  44.5 3.1 %collective-permute-done.7.got.got_a = bf16[128,2176]{1,0:T(8,128)(2,1)S(1)} collective-permute-done((bf16[128,2176]{1,0:T(8,128)(2,1)S(1)}, bf16[128,2176]{1,0:T(8,128)(2,1)S(1)}, u32[]{:S(2)}, u32[]{:S(2)}) %collective-permute-start.7) | collective-permute-done | bytes 557088 | tf_op jit(solution)/shard_map/ppermute | solution.py:641
  47.6 1.4 %shard_map.106 = (f32[2,96,1024]{2,1,0:T(8,128)S(1)}, bf16[2,96,1024]{2,1,0:T(8,128)(2,1)S(1)}) custom-call(s32[6]{0:T(128)S(1)} %concatenate.6.place, bf16[128,1152]{1,0:T(8,128)(2,1)S(1)} %get-tuple-element.46.keep.keep_a, f32[128,1024]{1,0:T(8,128)S(1)} %get-tuple-element.51.out_keep, bf16[128,2176]{1,0:T(8,128)(2,1)S(1)} %collective-permute-done.7.got.got_a, ...), custom_call_target="tpu_custom_call" | custom-call | flops 1000 | bytes 1000 | tf_op jit(solution)/shard_map/pallas_call | solution.py:615
  49.0 8.3 %collective-permute-done.10.got = bf16[2,96,1024]{2,1,0:T(8,128)(2,1)S(1)} collective-permute-done((bf16[2,96,1024]{2,1,0:T(8,128)(2,1)S(1)}, bf16[2,96,1024]{2,1,0:T(8,128)(2,1)S(1)}, u32[]{:S(2)}, u32[]{:S(2)}) %collective-permute-start.10) | collective-permute-done | bytes 393248 | tf_op jit(solution)/shard_map/ppermute | solution.py:641
  57.4 2.1 %collective-permute-done.8.got_b = bf16[128,2176]{1,0:T(8,128)(2,1)S(1)} collective-permute-done((bf16[128,2176]{1,0:T(8,128)(2,1)S(1)}, bf16[128,2176]{1,0:T(8,128)(2,1)S(1)}, u32[]{:S(2)}, u32[]{:S(2)}) %collective-permute-start.8) | collective-permute-done | bytes 557088 | tf_op jit(solution)/shard_map/ppermute | solution.py:641
  59.5 2.0 %shard_map.108 = (f32[2,160,1024]{2,1,0:T(8,128)S(1)}, bf16[2,160,1024]{2,1,0:T(8,128)(2,1)S(1)}) custom-call(s32[6]{0:T(128)S(1)} %concatenate.6.place, bf16[128,1152]{1,0:T(8,128)(2,1)S(1)} %get-tuple-element.46.keep.keep_a, bf16[128,2176]{1,0:T(8,128)(2,1)S(1)} %collective-permute-done.7.got.got_a, bf16[128,1152]{1,0:T(8,128)(2,1)S(1)} %get-tuple-element.48.keep_b, ...), custom_call_target="tpu_custom_call" | custom-call | flops 1000 | bytes 1000 | tf_op jit(solution)/shard_map/pallas_call | solution.py:615
  61.6 4.3 %collective-permute-start.11 = (bf16[96,1024]{1,0:T(8,128)(2,1)S(1)}, bf16[96,1024]{1,0:T(8,128)(2,1)S(1)}, u32[]{:S(2)}, u32[]{:S(2)}) collective-permute-start(bf16[96,1024]{1,0:T(8,128)(2,1)S(1)} %get-tuple-element.54.after), channel_id=1, source_target_pairs={{0,8},{1,9},{2,10},{3,11},{4,12},{5,13},{6,14},{7,15},{8,0},{9,1},... | collective-permute-start | bytes 589832 | tf_op jit(solution)/shard_map/ppermute | solution.py:641
  65.9 1.7 %collective-permute-start.4 = (bf16[4,192,256]{2,1,0:T(8,128)(2,1)S(1)}, bf16[4,192,256]{2,1,0:T(8,128)(2,1)S(1)}, u32[]{:S(2)}, u32[]{:S(2)}) collective-permute-start(bf16[4,192,256]{2,1,0:T(8,128)(2,1)S(1)} %get-tuple-element.43), channel_id=1, source_target_pairs={{0,1},{1,0},{2,3},{3,2},{4,5},{5,4},{6,7},{7,6},{8,9},{9,8},{10,11... | collective-permute-start | bytes 1179656 | tf_op jit(solution)/shard_map/ppermute | solution.py:641
  67.6 16.1 %collective-permute-done.11.got = bf16[96,1024]{1,0:T(8,128)(2,1)S(1)} collective-permute-done((bf16[96,1024]{1,0:T(8,128)(2,1)S(1)}, bf16[96,1024]{1,0:T(8,128)(2,1)S(1)}, u32[]{:S(2)}, u32[]{:S(2)}) %collective-permute-start.11) | collective-permute-done | bytes 196640 | tf_op jit(solution)/shard_map/ppermute | solution.py:641
  83.8 1.3 %collective-permute-start.12 = (bf16[96,1024]{1,0:T(8,128)(2,1)S(1)}, bf16[96,1024]{1,0:T(8,128)(2,1)S(1)}, u32[]{:S(2)}, u32[]{:S(2)}) collective-permute-start(bf16[96,1024]{1,0:T(8,128)(2,1)S(1)} %shard_map.109.a0), channel_id=1, source_target_pairs={{0,2},{1,3},{2,0},{3,1},{4,6},{5,7},{6,4},{7,5},{8,10},{9,11},{10,... | collective-permute-start | bytes 589832 | tf_op jit(solution)/shard_map/ppermute | solution.py:641
  85.3 2.7 %collective-permute-start.15 = (bf16[96,1024]{1,0:T(8,128)(2,1)S(1)}, bf16[96,1024]{1,0:T(8,128)(2,1)S(1)}, u32[]{:S(2)}, u32[]{:S(2)}) collective-permute-start(bf16[96,1024]{1,0:T(8,128)(2,1)S(1)} %shard_map.109.a0), channel_id=1, source_target_pairs={{0,1},{1,0},{2,3},{3,2},{4,5},{5,4},{6,7},{7,6},{8,9},{9,8},{10,11... | collective-permute-start | bytes 589832 | tf_op jit(solution)/shard_map/ppermute | solution.py:641
  88.4 3.3 %collective-permute-start.16 = (bf16[96,1024]{1,0:T(8,128)(2,1)S(1)}, bf16[96,1024]{1,0:T(8,128)(2,1)S(1)}, u32[]{:S(2)}, u32[]{:S(2)}) collective-permute-start(bf16[96,1024]{1,0:T(8,128)(2,1)S(1)} %collective-permute-done.12.before.refs_1_.a1), channel_id=1, source_target_pairs={{0,1},{1,0},{2,3},{3,2},{4,5},{5,4},{6,7},{7,6},{8,9},{9,8},{10,11... | collective-permute-start | bytes 589832 | tf_op jit(solution)/shard_map/ppermute | solution.py:641
  91.7 6.9 %shard_map.110 = (bf16[192,1024]{1,0:T(8,128)(2,1)S(1)}, bf16[192,1024]{1,0:T(8,128)(2,1)S(1)}) custom-call(s32[6]{0:T(128)S(1)} %concatenate.6.place, bf16[4,192,256]{2,1,0:T(8,128)(2,1)S(1)} %get-tuple-element.42.own_a, bf16[4,192,256]{2,1,0:T(8,128)(2,1)S(1)} %collective-permute-done.4.got_a, bf16[4,192,256]{2,1,0:T(8,128)(2,1)S(1)} %get-tuple-element.44.own_b, ...), custom_call_target="tpu_custom_call" | custom-call | flops 1000 | bytes 1000 | tf_op jit(solution)/shard_map/pallas_call | solution.py:761
  100.0 4.8 %collective-permute-start.13 = (bf16[192,1024]{1,0:T(8,128)(2,1)S(1)}, bf16[192,1024]{1,0:T(8,128)(2,1)S(1)}, u32[]{:S(2)}, u32[]{:S(2)}) collective-permute-start(bf16[192,1024]{1,0:T(8,128)(2,1)S(1)} %get-tuple-element.57.refs_0_), channel_id=1, source_target_pairs={{0,0},{1,8},{2,2},{3,10},{4,4},{5,12},{6,6},{7,14},{8,1},{9,9},{10... | collective-permute-start | bytes 1179656 | tf_op jit(solution)/shard_map/ppermute | solution.py:641
  104.9 2.7 %collective-permute-done.19.b1 = bf16[160,1024]{1,0:T(8,128)(2,1)S(1)} collective-permute-done((bf16[160,1024]{1,0:T(8,128)(2,1)S(1)}, bf16[160,1024]{1,0:T(8,128)(2,1)S(1)}, u32[]{:S(2)}, u32[]{:S(2)}) %collective-permute-start.19) | collective-permute-done | bytes 327712 | tf_op jit(solution)/shard_map/ppermute | solution.py:641
  107.6 1.3 %collective-permute-start.21 = (bf16[160,1024]{1,0:T(8,128)(2,1)S(1)}, bf16[160,1024]{1,0:T(8,128)(2,1)S(1)}, u32[]{:S(2)}, u32[]{:S(2)}) collective-permute-start(bf16[160,1024]{1,0:T(8,128)(2,1)S(1)} %collective-permute-done.19.b1), channel_id=1, source_target_pairs={{0,1},{1,0},{2,3},{3,2},{4,5},{5,4},{6,7},{7,6},{8,9},{9,8},{10,11... | collective-permute-start | bytes 983048 | tf_op jit(solution)/shard_map/ppermute | solution.py:641
  109.0 1.3 %collective-permute-done.21.b3 = bf16[160,1024]{1,0:T(8,128)(2,1)S(1)} collective-permute-done((bf16[160,1024]{1,0:T(8,128)(2,1)S(1)}, bf16[160,1024]{1,0:T(8,128)(2,1)S(1)}, u32[]{:S(2)}, u32[]{:S(2)}) %collective-permute-start.21) | collective-permute-done | bytes 327712 | tf_op jit(solution)/shard_map/ppermute | solution.py:641
  110.2 3.0 %shard_map.113 = (f32[1024,768]{1,0:T(8,128)}, f32[1024,256]{1,0:T(8,128)}) custom-call(s32[6]{0:T(128)S(1)} %concatenate.6.place, bf16[96,1024]{1,0:T(8,128)(2,1)S(1)} %shard_map.109.a0, bf16[96,1024]{1,0:T(8,128)(2,1)S(1)} %collective-permute-done.12.before.refs_1_.a1, bf16[96,1024]{1,0:T(8,128)(2,1)S(1)} %collective-permute-done.15.refs_2_.a2, ...), custom_call_target="tpu_custom_call" | custom-call | flops 1000 | bytes 1000 | tf_op jit(solution)/shard_map/pallas_call | solution.py:615
  113.3 4.0 %collective-permute-done.13.r0 = bf16[192,1024]{1,0:T(8,128)(2,1)S(1)} collective-permute-done((bf16[192,1024]{1,0:T(8,128)(2,1)S(1)}, bf16[192,1024]{1,0:T(8,128)(2,1)S(1)}, u32[]{:S(2)}, u32[]{:S(2)}) %collective-permute-start.13) | collective-permute-done | bytes 393248 | tf_op jit(solution)/shard_map/ppermute | solution.py:641
  117.2 5.1 %collective-permute-done.14.r1 = bf16[192,1024]{1,0:T(8,128)(2,1)S(1)} collective-permute-done((bf16[192,1024]{1,0:T(8,128)(2,1)S(1)}, bf16[192,1024]{1,0:T(8,128)(2,1)S(1)}, u32[]{:S(2)}, u32[]{:S(2)}) %collective-permute-start.14) | collective-permute-done | bytes 393248 | tf_op jit(solution)/shard_map/ppermute | solution.py:641
  122.4 1.9 %shard_map.114 = (bf16[2,96,1024]{2,1,0:T(8,128)(2,1)}, bf16[2,96,1024]{2,1,0:T(8,128)(2,1)}) custom-call(s32[6]{0:T(128)S(1)} %concatenate.6.place, bf16[192,1024]{1,0:T(8,128)(2,1)S(1)} %collective-permute-done.13.r0, bf16[192,1024]{1,0:T(8,128)(2,1)S(1)} %collective-permute-done.14.r1, f32[96,1024]{1,0:T(8,128)S(1)} %get-tuple-element.59.h0, ...), custom_call_target="tpu_custom_call" | custom-call | flops 1000 | bytes 1000 | tf_op jit(solution)/shard_map/pallas_call | solution.py:615
  (31 shorter events, 3.6 us)
Async XLA Ops:
  3.2 15.2 %collective-permute-start = (bf16[192,1024]{1,0:T(8,128)(2,1)S(1)}, bf16[192,1024]{1,0:T(8,128)(2,1)S(1)}, u32[]{:S(2)}, u32[]{:S(2)}) collective-permute-start(bf16[192,1024]{1,0:T(8,128)(2,1)S(1)} %get-tuple-element.36.after.m0), channel_id=1, source_target_pairs={{0,0},{1,8},{2,2},{3,10},{4,4},{5,12},{6,6},{7,14},{8,1},{9,9},{10... | collective-permute-start | bytes 1179656 | tf_op jit(solution)/shard_map/ppermute | solution.py:641
  11.3 14.0 %collective-permute-start.1 = (bf16[192,1024]{1,0:T(8,128)(2,1)S(1)}, bf16[192,1024]{1,0:T(8,128)(2,1)S(1)}, u32[]{:S(2)}, u32[]{:S(2)}) collective-permute-start(bf16[192,1024]{1,0:T(8,128)(2,1)S(1)} %get-tuple-element.37.m1), channel_id=1, source_target_pairs={{0,4},{1,12},{2,6},{3,14},{4,0},{5,8},{6,2},{7,10},{8,5},{9,13},{1... | collective-permute-start | bytes 1179656 | tf_op jit(solution)/shard_map/ppermute | solution.py:641
  18.5 8.2 %collective-permute-start.2 = (bf16[192,1024]{1,0:T(8,128)(2,1)S(1)}, bf16[192,1024]{1,0:T(8,128)(2,1)S(1)}, u32[]{:S(2)}, u32[]{:S(2)}) collective-permute-start(bf16[192,1024]{1,0:T(8,128)(2,1)S(1)} %collective-permute-done.p0), channel_id=1, source_target_pairs={{0,1},{1,0},{2,3},{3,2},{4,5},{5,4},{6,7},{7,6},{8,9},{9,8},{10,11... | collective-permute-start | bytes 1179656 | tf_op jit(solution)/shard_map/ppermute | solution.py:641
  25.3 1.7 %collective-permute-start.3 = (bf16[192,1024]{1,0:T(8,128)(2,1)S(1)}, bf16[192,1024]{1,0:T(8,128)(2,1)S(1)}, u32[]{:S(2)}, u32[]{:S(2)}) collective-permute-start(bf16[192,1024]{1,0:T(8,128)(2,1)S(1)} %collective-permute-done.1.p1), channel_id=1, source_target_pairs={{0,1},{1,0},{2,3},{3,2},{4,5},{5,4},{6,7},{7,6},{8,9},{9,8},{10,11... | collective-permute-start | bytes 1179656 | tf_op jit(solution)/shard_map/ppermute | solution.py:641
  25.4 10.2 %collective-permute-start.5 = (bf16[192,1024]{1,0:T(8,128)(2,1)S(1)}, bf16[192,1024]{1,0:T(8,128)(2,1)S(1)}, u32[]{:S(2)}, u32[]{:S(2)}) collective-permute-start(bf16[192,1024]{1,0:T(8,128)(2,1)S(1)} %pad_maximum_fusion), channel_id=1, source_target_pairs={{0,2},{1,3},{2,0},{3,1},{4,6},{5,7},{6,4},{7,5},{8,10},{9,11},{10,... | collective-permute-start | bytes 1179656 | tf_op jit(solution)/shard_map/ppermute | solution.py:641
  32.3 15.3 %collective-permute-start.7 = (bf16[128,2176]{1,0:T(8,128)(2,1)S(1)}, bf16[128,2176]{1,0:T(8,128)(2,1)S(1)}, u32[]{:S(2)}, u32[]{:S(2)}) collective-permute-start(bf16[128,2176]{1,0:T(8,128)(2,1)S(1)} %get-tuple-element.47), channel_id=1, source_target_pairs={{0,2},{1,3},{2,0},{3,1},{4,6},{5,7},{6,4},{7,5},{8,10},{9,11},{10,... | collective-permute-start | bytes 1671176 | tf_op jit(solution)/shard_map/ppermute | solution.py:641
  35.6 8.9 %collective-permute-start.9 = (bf16[192,1024]{1,0:T(8,128)(2,1)S(1)}, bf16[192,1024]{1,0:T(8,128)(2,1)S(1)}, u32[]{:S(2)}, u32[]{:S(2)}) collective-permute-start(bf16[192,1024]{1,0:T(8,128)(2,1)S(1)} %collective-permute-done.5.after.n0), channel_id=1, source_target_pairs={{0,1},{1,0},{2,3},{3,2},{4,5},{5,4},{6,7},{7,6},{8,9},{9,8},{10,11... | collective-permute-start | bytes 1179656 | tf_op jit(solution)/shard_map/ppermute | solution.py:641
  43.2 16.3 %collective-permute-start.8 = (bf16[128,2176]{1,0:T(8,128)(2,1)S(1)}, bf16[128,2176]{1,0:T(8,128)(2,1)S(1)}, u32[]{:S(2)}, u32[]{:S(2)}) collective-permute-start(bf16[128,2176]{1,0:T(8,128)(2,1)S(1)} %get-tuple-element.50), channel_id=1, source_target_pairs={{0,2},{1,3},{2,0},{3,1},{4,6},{5,7},{6,4},{7,5},{8,10},{9,11},{10,... | collective-permute-start | bytes 1671176 | tf_op jit(solution)/shard_map/ppermute | solution.py:641
  48.9 8.4 %collective-permute-start.10 = (bf16[2,96,1024]{2,1,0:T(8,128)(2,1)S(1)}, bf16[2,96,1024]{2,1,0:T(8,128)(2,1)S(1)}, u32[]{:S(2)}, u32[]{:S(2)}) collective-permute-start(bf16[2,96,1024]{2,1,0:T(8,128)(2,1)S(1)} %get-tuple-element.53), channel_id=1, source_target_pairs={{0,4},{1,5},{2,6},{3,7},{4,0},{5,1},{6,2},{7,3},{8,12},{9,13},{10,... | collective-permute-start | bytes 1179656 | tf_op jit(solution)/shard_map/ppermute | solution.py:641
  61.5 23.5 %collective-permute-start.17 = (bf16[2,160,1024]{2,1,0:T(8,128)(2,1)S(1)}, bf16[2,160,1024]{2,1,0:T(8,128)(2,1)S(1)}, u32[]{:S(2)}, u32[]{:S(2)}) collective-permute-start(bf16[2,160,1024]{2,1,0:T(8,128)(2,1)S(1)} %get-tuple-element.55.after), channel_id=1, source_target_pairs={{0,4},{1,5},{2,6},{3,7},{4,0},{5,1},{6,2},{7,3},{8,12},{9,13},{10,... | collective-permute-start | bytes 1966088 | tf_op jit(solution)/shard_map/ppermute | solution.py:641
  61.6 22.2 %collective-permute-start.11 = (bf16[96,1024]{1,0:T(8,128)(2,1)S(1)}, bf16[96,1024]{1,0:T(8,128)(2,1)S(1)}, u32[]{:S(2)}, u32[]{:S(2)}) collective-permute-start(bf16[96,1024]{1,0:T(8,128)(2,1)S(1)} %get-tuple-element.54.after), channel_id=1, source_target_pairs={{0,8},{1,9},{2,10},{3,11},{4,12},{5,13},{6,14},{7,15},{8,0},{9,1},... | collective-permute-start | bytes 589832 | tf_op jit(solution)/shard_map/ppermute | solution.py:641
  65.9 25.8 %collective-permute-start.4 = (bf16[4,192,256]{2,1,0:T(8,128)(2,1)S(1)}, bf16[4,192,256]{2,1,0:T(8,128)(2,1)S(1)}, u32[]{:S(2)}, u32[]{:S(2)}) collective-permute-start(bf16[4,192,256]{2,1,0:T(8,128)(2,1)S(1)} %get-tuple-element.43), channel_id=1, source_target_pairs={{0,1},{1,0},{2,3},{3,2},{4,5},{5,4},{6,7},{7,6},{8,9},{9,8},{10,11... | collective-permute-start | bytes 1179656 | tf_op jit(solution)/shard_map/ppermute | solution.py:641
  67.6 24.1 %collective-permute-start.6 = (bf16[4,192,256]{2,1,0:T(8,128)(2,1)S(1)}, bf16[4,192,256]{2,1,0:T(8,128)(2,1)S(1)}, u32[]{:S(2)}, u32[]{:S(2)}) collective-permute-start(bf16[4,192,256]{2,1,0:T(8,128)(2,1)S(1)} %get-tuple-element.45), channel_id=1, source_target_pairs={{0,1},{1,0},{2,3},{3,2},{4,5},{5,4},{6,7},{7,6},{8,9},{9,8},{10,11... | collective-permute-start | bytes 1179656 | tf_op jit(solution)/shard_map/ppermute | solution.py:641
  83.8 4.6 %collective-permute-start.12 = (bf16[96,1024]{1,0:T(8,128)(2,1)S(1)}, bf16[96,1024]{1,0:T(8,128)(2,1)S(1)}, u32[]{:S(2)}, u32[]{:S(2)}) collective-permute-start(bf16[96,1024]{1,0:T(8,128)(2,1)S(1)} %shard_map.109.a0), channel_id=1, source_target_pairs={{0,2},{1,3},{2,0},{3,1},{4,6},{5,7},{6,4},{7,5},{8,10},{9,11},{10,... | collective-permute-start | bytes 589832 | tf_op jit(solution)/shard_map/ppermute | solution.py:641
  85.2 13.5 %collective-permute-start.18 = (bf16[160,1024]{1,0:T(8,128)(2,1)S(1)}, bf16[160,1024]{1,0:T(8,128)(2,1)S(1)}, u32[]{:S(2)}, u32[]{:S(2)}) collective-permute-start(bf16[160,1024]{1,0:T(8,128)(2,1)S(1)} %get-tuple-element.63), channel_id=1, source_target_pairs={{0,8},{1,9},{2,10},{3,11},{4,12},{5,13},{6,14},{7,15},{8,0},{9,1},... | collective-permute-start | bytes 983048 | tf_op jit(solution)/shard_map/ppermute | solution.py:641
  85.3 13.3 %collective-permute-start.15 = (bf16[96,1024]{1,0:T(8,128)(2,1)S(1)}, bf16[96,1024]{1,0:T(8,128)(2,1)S(1)}, u32[]{:S(2)}, u32[]{:S(2)}) collective-permute-start(bf16[96,1024]{1,0:T(8,128)(2,1)S(1)} %shard_map.109.a0), channel_id=1, source_target_pairs={{0,1},{1,0},{2,3},{3,2},{4,5},{5,4},{6,7},{7,6},{8,9},{9,8},{10,11... | collective-permute-start | bytes 589832 | tf_op jit(solution)/shard_map/ppermute | solution.py:641
  88.4 10.2 %collective-permute-start.16 = (bf16[96,1024]{1,0:T(8,128)(2,1)S(1)}, bf16[96,1024]{1,0:T(8,128)(2,1)S(1)}, u32[]{:S(2)}, u32[]{:S(2)}) collective-permute-start(bf16[96,1024]{1,0:T(8,128)(2,1)S(1)} %collective-permute-done.12.before.refs_1_.a1), channel_id=1, source_target_pairs={{0,1},{1,0},{2,3},{3,2},{4,5},{5,4},{6,7},{7,6},{8,9},{9,8},{10,11... | collective-permute-start | bytes 589832 | tf_op jit(solution)/shard_map/ppermute | solution.py:641
  98.6 23.8 %copy-start = (f32[1024]{0:T(1024)S(1)}, f32[1024]{0:T(1024)}, u32[]{:S(2)}) copy-start(f32[1024]{0:T(1024)} %param.13) | copy-start | bytes 12292
  98.8 8.9 %collective-permute-start.19 = (bf16[160,1024]{1,0:T(8,128)(2,1)S(1)}, bf16[160,1024]{1,0:T(8,128)(2,1)S(1)}, u32[]{:S(2)}, u32[]{:S(2)}) collective-permute-start(bf16[160,1024]{1,0:T(8,128)(2,1)S(1)} %shard_map.112.b0), channel_id=1, source_target_pairs={{0,2},{1,3},{2,0},{3,1},{4,6},{5,7},{6,4},{7,5},{8,10},{9,11},{10,... | collective-permute-start | bytes 983048 | tf_op jit(solution)/shard_map/ppermute | solution.py:641
  100.0 17.3 %collective-permute-start.13 = (bf16[192,1024]{1,0:T(8,128)(2,1)S(1)}, bf16[192,1024]{1,0:T(8,128)(2,1)S(1)}, u32[]{:S(2)}, u32[]{:S(2)}) collective-permute-start(bf16[192,1024]{1,0:T(8,128)(2,1)S(1)} %get-tuple-element.57.refs_0_), channel_id=1, source_target_pairs={{0,0},{1,8},{2,2},{3,10},{4,4},{5,12},{6,6},{7,14},{8,1},{9,9},{10... | collective-permute-start | bytes 1179656 | tf_op jit(solution)/shard_map/ppermute | solution.py:641
  104.8 17.6 %collective-permute-start.14 = (bf16[192,1024]{1,0:T(8,128)(2,1)S(1)}, bf16[192,1024]{1,0:T(8,128)(2,1)S(1)}, u32[]{:S(2)}, u32[]{:S(2)}) collective-permute-start(bf16[192,1024]{1,0:T(8,128)(2,1)S(1)} %get-tuple-element.58), channel_id=1, source_target_pairs={{0,4},{1,12},{2,6},{3,14},{4,0},{5,8},{6,2},{7,10},{8,5},{9,13},{1... | collective-permute-start | bytes 1179656 | tf_op jit(solution)/shard_map/ppermute | solution.py:641
  104.9 4.1 %collective-permute-start.20 = (bf16[160,1024]{1,0:T(8,128)(2,1)S(1)}, bf16[160,1024]{1,0:T(8,128)(2,1)S(1)}, u32[]{:S(2)}, u32[]{:S(2)}) collective-permute-start(bf16[160,1024]{1,0:T(8,128)(2,1)S(1)} %shard_map.112.b0), channel_id=1, source_target_pairs={{0,1},{1,0},{2,3},{3,2},{4,5},{5,4},{6,7},{7,6},{8,9},{9,8},{10,11... | collective-permute-start | bytes 983048 | tf_op jit(solution)/shard_map/ppermute | solution.py:641
  107.6 2.6 %collective-permute-start.21 = (bf16[160,1024]{1,0:T(8,128)(2,1)S(1)}, bf16[160,1024]{1,0:T(8,128)(2,1)S(1)}, u32[]{:S(2)}, u32[]{:S(2)}) collective-permute-start(bf16[160,1024]{1,0:T(8,128)(2,1)S(1)} %collective-permute-done.19.b1), channel_id=1, source_target_pairs={{0,1},{1,0},{2,3},{3,2},{4,5},{5,4},{6,7},{7,6},{8,9},{9,8},{10,11... | collective-permute-start | bytes 983048 | tf_op jit(solution)/shard_map/ppermute | solution.py:641

commit v13 on v12

--- a/solution.py
+++ b/solution.py
@@ -301,7 +301,7 @@
 
 
 def norm_block(
-    k, place, patch_hbm, cot_hbm, index_hbm, gain_hbm, out_ref, hidden_ref,
+    k, place, patch_hbm, cot_hbm, index_hbm, gain_hbm, out_ref, hidden_ref, unit_ref, inv_ref,
     patch_ref, cot_ref, index_ref, gain_ref, sems,
 ):
     s = k ^ place[PAR]
@@ -338,7 +338,11 @@
     hidden_ref[...] = hidden
     center = hidden - jnp.mean(hidden, axis=-1, keepdims=True)
     spread = jnp.mean(center * center, axis=-1, keepdims=True)
-    normed = center * lax.rsqrt(spread + epsilon) * gain_ref[...]
+    inv_std = lax.rsqrt(spread + epsilon)
+    unit = center * inv_std
+    unit_ref[...] = unit
+    inv_ref[...] = inv_std + jnp.zeros(inv_ref.shape, jnp.float32)
+    normed = unit * gain_ref[...]
     live = live_column(place[KEPT + s], rows)
     out_ref[:rows, :] = jnp.where(live, normed, MARK).astype(out_ref.dtype)
     copies[3].wait()
@@ -352,11 +356,11 @@
 
 def norm_second(
     place, patch_hbm, cot_hbm, index_hbm, gain_hbm, w_in_hbm, w_out_hbm, after,
-    out_ref, hidden_ref, wq, wk, wv, wo, *refs,
+    out_ref, hidden_ref, unit_ref, inv_ref, wq, wk, wv, wo, *refs,
 ):
     del after
     staged = load_weights(place[CORE], w_in_hbm, w_out_hbm, wq, wk, wv, wo, refs[-1])
-    norm_block(1, place, patch_hbm, cot_hbm, index_hbm, gain_hbm, out_ref, hidden_ref, *refs[:-1])
+    norm_block(1, place, patch_hbm, cot_hbm, index_hbm, gain_hbm, out_ref, hidden_ref, unit_ref, inv_ref, *refs[:-1])
     for copy in staged:
         copy.wait()
 
@@ -433,9 +437,33 @@
     attend_pairs(place, 0, (p0, p1, p2, p3), *refs)
 
 
-def attend_second(place, p0, p1, p2, p3, wq, wk, wv, wo, after, *refs):
+def pieces_of(refs, rows):
+    pieces = []
+    for ref, at in refs:
+        t, j = at // 2, at % 2
+        pieces.append(ref[64 * j : 64 * j + 64, rows * t : rows * t + rows])
+    return jnp.concatenate(pieces, axis=0)
+
+
+def first_pieces(a, rows):
+    return pieces_of(((a, 0), (a, 2), (a, 4), (a, 5)), rows)
+
+
+def second_pieces(a, b, rows):
+    return pieces_of(((a, 1), (b, 0), (b, 1), (a, 3), (b, 2), (b, 3), (b, 4), (b, 5)), rows)
+
+
+def attend_second(
+    place, p0, p1, p2, p3, wq, wk, wv, wo, keep_a, after,
+    own, oth, own_first, own_second, out_keep, send, keep_b, norm_s, grad_s, att_s,
+):
     del after
-    attend_pairs(place, 2, (p0, p1, p2, p3), wq, wk, wv, wo, *refs)
+    attend_pairs(
+        place, 2, (p0, p1, p2, p3), wq, wk, wv, wo, own, oth, keep_b, out_keep, send, norm_s, grad_s, att_s
+    )
+    rows = norm_s.shape[0]
+    own_first[...] = dot_nn(first_pieces(keep_a, rows), norm_s[...])
+    own_second[...] = dot_nn(second_pieces(keep_a, keep_b, rows), norm_s[...])
 
 
 def in_order(place, own, got):
@@ -475,21 +503,16 @@
         o1[block:, :] = total[block:].astype(o1.dtype)
 
 
-def return_kernel(place, r0, r1, h0, h1, m0, m1, gain_ref, after, encoded, d_patches):
+def return_kernel(place, r0, r1, h0, u0, i0, h1, u1, i1, m0, m1, gain_ref, after, encoded, d_patches):
     del after
-    par = place[PAR]
     rows = r0.shape[0] // 2
-    for k, (r_ref, m_ref, hidden_ref) in enumerate(((r0, m0, h0), (r1, m1, h1))):
-        s = k ^ par
+    for k, (r_ref, hidden, unit, inv_std, m_ref) in enumerate(((r0, h0, u0, i0, m0), (r1, h1, u1, i1, m1))):
+        s = k ^ place[PAR]
         live = live_column(place[KEPT + s], rows)
-        hidden = hidden_ref[...]
         projected = r_ref[:rows, :].astype(jnp.float32)
-        encoded[s] = jnp.where(live, hidden + projected, 0.0).astype(encoded.dtype)
-        center = hidden - jnp.mean(hidden, axis=-1, keepdims=True)
-        spread = jnp.mean(center * center, axis=-1, keepdims=True)
-        inv_std = lax.rsqrt(spread + epsilon)
-        unit = center * inv_std
-        d_hidden = norm_backward(r_ref[rows:, :].astype(jnp.float32), gain_ref[...], unit, inv_std)
+        encoded[s] = jnp.where(live, hidden[...] + projected, 0.0).astype(encoded.dtype)
+        d_normed = r_ref[rows:, :].astype(jnp.float32)
+        d_hidden = norm_backward(d_normed, gain_ref[...], unit[...], inv_std[:, 0:1])
         value = m_ref[rows:, :].astype(jnp.float32) + d_hidden
         d_patches[s] = jnp.where(live, value, 0.0).astype(d_patches.dtype)
 
@@ -509,45 +532,22 @@
             ref[spot, count:, columns * j : columns * j + columns] = value[tall * j : tall * j + tall, :]
 
 
-def piece_of(ref, at, rows):
-    t, j = at // 2, at % 2
-    return ref[64 * j : 64 * j + 64, rows * t : rows * t + rows]
-
-
-def weight_first(
-    place, keep, out_keep, got, p0, p1, p2, p3, n0, n1,
-    part_keep, part_send, tokens, left, total, out_total,
-):
-    block = p0.shape[0] // 2
-    rows = 4 * block
-    for i, ref in enumerate((p0, p1, p2, p3)):
-        tokens[i * block : (i + 1) * block, :] = ref[:block, :]
-    tokens[rows : rows + 2 * block, :] = n0[...]
-    tokens[rows + 2 * block :, :] = n1[...]
-    for side, ref in enumerate((keep, got)):
-        for i, at in enumerate((0, 2, 4, 5)):
-            left[side, 64 * i : 64 * i + 64, :] = piece_of(ref, at, rows)
-    total[...] = dot_nn(left[0], tokens[:rows, :]) + dot_nn(left[1], tokens[rows:, :])
+def weight_first(place, own, out_keep, got, n0, n1, part_keep, part_send, tokens, total, out_total):
+    half, rows = n0.shape[0], 2 * n0.shape[0]
+    tokens[:half, :] = n0[...]
+    tokens[half:, :] = n1[...]
+    total[...] = own[...] + dot_nn(first_pieces(got, rows), tokens[...])
     put_parts(place, total, out_keep, got, part_keep, part_send, out_total)
 
 
 def weight_second(
-    place, keep_a, got_a, keep_b, out_keep, got_b, p0, p1, p2, p3, n0, n1, after,
-    part_keep, part_send, tokens, left, total, out_total,
+    place, own, out_keep, got_a, got_b, n0, n1, after, part_keep, part_send, tokens, total, out_total
 ):
     del after
-    block = p0.shape[0] // 2
-    rows = 4 * block
-    for i, ref in enumerate((p0, p1, p2, p3)):
-        tokens[i * block : (i + 1) * block, :] = ref[:block, :]
-    tokens[rows : rows + 2 * block, :] = n0[...]
-    tokens[rows + 2 * block :, :] = n1[...]
-    for side, (a, b) in enumerate(((keep_a, keep_b), (got_a, got_b))):
-        for i, (ref, at) in enumerate(
-            ((a, 1), (b, 0), (b, 1), (a, 3), (b, 2), (b, 3), (b, 4), (b, 5))
-        ):
-            left[side, 64 * i : 64 * i + 64, :] = piece_of(ref, at, rows)
-    total[...] = dot_nn(left[0], tokens[:rows, :]) + dot_nn(left[1], tokens[rows:, :])
+    half, rows = n0.shape[0], 2 * n0.shape[0]
+    tokens[:half, :] = n0[...]
+    tokens[half:, :] = n1[...]
+    total[...] = own[...] + dot_nn(second_pieces(got_a, got_b, rows), tokens[...])
     put_parts(place, total, out_keep, got_b, part_keep, part_send, out_total)
 
 
@@ -670,13 +670,14 @@
         pltpu.VMEM(gain_row.shape, f32),
         pltpu.SemaphoreType.DMA((4,)),
     ]
-    first_in, first_hidden = call(
-        norm_first, rows_in, [pay, held], 24, place, scratch=scratch, specs=[any_spec] * 4
-    )
-    second_in, second_hidden, wq, wk, wv, wo = call(
+    kept = [held, held, struct((slots, 128), f32)]
+    first_in, *first_kept = call(
+        norm_first, rows_in, [pay] + kept, 24, place, scratch=scratch, specs=[any_spec] * 4
+    )
+    second_in, *second_kept, wq, wk, wv, wo = call(
         norm_second,
         (*rows_in, in_hbm(w_qkv), in_hbm(w_out), first_in),
-        [pay, held] + own_w,
+        [pay] + kept + own_w,
         24,
         place,
         scratch=scratch + [pltpu.SemaphoreType.DMA((8 * pairs,))],
@@ -695,33 +696,43 @@
 
     staged = (wq, wk, wv, wo)
 
-    def attend(kernel, after):
+    def attend(kernel, args, outs, scratch):
         return call(
             kernel,
-            (*here, *staged, *after),
-            [half_rows] * 2 + [half_t, struct(out_half, f32), half_send],
+            (*here, *staged, *args),
+            outs,
             32,
             place,
-            scratch=[pltpu.VMEM((rows, width), bf16)] * 2 + [pltpu.VMEM((2, 64 * pairs, rows), bf16)],
-            specs=[VMEM_SPEC] * 8 + [any_spec] * len(after),
+            scratch=scratch
+            + [pltpu.VMEM((rows, width), bf16)] * 2
+            + [pltpu.VMEM((2, 64 * pairs, rows), bf16)],
+            specs=[VMEM_SPEC] * (8 + len(args[:1])) + [any_spec] * len(args[1:]),
         )
 
-    own_a, oth_a, keep_a, out_keep_a, send_a = attend(attend_first, ())
+    out_own = struct(out_half, f32)
+    own_a, oth_a, keep_a, out_keep_a, send_a = attend(
+        attend_first, (), [half_rows] * 2 + [half_t, out_own, half_send], []
+    )
     got_a = to_x(send_a)
     core_a = to_core(oth_a)
-    own_b, oth_b, keep_b, out_keep_b, send_b = attend(attend_second, (from_x,))
+    own_b, oth_b, own_first, own_second, out_keep_b, send_b = attend(
+        attend_second,
+        (keep_a, from_x),
+        [half_rows] * 2 + [struct((width // 4, width), f32), struct((width // 2, width), f32), out_own, half_send],
+        [pltpu.VMEM(half_t.shape, bf16)],
+    )
     got_b = to_x(send_b)
     core_b = to_core(oth_b)
 
     def parts_of(kernel, args, tall, scratch, after=()):
         return call(
             kernel,
-            (*args, *here, *there, *after),
+            (*args, *there, *after),
             [struct((2, tall, width), f32), struct((2, tall, width))],
             16,
             place,
-            scratch=[pltpu.VMEM((2 * rows, width), bf16)] + scratch + [pltpu.VMEM(out_half, f32)],
-            specs=[VMEM_SPEC] * (len(args) + 6) + [any_spec] * len(after),
+            scratch=[pltpu.VMEM((rows, width), bf16)] + scratch + [pltpu.VMEM(out_half, f32)],
+            specs=[VMEM_SPEC] * (len(args) + 2) + [any_spec] * len(after),
         )
 
     def pair_sums(keep, part):
@@ -742,16 +753,16 @@
 
     keep, part = parts_of(
         weight_first,
-        (keep_a, out_keep_a, got_a),
+        (own_first, out_keep_a, got_a),
         96,
-        [pltpu.VMEM((2, 256, rows), bf16), pltpu.VMEM((256, width), f32)],
+        [pltpu.VMEM((256, width), f32)],
     )
     first_sum, paired, first_got = pair_sums(keep, part)
     keep, part = parts_of(
         weight_second,
-        (keep_a, got_a, keep_b, out_keep_b, got_b),
+        (own_second, out_keep_b, got_a, got_b),
         160,
-        [pltpu.VMEM((2, 512, rows), bf16), pltpu.VMEM((512, width), f32)],
+        [pltpu.VMEM((512, width), f32)],
         (paired,),
     )
     started = part
@@ -783,11 +794,11 @@
     )
     encoded, d_patches = call(
         return_kernel,
-        (*back, first_hidden, second_hidden, *mine, gain_row, in_hbm(qkv_grad)),
+        (*back, *first_kept, *second_kept, *mine, gain_row, in_hbm(qkv_grad)),
         [struct(patches.shape)] * 2,
         12,
         place,
-        specs=[VMEM_SPEC] * 7 + [any_spec],
+        specs=[VMEM_SPEC] * 11 + [any_spec],
     )
     return (encoded, d_patches, qkv_grad, out_grad)
 

time: 124 us -> 125 us (level); the launches traced: 124 us -> 124 us
  waiting for transfers between devices: 59.5 us -> 57.3 us
  starting transfers between devices: 32 us -> 33.5 us
    ppermute x22, waiting for transfers between devices: 59.5 us -> 57.3 us  [send(): return lax.ppermute(value, AXES, line_perm(move, reps))]
    ppermute x22, starting transfers between devices: 32 us -> 33.5 us  [send(): return lax.ppermute(value, AXES, line_perm(move, reps))]
  transfers between devices with their start and end apart: 22 -> 22, of which waited for: 14 -> 14; matrix products, arithmetic and copies ran while one was open for 0% -> 0% of each run, Pallas kernels for 20% -> 18%
where the time goes in v13:
time: 125 us; the launch traced here: 124 us
  waiting for transfers between devices  57.3 us (46%)
  starting transfers between devices  33.5 us (27%)
  Pallas kernels  31.3 us (25%)
    ppermute x22, waiting for transfers between devices, send(): return lax.ppermute(value, AXES, line_perm(move, reps))  57.3 us
    ppermute x22, starting transfers between devices, send(): return lax.ppermute(value, AXES, line_perm(move, reps))  33.5 us
    pallas_call x12, Pallas kernels, call(): pl.pallas_call(kernel, in_specs=specs, out_specs=VMEM_SPEC if single else...  24.3 us
    pallas_call x1, Pallas kernels, chip_shards(): pl.pallas_call(rows_kernel, grid_spec=pltpu.PrefetchScalarGridSpec(num_sc...  7.06 us
  transfers between devices with their start and end apart: 22, of which 14 were waited for; matrix products, arithmetic and copies ran while one was open for 0% of the time, Pallas kernels for 18%

profile of v13, /device:TPU:9, one launch (start us, length us, event | category | flops | bytes accessed | tf_op | source)
XLA Modules:
  0.0 123.7 jit_solution(3602964987981238282)
XLA Ops:
  1.4 1.9 %shard_map.102 = (bf16[192,1024]{1,0:T(8,128)(2,1)S(1)}, f32[96,1024]{1,0:T(8,128)S(1)}, f32[96,1024]{1,0:T(8,128)S(1)}, f32[96,128]{1,0:T(8,128)S(1)}) custom-call(s32[6]{0:T(128)S(1)} %concatenate.6.place, bf16[2,96,1024]{2,1,0:T(8,128)(2,1)} %patch_hbm.3, bf16[2,96,1024]{2,1,0:T(8,128)(2,1)} %cot_hbm.3, s32[2,96]{1,0:T(2,128)} %index_hbm.3, f32[1,1024]{1,0:T(1,128)} %bitcast.6), custom_call_target="tpu_custom_call" | custom-call | flops 1000 | bytes 1000 | tf_op jit(solution)/shard_map/pallas_call | solution.py:615
  3.2 3.2 %shard_map.103 = (bf16[192,1024]{1,0:T(8,128)(2,1)S(1)}, f32[96,1024]{1,0:T(8,128)S(1)}, f32[96,1024]{1,0:T(8,128)S(1)}, f32[96,128]{1,0:T(8,128)S(1)}, bf16[102...) custom-call(s32[6]{0:T(128)S(1)} %concatenate.6.place, ...), custom_call_target="tpu_custom_call" | custom-call | flops 1000 | bytes 1000 | tf_op jit(solution)/shard_map/pallas_call | solution.py:615
  6.5 1.9 %collective-permute-start.1 = (bf16[192,1024]{1,0:T(8,128)(2,1)S(1)}, bf16[192,1024]{1,0:T(8,128)(2,1)S(1)}, u32[]{:S(2)}, u32[]{:S(2)}) collective-permute-start(bf16[192,1024]{1,0:T(8,128)(2,1)S(1)} %get-tuple-element.42.m1), channel_id=1, source_target_pairs={{0,4},{1,12},{2,6},{3,14},{4,0},{5,8},{6,2},{7,10},{8,5},{9,13},{1... | collective-permute-start | bytes 1179656 | tf_op jit(solution)/shard_map/ppermute | solution.py:641
  8.4 2.9 %collective-permute-start = (bf16[192,1024]{1,0:T(8,128)(2,1)S(1)}, bf16[192,1024]{1,0:T(8,128)(2,1)S(1)}, u32[]{:S(2)}, u32[]{:S(2)}) collective-permute-start(bf16[192,1024]{1,0:T(8,128)(2,1)S(1)} %get-tuple-element.41.after.m0), channel_id=1, source_target_pairs={{0,0},{1,8},{2,2},{3,10},{4,4},{5,12},{6,6},{7,14},{8,1},{9,9},{10... | collective-permute-start | bytes 1179656 | tf_op jit(solution)/shard_map/ppermute | solution.py:641
  11.3 6.0 %collective-permute-done.1.p1 = bf16[192,1024]{1,0:T(8,128)(2,1)S(1)} collective-permute-done((bf16[192,1024]{1,0:T(8,128)(2,1)S(1)}, bf16[192,1024]{1,0:T(8,128)(2,1)S(1)}, u32[]{:S(2)}, u32[]{:S(2)}) %collective-permute-start.1) | collective-permute-done | bytes 393248 | tf_op jit(solution)/shard_map/ppermute | solution.py:641
  17.7 8.1 %collective-permute-done.p0 = bf16[192,1024]{1,0:T(8,128)(2,1)S(1)} collective-permute-done((bf16[192,1024]{1,0:T(8,128)(2,1)S(1)}, bf16[192,1024]{1,0:T(8,128)(2,1)S(1)}, u32[]{:S(2)}, u32[]{:S(2)}) %collective-permute-start) | collective-permute-done | bytes 393248 | tf_op jit(solution)/shard_map/ppermute | solution.py:641
  25.8 1.3 %collective-permute-start.5 = (bf16[192,1024]{1,0:T(8,128)(2,1)S(1)}, bf16[192,1024]{1,0:T(8,128)(2,1)S(1)}, u32[]{:S(2)}, u32[]{:S(2)}) collective-permute-start(bf16[192,1024]{1,0:T(8,128)(2,1)S(1)} %pad_maximum_fusion), channel_id=1, source_target_pairs={{0,2},{1,3},{2,0},{3,1},{4,6},{5,7},{6,4},{7,5},{8,10},{9,11},{10,... | collective-permute-start | bytes 1179656 | tf_op jit(solution)/shard_map/ppermute | solution.py:641
  27.5 5.2 %shard_map.104 = (bf16[4,192,256]{2,1,0:T(8,128)(2,1)S(1)}, bf16[4,192,256]{2,1,0:T(8,128)(2,1)S(1)}, bf16[128,1152]{1,0:T(8,128)(2,1)S(1)}, f32[128,1024]{1,0:T(8,128)S(1)}, bf16[128,2176]{1,0:T(8,128)(2,1)S(1)}) custom-call(s32[6]{0:T(128)S(1)} %concatenate.6.place, bf16[192,1024]{1,0:T(8,128)(2,1)S(1)} %collective-permute-done.p0, ...), custom_call_target="tpu_custom_call" | custom-call | flops 1000 | bytes 1000 | tf_op jit(solution)/shard_map/pallas_call | solution.py:615
  32.7 1.3 %collective-permute-start.7 = (bf16[128,2176]{1,0:T(8,128)(2,1)S(1)}, bf16[128,2176]{1,0:T(8,128)(2,1)S(1)}, u32[]{:S(2)}, u32[]{:S(2)}) collective-permute-start(bf16[128,2176]{1,0:T(8,128)(2,1)S(1)} %get-tuple-element.54), channel_id=1, source_target_pairs={{0,2},{1,3},{2,0},{3,1},{4,6},{5,7},{6,4},{7,5},{8,10},{9,11},{10,... | collective-permute-start | bytes 1671176 | tf_op jit(solution)/shard_map/ppermute | solution.py:641
  34.0 2.1 %collective-permute-done.5.after.n0 = bf16[192,1024]{1,0:T(8,128)(2,1)S(1)} collective-permute-done((bf16[192,1024]{1,0:T(8,128)(2,1)S(1)}, bf16[192,1024]{1,0:T(8,128)(2,1)S(1)}, u32[]{:S(2)}, u32[]{:S(2)}) %collective-permute-start.5) | collective-permute-done | bytes 393248 | tf_op jit(solution)/shard_map/ppermute | solution.py:641
  36.1 2.3 %collective-permute-start.9 = (bf16[192,1024]{1,0:T(8,128)(2,1)S(1)}, bf16[192,1024]{1,0:T(8,128)(2,1)S(1)}, u32[]{:S(2)}, u32[]{:S(2)}) collective-permute-start(bf16[192,1024]{1,0:T(8,128)(2,1)S(1)} %collective-permute-done.5.after.n0), channel_id=1, source_target_pairs={{0,1},{1,0},{2,3},{3,2},{4,5},{5,4},{6,7},{7,6},{8,9},{9,8},{10,11... | collective-permute-start | bytes 1179656 | tf_op jit(solution)/shard_map/ppermute | solution.py:641
  38.4 6.1 %shard_map.105 = (bf16[4,192,256]{2,1,0:T(8,128)(2,1)S(1)}, bf16[4,192,256]{2,1,0:T(8,128)(2,1)S(1)}, f32[256,1024]{1,0:T(8,128)S(1)}, f32[512,1024]{1,0:T(8,128...) custom-call(s32[6]{0:T(128)S(1)} %concatenate.6.place, bf16[192,1024]{1,0:T(8,128)(2,1)S(1)} %collective-permute-done.p0, ...), custom_call_target="tpu_custom_call" | custom-call | flops 1000 | bytes 1000 | tf_op jit(solution)/shard_map/pallas_call | solution.py:615
  44.5 1.3 %collective-permute-start.8 = (bf16[128,2176]{1,0:T(8,128)(2,1)S(1)}, bf16[128,2176]{1,0:T(8,128)(2,1)S(1)}, u32[]{:S(2)}, u32[]{:S(2)}) collective-permute-start(bf16[128,2176]{1,0:T(8,128)(2,1)S(1)} %get-tuple-element.55), channel_id=1, source_target_pairs={{0,2},{1,3},{2,0},{3,1},{4,6},{5,7},{6,4},{7,5},{8,10},{9,11},{10,... | collective-permute-start | bytes 1671176 | tf_op jit(solution)/shard_map/ppermute | solution.py:641
  45.7 2.3 %collective-permute-done.7.got.got_a = bf16[128,2176]{1,0:T(8,128)(2,1)S(1)} collective-permute-done((bf16[128,2176]{1,0:T(8,128)(2,1)S(1)}, bf16[128,2176]{1,0:T(8,128)(2,1)S(1)}, u32[]{:S(2)}, u32[]{:S(2)}) %collective-permute-start.7) | collective-permute-done | bytes 557088 | tf_op jit(solution)/shard_map/ppermute | solution.py:641
  49.1 2.0 %collective-permute-start.10 = (bf16[2,96,1024]{2,1,0:T(8,128)(2,1)S(1)}, bf16[2,96,1024]{2,1,0:T(8,128)(2,1)S(1)}, u32[]{:S(2)}, u32[]{:S(2)}) collective-permute-start(bf16[2,96,1024]{2,1,0:T(8,128)(2,1)S(1)} %get-tuple-element.59), channel_id=1, source_target_pairs={{0,4},{1,5},{2,6},{3,7},{4,0},{5,1},{6,2},{7,3},{8,12},{9,13},{10,... | collective-permute-start | bytes 1179656 | tf_op jit(solution)/shard_map/ppermute | solution.py:641
  51.1 7.1 %collective-permute-done.10.got = bf16[2,96,1024]{2,1,0:T(8,128)(2,1)S(1)} collective-permute-done((bf16[2,96,1024]{2,1,0:T(8,128)(2,1)S(1)}, bf16[2,96,1024]{2,1,0:T(8,128)(2,1)S(1)}, u32[]{:S(2)}, u32[]{:S(2)}) %collective-permute-start.10) | collective-permute-done | bytes 393248 | tf_op jit(solution)/shard_map/ppermute | solution.py:641
  58.3 1.6 %collective-permute-done.8.got_b = bf16[128,2176]{1,0:T(8,128)(2,1)S(1)} collective-permute-done((bf16[128,2176]{1,0:T(8,128)(2,1)S(1)}, bf16[128,2176]{1,0:T(8,128)(2,1)S(1)}, u32[]{:S(2)}, u32[]{:S(2)}) %collective-permute-start.8) | collective-permute-done | bytes 557088 | tf_op jit(solution)/shard_map/ppermute | solution.py:641
  60.0 1.5 %shard_map.108 = (f32[2,160,1024]{2,1,0:T(8,128)S(1)}, bf16[2,160,1024]{2,1,0:T(8,128)(2,1)S(1)}) custom-call(s32[6]{0:T(128)S(1)} %concatenate.6.place, f32[512,1024]{1,0:T(8,128)S(1)} %get-tuple-element.52.own, f32[128,1024]{1,0:T(8,128)S(1)} %get-tuple-element.53.out_keep, bf16[128,2176]{1,0:T(8,128)(2,1)S(1)} %collective-permute-done.7.got.got_a, ...), custom_call_target="tpu_custom_call" | custom-call | flops 1000 | bytes 1000 | tf_op jit(solution)/shard_map/pallas_call | solution.py:615
  61.4 2.0 %collective-permute-start.17 = (bf16[2,160,1024]{2,1,0:T(8,128)(2,1)S(1)}, bf16[2,160,1024]{2,1,0:T(8,128)(2,1)S(1)}, u32[]{:S(2)}, u32[]{:S(2)}) collective-permute-start(bf16[2,160,1024]{2,1,0:T(8,128)(2,1)S(1)} %get-tuple-element.61.after), channel_id=1, source_target_pairs={{0,4},{1,5},{2,6},{3,7},{4,0},{5,1},{6,2},{7,3},{8,12},{9,13},{10,... | collective-permute-start | bytes 1966088 | tf_op jit(solution)/shard_map/ppermute | solution.py:641
  63.4 2.2 %collective-permute-start.11 = (bf16[96,1024]{1,0:T(8,128)(2,1)S(1)}, bf16[96,1024]{1,0:T(8,128)(2,1)S(1)}, u32[]{:S(2)}, u32[]{:S(2)}) collective-permute-start(bf16[96,1024]{1,0:T(8,128)(2,1)S(1)} %get-tuple-element.60.after), channel_id=1, source_target_pairs={{0,8},{1,9},{2,10},{3,11},{4,12},{5,13},{6,14},{7,15},{8,0},{9,1},... | collective-permute-start | bytes 589832 | tf_op jit(solution)/shard_map/ppermute | solution.py:641
  65.6 1.4 %collective-permute-start.6 = (bf16[4,192,256]{2,1,0:T(8,128)(2,1)S(1)}, bf16[4,192,256]{2,1,0:T(8,128)(2,1)S(1)}, u32[]{:S(2)}, u32[]{:S(2)}) collective-permute-start(bf16[4,192,256]{2,1,0:T(8,128)(2,1)S(1)} %get-tuple-element.51), channel_id=1, source_target_pairs={{0,1},{1,0},{2,3},{3,2},{4,5},{5,4},{6,7},{7,6},{8,9},{9,8},{10,11... | collective-permute-start | bytes 1179656 | tf_op jit(solution)/shard_map/ppermute | solution.py:641
  67.0 16.7 %collective-permute-done.11.got = bf16[96,1024]{1,0:T(8,128)(2,1)S(1)} collective-permute-done((bf16[96,1024]{1,0:T(8,128)(2,1)S(1)}, bf16[96,1024]{1,0:T(8,128)(2,1)S(1)}, u32[]{:S(2)}, u32[]{:S(2)}) %collective-permute-start.11) | collective-permute-done | bytes 196640 | tf_op jit(solution)/shard_map/ppermute | solution.py:641
  85.6 1.8 %collective-permute-start.15 = (bf16[96,1024]{1,0:T(8,128)(2,1)S(1)}, bf16[96,1024]{1,0:T(8,128)(2,1)S(1)}, u32[]{:S(2)}, u32[]{:S(2)}) collective-permute-start(bf16[96,1024]{1,0:T(8,128)(2,1)S(1)} %shard_map.109.a0), channel_id=1, source_target_pairs={{0,1},{1,0},{2,3},{3,2},{4,5},{5,4},{6,7},{7,6},{8,9},{9,8},{10,11... | collective-permute-start | bytes 589832 | tf_op jit(solution)/shard_map/ppermute | solution.py:641
  88.3 2.9 %collective-permute-start.16 = (bf16[96,1024]{1,0:T(8,128)(2,1)S(1)}, bf16[96,1024]{1,0:T(8,128)(2,1)S(1)}, u32[]{:S(2)}, u32[]{:S(2)}) collective-permute-start(bf16[96,1024]{1,0:T(8,128)(2,1)S(1)} %collective-permute-done.12.before.refs_1_.a1), channel_id=1, source_target_pairs={{0,1},{1,0},{2,3},{3,2},{4,5},{5,4},{6,7},{7,6},{8,9},{9,8},{10,11... | collective-permute-start | bytes 589832 | tf_op jit(solution)/shard_map/ppermute | solution.py:641
  91.2 7.1 %shard_map.110 = (bf16[192,1024]{1,0:T(8,128)(2,1)S(1)}, bf16[192,1024]{1,0:T(8,128)(2,1)S(1)}) custom-call(s32[6]{0:T(128)S(1)} %concatenate.6.place, bf16[4,192,256]{2,1,0:T(8,128)(2,1)S(1)} %get-tuple-element.47.own_a, bf16[4,192,256]{2,1,0:T(8,128)(2,1)S(1)} %collective-permute-done.4.got_a, bf16[4,192,256]{2,1,0:T(8,128)(2,1)S(1)} %get-tuple-element.50.own_b, ...), custom_call_target="tpu_custom_call" | custom-call | flops 1000 | bytes 1000 | tf_op jit(solution)/shard_map/pallas_call | solution.py:772
  100.4 5.7 %collective-permute-start.13 = (bf16[192,1024]{1,0:T(8,128)(2,1)S(1)}, bf16[192,1024]{1,0:T(8,128)(2,1)S(1)}, u32[]{:S(2)}, u32[]{:S(2)}) collective-permute-start(bf16[192,1024]{1,0:T(8,128)(2,1)S(1)} %get-tuple-element.63.refs_0_), channel_id=1, source_target_pairs={{0,0},{1,8},{2,2},{3,10},{4,4},{5,12},{6,6},{7,14},{8,1},{9,9},{10... | collective-permute-start | bytes 1179656 | tf_op jit(solution)/shard_map/ppermute | solution.py:641
  106.2 2.1 %collective-permute-done.19.b1 = bf16[160,1024]{1,0:T(8,128)(2,1)S(1)} collective-permute-done((bf16[160,1024]{1,0:T(8,128)(2,1)S(1)}, bf16[160,1024]{1,0:T(8,128)(2,1)S(1)}, u32[]{:S(2)}, u32[]{:S(2)}) %collective-permute-start.19) | collective-permute-done | bytes 327712 | tf_op jit(solution)/shard_map/ppermute | solution.py:641
  108.3 1.3 %collective-permute-start.21 = (bf16[160,1024]{1,0:T(8,128)(2,1)S(1)}, bf16[160,1024]{1,0:T(8,128)(2,1)S(1)}, u32[]{:S(2)}, u32[]{:S(2)}) collective-permute-start(bf16[160,1024]{1,0:T(8,128)(2,1)S(1)} %collective-permute-done.19.b1), channel_id=1, source_target_pairs={{0,1},{1,0},{2,3},{3,2},{4,5},{5,4},{6,7},{7,6},{8,9},{9,8},{10,11... | collective-permute-start | bytes 983048 | tf_op jit(solution)/shard_map/ppermute | solution.py:641
  110.9 3.0 %shard_map.113 = (f32[1024,768]{1,0:T(8,128)}, f32[1024,256]{1,0:T(8,128)}) custom-call(s32[6]{0:T(128)S(1)} %concatenate.6.place, bf16[96,1024]{1,0:T(8,128)(2,1)S(1)} %shard_map.109.a0, bf16[96,1024]{1,0:T(8,128)(2,1)S(1)} %collective-permute-done.12.before.refs_1_.a1, bf16[96,1024]{1,0:T(8,128)(2,1)S(1)} %collective-permute-done.15.refs_2_.a2, ...), custom_call_target="tpu_custom_call" | custom-call | flops 1000 | bytes 1000 | tf_op jit(solution)/shard_map/pallas_call | solution.py:615
  113.9 3.6 %collective-permute-done.13.r0 = bf16[192,1024]{1,0:T(8,128)(2,1)S(1)} collective-permute-done((bf16[192,1024]{1,0:T(8,128)(2,1)S(1)}, bf16[192,1024]{1,0:T(8,128)(2,1)S(1)}, u32[]{:S(2)}, u32[]{:S(2)}) %collective-permute-start.13) | collective-permute-done | bytes 393248 | tf_op jit(solution)/shard_map/ppermute | solution.py:641
  117.5 4.2 %collective-permute-done.14.r1 = bf16[192,1024]{1,0:T(8,128)(2,1)S(1)} collective-permute-done((bf16[192,1024]{1,0:T(8,128)(2,1)S(1)}, bf16[192,1024]{1,0:T(8,128)(2,1)S(1)}, u32[]{:S(2)}, u32[]{:S(2)}) %collective-permute-start.14) | collective-permute-done | bytes 393248 | tf_op jit(solution)/shard_map/ppermute | solution.py:641
  121.8 2.0 %shard_map.114 = (bf16[2,96,1024]{2,1,0:T(8,128)(2,1)}, bf16[2,96,1024]{2,1,0:T(8,128)(2,1)}) custom-call(s32[6]{0:T(128)S(1)} %concatenate.6.place, bf16[192,1024]{1,0:T(8,128)(2,1)S(1)} %collective-permute-done.13.r0, bf16[192,1024]{1,0:T(8,128)(2,1)S(1)} %collective-permute-done.14.r1, f32[96,1024]{1,0:T(8,128)S(1)} %get-tuple-element.65.h0, ...), custom_call_target="tpu_custom_call" | custom-call | flops 1000 | bytes 1000 | tf_op jit(solution)/shard_map/pallas_call | solution.py:615
  (31 shorter events, 9.0 us)
Async XLA Ops:
  6.5 10.8 %collective-permute-start.1 = (bf16[192,1024]{1,0:T(8,128)(2,1)S(1)}, bf16[192,1024]{1,0:T(8,128)(2,1)S(1)}, u32[]{:S(2)}, u32[]{:S(2)}) collective-permute-start(bf16[192,1024]{1,0:T(8,128)(2,1)S(1)} %get-tuple-element.42.m1), channel_id=1, source_target_pairs={{0,4},{1,12},{2,6},{3,14},{4,0},{5,8},{6,2},{7,10},{8,5},{9,13},{1... | collective-permute-start | bytes 1179656 | tf_op jit(solution)/shard_map/ppermute | solution.py:641
  8.4 17.4 %collective-permute-start = (bf16[192,1024]{1,0:T(8,128)(2,1)S(1)}, bf16[192,1024]{1,0:T(8,128)(2,1)S(1)}, u32[]{:S(2)}, u32[]{:S(2)}) collective-permute-start(bf16[192,1024]{1,0:T(8,128)(2,1)S(1)} %get-tuple-element.41.after.m0), channel_id=1, source_target_pairs={{0,0},{1,8},{2,2},{3,10},{4,4},{5,12},{6,6},{7,14},{8,1},{9,9},{10... | collective-permute-start | bytes 1179656 | tf_op jit(solution)/shard_map/ppermute | solution.py:641
  17.3 9.8 %collective-permute-start.3 = (bf16[192,1024]{1,0:T(8,128)(2,1)S(1)}, bf16[192,1024]{1,0:T(8,128)(2,1)S(1)}, u32[]{:S(2)}, u32[]{:S(2)}) collective-permute-start(bf16[192,1024]{1,0:T(8,128)(2,1)S(1)} %collective-permute-done.1.p1), channel_id=1, source_target_pairs={{0,1},{1,0},{2,3},{3,2},{4,5},{5,4},{6,7},{7,6},{8,9},{9,8},{10,11... | collective-permute-start | bytes 1179656 | tf_op jit(solution)/shard_map/ppermute | solution.py:641
  25.8 1.7 %collective-permute-start.2 = (bf16[192,1024]{1,0:T(8,128)(2,1)S(1)}, bf16[192,1024]{1,0:T(8,128)(2,1)S(1)}, u32[]{:S(2)}, u32[]{:S(2)}) collective-permute-start(bf16[192,1024]{1,0:T(8,128)(2,1)S(1)} %collective-permute-done.p0), channel_id=1, source_target_pairs={{0,1},{1,0},{2,3},{3,2},{4,5},{5,4},{6,7},{7,6},{8,9},{9,8},{10,11... | collective-permute-start | bytes 1179656 | tf_op jit(solution)/shard_map/ppermute | solution.py:641
  25.8 10.2 %collective-permute-start.5 = (bf16[192,1024]{1,0:T(8,128)(2,1)S(1)}, bf16[192,1024]{1,0:T(8,128)(2,1)S(1)}, u32[]{:S(2)}, u32[]{:S(2)}) collective-permute-start(bf16[192,1024]{1,0:T(8,128)(2,1)S(1)} %pad_maximum_fusion), channel_id=1, source_target_pairs={{0,2},{1,3},{2,0},{3,1},{4,6},{5,7},{6,4},{7,5},{8,10},{9,11},{10,... | collective-permute-start | bytes 1179656 | tf_op jit(solution)/shard_map/ppermute | solution.py:641
  32.7 15.3 %collective-permute-start.7 = (bf16[128,2176]{1,0:T(8,128)(2,1)S(1)}, bf16[128,2176]{1,0:T(8,128)(2,1)S(1)}, u32[]{:S(2)}, u32[]{:S(2)}) collective-permute-start(bf16[128,2176]{1,0:T(8,128)(2,1)S(1)} %get-tuple-element.54), channel_id=1, source_target_pairs={{0,2},{1,3},{2,0},{3,1},{4,6},{5,7},{6,4},{7,5},{8,10},{9,11},{10,... | collective-permute-start | bytes 1671176 | tf_op jit(solution)/shard_map/ppermute | solution.py:641
  36.1 9.7 %collective-permute-start.9 = (bf16[192,1024]{1,0:T(8,128)(2,1)S(1)}, bf16[192,1024]{1,0:T(8,128)(2,1)S(1)}, u32[]{:S(2)}, u32[]{:S(2)}) collective-permute-start(bf16[192,1024]{1,0:T(8,128)(2,1)S(1)} %collective-permute-done.5.after.n0), channel_id=1, source_target_pairs={{0,1},{1,0},{2,3},{3,2},{4,5},{5,4},{6,7},{7,6},{8,9},{9,8},{10,11... | collective-permute-start | bytes 1179656 | tf_op jit(solution)/shard_map/ppermute | solution.py:641
  44.5 15.5 %collective-permute-start.8 = (bf16[128,2176]{1,0:T(8,128)(2,1)S(1)}, bf16[128,2176]{1,0:T(8,128)(2,1)S(1)}, u32[]{:S(2)}, u32[]{:S(2)}) collective-permute-start(bf16[128,2176]{1,0:T(8,128)(2,1)S(1)} %get-tuple-element.55), channel_id=1, source_target_pairs={{0,2},{1,3},{2,0},{3,1},{4,6},{5,7},{6,4},{7,5},{8,10},{9,11},{10,... | collective-permute-start | bytes 1671176 | tf_op jit(solution)/shard_map/ppermute | solution.py:641
  49.1 9.1 %collective-permute-start.10 = (bf16[2,96,1024]{2,1,0:T(8,128)(2,1)S(1)}, bf16[2,96,1024]{2,1,0:T(8,128)(2,1)S(1)}, u32[]{:S(2)}, u32[]{:S(2)}) collective-permute-start(bf16[2,96,1024]{2,1,0:T(8,128)(2,1)S(1)} %get-tuple-element.59), channel_id=1, source_target_pairs={{0,4},{1,5},{2,6},{3,7},{4,0},{5,1},{6,2},{7,3},{8,12},{9,13},{10,... | collective-permute-start | bytes 1179656 | tf_op jit(solution)/shard_map/ppermute | solution.py:641
  61.4 23.6 %collective-permute-start.17 = (bf16[2,160,1024]{2,1,0:T(8,128)(2,1)S(1)}, bf16[2,160,1024]{2,1,0:T(8,128)(2,1)S(1)}, u32[]{:S(2)}, u32[]{:S(2)}) collective-permute-start(bf16[2,160,1024]{2,1,0:T(8,128)(2,1)S(1)} %get-tuple-element.61.after), channel_id=1, source_target_pairs={{0,4},{1,5},{2,6},{3,7},{4,0},{5,1},{6,2},{7,3},{8,12},{9,13},{10,... | collective-permute-start | bytes 1966088 | tf_op jit(solution)/shard_map/ppermute | solution.py:641
  63.4 20.3 %collective-permute-start.11 = (bf16[96,1024]{1,0:T(8,128)(2,1)S(1)}, bf16[96,1024]{1,0:T(8,128)(2,1)S(1)}, u32[]{:S(2)}, u32[]{:S(2)}) collective-permute-start(bf16[96,1024]{1,0:T(8,128)(2,1)S(1)} %get-tuple-element.60.after), channel_id=1, source_target_pairs={{0,8},{1,9},{2,10},{3,11},{4,12},{5,13},{6,14},{7,15},{8,0},{9,1},... | collective-permute-start | bytes 589832 | tf_op jit(solution)/shard_map/ppermute | solution.py:641
  65.6 25.6 %collective-permute-start.6 = (bf16[4,192,256]{2,1,0:T(8,128)(2,1)S(1)}, bf16[4,192,256]{2,1,0:T(8,128)(2,1)S(1)}, u32[]{:S(2)}, u32[]{:S(2)}) collective-permute-start(bf16[4,192,256]{2,1,0:T(8,128)(2,1)S(1)} %get-tuple-element.51), channel_id=1, source_target_pairs={{0,1},{1,0},{2,3},{3,2},{4,5},{5,4},{6,7},{7,6},{8,9},{9,8},{10,11... | collective-permute-start | bytes 1179656 | tf_op jit(solution)/shard_map/ppermute | solution.py:641
  67.0 24.2 %collective-permute-start.4 = (bf16[4,192,256]{2,1,0:T(8,128)(2,1)S(1)}, bf16[4,192,256]{2,1,0:T(8,128)(2,1)S(1)}, u32[]{:S(2)}, u32[]{:S(2)}) collective-permute-start(bf16[4,192,256]{2,1,0:T(8,128)(2,1)S(1)} %get-tuple-element.48), channel_id=1, source_target_pairs={{0,1},{1,0},{2,3},{3,2},{4,5},{5,4},{6,7},{7,6},{8,9},{9,8},{10,11... | collective-permute-start | bytes 1179656 | tf_op jit(solution)/shard_map/ppermute | solution.py:641
  83.7 4.6 %collective-permute-start.12 = (bf16[96,1024]{1,0:T(8,128)(2,1)S(1)}, bf16[96,1024]{1,0:T(8,128)(2,1)S(1)}, u32[]{:S(2)}, u32[]{:S(2)}) collective-permute-start(bf16[96,1024]{1,0:T(8,128)(2,1)S(1)} %shard_map.109.a0), channel_id=1, source_target_pairs={{0,2},{1,3},{2,0},{3,1},{4,6},{5,7},{6,4},{7,5},{8,10},{9,11},{10,... | collective-permute-start | bytes 589832 | tf_op jit(solution)/shard_map/ppermute | solution.py:641
  85.1 14.2 %collective-permute-start.18 = (bf16[160,1024]{1,0:T(8,128)(2,1)S(1)}, bf16[160,1024]{1,0:T(8,128)(2,1)S(1)}, u32[]{:S(2)}, u32[]{:S(2)}) collective-permute-start(bf16[160,1024]{1,0:T(8,128)(2,1)S(1)} %get-tuple-element.73), channel_id=1, source_target_pairs={{0,8},{1,9},{2,10},{3,11},{4,12},{5,13},{6,14},{7,15},{8,0},{9,1},... | collective-permute-start | bytes 983048 | tf_op jit(solution)/shard_map/ppermute | solution.py:641
  85.6 12.7 %collective-permute-start.15 = (bf16[96,1024]{1,0:T(8,128)(2,1)S(1)}, bf16[96,1024]{1,0:T(8,128)(2,1)S(1)}, u32[]{:S(2)}, u32[]{:S(2)}) collective-permute-start(bf16[96,1024]{1,0:T(8,128)(2,1)S(1)} %shard_map.109.a0), channel_id=1, source_target_pairs={{0,1},{1,0},{2,3},{3,2},{4,5},{5,4},{6,7},{7,6},{8,9},{9,8},{10,11... | collective-permute-start | bytes 589832 | tf_op jit(solution)/shard_map/ppermute | solution.py:641
  88.3 10.0 %collective-permute-start.16 = (bf16[96,1024]{1,0:T(8,128)(2,1)S(1)}, bf16[96,1024]{1,0:T(8,128)(2,1)S(1)}, u32[]{:S(2)}, u32[]{:S(2)}) collective-permute-start(bf16[96,1024]{1,0:T(8,128)(2,1)S(1)} %collective-permute-done.12.before.refs_1_.a1), channel_id=1, source_target_pairs={{0,1},{1,0},{2,3},{3,2},{4,5},{5,4},{6,7},{7,6},{8,9},{9,8},{10,11... | collective-permute-start | bytes 589832 | tf_op jit(solution)/shard_map/ppermute | solution.py:641
  99.4 22.4 %copy-start = (f32[1024]{0:T(1024)S(1)}, f32[1024]{0:T(1024)}, u32[]{:S(2)}) copy-start(f32[1024]{0:T(1024)} %param.13) | copy-start | bytes 12292
  99.4 8.9 %collective-permute-start.19 = (bf16[160,1024]{1,0:T(8,128)(2,1)S(1)}, bf16[160,1024]{1,0:T(8,128)(2,1)S(1)}, u32[]{:S(2)}, u32[]{:S(2)}) collective-permute-start(bf16[160,1024]{1,0:T(8,128)(2,1)S(1)} %shard_map.112.b0), channel_id=1, source_target_pairs={{0,2},{1,3},{2,0},{3,1},{4,6},{5,7},{6,4},{7,5},{8,10},{9,11},{10,... | collective-permute-start | bytes 983048 | tf_op jit(solution)/shard_map/ppermute | solution.py:641
  100.4 17.2 %collective-permute-start.13 = (bf16[192,1024]{1,0:T(8,128)(2,1)S(1)}, bf16[192,1024]{1,0:T(8,128)(2,1)S(1)}, u32[]{:S(2)}, u32[]{:S(2)}) collective-permute-start(bf16[192,1024]{1,0:T(8,128)(2,1)S(1)} %get-tuple-element.63.refs_0_), channel_id=1, source_target_pairs={{0,0},{1,8},{2,2},{3,10},{4,4},{5,12},{6,6},{7,14},{8,1},{9,9},{10... | collective-permute-start | bytes 1179656 | tf_op jit(solution)/shard_map/ppermute | solution.py:641
  106.0 15.7 %collective-permute-start.14 = (bf16[192,1024]{1,0:T(8,128)(2,1)S(1)}, bf16[192,1024]{1,0:T(8,128)(2,1)S(1)}, u32[]{:S(2)}, u32[]{:S(2)}) collective-permute-start(bf16[192,1024]{1,0:T(8,128)(2,1)S(1)} %get-tuple-element.64), channel_id=1, source_target_pairs={{0,4},{1,12},{2,6},{3,14},{4,0},{5,8},{6,2},{7,10},{8,5},{9,13},{1... | collective-permute-start | bytes 1179656 | tf_op jit(solution)/shard_map/ppermute | solution.py:641
  106.1 3.5 %collective-permute-start.20 = (bf16[160,1024]{1,0:T(8,128)(2,1)S(1)}, bf16[160,1024]{1,0:T(8,128)(2,1)S(1)}, u32[]{:S(2)}, u32[]{:S(2)}) collective-permute-start(bf16[160,1024]{1,0:T(8,128)(2,1)S(1)} %shard_map.112.b0), channel_id=1, source_target_pairs={{0,1},{1,0},{2,3},{3,2},{4,5},{5,4},{6,7},{7,6},{8,9},{9,8},{10,11... | collective-permute-start | bytes 983048 | tf_op jit(solution)/shard_map/ppermute | solution.py:641
  108.3 2.6 %collective-permute-start.21 = (bf16[160,1024]{1,0:T(8,128)(2,1)S(1)}, bf16[160,1024]{1,0:T(8,128)(2,1)S(1)}, u32[]{:S(2)}, u32[]{:S(2)}) collective-permute-start(bf16[160,1024]{1,0:T(8,128)(2,1)S(1)} %collective-permute-done.19.b1), channel_id=1, source_target_pairs={{0,1},{1,0},{2,3},{3,2},{4,5},{5,4},{6,7},{7,6},{8,9},{9,8},{10,11... | collective-permute-start | bytes 983048 | tf_op jit(solution)/shard_map/ppermute | solution.py:641

commit v14 on v12

--- a/solution.py
+++ b/solution.py
@@ -429,13 +429,45 @@
     send[:, 3 * rows :] = dot_nn(att_s[1], grad_s[...]).astype(send.dtype)
 
 
-def attend_first(place, p0, p1, p2, p3, *refs):
-    attend_pairs(place, 0, (p0, p1, p2, p3), *refs)
+def pieces_of(refs, rows):
+    pieces = []
+    for ref, at in refs:
+        t, j = at // 2, at % 2
+        pieces.append(ref[64 * j : 64 * j + 64, rows * t : rows * t + rows])
+    return jnp.concatenate(pieces, axis=0)
+
+
+def first_pieces(a, rows):
+    return pieces_of(((a, 0), (a, 2), (a, 4), (a, 5)), rows)
+
+
+def second_pieces(a, b, rows):
+    return pieces_of(((a, 1), (b, 0), (b, 1), (a, 3), (b, 2), (b, 3), (b, 4), (b, 5)), rows)
+
+
+def block_rows(refs):
+    return jnp.concatenate([ref[64 * at : 64 * at + 64, :] for ref, at in refs], axis=0)
+
+
+def attend_half(
+    first_pair, place, p0, p1, p2, p3, wq, wk, wv, wo,
+    own, oth, own_part, out_keep, send, keep, norm_s, grad_s, att_s,
+):
+    attend_pairs(
+        place, first_pair, (p0, p1, p2, p3), wq, wk, wv, wo,
+        own, oth, keep, out_keep, send, norm_s, grad_s, att_s,
+    )
+    rows = norm_s.shape[0]
+    own_part[...] = dot_nn(pieces_of([(keep, at) for at in range(6)], rows), norm_s[...])
+
+
+def attend_first(place, *refs):
+    attend_half(0, place, *refs)
 
 
 def attend_second(place, p0, p1, p2, p3, wq, wk, wv, wo, after, *refs):
     del after
-    attend_pairs(place, 2, (p0, p1, p2, p3), wq, wk, wv, wo, *refs)
+    attend_half(2, place, p0, p1, p2, p3, wq, wk, wv, wo, *refs)
 
 
 def in_order(place, own, got):
@@ -509,45 +541,23 @@
             ref[spot, count:, columns * j : columns * j + columns] = value[tall * j : tall * j + tall, :]
 
 
-def piece_of(ref, at, rows):
-    t, j = at // 2, at % 2
-    return ref[64 * j : 64 * j + 64, rows * t : rows * t + rows]
-
-
-def weight_first(
-    place, keep, out_keep, got, p0, p1, p2, p3, n0, n1,
-    part_keep, part_send, tokens, left, total, out_total,
-):
-    block = p0.shape[0] // 2
-    rows = 4 * block
-    for i, ref in enumerate((p0, p1, p2, p3)):
-        tokens[i * block : (i + 1) * block, :] = ref[:block, :]
-    tokens[rows : rows + 2 * block, :] = n0[...]
-    tokens[rows + 2 * block :, :] = n1[...]
-    for side, ref in enumerate((keep, got)):
-        for i, at in enumerate((0, 2, 4, 5)):
-            left[side, 64 * i : 64 * i + 64, :] = piece_of(ref, at, rows)
-    total[...] = dot_nn(left[0], tokens[:rows, :]) + dot_nn(left[1], tokens[rows:, :])
+def weight_first(place, own, out_keep, got, n0, n1, *refs):
+    part_keep, part_send, tokens, total, out_total = refs[-5:]
+    half, rows = n0.shape[0], 2 * n0.shape[0]
+    tokens[:half, :] = n0[...]
+    tokens[half:, :] = n1[...]
+    mine = block_rows(((own, 0), (own, 2), (own, 4), (own, 5)))
+    total[...] = mine + dot_nn(first_pieces(got, rows), tokens[...])
     put_parts(place, total, out_keep, got, part_keep, part_send, out_total)
 
 
-def weight_second(
-    place, keep_a, got_a, keep_b, out_keep, got_b, p0, p1, p2, p3, n0, n1, after,
-    part_keep, part_send, tokens, left, total, out_total,
-):
-    del after
-    block = p0.shape[0] // 2
-    rows = 4 * block
-    for i, ref in enumerate((p0, p1, p2, p3)):
-        tokens[i * block : (i + 1) * block, :] = ref[:block, :]
-    tokens[rows : rows + 2 * block, :] = n0[...]
-    tokens[rows + 2 * block :, :] = n1[...]
-    for side, (a, b) in enumerate(((keep_a, keep_b), (got_a, got_b))):
-        for i, (ref, at) in enumerate(
-            ((a, 1), (b, 0), (b, 1), (a, 3), (b, 2), (b, 3), (b, 4), (b, 5))
-        ):
-            left[side, 64 * i : 64 * i + 64, :] = piece_of(ref, at, rows)
-    total[...] = dot_nn(left[0], tokens[:rows, :]) + dot_nn(left[1], tokens[rows:, :])
+def weight_second(place, a, b, out_keep, got_a, got_b, n0, n1, *refs):
+    part_keep, part_send, tokens, total, out_total = refs[-5:]
+    half, rows = n0.shape[0], 2 * n0.shape[0]
+    tokens[:half, :] = n0[...]
+    tokens[half:, :] = n1[...]
+    mine = block_rows(((a, 1), (b, 0), (b, 1), (a, 3), (b, 2), (b, 3), (b, 4), (b, 5)))
+    total[...] = mine + dot_nn(second_pieces(got_a, got_b, rows), tokens[...])
     put_parts(place, total, out_keep, got_b, part_keep, part_send, out_total)
 
 
@@ -695,33 +705,37 @@
 
     staged = (wq, wk, wv, wo)
 
+    out_own = struct(out_half, f32)
+
     def attend(kernel, after):
         return call(
             kernel,
             (*here, *staged, *after),
-            [half_rows] * 2 + [half_t, struct(out_half, f32), half_send],
+            [half_rows] * 2 + [struct((192 * pairs, width), f32), out_own, half_send],
             32,
             place,
-            scratch=[pltpu.VMEM((rows, width), bf16)] * 2 + [pltpu.VMEM((2, 64 * pairs, rows), bf16)],
+            scratch=[pltpu.VMEM(half_t.shape, bf16)]
+            + [pltpu.VMEM((rows, width), bf16)] * 2
+            + [pltpu.VMEM((2, 64 * pairs, rows), bf16)],
             specs=[VMEM_SPEC] * 8 + [any_spec] * len(after),
         )
 
-    own_a, oth_a, keep_a, out_keep_a, send_a = attend(attend_first, ())
+    own_a, oth_a, part_a, out_keep_a, send_a = attend(attend_first, ())
     got_a = to_x(send_a)
     core_a = to_core(oth_a)
-    own_b, oth_b, keep_b, out_keep_b, send_b = attend(attend_second, (from_x,))
+    own_b, oth_b, part_b, out_keep_b, send_b = attend(attend_second, (from_x,))
     got_b = to_x(send_b)
     core_b = to_core(oth_b)
 
     def parts_of(kernel, args, tall, scratch, after=()):
         return call(
             kernel,
-            (*args, *here, *there, *after),
+            (*args, *there, *after, *here),
             [struct((2, tall, width), f32), struct((2, tall, width))],
             16,
             place,
-            scratch=[pltpu.VMEM((2 * rows, width), bf16)] + scratch + [pltpu.VMEM(out_half, f32)],
-            specs=[VMEM_SPEC] * (len(args) + 6) + [any_spec] * len(after),
+            scratch=[pltpu.VMEM((rows, width), bf16)] + scratch + [pltpu.VMEM(out_half, f32)],
+            specs=[VMEM_SPEC] * (len(args) + 2) + [any_spec] * (len(after) + 4),
         )
 
     def pair_sums(keep, part):
@@ -742,16 +756,16 @@
 
     keep, part = parts_of(
         weight_first,
-        (keep_a, out_keep_a, got_a),
+        (part_a, out_keep_a, got_a),
         96,
-        [pltpu.VMEM((2, 256, rows), bf16), pltpu.VMEM((256, width), f32)],
+        [pltpu.VMEM((256, width), f32)],
     )
     first_sum, paired, first_got = pair_sums(keep, part)
     keep, part = parts_of(
         weight_second,
-        (keep_a, got_a, keep_b, out_keep_b, got_b),
+        (part_a, part_b, out_keep_b, got_a, got_b),
         160,
-        [pltpu.VMEM((2, 512, rows), bf16), pltpu.VMEM((512, width), f32)],
+        [pltpu.VMEM((512, width), f32)],
         (paired,),
     )
     started = part

time: 124 us -> 124 us (level)
  transfers between devices with their start and end apart: 22 -> 22, of which waited for: 14 -> 14; matrix products, arithmetic and copies ran while one was open for 0% -> 0% of each run, Pallas kernels for 20% -> 21%
where the time goes in v14:
time: 124 us
  waiting for transfers between devices  60 us (48%)
  Pallas kernels  31.1 us (25%)
  starting transfers between devices  31 us (25%)
    ppermute x22, waiting for transfers between devices, send(): return lax.ppermute(value, AXES, line_perm(move, reps))  60 us
    ppermute x22, starting transfers between devices, send(): return lax.ppermute(value, AXES, line_perm(move, reps))  31 us
    pallas_call x12, Pallas kernels, call(): pl.pallas_call(kernel, in_specs=specs, out_specs=VMEM_SPEC if single else...  24.2 us
    pallas_call x1, Pallas kernels, chip_shards(): pl.pallas_call(rows_kernel, grid_spec=pltpu.PrefetchScalarGridSpec(num_sc...  6.87 us
  transfers between devices with their start and end apart: 22, of which 14 were waited for; matrix products, arithmetic and copies ran while one was open for 0% of the time, Pallas kernels for 21%

profile of v14, /device:TPU:9, one launch (start us, length us, event | category | flops | bytes accessed | tf_op | source)
XLA Modules:
  0.0 123.7 jit_solution(7982786961011427666)
XLA Ops:
  1.4 1.9 %shard_map.102 = (bf16[192,1024]{1,0:T(8,128)(2,1)S(1)}, f32[96,1024]{1,0:T(8,128)S(1)}) custom-call(s32[6]{0:T(128)S(1)} %concatenate.6.place, bf16[2,96,1024]{2,1,0:T(8,128)(2,1)} %patch_hbm.3, bf16[2,96,1024]{2,1,0:T(8,128)(2,1)} %cot_hbm.3, s32[2,96]{1,0:T(2,128)} %index_hbm.3, f32[1,1024]{1,0:T(1,128)} %bitcast.6), custom_call_target="tpu_custom_call" | custom-call | flops 1000 | bytes 1000 | tf_op jit(solution)/shard_map/pallas_call | solution.py:625
  3.2 4.8 %collective-permute-start = (bf16[192,1024]{1,0:T(8,128)(2,1)S(1)}, bf16[192,1024]{1,0:T(8,128)(2,1)S(1)}, u32[]{:S(2)}, u32[]{:S(2)}) collective-permute-start(bf16[192,1024]{1,0:T(8,128)(2,1)S(1)} %get-tuple-element.36.after.m0), channel_id=1, source_target_pairs={{0,0},{1,8},{2,2},{3,10},{4,4},{5,12},{6,6},{7,14},{8,1},{9,9},{10... | collective-permute-start | bytes 1179656 | tf_op jit(solution)/shard_map/ppermute | solution.py:651
  8.0 3.2 %shard_map.103 = (bf16[192,1024]{1,0:T(8,128)(2,1)S(1)}, f32[96,1024]{1,0:T(8,128)S(1)}, bf16[1024,512]{1,0:T(8,128)(2,1)S(1)}, bf16[1024,512]{1,0:T(8,128)(2,1)...) custom-call(s32[6]{0:T(128)S(1)} %concatenate.6.place, bf16[2,96,1024]{2,1,0:T(8,128)(2,1)} %patch_hbm.3, ...), custom_call_target="tpu_custom_call" | custom-call | flops 1000 | bytes 1000 | tf_op jit(solution)/shard_map/pallas_call | solution.py:625
  11.3 7.1 %collective-permute-done.refs_0_.p0.refs_1_ = bf16[192,1024]{1,0:T(8,128)(2,1)S(1)} collective-permute-done((bf16[192,1024]{1,0:T(8,128)(2,1)S(1)}, bf16[192,1024]{1,0:T(8,128)(2,1)S(1)}, u32[]{:S(2)}, u32[]{:S(2)}) %collective-permute-start) | collective-permute-done | bytes 393248 | tf_op jit(solution)/shard_map/ppermute | solution.py:651
  18.5 6.8 %collective-permute-done.1.refs_1_.p1.refs_2_ = bf16[192,1024]{1,0:T(8,128)(2,1)S(1)} collective-permute-done((bf16[192,1024]{1,0:T(8,128)(2,1)S(1)}, bf16[192,1024]{1,0:T(8,128)(2,1)S(1)}, u32[]{:S(2)}, u32[]{:S(2)}) %collective-permute-start.1) | collective-permute-done | bytes 393248 | tf_op jit(solution)/shard_map/ppermute | solution.py:651
  25.4 1.3 %collective-permute-start.5 = (bf16[192,1024]{1,0:T(8,128)(2,1)S(1)}, bf16[192,1024]{1,0:T(8,128)(2,1)S(1)}, u32[]{:S(2)}, u32[]{:S(2)}) collective-permute-start(bf16[192,1024]{1,0:T(8,128)(2,1)S(1)} %pad_maximum_fusion), channel_id=1, source_target_pairs={{0,2},{1,3},{2,0},{3,1},{4,6},{5,7},{6,4},{7,5},{8,10},{9,11},{10,... | collective-permute-start | bytes 1179656 | tf_op jit(solution)/shard_map/ppermute | solution.py:651
  27.0 5.6 %shard_map.104 = (bf16[4,192,256]{2,1,0:T(8,128)(2,1)S(1)}, bf16[4,192,256]{2,1,0:T(8,128)(2,1)S(1)}, f32[384,1024]{1,0:T(8,128)S(1)}, f32[128,1024]{1,0:T(8,128)S(1)}, bf16[128,2176]{1,0:T(8,128)(2,1)S(1)}) custom-call(s32[6]{0:T(128)S(1)} %concatenate.6.place, bf16[192,1024]{1,0:T(8,128)(2,1)S(1)} %collective-permute-done.refs_0_.p0.refs_1_, ...), custom_call_target="tpu_custom_call" | custom-call | flops 1000 | bytes 1000 | tf_op jit(solution)/shard_map/pallas_call | solution.py:625
  32.7 1.3 %collective-permute-start.7 = (bf16[128,2176]{1,0:T(8,128)(2,1)S(1)}, bf16[128,2176]{1,0:T(8,128)(2,1)S(1)}, u32[]{:S(2)}, u32[]{:S(2)}) collective-permute-start(bf16[128,2176]{1,0:T(8,128)(2,1)S(1)} %get-tuple-element.49), channel_id=1, source_target_pairs={{0,2},{1,3},{2,0},{3,1},{4,6},{5,7},{6,4},{7,5},{8,10},{9,11},{10,... | collective-permute-start | bytes 1671176 | tf_op jit(solution)/shard_map/ppermute | solution.py:651
  34.0 1.7 %collective-permute-done.5.after.n0 = bf16[192,1024]{1,0:T(8,128)(2,1)S(1)} collective-permute-done((bf16[192,1024]{1,0:T(8,128)(2,1)S(1)}, bf16[192,1024]{1,0:T(8,128)(2,1)S(1)}, u32[]{:S(2)}, u32[]{:S(2)}) %collective-permute-start.5) | collective-permute-done | bytes 393248 | tf_op jit(solution)/shard_map/ppermute | solution.py:651
  35.6 2.3 %collective-permute-start.9 = (bf16[192,1024]{1,0:T(8,128)(2,1)S(1)}, bf16[192,1024]{1,0:T(8,128)(2,1)S(1)}, u32[]{:S(2)}, u32[]{:S(2)}) collective-permute-start(bf16[192,1024]{1,0:T(8,128)(2,1)S(1)} %collective-permute-done.5.after.n0), channel_id=1, source_target_pairs={{0,1},{1,0},{2,3},{3,2},{4,5},{5,4},{6,7},{7,6},{8,9},{9,8},{10,11... | collective-permute-start | bytes 1179656 | tf_op jit(solution)/shard_map/ppermute | solution.py:651
  37.9 5.6 %shard_map.105 = (bf16[4,192,256]{2,1,0:T(8,128)(2,1)S(1)}, bf16[4,192,256]{2,1,0:T(8,128)(2,1)S(1)}, f32[384,1024]{1,0:T(8,128)S(1)}, f32[128,1024]{1,0:T(8,128)S(1)}, bf16[128,2176]{1,0:T(8,128)(2,1)S(1)}) custom-call(s32[6]{0:T(128)S(1)} %concatenate.6.place, bf16[192,1024]{1,0:T(8,128)(2,1)S(1)} %collective-permute-done.refs_0_.p0.refs_1_, ...), custom_call_target="tpu_custom_call" | custom-call | flops 1000 | bytes 1000 | tf_op jit(solution)/shard_map/pallas_call | solution.py:625
  43.6 1.3 %collective-permute-start.8 = (bf16[128,2176]{1,0:T(8,128)(2,1)S(1)}, bf16[128,2176]{1,0:T(8,128)(2,1)S(1)}, u32[]{:S(2)}, u32[]{:S(2)}) collective-permute-start(bf16[128,2176]{1,0:T(8,128)(2,1)S(1)} %get-tuple-element.50), channel_id=1, source_target_pairs={{0,2},{1,3},{2,0},{3,1},{4,6},{5,7},{6,4},{7,5},{8,10},{9,11},{10,... | collective-permute-start | bytes 1671176 | tf_op jit(solution)/shard_map/ppermute | solution.py:651
  44.9 2.7 %collective-permute-done.7.got.got_a = bf16[128,2176]{1,0:T(8,128)(2,1)S(1)} collective-permute-done((bf16[128,2176]{1,0:T(8,128)(2,1)S(1)}, bf16[128,2176]{1,0:T(8,128)(2,1)S(1)}, u32[]{:S(2)}, u32[]{:S(2)}) %collective-permute-start.7) | collective-permute-done | bytes 557088 | tf_op jit(solution)/shard_map/ppermute | solution.py:651
  48.8 8.3 %collective-permute-done.10.got = bf16[2,96,1024]{2,1,0:T(8,128)(2,1)S(1)} collective-permute-done((bf16[2,96,1024]{2,1,0:T(8,128)(2,1)S(1)}, bf16[2,96,1024]{2,1,0:T(8,128)(2,1)S(1)}, u32[]{:S(2)}, u32[]{:S(2)}) %collective-permute-start.10) | collective-permute-done | bytes 393248 | tf_op jit(solution)/shard_map/ppermute | solution.py:651
  57.1 2.4 %collective-permute-done.8.got_b = bf16[128,2176]{1,0:T(8,128)(2,1)S(1)} collective-permute-done((bf16[128,2176]{1,0:T(8,128)(2,1)S(1)}, bf16[128,2176]{1,0:T(8,128)(2,1)S(1)}, u32[]{:S(2)}, u32[]{:S(2)}) %collective-permute-start.8) | collective-permute-done | bytes 557088 | tf_op jit(solution)/shard_map/ppermute | solution.py:651
  59.5 1.5 %shard_map.108 = (f32[2,160,1024]{2,1,0:T(8,128)S(1)}, bf16[2,160,1024]{2,1,0:T(8,128)(2,1)S(1)}) custom-call(s32[6]{0:T(128)S(1)} %concatenate.6.place, f32[384,1024]{1,0:T(8,128)S(1)} %get-tuple-element.46.own.a, f32[384,1024]{1,0:T(8,128)S(1)} %get-tuple-element.47.b, f32[128,1024]{1,0:T(8,128)S(1)} %get-tuple-element.48.out_keep, ...), custom_call_target="tpu_custom_call" | custom-call | flops 1000 | bytes 1000 | tf_op jit(solution)/shard_map/pallas_call | solution.py:625
  61.0 4.3 %collective-permute-start.11 = (bf16[96,1024]{1,0:T(8,128)(2,1)S(1)}, bf16[96,1024]{1,0:T(8,128)(2,1)S(1)}, u32[]{:S(2)}, u32[]{:S(2)}) collective-permute-start(bf16[96,1024]{1,0:T(8,128)(2,1)S(1)} %get-tuple-element.54.refs_0_), channel_id=1, source_target_pairs={{0,8},{1,9},{2,10},{3,11},{4,12},{5,13},{6,14},{7,15},{8,0},{9,1},... | collective-permute-start | bytes 589832 | tf_op jit(solution)/shard_map/ppermute | solution.py:651
  65.4 1.4 %collective-permute-start.4 = (bf16[4,192,256]{2,1,0:T(8,128)(2,1)S(1)}, bf16[4,192,256]{2,1,0:T(8,128)(2,1)S(1)}, u32[]{:S(2)}, u32[]{:S(2)}) collective-permute-start(bf16[4,192,256]{2,1,0:T(8,128)(2,1)S(1)} %get-tuple-element.43), channel_id=1, source_target_pairs={{0,1},{1,0},{2,3},{3,2},{4,5},{5,4},{6,7},{7,6},{8,9},{9,8},{10,11... | collective-permute-start | bytes 1179656 | tf_op jit(solution)/shard_map/ppermute | solution.py:651
  66.8 16.7 %collective-permute-done.11.got = bf16[96,1024]{1,0:T(8,128)(2,1)S(1)} collective-permute-done((bf16[96,1024]{1,0:T(8,128)(2,1)S(1)}, bf16[96,1024]{1,0:T(8,128)(2,1)S(1)}, u32[]{:S(2)}, u32[]{:S(2)}) %collective-permute-start.11) | collective-permute-done | bytes 196640 | tf_op jit(solution)/shard_map/ppermute | solution.py:651
  83.5 1.3 %collective-permute-start.12 = (bf16[96,1024]{1,0:T(8,128)(2,1)S(1)}, bf16[96,1024]{1,0:T(8,128)(2,1)S(1)}, u32[]{:S(2)}, u32[]{:S(2)}) collective-permute-start(bf16[96,1024]{1,0:T(8,128)(2,1)S(1)} %shard_map.109.a0), channel_id=1, source_target_pairs={{0,2},{1,3},{2,0},{3,1},{4,6},{5,7},{6,4},{7,5},{8,10},{9,11},{10,... | collective-permute-start | bytes 589832 | tf_op jit(solution)/shard_map/ppermute | solution.py:651
  85.0 2.2 %collective-permute-start.15 = (bf16[96,1024]{1,0:T(8,128)(2,1)S(1)}, bf16[96,1024]{1,0:T(8,128)(2,1)S(1)}, u32[]{:S(2)}, u32[]{:S(2)}) collective-permute-start(bf16[96,1024]{1,0:T(8,128)(2,1)S(1)} %shard_map.109.a0), channel_id=1, source_target_pairs={{0,1},{1,0},{2,3},{3,2},{4,5},{5,4},{6,7},{7,6},{8,9},{9,8},{10,11... | collective-permute-start | bytes 589832 | tf_op jit(solution)/shard_map/ppermute | solution.py:651
  88.1 3.0 %collective-permute-start.16 = (bf16[96,1024]{1,0:T(8,128)(2,1)S(1)}, bf16[96,1024]{1,0:T(8,128)(2,1)S(1)}, u32[]{:S(2)}, u32[]{:S(2)}) collective-permute-start(bf16[96,1024]{1,0:T(8,128)(2,1)S(1)} %collective-permute-done.12.before.refs_1_.a1), channel_id=1, source_target_pairs={{0,1},{1,0},{2,3},{3,2},{4,5},{5,4},{6,7},{7,6},{8,9},{9,8},{10,11... | collective-permute-start | bytes 589832 | tf_op jit(solution)/shard_map/ppermute | solution.py:651
  91.1 6.9 %shard_map.110 = (bf16[192,1024]{1,0:T(8,128)(2,1)S(1)}, bf16[192,1024]{1,0:T(8,128)(2,1)S(1)}) custom-call(s32[6]{0:T(128)S(1)} %concatenate.6.place, bf16[4,192,256]{2,1,0:T(8,128)(2,1)S(1)} %get-tuple-element.42.own_a, bf16[4,192,256]{2,1,0:T(8,128)(2,1)S(1)} %collective-permute-done.4.got_a, bf16[4,192,256]{2,1,0:T(8,128)(2,1)S(1)} %get-tuple-element.44.own_b, ...), custom_call_target="tpu_custom_call" | custom-call | flops 1000 | bytes 1000 | tf_op jit(solution)/shard_map/pallas_call | solution.py:775
  98.2 1.2 collective-permute-start.19
  99.4 4.8 %collective-permute-start.13 = (bf16[192,1024]{1,0:T(8,128)(2,1)S(1)}, bf16[192,1024]{1,0:T(8,128)(2,1)S(1)}, u32[]{:S(2)}, u32[]{:S(2)}) collective-permute-start(bf16[192,1024]{1,0:T(8,128)(2,1)S(1)} %get-tuple-element.57.refs_0_), channel_id=1, source_target_pairs={{0,0},{1,8},{2,2},{3,10},{4,4},{5,12},{6,6},{7,14},{8,1},{9,9},{10... | collective-permute-start | bytes 1179656 | tf_op jit(solution)/shard_map/ppermute | solution.py:651
  104.4 2.7 %collective-permute-done.19.b1 = bf16[160,1024]{1,0:T(8,128)(2,1)S(1)} collective-permute-done((bf16[160,1024]{1,0:T(8,128)(2,1)S(1)}, bf16[160,1024]{1,0:T(8,128)(2,1)S(1)}, u32[]{:S(2)}, u32[]{:S(2)}) %collective-permute-start.19) | collective-permute-done | bytes 327712 | tf_op jit(solution)/shard_map/ppermute | solution.py:651
  107.1 1.3 %collective-permute-start.21 = (bf16[160,1024]{1,0:T(8,128)(2,1)S(1)}, bf16[160,1024]{1,0:T(8,128)(2,1)S(1)}, u32[]{:S(2)}, u32[]{:S(2)}) collective-permute-start(bf16[160,1024]{1,0:T(8,128)(2,1)S(1)} %collective-permute-done.19.b1), channel_id=1, source_target_pairs={{0,1},{1,0},{2,3},{3,2},{4,5},{5,4},{6,7},{7,6},{8,9},{9,8},{10,11... | collective-permute-start | bytes 983048 | tf_op jit(solution)/shard_map/ppermute | solution.py:651
  108.4 1.3 %collective-permute-done.21.b3 = bf16[160,1024]{1,0:T(8,128)(2,1)S(1)} collective-permute-done((bf16[160,1024]{1,0:T(8,128)(2,1)S(1)}, bf16[160,1024]{1,0:T(8,128)(2,1)S(1)}, u32[]{:S(2)}, u32[]{:S(2)}) %collective-permute-start.21) | collective-permute-done | bytes 327712 | tf_op jit(solution)/shard_map/ppermute | solution.py:651
  109.7 3.0 %shard_map.113 = (f32[1024,768]{1,0:T(8,128)}, f32[1024,256]{1,0:T(8,128)}) custom-call(s32[6]{0:T(128)S(1)} %concatenate.6.place, bf16[96,1024]{1,0:T(8,128)(2,1)S(1)} %shard_map.109.a0, bf16[96,1024]{1,0:T(8,128)(2,1)S(1)} %collective-permute-done.12.before.refs_1_.a1, bf16[96,1024]{1,0:T(8,128)(2,1)S(1)} %collective-permute-done.15.refs_2_.a2, ...), custom_call_target="tpu_custom_call" | custom-call | flops 1000 | bytes 1000 | tf_op jit(solution)/shard_map/pallas_call | solution.py:625
  112.7 4.0 %collective-permute-done.13.r0 = bf16[192,1024]{1,0:T(8,128)(2,1)S(1)} collective-permute-done((bf16[192,1024]{1,0:T(8,128)(2,1)S(1)}, bf16[192,1024]{1,0:T(8,128)(2,1)S(1)}, u32[]{:S(2)}, u32[]{:S(2)}) %collective-permute-start.13) | collective-permute-done | bytes 393248 | tf_op jit(solution)/shard_map/ppermute | solution.py:651
  116.7 5.1 %collective-permute-done.14.r1 = bf16[192,1024]{1,0:T(8,128)(2,1)S(1)} collective-permute-done((bf16[192,1024]{1,0:T(8,128)(2,1)S(1)}, bf16[192,1024]{1,0:T(8,128)(2,1)S(1)}, u32[]{:S(2)}, u32[]{:S(2)}) %collective-permute-start.14) | collective-permute-done | bytes 393248 | tf_op jit(solution)/shard_map/ppermute | solution.py:651
  121.8 1.9 %shard_map.114 = (bf16[2,96,1024]{2,1,0:T(8,128)(2,1)}, bf16[2,96,1024]{2,1,0:T(8,128)(2,1)}) custom-call(s32[6]{0:T(128)S(1)} %concatenate.6.place, bf16[192,1024]{1,0:T(8,128)(2,1)S(1)} %collective-permute-done.13.r0, bf16[192,1024]{1,0:T(8,128)(2,1)S(1)} %collective-permute-done.14.r1, f32[96,1024]{1,0:T(8,128)S(1)} %get-tuple-element.59.h0, ...), custom_call_target="tpu_custom_call" | custom-call | flops 1000 | bytes 1000 | tf_op jit(solution)/shard_map/pallas_call | solution.py:625
  (31 shorter events, 4.0 us)
Async XLA Ops:
  3.2 15.2 %collective-permute-start = (bf16[192,1024]{1,0:T(8,128)(2,1)S(1)}, bf16[192,1024]{1,0:T(8,128)(2,1)S(1)}, u32[]{:S(2)}, u32[]{:S(2)}) collective-permute-start(bf16[192,1024]{1,0:T(8,128)(2,1)S(1)} %get-tuple-element.36.after.m0), channel_id=1, source_target_pairs={{0,0},{1,8},{2,2},{3,10},{4,4},{5,12},{6,6},{7,14},{8,1},{9,9},{10... | collective-permute-start | bytes 1179656 | tf_op jit(solution)/shard_map/ppermute | solution.py:651
  11.3 14.0 %collective-permute-start.1 = (bf16[192,1024]{1,0:T(8,128)(2,1)S(1)}, bf16[192,1024]{1,0:T(8,128)(2,1)S(1)}, u32[]{:S(2)}, u32[]{:S(2)}) collective-permute-start(bf16[192,1024]{1,0:T(8,128)(2,1)S(1)} %get-tuple-element.37.m1), channel_id=1, source_target_pairs={{0,4},{1,12},{2,6},{3,14},{4,0},{5,8},{6,2},{7,10},{8,5},{9,13},{1... | collective-permute-start | bytes 1179656 | tf_op jit(solution)/shard_map/ppermute | solution.py:651
  18.5 8.2 %collective-permute-start.2 = (bf16[192,1024]{1,0:T(8,128)(2,1)S(1)}, bf16[192,1024]{1,0:T(8,128)(2,1)S(1)}, u32[]{:S(2)}, u32[]{:S(2)}) collective-permute-start(bf16[192,1024]{1,0:T(8,128)(2,1)S(1)} %collective-permute-done.refs_0_.p0.refs_1_), channel_id=1, source_target_pairs={{0,1},{1,0},{2,3},{3,2},{4,5},{5,4},{6,7},{7,6},{8,9},{9,8},{10,11... | collective-permute-start | bytes 1179656 | tf_op jit(solution)/shard_map/ppermute | solution.py:651
  25.3 1.7 %collective-permute-start.3 = (bf16[192,1024]{1,0:T(8,128)(2,1)S(1)}, bf16[192,1024]{1,0:T(8,128)(2,1)S(1)}, u32[]{:S(2)}, u32[]{:S(2)}) collective-permute-start(bf16[192,1024]{1,0:T(8,128)(2,1)S(1)} %collective-permute-done.1.refs_1_.p1.refs_2_), channel_id=1, source_target_pairs={{0,1},{1,0},{2,3},{3,2},{4,5},{5,4},{6,7},{7,6},{8,9},{9,8},{10,11... | collective-permute-start | bytes 1179656 | tf_op jit(solution)/shard_map/ppermute | solution.py:651
  25.4 10.2 %collective-permute-start.5 = (bf16[192,1024]{1,0:T(8,128)(2,1)S(1)}, bf16[192,1024]{1,0:T(8,128)(2,1)S(1)}, u32[]{:S(2)}, u32[]{:S(2)}) collective-permute-start(bf16[192,1024]{1,0:T(8,128)(2,1)S(1)} %pad_maximum_fusion), channel_id=1, source_target_pairs={{0,2},{1,3},{2,0},{3,1},{4,6},{5,7},{6,4},{7,5},{8,10},{9,11},{10,... | collective-permute-start | bytes 1179656 | tf_op jit(solution)/shard_map/ppermute | solution.py:651
  32.7 14.9 %collective-permute-start.7 = (bf16[128,2176]{1,0:T(8,128)(2,1)S(1)}, bf16[128,2176]{1,0:T(8,128)(2,1)S(1)}, u32[]{:S(2)}, u32[]{:S(2)}) collective-permute-start(bf16[128,2176]{1,0:T(8,128)(2,1)S(1)} %get-tuple-element.49), channel_id=1, source_target_pairs={{0,2},{1,3},{2,0},{3,1},{4,6},{5,7},{6,4},{7,5},{8,10},{9,11},{10,... | collective-permute-start | bytes 1671176 | tf_op jit(solution)/shard_map/ppermute | solution.py:651
  35.6 9.2 %collective-permute-start.9 = (bf16[192,1024]{1,0:T(8,128)(2,1)S(1)}, bf16[192,1024]{1,0:T(8,128)(2,1)S(1)}, u32[]{:S(2)}, u32[]{:S(2)}) collective-permute-start(bf16[192,1024]{1,0:T(8,128)(2,1)S(1)} %collective-permute-done.5.after.n0), channel_id=1, source_target_pairs={{0,1},{1,0},{2,3},{3,2},{4,5},{5,4},{6,7},{7,6},{8,9},{9,8},{10,11... | collective-permute-start | bytes 1179656 | tf_op jit(solution)/shard_map/ppermute | solution.py:651
  43.6 15.9 %collective-permute-start.8 = (bf16[128,2176]{1,0:T(8,128)(2,1)S(1)}, bf16[128,2176]{1,0:T(8,128)(2,1)S(1)}, u32[]{:S(2)}, u32[]{:S(2)}) collective-permute-start(bf16[128,2176]{1,0:T(8,128)(2,1)S(1)} %get-tuple-element.50), channel_id=1, source_target_pairs={{0,2},{1,3},{2,0},{3,1},{4,6},{5,7},{6,4},{7,5},{8,10},{9,11},{10,... | collective-permute-start | bytes 1671176 | tf_op jit(solution)/shard_map/ppermute | solution.py:651
  48.7 8.3 %collective-permute-start.10 = (bf16[2,96,1024]{2,1,0:T(8,128)(2,1)S(1)}, bf16[2,96,1024]{2,1,0:T(8,128)(2,1)S(1)}, u32[]{:S(2)}, u32[]{:S(2)}) collective-permute-start(bf16[2,96,1024]{2,1,0:T(8,128)(2,1)S(1)} %get-tuple-element.53), channel_id=1, source_target_pairs={{0,4},{1,5},{2,6},{3,7},{4,0},{5,1},{6,2},{7,3},{8,12},{9,13},{10,... | collective-permute-start | bytes 1179656 | tf_op jit(solution)/shard_map/ppermute | solution.py:651
  61.0 23.8 %collective-permute-start.17 = (bf16[2,160,1024]{2,1,0:T(8,128)(2,1)S(1)}, bf16[2,160,1024]{2,1,0:T(8,128)(2,1)S(1)}, u32[]{:S(2)}, u32[]{:S(2)}) collective-permute-start(bf16[2,160,1024]{2,1,0:T(8,128)(2,1)S(1)} %get-tuple-element.55.after), channel_id=1, source_target_pairs={{0,4},{1,5},{2,6},{3,7},{4,0},{5,1},{6,2},{7,3},{8,12},{9,13},{10,... | collective-permute-start | bytes 1966088 | tf_op jit(solution)/shard_map/ppermute | solution.py:651
  61.0 22.4 %collective-permute-start.11 = (bf16[96,1024]{1,0:T(8,128)(2,1)S(1)}, bf16[96,1024]{1,0:T(8,128)(2,1)S(1)}, u32[]{:S(2)}, u32[]{:S(2)}) collective-permute-start(bf16[96,1024]{1,0:T(8,128)(2,1)S(1)} %get-tuple-element.54.refs_0_), channel_id=1, source_target_pairs={{0,8},{1,9},{2,10},{3,11},{4,12},{5,13},{6,14},{7,15},{8,0},{9,1},... | collective-permute-start | bytes 589832 | tf_op jit(solution)/shard_map/ppermute | solution.py:651
  65.4 25.8 %collective-permute-start.4 = (bf16[4,192,256]{2,1,0:T(8,128)(2,1)S(1)}, bf16[4,192,256]{2,1,0:T(8,128)(2,1)S(1)}, u32[]{:S(2)}, u32[]{:S(2)}) collective-permute-start(bf16[4,192,256]{2,1,0:T(8,128)(2,1)S(1)} %get-tuple-element.43), channel_id=1, source_target_pairs={{0,1},{1,0},{2,3},{3,2},{4,5},{5,4},{6,7},{7,6},{8,9},{9,8},{10,11... | collective-permute-start | bytes 1179656 | tf_op jit(solution)/shard_map/ppermute | solution.py:651
  66.8 24.3 %collective-permute-start.6 = (bf16[4,192,256]{2,1,0:T(8,128)(2,1)S(1)}, bf16[4,192,256]{2,1,0:T(8,128)(2,1)S(1)}, u32[]{:S(2)}, u32[]{:S(2)}) collective-permute-start(bf16[4,192,256]{2,1,0:T(8,128)(2,1)S(1)} %get-tuple-element.45), channel_id=1, source_target_pairs={{0,1},{1,0},{2,3},{3,2},{4,5},{5,4},{6,7},{7,6},{8,9},{9,8},{10,11... | collective-permute-start | bytes 1179656 | tf_op jit(solution)/shard_map/ppermute | solution.py:651
  83.5 4.6 %collective-permute-start.12 = (bf16[96,1024]{1,0:T(8,128)(2,1)S(1)}, bf16[96,1024]{1,0:T(8,128)(2,1)S(1)}, u32[]{:S(2)}, u32[]{:S(2)}) collective-permute-start(bf16[96,1024]{1,0:T(8,128)(2,1)S(1)} %shard_map.109.a0), channel_id=1, source_target_pairs={{0,2},{1,3},{2,0},{3,1},{4,6},{5,7},{6,4},{7,5},{8,10},{9,11},{10,... | collective-permute-start | bytes 589832 | tf_op jit(solution)/shard_map/ppermute | solution.py:651
  85.0 13.2 %collective-permute-start.18 = (bf16[160,1024]{1,0:T(8,128)(2,1)S(1)}, bf16[160,1024]{1,0:T(8,128)(2,1)S(1)}, u32[]{:S(2)}, u32[]{:S(2)}) collective-permute-start(bf16[160,1024]{1,0:T(8,128)(2,1)S(1)} %get-tuple-element.63), channel_id=1, source_target_pairs={{0,8},{1,9},{2,10},{3,11},{4,12},{5,13},{6,14},{7,15},{8,0},{9,1},... | collective-permute-start | bytes 983048 | tf_op jit(solution)/shard_map/ppermute | solution.py:651
  85.0 13.0 %collective-permute-start.15 = (bf16[96,1024]{1,0:T(8,128)(2,1)S(1)}, bf16[96,1024]{1,0:T(8,128)(2,1)S(1)}, u32[]{:S(2)}, u32[]{:S(2)}) collective-permute-start(bf16[96,1024]{1,0:T(8,128)(2,1)S(1)} %shard_map.109.a0), channel_id=1, source_target_pairs={{0,1},{1,0},{2,3},{3,2},{4,5},{5,4},{6,7},{7,6},{8,9},{9,8},{10,11... | collective-permute-start | bytes 589832 | tf_op jit(solution)/shard_map/ppermute | solution.py:651
  88.1 9.9 %collective-permute-start.16 = (bf16[96,1024]{1,0:T(8,128)(2,1)S(1)}, bf16[96,1024]{1,0:T(8,128)(2,1)S(1)}, u32[]{:S(2)}, u32[]{:S(2)}) collective-permute-start(bf16[96,1024]{1,0:T(8,128)(2,1)S(1)} %collective-permute-done.12.before.refs_1_.a1), channel_id=1, source_target_pairs={{0,1},{1,0},{2,3},{3,2},{4,5},{5,4},{6,7},{7,6},{8,9},{9,8},{10,11... | collective-permute-start | bytes 589832 | tf_op jit(solution)/shard_map/ppermute | solution.py:651
  98.2 23.6 %copy-start = (f32[1024]{0:T(1024)S(1)}, f32[1024]{0:T(1024)}, u32[]{:S(2)}) copy-start(f32[1024]{0:T(1024)} %param.13) | copy-start | bytes 12292
  98.2 8.9 %collective-permute-start.19 = (bf16[160,1024]{1,0:T(8,128)(2,1)S(1)}, bf16[160,1024]{1,0:T(8,128)(2,1)S(1)}, u32[]{:S(2)}, u32[]{:S(2)}) collective-permute-start(bf16[160,1024]{1,0:T(8,128)(2,1)S(1)} %shard_map.112.b0), channel_id=1, source_target_pairs={{0,2},{1,3},{2,0},{3,1},{4,6},{5,7},{6,4},{7,5},{8,10},{9,11},{10,... | collective-permute-start | bytes 983048 | tf_op jit(solution)/shard_map/ppermute | solution.py:651
  99.4 17.3 %collective-permute-start.13 = (bf16[192,1024]{1,0:T(8,128)(2,1)S(1)}, bf16[192,1024]{1,0:T(8,128)(2,1)S(1)}, u32[]{:S(2)}, u32[]{:S(2)}) collective-permute-start(bf16[192,1024]{1,0:T(8,128)(2,1)S(1)} %get-tuple-element.57.refs_0_), channel_id=1, source_target_pairs={{0,0},{1,8},{2,2},{3,10},{4,4},{5,12},{6,6},{7,14},{8,1},{9,9},{10... | collective-permute-start | bytes 1179656 | tf_op jit(solution)/shard_map/ppermute | solution.py:651
  104.2 17.6 %collective-permute-start.14 = (bf16[192,1024]{1,0:T(8,128)(2,1)S(1)}, bf16[192,1024]{1,0:T(8,128)(2,1)S(1)}, u32[]{:S(2)}, u32[]{:S(2)}) collective-permute-start(bf16[192,1024]{1,0:T(8,128)(2,1)S(1)} %get-tuple-element.58), channel_id=1, source_target_pairs={{0,4},{1,12},{2,6},{3,14},{4,0},{5,8},{6,2},{7,10},{8,5},{9,13},{1... | collective-permute-start | bytes 1179656 | tf_op jit(solution)/shard_map/ppermute | solution.py:651
  104.3 4.1 %collective-permute-start.20 = (bf16[160,1024]{1,0:T(8,128)(2,1)S(1)}, bf16[160,1024]{1,0:T(8,128)(2,1)S(1)}, u32[]{:S(2)}, u32[]{:S(2)}) collective-permute-start(bf16[160,1024]{1,0:T(8,128)(2,1)S(1)} %shard_map.112.b0), channel_id=1, source_target_pairs={{0,1},{1,0},{2,3},{3,2},{4,5},{5,4},{6,7},{7,6},{8,9},{9,8},{10,11... | collective-permute-start | bytes 983048 | tf_op jit(solution)/shard_map/ppermute | solution.py:651
  107.1 2.6 %collective-permute-start.21 = (bf16[160,1024]{1,0:T(8,128)(2,1)S(1)}, bf16[160,1024]{1,0:T(8,128)(2,1)S(1)}, u32[]{:S(2)}, u32[]{:S(2)}) collective-permute-start(bf16[160,1024]{1,0:T(8,128)(2,1)S(1)} %collective-permute-done.19.b1), channel_id=1, source_target_pairs={{0,1},{1,0},{2,3},{3,2},{4,5},{5,4},{6,7},{7,6},{8,9},{9,8},{10,11... | collective-permute-start | bytes 983048 | tf_op jit(solution)/shard_map/ppermute | solution.py:651
